TPU v7x, 32 devices: a whole 2x2x4 slice. The times are simulated.
32 devices in a mesh: rep: 2 (over y), gx: 4 (over z), gy: 2 (over x), gz: 2 (over core).
Axes of the slice: x: 2, y: 2, z: 4, core: 2. Of those that a mesh axis runs over, the one named last changes fastest.
Arguments:
- hidden: bfloat16 [128, 16384], P(('rep', 'gx'), ('gy', 'gz')), parts along dimension 0
- attention_norm_gain: bfloat16 [16384], P(('gy', 'gz')), may hold values from 0.099609375 to 1.8984375
- query_weight: bfloat16 [16384, 16384], P(('gy', 'gz'), 'gx'), may hold values from -0.046875 to 0.046875
- slot_down_factors: bfloat16 [4, 16384, 64], P('gx', ('gy', 'gz')), may hold values from -0.046875 to 0.046875
- adapter_up_factors: bfloat16 [4, 64, 16384], P(None, None, 'gx'), may hold values from -0.75 to 0.75
- adapter_of_row: int32 [128], P('rep'), parts along dimension 0, may hold values from 0 to 4, as said below
- padded_adapter_rank: int32 [4], replicated, may hold values from 16 to 64, as said below
- adapter_in_slot: int32 [4], replicated, may hold values from 0 to 3, each once
- segment_starts: int32 [10], P('rep'), parts along dimension 0, may hold values from 0 to 34, as said below
Outputs:
- query: bfloat16 [128, 16384], P(('rep', 'gy', 'gz'), 'gx'), parts along dimension 0
There are 2 independent parts, one for each index of `rep`. A program takes and returns all parts, laid end to end along the dimension named above; an argument that names none is the same for every part. Nothing has to cross between parts.
Inputs may be any that keep to these rules, and one draw needn't show every extreme that they name: `adapter_of_row`: Non-decreasing; rows of adapter a lie from segment_starts[a] to segment_starts[a+1] - 1; rows from segment_starts[4] on have 4. Every adapter has 1 to 16 rows, one has exactly 16 and one exactly 1. `padded_adapter_rank`: multiples of 16; some adapter has 64 and some 16. segment_starts[0] = 0, increasing, consistent with adapter_of_row; segment_starts[4] is the number of adapted rows. `adapter_in_slot`: storage slot s lies on index s // 1 of gx.
All inputs are finite; a program needn't handle non-finite values.
Results may differ from a plain program's by a relative error of at most 0.0052.
Values may be sent and summed in bfloat16 or wider, within the bound.
No kernel may reach another device: no remote copies, remote signals or barrier semaphores. Data moves between devices by JAX's collectives and lax.ppermute only.
A program may use at most 128 MiB of HBM per device.

v0:
```python
import jax
import jax.numpy as jnp
from jax import lax
from jax.sharding import PartitionSpec as P

EPSILON = 1e-05
ADAPTER_ALPHA = 32.0


def body(
    hidden,
    attention_norm_gain,
    query_weight,
    slot_down_factors,
    adapter_up_factors,
    adapter_of_row,
    padded_adapter_rank,
    adapter_in_slot,
    segment_starts,
):
    groups = lax.axis_size(("gy", "gz"))
    width = hidden.shape[1] * groups
    gain_f32 = attention_norm_gain.astype(jnp.float32)
    own_f32 = hidden.astype(jnp.float32)
    partial_sq = jnp.sum(own_f32 * own_f32, axis=1, keepdims=True)
    total_sq = lax.psum(partial_sq, ("gy", "gz"))
    own_normed = (own_f32 * lax.rsqrt(total_sq / width + EPSILON) * gain_f32).astype(jnp.bfloat16)
    normed = lax.all_gather(own_normed, "gx", axis=0, tiled=True)
    rows_total = normed.shape[0]
    rows_here = rows_total // groups
    plain_query_rows = lax.psum_scatter(
        jnp.dot(normed, query_weight, preferred_element_type=jnp.float32),
        ("gy", "gz"),
        scatter_dimension=0,
        tiled=True,
    )
    adapter_total = padded_adapter_rank.shape[0]
    rank_columns = slot_down_factors.shape[2]
    capacity = rows_total // adapter_total
    per_slot_result = slot_down_factors.shape[0]
    home_index = lax.axis_index("gx")
    padded = jnp.concatenate([normed, jnp.zeros((capacity, normed.shape[1]), jnp.bfloat16)], axis=0)
    padded_ids = jnp.concatenate(
        [adapter_of_row, jnp.full((capacity,), adapter_total, jnp.int32)], axis=0
    )
    collected = jnp.zeros((rows_total + capacity, rank_columns), jnp.float32)
    row_offsets = jnp.arange(capacity, dtype=jnp.int32)
    col_offsets = jnp.arange(rank_columns, dtype=jnp.int32)
    adapter_id = adapter_in_slot[home_index * per_slot_result + 0]
    seg_begin = segment_starts[adapter_id]
    seg_finish = segment_starts[adapter_id + 1]
    local_rank = padded_adapter_rank[adapter_id]
    segment_rows = lax.dynamic_slice_in_dim(padded, seg_begin, capacity, 0)
    segment_ids = lax.dynamic_slice_in_dim(padded_ids, seg_begin, capacity, 0)
    query_projected = jnp.dot(
        segment_rows, slot_down_factors[0], preferred_element_type=jnp.float32
    )
    row_live = (seg_begin + row_offsets < seg_finish) & (segment_ids == adapter_id)
    live_mask = row_live[:, None] & (col_offsets < local_rank)[None, :]
    scaled_delta = jnp.where(
        live_mask,
        query_projected * (ADAPTER_ALPHA / local_rank.astype(jnp.float32)),
        jnp.zeros((), jnp.float32),
    )
    collected = lax.dynamic_update_slice_in_dim(collected, scaled_delta, seg_begin, 0)
    down_terms = collected[:rows_total]
    block_index = lax.axis_index(("gy", "gz"))
    summed_all = lax.psum(down_terms, ("gx", "gy", "gz"))
    down_here = lax.dynamic_slice_in_dim(summed_all, block_index * rows_here, rows_here, 0)
    down_bf16 = down_here.astype(jnp.bfloat16)
    ids_here = lax.dynamic_slice_in_dim(adapter_of_row, block_index * rows_here, rows_here, 0)
    onehot = ids_here[:, None] == jnp.arange(adapter_total, dtype=jnp.int32)[None, :]
    spread_rows = jnp.where(onehot[:, :, None], down_bf16[:, None, :], jnp.zeros((), jnp.bfloat16))
    spread_rows = spread_rows.reshape(rows_here, adapter_total * rank_columns)
    flattened_up = adapter_up_factors.reshape(
        adapter_total * rank_columns, adapter_up_factors.shape[2]
    )
    adapter_delta = jnp.dot(spread_rows, flattened_up, preferred_element_type=jnp.float32)
    return (plain_query_rows + adapter_delta).astype(jnp.bfloat16)


def solution(mesh):
    return jax.shard_map(
        body,
        mesh=mesh,
        in_specs=(
            P(("rep", "gx"), ("gy", "gz")),
            P(("gy", "gz")),
            P(("gy", "gz"), "gx"),
            P("gx", ("gy", "gz"), None),
            P(None, None, "gx"),
            P("rep"),
            P(),
            P(),
            P("rep"),
        ),
        out_specs=P(("rep", "gy", "gz"), "gx"),
        check_vma=False,
    )
```

profile of v0, /device:TPU:0, one launch (start us, length us, event | category | flops | bytes accessed | tf_op | source)
XLA Modules:
  0.0 127.1 jit_solution(15466475408509075988)
XLA Ops:
  6.5 0.0 copy-start
  6.5 0.0 copy-start.1
  6.6 0.0 reduce-scatter.2.cloned.1.call-start
  6.6 1.2 fusion.4
  7.8 8.3 %psum.14 = f32[16,1]{0,1:T(1,128)S(1)} all-reduce(f32[16,1]{0,1:T(1,128)S(1)} %bitcast.19), channel_id=1, replica_groups=mesh['rep'=2,'gx'=4,'gy'=2,'gz'=2] {'gy','gz'}, use_global_device_ids=true, to_apply=%region_1.0 | all-reduce | flops 16 | bytes 128 | tf_op jit(solution)/shard_map/psum | solution.py:26
  16.2 0.7 convert_element_type.19
  16.9 1.0 fusion.6
  17.9 15.5 %all_gather.3 = bf16[64,4096]{1,0:T(8,128)(2,1)S(1)} all-gather(bf16[16,4096]{1,0:T(8,128)(2,1)S(1)} %fusion.6), channel_id=1, replica_groups=mesh['rep'=2,'gx'=4,'gy'=2,'gz'=2] {'gx'}, dimensions={0}, use_global_device_ids=true | all-gather | bytes 655360 | tf_op jit(solution)/shard_map/all_gather | solution.py:28
  33.4 14.6 %fusion.15 = f32[64,4096]{1,0:T(8,128)} fusion(bf16[64,4096]{1,0:T(8,128)(2,1)S(1)} %all_gather.3, bf16[4096,4096]{1,0:T(8,128)(2,1)} %param.11), kind=kOutput, calls=%fused_computation.25 | convolution fusion | flops 2147483648 | bytes 35127296 | tf_op jit(solution)/shard_map/dot_general | solution.py:32
  47.9 0.0 reduce-scatter.2.cloned.1.call-update
  47.9 0.0 copy-done.4
  47.9 0.6 dynamic_slice.25
  53.1 0.0 copy-done.5
  53.1 0.7 dynamic_slice.29
  54.4 0.0 copy-done.2
  54.4 0.6 fusion.14
  57.0 0.1 dynamic_slice.24
  57.1 0.7 iota_compare_fusion.1
  57.8 2.0 %compare_and_fusion = pred[16]{0:T(512)(128)(4,1)S(1)} fusion(s32[]{:T(128)S(6)} %select_n.33, s32[64]{0:T(128)S(1)} %copy-done.3, s32[]{:T(128)} %bitcast.2, s32[]{:T(128)} %bitcast.4, s32[]{:T(128)} %bitcast.3), kind=kLoop, calls=%fused_computation.18 | loop fusion | flops 64 | bytes 288 | tf_op jit(solution)/shard_map/and | solution.py:58
  59.7 0.2 fusion.2
  60.0 0.2 dynamic_update_slice.3
  60.2 57.8 %psum.15 = bf16[64,64]{1,0:T(8,128)(2,1)S(1)} all-reduce(f32[64,64]{1,0:T(8,128)S(1)} %slice.4), channel_id=1, replica_groups=mesh['rep'=2,'gx'=4,'gy'=2,'gz'=2] {'gx','gy','gz'}, use_global_device_ids=true, to_apply=%region_3.4 | all-reduce | flops 4096 | bytes 24576 | tf_op jit(solution)/shard_map/psum | solution.py:68
  118.1 0.0 reduce-scatter.2.cloned.1.call-done
  118.1 2.1 %fusion.1 = bf16[16,4096]{1,0:T(8,128)(2,1)} fusion(f32[16,4096]{1,0:T(8,128)} %reduce-scatter.2.cloned.1.call-done, bf16[4,64,4096]{2,1,0:T(8,128)(2,1)S(1)} %copy-done, pred[16,4]{0,1:T(4,128)(4,1)S(1)} %iota_compare_fusion, bf16[16,64]{1,0:T(8,128)(2,1)S(1)} %dynamic-slice_convert_fusion), kind=kOutput, calls=%fused_computation.2 | convolution fusion | flops 33689600 | bytes 2492480 | tf_op jit(solution)/shard_map/dot_general | solution.py:78
  (12 shorter events, 0.0 us)
Async XLA Ops:
  6.5 111.6 %copy-start = (bf16[4,64,4096]{2,1,0:T(8,128)(2,1)S(1)}, bf16[4,64,4096]{2,1,0:T(8,128)(2,1)}, u32[]{:S(2)}) copy-start(bf16[4,64,4096]{2,1,0:T(8,128)(2,1)} %param.13) | copy-start | bytes 6291460
  6.5 41.4 %copy-start.4 = (s32[4]{0:T(128)S(1)}, s32[4]{0:T(128)}, u32[]{:S(2)}) copy-start(s32[4]{0:T(128)} %param.16) | copy-start | bytes 52
  6.5 46.5 %copy-start.5 = (s32[4]{0:T(128)S(1)}, s32[4]{0:T(128)}, u32[]{:S(2)}) copy-start(s32[4]{0:T(128)} %param.15) | copy-start | bytes 52
  6.5 47.9 %copy-start.2 = (s32[5]{0:T(128)S(1)}, s32[5]{0:T(128)}, u32[]{:S(2)}) copy-start(s32[5]{0:T(128)} %param.17) | copy-start | bytes 64
  6.5 50.4 %copy-start.3 = (s32[64]{0:T(128)S(1)}, s32[64]{0:T(128)}, u32[]{:S(2)}) copy-start(s32[64]{0:T(128)} %param.14) | copy-start | bytes 772
  6.5 53.2 %copy-start.1 = (bf16[1,4096,64]{1,2,0:T(8,128)(2,1)S(1)}, bf16[1,4096,64]{1,2,0:T(8,128)(2,1)}, u32[]{:S(2)}) copy-start(bf16[1,4096,64]{1,2,0:T(8,128)(2,1)} %param.12) | copy-start | bytes 1572868
  6.6 111.5 %reduce-scatter.2.cloned.1.call-start = ((), (), s32[]{:S(2)}) async-start(), calls=%async_computation.1 | async-start | bytes 1310720 | tf_op jit(solution)/shard_map/reduce_scatter | solution.py:31
Sparse Core Ops, SparseCore 0:
  48.1 26.1 reduce-scatter.1
where the time goes:
time: 127 us
  blocking collectives  81.7 us (64%)
  between operations  20.7 us (16%)
  matrix products  16.9 us (13%)
  other arithmetic  5.58 us (4%)
  local copies, waits for them, and re-layouts  2.16 us (2%)
    psum x1, blocking collectives, body(): summed_all = lax.psum(down_terms, ('gx', 'gy', 'gz'))  57.8 us
    all_gather x1, blocking collectives, body(): normed = lax.all_gather(own_normed, 'gx', axis=0, tiled=True)  15.5 us
    dot_general x1, matrix products, body(): jnp.dot(normed, query_weight, preferred_element_type=jnp.float32)  14.6 us
    psum x1, blocking collectives, body(): total_sq = lax.psum(partial_sq, ('gy', 'gz'))  8.34 us
  transfers between devices with their start and end apart: 1, of which 0 were waited for; matrix products, arithmetic and copies ran while one was open for 4% of the time, Pallas kernels for 0%

commit v1 on v0

v1 whole, which is shorter than its diff:
```python
import functools

import jax
import jax.numpy as jnp
from jax import lax
from jax.experimental import pallas as pl
from jax.experimental.pallas import tpu as pltpu
from jax.sharding import PartitionSpec as P

EPSILON = 1e-05
ADAPTER_ALPHA = 32.0
LANES = 128
MIB = 1 << 20

VMEM = pl.BlockSpec(memory_space=pltpu.VMEM)
SMEM = pl.BlockSpec(memory_space=pltpu.SMEM)
ANY = pl.BlockSpec(memory_space=pl.ANY)


def params(mib):
    return pltpu.CompilerParams(vmem_limit_bytes=mib * MIB)


def cost(flops, moved):
    return pl.CostEstimate(flops=flops, bytes_accessed=moved, transcendentals=0)


def fetch_kernel(pieces, w_hbm, gain_ref, *refs):
    gain_out, chunks, sems = refs[0], refs[1:-1], refs[-1]
    depth = w_hbm.shape[0] // pieces
    copies = []
    first = 0
    for c, chunk in enumerate(chunks):
        width = chunk.shape[1]
        for p in range(pieces):
            here = pl.ds(p * depth, depth)
            copies.append(
                pltpu.make_async_copy(
                    w_hbm.at[here, pl.ds(first, width)], chunk.at[here], sems.at[c, p]
                )
            )
        first += width
    for copy in copies:
        copy.start()
    gain_out[...] = gain_ref[...].astype(jnp.float32)
    for copy in copies:
        copy.wait()


def rows_kernel(n, *refs):
    place, rank_ref, slot_ref, start_ref, gain_ref, down_ref = refs[:6]
    blocks = refs[6 : 6 + n]
    x_ref, small_ref = refs[6 + n :]
    home = place[0]
    block_rows = blocks[0].shape[0]
    rows = n * block_rows
    gain = gain_ref[...]
    for k in range(n):
        source = lax.rem(home - k + n, n)
        begin = pl.multiple_of(source * block_rows, block_rows)
        values = blocks[k][...].astype(jnp.float32)
        squares = jnp.sum(values * values, axis=1, keepdims=True)
        x_ref[pl.ds(begin, block_rows), :] = (values * gain).astype(jnp.bfloat16)
        small_ref[pl.ds(begin, block_rows), LANES:] = jnp.broadcast_to(squares, (block_rows, LANES))
    slots, rank_columns = down_ref.shape[0], down_ref.shape[1]
    row = lax.broadcasted_iota(jnp.int32, (rows, rank_columns), 0)
    col = lax.broadcasted_iota(jnp.int32, (rows, rank_columns), 1)
    total = jnp.zeros((rows, rank_columns), jnp.float32)
    for s in range(slots):
        adapter = slot_ref[home * slots + s]
        rank = rank_ref[adapter]
        live = (row >= start_ref[adapter]) & (row < start_ref[adapter + 1]) & (col < rank)
        projected = lax.dot_general(
            x_ref[...], down_ref[s], (((1,), (1,)), ((), ())), preferred_element_type=jnp.float32
        )
        scale = ADAPTER_ALPHA / jnp.full((rows, rank_columns), rank, jnp.int32).astype(jnp.float32)
        total = total + jnp.where(live, projected * scale, 0.0)
    small_ref[:, :LANES] = jnp.zeros((rows, LANES), jnp.float32)
    small_ref[:, :rank_columns] = total


def slice_kernel(n, offset, place, small_ref, *outs):
    g = place[1]
    rows_here = outs[0].shape[0]
    for k in range(n):
        owner = offset(g, k)
        begin = pl.multiple_of(owner * rows_here, rows_here)
        outs[k][...] = small_ref[pl.ds(begin, rows_here), :]


def chunk_kernel(n, offset, step, place, x_ref, w_ref, *refs):
    outs, acc = refs[:n], refs[n]
    g = place[1]
    rows_here, width = outs[0].shape
    for c in range(0, width, step):
        acc[:, c : c + step] = jnp.dot(
            x_ref[...], w_ref[:, c : c + step], preferred_element_type=jnp.float32
        )
    for k in range(n):
        begin = pl.multiple_of(offset(g, k) * rows_here, rows_here)
        outs[k][...] = acc[pl.ds(begin, rows_here), :].astype(outs[k].dtype)


def final_kernel(n, n_small, n_down, chunks, width, *refs):
    place, start_ref, up_ref = refs[:3]
    refs = refs[3:]
    smalls, refs = refs[:n_small], refs[n_small:]
    downs, refs = refs[:n_down], refs[n_down:]
    parts, out_ref = refs[: n * chunks], refs[n * chunks]
    g = place[1]
    rows_here = out_ref.shape[0]
    adapters, rank_columns, _ = up_ref.shape
    own = smalls[0][...]
    for other in smalls[1:]:
        own = own + other[...]
    mean_sq = own[:, LANES : LANES + 1] / width
    scale = lax.rsqrt(mean_sq + EPSILON)
    down = own[:, :rank_columns]
    for other in downs:
        down = down + other[:, :rank_columns]
    live_rows = mean_sq < jnp.inf
    down = jnp.where(live_rows, down * scale, 0.0).astype(jnp.bfloat16)
    row = lax.broadcasted_iota(jnp.int32, (rows_here, rank_columns), 0) + g * rows_here
    spread = jnp.concatenate(
        [
            jnp.where((row >= start_ref[a]) & (row < start_ref[a + 1]), down, jnp.zeros_like(down))
            for a in range(adapters)
        ],
        axis=1,
    )
    columns = out_ref.shape[1] // chunks
    for c in range(chunks):
        here = slice(c * columns, (c + 1) * columns)
        delta = jnp.zeros((rows_here, columns), jnp.float32)
        total = parts[c * n][...]
        for k in range(1, n):
            total = total + parts[c * n + k][...].astype(jnp.float32)
        up = up_ref[:, :, here].reshape(adapters * rank_columns, columns)
        delta = jnp.dot(spread, up, preferred_element_type=jnp.float32)
        base = jnp.where(live_rows, total * scale, 0.0)
        out_ref[:, here] = (base + delta).astype(out_ref.dtype)


def body(
    hidden,
    attention_norm_gain,
    query_weight,
    slot_down_factors,
    adapter_up_factors,
    adapter_of_row,
    padded_adapter_rank,
    adapter_in_slot,
    segment_starts,
):
    n_x, n_y, n_z = lax.axis_size("gx"), lax.axis_size("gy"), lax.axis_size("gz")
    groups = n_y * n_z
    block_rows, depth = hidden.shape
    columns = query_weight.shape[1]
    rows = n_x * block_rows
    rows_here = rows // groups
    home = lax.axis_index("gx")
    place = jnp.stack([home, lax.axis_index(("gy", "gz"))]).astype(jnp.int32)

    def offset(g, k):
        y = lax.rem(g // n_z + k // n_z, n_y)
        z = lax.rem(lax.rem(g, n_z) + k % n_z, n_z)
        return y * n_z + z

    def send_x(value, k):
        return lax.ppermute(value, "gx", [(j, (j + k) % n_x) for j in range(n_x)])

    def send_g(value, k):
        pairs = []
        for g in range(groups):
            y, z = (g // n_z + k // n_z) % n_y, (g % n_z + k % n_z) % n_z
            pairs.append((g, y * n_z + z))
        return lax.ppermute(value, ("gy", "gz"), pairs)

    blocks = [hidden] + [send_x(hidden, k) for k in range(1, n_x)]

    chunks = 4
    width = columns // chunks
    pieces = 4
    gain, *weights = pl.pallas_call(
        functools.partial(fetch_kernel, pieces),
        out_shape=[jax.ShapeDtypeStruct((1, depth), jnp.float32)]
        + [pltpu.VMEM((depth, width), query_weight.dtype)] * chunks,
        in_specs=[ANY, VMEM],
        out_specs=[VMEM] * (1 + chunks),
        scratch_shapes=[pltpu.SemaphoreType.DMA((chunks, pieces))],
        cost_estimate=cost(0, 2 * query_weight.size),
        compiler_params=params(12),
        name="fetch_weight",
    )(query_weight, attention_norm_gain.reshape(1, depth))

    x, small = pl.pallas_call(
        functools.partial(rows_kernel, n_x),
        out_shape=(
            jax.ShapeDtypeStruct((rows, depth), jnp.bfloat16),
            jax.ShapeDtypeStruct((rows, 2 * LANES), jnp.float32),
        ),
        in_specs=[SMEM] * 4 + [VMEM] * (2 + n_x),
        out_specs=(VMEM, VMEM),
        compiler_params=params(12),
        name="scaled_rows",
    )(
        place,
        padded_adapter_rank,
        adapter_in_slot,
        segment_starts,
        gain,
        jnp.swapaxes(slot_down_factors, 1, 2),
        *blocks,
    )

    small_parts = pl.pallas_call(
        functools.partial(slice_kernel, groups, offset),
        out_shape=[jax.ShapeDtypeStruct((rows_here, 2 * LANES), jnp.float32)] * groups,
        in_specs=[SMEM, VMEM],
        out_specs=[VMEM] * groups,
        compiler_params=params(12),
        name="small_parts",
    )(place, small)
    smalls = [small_parts[0]] + [send_g(small_parts[k], k) for k in range(1, groups)]

    step = min(width, 512)
    parts = []
    for c in range(chunks):
        dtypes = [jnp.float32] + [jnp.bfloat16] * (groups - 1)
        made = pl.pallas_call(
            functools.partial(chunk_kernel, groups, offset, step),
            out_shape=[jax.ShapeDtypeStruct((rows_here, width), t) for t in dtypes],
            in_specs=[SMEM, VMEM, VMEM],
            out_specs=[VMEM] * groups,
            scratch_shapes=[pltpu.VMEM((rows, width), jnp.float32)],
            cost_estimate=cost(2 * rows * depth * width, 2 * depth * width),
            compiler_params=params(12),
        name="product",
        )(place, x, pltpu.with_memory_space_constraint(weights[c], pltpu.VMEM))
        parts += [made[0]] + [send_g(made[k], k) for k in range(1, groups)]
        if c == 0:
            down = smalls[0][:, :LANES]
            for other in smalls[1:]:
                down = down + other[:, :LANES]
            downs = [send_x(down, k) for k in range(1, n_x)]

    return pl.pallas_call(
        functools.partial(
            final_kernel, groups, groups, n_x - 1, chunks, depth * groups
        ),
        out_shape=jax.ShapeDtypeStruct((rows_here, columns), jnp.bfloat16),
        in_specs=[SMEM] * 2 + [VMEM] * (1 + groups + n_x - 1 + groups * chunks),
        out_specs=VMEM,
        compiler_params=params(12),
        name="query_rows",
    )(place, segment_starts, adapter_up_factors, *smalls, *downs, *parts)


def solution(mesh):
    return jax.shard_map(
        body,
        mesh=mesh,
        in_specs=(
            P(("rep", "gx"), ("gy", "gz")),
            P(("gy", "gz")),
            P(("gy", "gz"), "gx"),
            P("gx", ("gy", "gz"), None),
            P(None, None, "gx"),
            P("rep"),
            P(),
            P(),
            P("rep"),
        ),
        out_specs=P(("rep", "gy", "gz"), "gx"),
        check_vma=False,
    )
```

time: 127 us -> 48.8 us (0.38)
  blocking collectives: 81.7 us -> 0 us
  Pallas kernels: 0 us -> 22.7 us
  between operations: 20.7 us -> 0.21 us
  starting transfers between devices: 0.04 us -> 19.9 us
  matrix products: 16.9 us -> 0 us
  other arithmetic: 5.58 us -> 0.09 us
  waiting for transfers between devices: 0.03 us -> 5 us
  local copies, waits for them, and re-layouts: 2.16 us -> 0.74 us
    psum x2 -> x0, blocking collectives: 66.2 us -> none  [the longest x1 57.8 us: body(): summed_all = lax.psum(down_terms, ('gx', 'gy', 'gz'))]
    pallas_call x0 -> x8, Pallas kernels: none -> 22.7 us  [the longest x1 10.9 us: body(): pl.pallas_call(functools.partial(fetch_kernel, pieces), out_shape=[jax.Sh...]
    ppermute x0 -> x21, starting transfers between devices: none -> 19.9 us  [the longest x15 9.94 us: send_g(): return lax.ppermute(value, ('gy', 'gz'), pairs)]
    dot_general x3 -> x0, matrix products: 16.9 us -> none  [the longest x1 14.6 us: body(): jnp.dot(normed, query_weight, preferred_element_type=jnp.float32)]
    all_gather x1 -> x0, blocking collectives: 15.5 us -> none  [body(): normed = lax.all_gather(own_normed, 'gx', axis=0, tiled=True)]
    ppermute x0 -> x21, waiting for transfers between devices: none -> 5 us  [the longest x15 2.82 us: send_g(): return lax.ppermute(value, ('gy', 'gz'), pairs)]
    and x1 -> x0, other arithmetic: 1.98 us -> none  [body(): (seg_begin + row_offsets < seg_finish) & (segment_ids == adapter_id)]
    dynamic_slice x4 -> x0, local copies, waits for them, and re-layouts: 1.94 us -> none  [the longest x1 0.65 us: body(): local_rank = padded_adapter_rank[adapter_id]]
  transfers between devices with their start and end apart: 1 -> 21, of which waited for: 0 -> 4; matrix products, arithmetic and copies ran while one was open for 4% -> 2% of each run, Pallas kernels for 0% -> 40%
where the time goes in v1:
time: 48.8 us; the launch traced here: 48.6 us
  Pallas kernels  22.7 us (47%)
  starting transfers between devices  19.9 us (41%)
  waiting for transfers between devices  5 us (10%)
  local copies, waits for them, and re-layouts  0.74 us (2%)
    pallas_call x1, Pallas kernels, body(): pl.pallas_call(functools.partial(fetch_kernel, pieces), out_shape=[jax.Sh...  10.9 us
    ppermute x15, starting transfers between devices, send_g(): return lax.ppermute(value, ('gy', 'gz'), pairs)  9.94 us
    ppermute x6, starting transfers between devices, send_x(): return lax.ppermute(value, 'gx', [(j, (j + k) % n_x) for j in range(n_x)])  9.93 us
    pallas_call x4, Pallas kernels, body(): pl.pallas_call(functools.partial(chunk_kernel, groups, offset, step), out...  8.51 us
    ppermute x15, waiting for transfers between devices, send_g(): return lax.ppermute(value, ('gy', 'gz'), pairs)  2.82 us
    ppermute x6, waiting for transfers between devices, send_x(): return lax.ppermute(value, 'gx', [(j, (j + k) % n_x) for j in range(n_x)])  2.17 us
    pallas_call x1, Pallas kernels, body(): pl.pallas_call(functools.partial(final_kernel, groups, groups, n_x - 1, c...  1.72 us
    pallas_call x1, Pallas kernels, body(): pl.pallas_call(functools.partial(rows_kernel, n_x), out_shape=(jax.ShapeD...  1 us
  transfers between devices with their start and end apart: 21, of which 4 were waited for; matrix products, arithmetic and copies ran while one was open for 2% of the time, Pallas kernels for 40%

profile of v1, /device:TPU:0, one launch (start us, length us, event | category | flops | bytes accessed | tf_op | source)
XLA Modules:
  0.0 48.6 jit_solution(15833063690325688994)
XLA Ops:
  0.0 4.0 %collective-permute-start.1 = (bf16[16,4096]{1,0:T(8,128)(2,1)}, bf16[16,4096]{1,0:T(8,128)(2,1)S(1)}, u32[]{:S(2)}, u32[]{:S(2)}) collective-permute-start(bf16[16,4096]{1,0:T(8,128)(2,1)} %refs_6_.1), channel_id=1, source_target_pairs={{0,8},{4,12},{8,0},{12,4},{1,9},{5,13},{9,1},{13,5},{2,10},{6,14},... | collective-permute-start | bytes 393224 | tf_op jit(solution)/shard_map/ppermute | solution.py:170
  4.0 1.6 %collective-permute-start = (bf16[16,4096]{1,0:T(8,128)(2,1)}, bf16[16,4096]{1,0:T(8,128)(2,1)S(1)}, u32[]{:S(2)}, u32[]{:S(2)}) collective-permute-start(bf16[16,4096]{1,0:T(8,128)(2,1)} %refs_6_.1), channel_id=1, source_target_pairs={{0,4},{4,8},{8,12},{12,0},{1,5},{5,9},{9,13},{13,1},{2,6},{6,10},{... | collective-permute-start | bytes 393224 | tf_op jit(solution)/shard_map/ppermute | solution.py:170
  5.6 2.2 %collective-permute-start.2 = (bf16[16,4096]{1,0:T(8,128)(2,1)}, bf16[16,4096]{1,0:T(8,128)(2,1)S(1)}, u32[]{:S(2)}, u32[]{:S(2)}) collective-permute-start(bf16[16,4096]{1,0:T(8,128)(2,1)} %refs_6_.1), channel_id=1, source_target_pairs={{0,12},{4,0},{8,4},{12,8},{1,13},{5,1},{9,5},{13,9},{2,14},{6,2},{... | collective-permute-start | bytes 393224 | tf_op jit(solution)/shard_map/ppermute | solution.py:170
  7.9 0.7 %reshape.3.gain_ref = bf16[1,4096]{1,0:T(2,128)(2,1)S(1)} reshape(bf16[4096]{0:T(1024)(128)(2,1)} %param.10) | data formatting | bytes 16384 | tf_op jit(solution)/shard_map/reshape | solution.py:194
  8.6 10.9 %fetch_weight.1 = (f32[1,4096]{1,0:T(1,128)S(1)}, bf16[4096,1024]{1,0:T(8,128)(2,1)S(1)}, bf16[4096,1024]{1,0:T(8,128)(2,1)S(1)}, bf16[4096,1024]{1,0:T(8,128)(2,1)S(1)}, bf16[4096,1024]{1,0:T(8,128)(2,1)S(1)}) custom-call(bf16[4096,4096]{1,0:T(8,128)(2,1)} %w_hbm.1, bf16[1,4096]{1,0:T(2,128)(2,1)S(1)} %reshape.3.gain_ref), custom_call_target="tpu_custom_call" | custom-call | bytes 33554432 | tf_op jit(solution)/shard_map/fetch_weight/pallas_call | solution.py:184
  19.7 1.0 %scaled_rows.1 = (bf16[64,4096]{1,0:T(8,128)(2,1)S(1)}, f32[64,256]{1,0:T(8,128)S(1)}) custom-call(s32[2]{0:T(128)S(1)} %pad_add_fusion.refs_0_.place, s32[4]{0:T(128)S(1)} %copy-done.4, s32[4]{0:T(128)S(1)} %copy-done.5, s32[5]{0:T(128)S(1)} %copy-done.3, f32[1,4096]{1,0:T(1,128)S(1)} %get-tuple-element.32.refs_4_, bf16[1,64,4096]{2,1,0:T(8,128)(2,1)S(1)} %bitcast.3, ...), custom_call_target="tpu_custom_call" | custom-call | tf_op jit(solution)/shard_map/scaled_rows/pallas_call | solution.py:196
  20.7 0.6 %small_parts.1 = (f32[16,256]{1,0:T(8,128)S(1)}, f32[16,256]{1,0:T(8,128)S(1)}, f32[16,256]{1,0:T(8,128)S(1)}, f32[16,256]{1,0:T(8,128)S(1)}) custom-call(s32[2]{0:T(128)S(1)} %pad_add_fusion.refs_0_.place, f32[64,256]{1,0:T(8,128)S(1)} %get-tuple-element.33.small_ref), custom_call_target="tpu_custom_call" | custom-call | tf_op jit(solution)/shard_map/small_parts/pallas_call | solution.py:216
  21.4 1.6 %collective-permute-start.4 = (f32[16,256]{1,0:T(8,128)S(1)}, f32[16,256]{1,0:T(8,128)S(1)}, u32[]{:S(2)}, u32[]{:S(2)}) collective-permute-start(f32[16,256]{1,0:T(8,128)S(1)} %get-tuple-element.36), channel_id=1, source_target_pairs={{0,2},{1,3},{2,0},{3,1},{4,6},{5,7},{6,4},{7,5},{8,10},{9,11},{10,... | collective-permute-start | bytes 49160 | tf_op jit(solution)/shard_map/ppermute | solution.py:177
  23.2 2.1 %product.7 = (f32[16,1024]{1,0:T(8,128)S(1)}, bf16[16,1024]{1,0:T(8,128)(2,1)S(1)}, bf16[16,1024]{1,0:T(8,128)(2,1)S(1)}, bf16[16,1024]{1,0:T(8,128)(2,1)S(1)}) custom-call(s32[2]{0:T(128)S(1)} %pad_add_fusion.refs_0_.place, bf16[64,4096]{1,0:T(8,128)(2,1)S(1)} %get-tuple-element.38.x_ref, bf16[4096,1024]{1,0:T(8,128)(2,1)S(1)} %get-tuple-element.54.w_ref), custom_call_target="tpu_custom_call" | custom-call | flops 536870912 | bytes 8388608 | tf_op jit(solution)/shard_map/product/pallas_call | solution.py:230
  25.4 2.1 %product.6 = (f32[16,1024]{1,0:T(8,128)S(1)}, bf16[16,1024]{1,0:T(8,128)(2,1)S(1)}, bf16[16,1024]{1,0:T(8,128)(2,1)S(1)}, bf16[16,1024]{1,0:T(8,128)(2,1)S(1)}) custom-call(s32[2]{0:T(128)S(1)} %pad_add_fusion.refs_0_.place, bf16[64,4096]{1,0:T(8,128)(2,1)S(1)} %get-tuple-element.38.x_ref, bf16[4096,1024]{1,0:T(8,128)(2,1)S(1)} %get-tuple-element.49.w_ref), custom_call_target="tpu_custom_call" | custom-call | flops 536870912 | bytes 8388608 | tf_op jit(solution)/shard_map/product/pallas_call | solution.py:230
  27.9 1.5 %collective-permute-start.19 = (bf16[16,1024]{1,0:T(8,128)(2,1)S(1)}, bf16[16,1024]{1,0:T(8,128)(2,1)S(1)}, u32[]{:S(2)}, u32[]{:S(2)}) collective-permute-start(bf16[16,1024]{1,0:T(8,128)(2,1)S(1)} %get-tuple-element.57), channel_id=1, source_target_pairs={{0,2},{1,3},{2,0},{3,1},{4,6},{5,7},{6,4},{7,5},{8,10},{9,11},{10,... | collective-permute-start | bytes 98312 | tf_op jit(solution)/shard_map/ppermute | solution.py:177
  29.5 1.2 %collective-permute-start.7 = (f32[16,128]{1,0:T(8,128)S(1)}, f32[16,128]{1,0:T(8,128)S(1)}, u32[]{:S(2)}, u32[]{:S(2)}) collective-permute-start(f32[16,128]{1,0:T(8,128)S(1)} %slice_add_fusion), channel_id=1, source_target_pairs={{0,8},{4,12},{8,0},{12,4},{1,9},{5,13},{9,1},{13,5},{2,10},{6,14},... | collective-permute-start | bytes 24584 | tf_op jit(solution)/shard_map/ppermute | solution.py:170
  30.7 0.8 %collective-permute-start.6 = (f32[16,128]{1,0:T(8,128)S(1)}, f32[16,128]{1,0:T(8,128)S(1)}, u32[]{:S(2)}, u32[]{:S(2)}) collective-permute-start(f32[16,128]{1,0:T(8,128)S(1)} %slice_add_fusion), channel_id=1, source_target_pairs={{0,4},{4,8},{8,12},{12,0},{1,5},{5,9},{9,13},{13,1},{2,6},{6,10},{... | collective-permute-start | bytes 24584 | tf_op jit(solution)/shard_map/ppermute | solution.py:170
  31.5 2.1 %product.5 = (f32[16,1024]{1,0:T(8,128)S(1)}, bf16[16,1024]{1,0:T(8,128)(2,1)S(1)}, bf16[16,1024]{1,0:T(8,128)(2,1)S(1)}, bf16[16,1024]{1,0:T(8,128)(2,1)S(1)}) custom-call(s32[2]{0:T(128)S(1)} %pad_add_fusion.refs_0_.place, bf16[64,4096]{1,0:T(8,128)(2,1)S(1)} %get-tuple-element.38.x_ref, bf16[4096,1024]{1,0:T(8,128)(2,1)S(1)} %get-tuple-element.44.w_ref), custom_call_target="tpu_custom_call" | custom-call | flops 536870912 | bytes 8388608 | tf_op jit(solution)/shard_map/product/pallas_call | solution.py:230
  34.4 1.8 %collective-permute-done.6.refs_7_ = f32[16,128]{1,0:T(8,128)S(1)} collective-permute-done((f32[16,128]{1,0:T(8,128)S(1)}, f32[16,128]{1,0:T(8,128)S(1)}, u32[]{:S(2)}, u32[]{:S(2)}) %collective-permute-start.6) | collective-permute-done | bytes 8224 | tf_op jit(solution)/shard_map/ppermute | solution.py:170
  36.7 1.6 %collective-permute-start.12 = (bf16[16,1024]{1,0:T(8,128)(2,1)S(1)}, bf16[16,1024]{1,0:T(8,128)(2,1)S(1)}, u32[]{:S(2)}, u32[]{:S(2)}) collective-permute-start(bf16[16,1024]{1,0:T(8,128)(2,1)S(1)} %get-tuple-element.46), channel_id=1, source_target_pairs={{0,1},{1,0},{2,3},{3,2},{4,5},{5,4},{6,7},{7,6},{8,9},{9,8},{10,11... | collective-permute-start | bytes 98312 | tf_op jit(solution)/shard_map/ppermute | solution.py:177
  38.3 2.1 %product.4 = (f32[16,1024]{1,0:T(8,128)S(1)}, bf16[16,1024]{1,0:T(8,128)(2,1)S(1)}, bf16[16,1024]{1,0:T(8,128)(2,1)S(1)}, bf16[16,1024]{1,0:T(8,128)(2,1)S(1)}) custom-call(s32[2]{0:T(128)S(1)} %pad_add_fusion.refs_0_.place, bf16[64,4096]{1,0:T(8,128)(2,1)S(1)} %get-tuple-element.38.x_ref, bf16[4096,1024]{1,0:T(8,128)(2,1)S(1)} %get-tuple-element.39.w_ref), custom_call_target="tpu_custom_call" | custom-call | flops 536870912 | bytes 8388608 | tf_op jit(solution)/shard_map/product/pallas_call | solution.py:230
  40.5 0.6 %collective-permute-start.13 = (bf16[16,1024]{1,0:T(8,128)(2,1)S(1)}, bf16[16,1024]{1,0:T(8,128)(2,1)S(1)}, u32[]{:S(2)}, u32[]{:S(2)}) collective-permute-start(bf16[16,1024]{1,0:T(8,128)(2,1)S(1)} %get-tuple-element.47), channel_id=1, source_target_pairs={{0,2},{1,3},{2,0},{3,1},{4,6},{5,7},{6,4},{7,5},{8,10},{9,11},{10,... | collective-permute-start | bytes 98312 | tf_op jit(solution)/shard_map/ppermute | solution.py:177
  41.1 0.8 %collective-permute-start.14 = (bf16[16,1024]{1,0:T(8,128)(2,1)S(1)}, bf16[16,1024]{1,0:T(8,128)(2,1)S(1)}, u32[]{:S(2)}, u32[]{:S(2)}) collective-permute-start(bf16[16,1024]{1,0:T(8,128)(2,1)S(1)} %get-tuple-element.48), channel_id=1, source_target_pairs={{0,3},{1,2},{2,1},{3,0},{4,7},{5,6},{6,5},{7,4},{8,11},{9,10},{10,... | collective-permute-start | bytes 98312 | tf_op jit(solution)/shard_map/ppermute | solution.py:177
  41.9 0.8 %collective-permute-start.9 = (bf16[16,1024]{1,0:T(8,128)(2,1)S(1)}, bf16[16,1024]{1,0:T(8,128)(2,1)S(1)}, u32[]{:S(2)}, u32[]{:S(2)}) collective-permute-start(bf16[16,1024]{1,0:T(8,128)(2,1)S(1)} %get-tuple-element.41), channel_id=1, source_target_pairs={{0,1},{1,0},{2,3},{3,2},{4,5},{5,4},{6,7},{7,6},{8,9},{9,8},{10,11... | collective-permute-start | bytes 98312 | tf_op jit(solution)/shard_map/ppermute | solution.py:177
  43.2 0.9 %collective-permute-start.11 = (bf16[16,1024]{1,0:T(8,128)(2,1)S(1)}, bf16[16,1024]{1,0:T(8,128)(2,1)S(1)}, u32[]{:S(2)}, u32[]{:S(2)}) collective-permute-start(bf16[16,1024]{1,0:T(8,128)(2,1)S(1)} %get-tuple-element.43), channel_id=1, source_target_pairs={{0,3},{1,2},{2,1},{3,0},{4,7},{5,6},{6,5},{7,4},{8,11},{9,10},{10,... | collective-permute-start | bytes 98312 | tf_op jit(solution)/shard_map/ppermute | solution.py:177
  44.1 0.6 %collective-permute-done.13.refs_16_ = bf16[16,1024]{1,0:T(8,128)(2,1)S(1)} collective-permute-done((bf16[16,1024]{1,0:T(8,128)(2,1)S(1)}, bf16[16,1024]{1,0:T(8,128)(2,1)S(1)}, u32[]{:S(2)}, u32[]{:S(2)}) %collective-permute-start.13) | collective-permute-done | bytes 32800 | tf_op jit(solution)/shard_map/ppermute | solution.py:177
  44.8 2.1 %collective-permute-done.10.refs_12_ = bf16[16,1024]{1,0:T(8,128)(2,1)S(1)} collective-permute-done((bf16[16,1024]{1,0:T(8,128)(2,1)S(1)}, bf16[16,1024]{1,0:T(8,128)(2,1)S(1)}, u32[]{:S(2)}, u32[]{:S(2)}) %collective-permute-start.10) | collective-permute-done | bytes 32800 | tf_op jit(solution)/shard_map/ppermute | solution.py:177
  46.9 1.7 %query_rows.1 = bf16[16,4096]{1,0:T(8,128)(2,1)} custom-call(s32[2]{0:T(128)S(1)} %pad_add_fusion.refs_0_.place, s32[5]{0:T(128)S(1)} %copy-done.3, bf16[4,64,4096]{2,1,0:T(8,128)(2,1)S(1)} %copy-done, f32[16,256]{1,0:T(8,128)S(1)} %get-tuple-element.34.refs_3_, f32[16,256]{1,0:T(8,128)S(1)} %collective-permute-done.3.refs_4_, ...), custom_call_target="tpu_custom_call" | custom-call | tf_op jit(solution)/shard_map/query_rows/pallas_call | solution.py:247
  (41 shorter events, 2.8 us)
Async XLA Ops:
  0.0 19.7 %collective-permute-start.1 = (bf16[16,4096]{1,0:T(8,128)(2,1)}, bf16[16,4096]{1,0:T(8,128)(2,1)S(1)}, u32[]{:S(2)}, u32[]{:S(2)}) collective-permute-start(bf16[16,4096]{1,0:T(8,128)(2,1)} %refs_6_.1), channel_id=1, source_target_pairs={{0,8},{4,12},{8,0},{12,4},{1,9},{5,13},{9,1},{13,5},{2,10},{6,14},... | collective-permute-start | bytes 393224 | tf_op jit(solution)/shard_map/ppermute | solution.py:170
  4.0 15.6 %collective-permute-start = (bf16[16,4096]{1,0:T(8,128)(2,1)}, bf16[16,4096]{1,0:T(8,128)(2,1)S(1)}, u32[]{:S(2)}, u32[]{:S(2)}) collective-permute-start(bf16[16,4096]{1,0:T(8,128)(2,1)} %refs_6_.1), channel_id=1, source_target_pairs={{0,4},{4,8},{8,12},{12,0},{1,5},{5,9},{9,13},{13,1},{2,6},{6,10},{... | collective-permute-start | bytes 393224 | tf_op jit(solution)/shard_map/ppermute | solution.py:170
  5.6 14.1 %collective-permute-start.2 = (bf16[16,4096]{1,0:T(8,128)(2,1)}, bf16[16,4096]{1,0:T(8,128)(2,1)S(1)}, u32[]{:S(2)}, u32[]{:S(2)}) collective-permute-start(bf16[16,4096]{1,0:T(8,128)(2,1)} %refs_6_.1), channel_id=1, source_target_pairs={{0,12},{4,0},{8,4},{12,8},{1,13},{5,1},{9,5},{13,9},{2,14},{6,2},{... | collective-permute-start | bytes 393224 | tf_op jit(solution)/shard_map/ppermute | solution.py:170
  8.6 11.1 %copy-start.1 = (bf16[1,4096,64]{1,2,0:T(8,128)(2,1)S(1)}, bf16[1,4096,64]{1,2,0:T(8,128)(2,1)}, u32[]{:S(2)}) copy-start(bf16[1,4096,64]{1,2,0:T(8,128)(2,1)} %param.12) | copy-start | bytes 1572868
  8.6 11.1 %copy-start.2 = (bf16[16,4096]{1,0:T(8,128)(2,1)S(1)}, bf16[16,4096]{1,0:T(8,128)(2,1)}, u32[]{:S(2)}) copy-start(bf16[16,4096]{1,0:T(8,128)(2,1)} %refs_6_.1) | copy-start | bytes 393220
  21.3 8.1 %collective-permute-start.3 = (f32[16,256]{1,0:T(8,128)S(1)}, f32[16,256]{1,0:T(8,128)S(1)}, u32[]{:S(2)}, u32[]{:S(2)}) collective-permute-start(f32[16,256]{1,0:T(8,128)S(1)} %get-tuple-element.35), channel_id=1, source_target_pairs={{0,1},{1,0},{2,3},{3,2},{4,5},{5,4},{6,7},{7,6},{8,9},{9,8},{10,11... | collective-permute-start | bytes 49160 | tf_op jit(solution)/shard_map/ppermute | solution.py:177
  21.4 8.0 %collective-permute-start.4 = (f32[16,256]{1,0:T(8,128)S(1)}, f32[16,256]{1,0:T(8,128)S(1)}, u32[]{:S(2)}, u32[]{:S(2)}) collective-permute-start(f32[16,256]{1,0:T(8,128)S(1)} %get-tuple-element.36), channel_id=1, source_target_pairs={{0,2},{1,3},{2,0},{3,1},{4,6},{5,7},{6,4},{7,5},{8,10},{9,11},{10,... | collective-permute-start | bytes 49160 | tf_op jit(solution)/shard_map/ppermute | solution.py:177
  22.9 6.5 %collective-permute-start.5 = (f32[16,256]{1,0:T(8,128)S(1)}, f32[16,256]{1,0:T(8,128)S(1)}, u32[]{:S(2)}, u32[]{:S(2)}) collective-permute-start(f32[16,256]{1,0:T(8,128)S(1)} %get-tuple-element.37), channel_id=1, source_target_pairs={{0,3},{1,2},{2,1},{3,0},{4,7},{5,6},{6,5},{7,4},{8,11},{9,10},{10,... | collective-permute-start | bytes 49160 | tf_op jit(solution)/shard_map/ppermute | solution.py:177
  27.5 9.2 %collective-permute-start.18 = (bf16[16,1024]{1,0:T(8,128)(2,1)S(1)}, bf16[16,1024]{1,0:T(8,128)(2,1)S(1)}, u32[]{:S(2)}, u32[]{:S(2)}) collective-permute-start(bf16[16,1024]{1,0:T(8,128)(2,1)S(1)} %get-tuple-element.56), channel_id=1, source_target_pairs={{0,1},{1,0},{2,3},{3,2},{4,5},{5,4},{6,7},{7,6},{8,9},{9,8},{10,11... | collective-permute-start | bytes 98312 | tf_op jit(solution)/shard_map/ppermute | solution.py:177
  27.9 8.8 %collective-permute-start.19 = (bf16[16,1024]{1,0:T(8,128)(2,1)S(1)}, bf16[16,1024]{1,0:T(8,128)(2,1)S(1)}, u32[]{:S(2)}, u32[]{:S(2)}) collective-permute-start(bf16[16,1024]{1,0:T(8,128)(2,1)S(1)} %get-tuple-element.57), channel_id=1, source_target_pairs={{0,2},{1,3},{2,0},{3,1},{4,6},{5,7},{6,4},{7,5},{8,10},{9,11},{10,... | collective-permute-start | bytes 98312 | tf_op jit(solution)/shard_map/ppermute | solution.py:177
  29.4 4.2 %collective-permute-start.8 = (f32[16,128]{1,0:T(8,128)S(1)}, f32[16,128]{1,0:T(8,128)S(1)}, u32[]{:S(2)}, u32[]{:S(2)}) collective-permute-start(f32[16,128]{1,0:T(8,128)S(1)} %slice_add_fusion), channel_id=1, source_target_pairs={{0,12},{4,0},{8,4},{12,8},{1,13},{5,1},{9,5},{13,9},{2,14},{6,2},{... | collective-permute-start | bytes 24584 | tf_op jit(solution)/shard_map/ppermute | solution.py:170
  29.5 4.6 %collective-permute-start.7 = (f32[16,128]{1,0:T(8,128)S(1)}, f32[16,128]{1,0:T(8,128)S(1)}, u32[]{:S(2)}, u32[]{:S(2)}) collective-permute-start(f32[16,128]{1,0:T(8,128)S(1)} %slice_add_fusion), channel_id=1, source_target_pairs={{0,8},{4,12},{8,0},{12,4},{1,9},{5,13},{9,1},{13,5},{2,10},{6,14},... | collective-permute-start | bytes 24584 | tf_op jit(solution)/shard_map/ppermute | solution.py:170
  30.7 5.4 %collective-permute-start.6 = (f32[16,128]{1,0:T(8,128)S(1)}, f32[16,128]{1,0:T(8,128)S(1)}, u32[]{:S(2)}, u32[]{:S(2)}) collective-permute-start(f32[16,128]{1,0:T(8,128)S(1)} %slice_add_fusion), channel_id=1, source_target_pairs={{0,4},{4,8},{8,12},{12,0},{1,5},{5,9},{9,13},{13,1},{2,6},{6,10},{... | collective-permute-start | bytes 24584 | tf_op jit(solution)/shard_map/ppermute | solution.py:170
  31.5 15.4 %copy-start = (bf16[4,64,4096]{2,1,0:T(8,128)(2,1)S(1)}, bf16[4,64,4096]{2,1,0:T(8,128)(2,1)}, u32[]{:S(2)}) copy-start(bf16[4,64,4096]{2,1,0:T(8,128)(2,1)} %refs_2_.3) | copy-start | bytes 6291460
  33.7 6.8 %collective-permute-start.20 = (bf16[16,1024]{1,0:T(8,128)(2,1)S(1)}, bf16[16,1024]{1,0:T(8,128)(2,1)S(1)}, u32[]{:S(2)}, u32[]{:S(2)}) collective-permute-start(bf16[16,1024]{1,0:T(8,128)(2,1)S(1)} %get-tuple-element.58), channel_id=1, source_target_pairs={{0,3},{1,2},{2,1},{3,0},{4,7},{5,6},{6,5},{7,4},{8,11},{9,10},{10,... | collective-permute-start | bytes 98312 | tf_op jit(solution)/shard_map/ppermute | solution.py:177
  34.1 6.9 %collective-permute-start.15 = (bf16[16,1024]{1,0:T(8,128)(2,1)S(1)}, bf16[16,1024]{1,0:T(8,128)(2,1)S(1)}, u32[]{:S(2)}, u32[]{:S(2)}) collective-permute-start(bf16[16,1024]{1,0:T(8,128)(2,1)S(1)} %get-tuple-element.51), channel_id=1, source_target_pairs={{0,1},{1,0},{2,3},{3,2},{4,5},{5,4},{6,7},{7,6},{8,9},{9,8},{10,11... | collective-permute-start | bytes 98312 | tf_op jit(solution)/shard_map/ppermute | solution.py:177
  36.2 5.7 %collective-permute-start.16 = (bf16[16,1024]{1,0:T(8,128)(2,1)S(1)}, bf16[16,1024]{1,0:T(8,128)(2,1)S(1)}, u32[]{:S(2)}, u32[]{:S(2)}) collective-permute-start(bf16[16,1024]{1,0:T(8,128)(2,1)S(1)} %get-tuple-element.52), channel_id=1, source_target_pairs={{0,2},{1,3},{2,0},{3,1},{4,6},{5,7},{6,4},{7,5},{8,10},{9,11},{10,... | collective-permute-start | bytes 98312 | tf_op jit(solution)/shard_map/ppermute | solution.py:177
  36.7 6.0 %collective-permute-start.17 = (bf16[16,1024]{1,0:T(8,128)(2,1)S(1)}, bf16[16,1024]{1,0:T(8,128)(2,1)S(1)}, u32[]{:S(2)}, u32[]{:S(2)}) collective-permute-start(bf16[16,1024]{1,0:T(8,128)(2,1)S(1)} %get-tuple-element.53), channel_id=1, source_target_pairs={{0,3},{1,2},{2,1},{3,0},{4,7},{5,6},{6,5},{7,4},{8,11},{9,10},{10,... | collective-permute-start | bytes 98312 | tf_op jit(solution)/shard_map/ppermute | solution.py:177
  36.7 6.5 %collective-permute-start.12 = (bf16[16,1024]{1,0:T(8,128)(2,1)S(1)}, bf16[16,1024]{1,0:T(8,128)(2,1)S(1)}, u32[]{:S(2)}, u32[]{:S(2)}) collective-permute-start(bf16[16,1024]{1,0:T(8,128)(2,1)S(1)} %get-tuple-element.46), channel_id=1, source_target_pairs={{0,1},{1,0},{2,3},{3,2},{4,5},{5,4},{6,7},{7,6},{8,9},{9,8},{10,11... | collective-permute-start | bytes 98312 | tf_op jit(solution)/shard_map/ppermute | solution.py:177
  40.5 4.3 %collective-permute-start.13 = (bf16[16,1024]{1,0:T(8,128)(2,1)S(1)}, bf16[16,1024]{1,0:T(8,128)(2,1)S(1)}, u32[]{:S(2)}, u32[]{:S(2)}) collective-permute-start(bf16[16,1024]{1,0:T(8,128)(2,1)S(1)} %get-tuple-element.47), channel_id=1, source_target_pairs={{0,2},{1,3},{2,0},{3,1},{4,6},{5,7},{6,4},{7,5},{8,10},{9,11},{10,... | collective-permute-start | bytes 98312 | tf_op jit(solution)/shard_map/ppermute | solution.py:177
  41.1 3.7 %collective-permute-start.14 = (bf16[16,1024]{1,0:T(8,128)(2,1)S(1)}, bf16[16,1024]{1,0:T(8,128)(2,1)S(1)}, u32[]{:S(2)}, u32[]{:S(2)}) collective-permute-start(bf16[16,1024]{1,0:T(8,128)(2,1)S(1)} %get-tuple-element.48), channel_id=1, source_target_pairs={{0,3},{1,2},{2,1},{3,0},{4,7},{5,6},{6,5},{7,4},{8,11},{9,10},{10,... | collective-permute-start | bytes 98312 | tf_op jit(solution)/shard_map/ppermute | solution.py:177
  41.9 2.9 %collective-permute-start.9 = (bf16[16,1024]{1,0:T(8,128)(2,1)S(1)}, bf16[16,1024]{1,0:T(8,128)(2,1)S(1)}, u32[]{:S(2)}, u32[]{:S(2)}) collective-permute-start(bf16[16,1024]{1,0:T(8,128)(2,1)S(1)} %get-tuple-element.41), channel_id=1, source_target_pairs={{0,1},{1,0},{2,3},{3,2},{4,5},{5,4},{6,7},{7,6},{8,9},{9,8},{10,11... | collective-permute-start | bytes 98312 | tf_op jit(solution)/shard_map/ppermute | solution.py:177
  42.7 4.2 %collective-permute-start.10 = (bf16[16,1024]{1,0:T(8,128)(2,1)S(1)}, bf16[16,1024]{1,0:T(8,128)(2,1)S(1)}, u32[]{:S(2)}, u32[]{:S(2)}) collective-permute-start(bf16[16,1024]{1,0:T(8,128)(2,1)S(1)} %get-tuple-element.42), channel_id=1, source_target_pairs={{0,2},{1,3},{2,0},{3,1},{4,6},{5,7},{6,4},{7,5},{8,10},{9,11},{10,... | collective-permute-start | bytes 98312 | tf_op jit(solution)/shard_map/ppermute | solution.py:177
  43.2 3.7 %collective-permute-start.11 = (bf16[16,1024]{1,0:T(8,128)(2,1)S(1)}, bf16[16,1024]{1,0:T(8,128)(2,1)S(1)}, u32[]{:S(2)}, u32[]{:S(2)}) collective-permute-start(bf16[16,1024]{1,0:T(8,128)(2,1)S(1)} %get-tuple-element.43), channel_id=1, source_target_pairs={{0,3},{1,2},{2,1},{3,0},{4,7},{5,6},{6,5},{7,4},{8,11},{9,10},{10,... | collective-permute-start | bytes 98312 | tf_op jit(solution)/shard_map/ppermute | solution.py:177
  (3 other events, 33.3 us)

commit v2 on v1

v2 whole, which is shorter than its diff:
```python
import functools

import jax
import jax.numpy as jnp
from jax import lax
from jax.experimental import pallas as pl
from jax.experimental.pallas import tpu as pltpu
from jax.sharding import PartitionSpec as P

EPSILON = 1e-05
ADAPTER_ALPHA = 32.0
LANES = 128
MIB = 1 << 20

VMEM = pl.BlockSpec(memory_space=pltpu.VMEM)
SMEM = pl.BlockSpec(memory_space=pltpu.SMEM)
ANY = pl.BlockSpec(memory_space=pl.ANY)


def params(mib):
    return pltpu.CompilerParams(vmem_limit_bytes=mib * MIB)


def cost(flops, moved):
    return pl.CostEstimate(flops=flops, bytes_accessed=moved, transcendentals=0)


def weight_copies(w_hbm, first, w_vmem, sems):
    pieces = sems.shape[0]
    depth, width = w_vmem.shape
    step = depth // pieces
    return [
        pltpu.make_async_copy(
            w_hbm.at[pl.ds(p * step, step), pl.ds(first, width)],
            w_vmem.at[pl.ds(p * step, step)],
            sems.at[p],
        )
        for p in range(pieces)
    ]


def fetch_kernel(w_hbm, gain_ref, gain_out, w_vmem, sems):
    copies = weight_copies(w_hbm, 0, w_vmem, sems)
    for copy in copies:
        copy.start()
    gain_out[...] = gain_ref[...].astype(jnp.float32).reshape(gain_out.shape)
    for copy in copies:
        copy.wait()


def multiply(x_ref, w_ref, out_ref, first, step):
    width = w_ref.shape[1]
    for c in range(0, width, step):
        out_ref[:, first + c : first + c + step] = jnp.dot(
            x_ref[...], w_ref[:, c : c + step], preferred_element_type=jnp.float32
        )


def first_kernel(n, step, width, *refs):
    rank_ref, slot_ref, start_ref, gain_ref, down_ref, w_hbm, w_ref = refs[:7]
    blocks = refs[7 : 7 + n]
    x_ref, square_ref, down_out, base_ref, rest_ref, sems = refs[7 + n :]
    copies = weight_copies(w_hbm, w_ref.shape[1], rest_ref, sems)
    for copy in copies:
        copy.start()
    home = lax.axis_index("gx")
    block_rows = blocks[0].shape[0]
    rows = n * block_rows
    gain = gain_ref[...]
    for k in range(n):
        source = lax.rem(home - k + n, n)
        begin = pl.multiple_of(source * block_rows, block_rows)
        values = blocks[k][...].astype(jnp.float32)
        squares = jnp.sum(values * values, axis=1, keepdims=True) / width
        x_ref[pl.ds(begin, block_rows), :] = (values * gain).astype(jnp.bfloat16)
        square_ref[pl.ds(begin, block_rows), :] = jnp.broadcast_to(squares, (block_rows, LANES))
    slots, rank_columns = down_ref.shape[0], down_ref.shape[1]
    row = lax.broadcasted_iota(jnp.int32, (rows, rank_columns), 0)
    col = lax.broadcasted_iota(jnp.int32, (rows, rank_columns), 1)
    total = jnp.zeros((rows, rank_columns), jnp.float32)
    for s in range(slots):
        adapter = slot_ref[home * slots + s]
        rank = rank_ref[adapter]
        live = (row >= start_ref[adapter]) & (row < start_ref[adapter + 1]) & (col < rank)
        projected = lax.dot_general(
            x_ref[...], down_ref[s], (((1,), (1,)), ((), ())), preferred_element_type=jnp.float32
        )
        scale = ADAPTER_ALPHA / jnp.full((rows, rank_columns), rank, jnp.int32).astype(jnp.float32)
        total = total + jnp.where(live, projected * scale, 0.0)
    down_out[...] = jnp.zeros(down_out.shape, down_out.dtype)
    down_out[:, :rank_columns] = total.astype(down_out.dtype)
    multiply(x_ref, w_ref, base_ref, 0, step)
    for copy in copies:
        copy.wait()


def second_kernel(n_x, groups, step, offset, *refs):
    start_ref, x_ref, square_ref, base_ref, w_ref, up_ref = refs[:6]
    downs = refs[6 : 6 + n_x]
    outs, acc = refs[6 + n_x : -1], refs[-1]
    rows = x_ref.shape[0]
    done = base_ref.shape[1]
    columns = done + w_ref.shape[1]
    adapters, rank_columns, _ = up_ref.shape
    down = downs[0][:, :rank_columns]
    for other in downs[1:]:
        down = down + other[:, :rank_columns]
    row = lax.broadcasted_iota(jnp.int32, (rows, rank_columns), 0)
    spread = jnp.concatenate(
        [
            jnp.where((row >= start_ref[a]) & (row < start_ref[a + 1]), down, jnp.zeros_like(down))
            for a in range(adapters)
        ],
        axis=1,
    )
    for c in range(0, columns, step):
        here = slice(c, c + step)
        up = up_ref[:, :, here].reshape(adapters * rank_columns, step)
        delta = jnp.dot(spread, up, preferred_element_type=jnp.float32)
        if c < done:
            base = base_ref[:, here]
        else:
            base = jnp.dot(
                x_ref[...], w_ref[:, c - done : c - done + step], preferred_element_type=jnp.float32
            )
        acc[:, here] = base + delta
    square = square_ref[...]
    high = square.astype(jnp.bfloat16).astype(jnp.float32)
    low = jnp.where(high < jnp.inf, square - high, 0.0)
    lane = lax.broadcasted_iota(jnp.int32, square.shape, 1)
    acc[:, columns:] = jnp.where(lane < LANES // 2, high, low)
    g = lax.axis_index(("gy", "gz"))
    rows_here = outs[0].shape[0]
    for k in range(groups):
        begin = pl.multiple_of(offset(g, k) * rows_here, rows_here)
        outs[k][...] = acc[pl.ds(begin, rows_here), :].astype(outs[k].dtype)


def final_kernel(*refs):
    parts, out_ref = refs[:-1], refs[-1]
    columns = out_ref.shape[1]
    total = parts[0][...]
    for other in parts[1:]:
        total = total + other[...].astype(jnp.float32)
    mean_sq = total[:, columns : columns + 1] + total[:, columns + LANES - 1 :]
    scale = lax.rsqrt(mean_sq + EPSILON)
    value = jnp.where(mean_sq < jnp.inf, total[:, :columns] * scale, 0.0)
    out_ref[...] = value.astype(out_ref.dtype)


def body(
    hidden,
    attention_norm_gain,
    query_weight,
    slot_down_factors,
    adapter_up_factors,
    adapter_of_row,
    padded_adapter_rank,
    adapter_in_slot,
    segment_starts,
):
    n_x, n_y, n_z = lax.axis_size("gx"), lax.axis_size("gy"), lax.axis_size("gz")
    groups = n_y * n_z
    block_rows, depth = hidden.shape
    columns = query_weight.shape[1]
    rows = n_x * block_rows
    rows_here = rows // groups

    def offset(g, k):
        y = lax.rem(g // n_z + k // n_z, n_y)
        z = lax.rem(lax.rem(g, n_z) + k % n_z, n_z)
        return y * n_z + z

    def send_x(value, k):
        return lax.ppermute(value, "gx", [(j, (j + k) % n_x) for j in range(n_x)])

    def send_g(value, k):
        pairs = []
        for g in range(groups):
            y, z = (g // n_z + k // n_z) % n_y, (g % n_z + k % n_z) % n_z
            pairs.append((g, y * n_z + z))
        return lax.ppermute(value, ("gy", "gz"), pairs)

    blocks = [hidden] + [send_x(hidden, k) for k in range(1, n_x)]

    step = min(512, columns // 4)
    first = columns * 5 // 8 // step * step
    rest = columns - first
    pieces = 8
    f32, bf16 = jnp.float32, jnp.bfloat16
    gain, weight = pl.pallas_call(
        fetch_kernel,
        out_shape=(
            jax.ShapeDtypeStruct((1, depth), f32),
            pltpu.VMEM((depth, first), query_weight.dtype),
        ),
        in_specs=[ANY, VMEM],
        out_specs=(VMEM, VMEM),
        scratch_shapes=[pltpu.SemaphoreType.DMA((pieces,))],
        cost_estimate=cost(0, 2 * depth * first),
        compiler_params=params(12),
        name="fetch_weight",
    )(query_weight, attention_norm_gain)

    x, square, down, base, weight_rest = pl.pallas_call(
        functools.partial(first_kernel, n_x, step, depth * groups),
        out_shape=(
            jax.ShapeDtypeStruct((rows, depth), bf16),
            jax.ShapeDtypeStruct((rows, LANES), f32),
            jax.ShapeDtypeStruct((rows, LANES), bf16),
            jax.ShapeDtypeStruct((rows, first), f32),
            pltpu.VMEM((depth, rest), query_weight.dtype),
        ),
        in_specs=[SMEM] * 3 + [VMEM] * 2 + [ANY] + [VMEM] * (1 + n_x),
        out_specs=(VMEM,) * 5,
        scratch_shapes=[pltpu.SemaphoreType.DMA((pieces,))],
        cost_estimate=cost(2 * rows * depth * first, 2 * depth * rest),
        compiler_params=params(16),
        name="first_columns",
    )(
        padded_adapter_rank,
        adapter_in_slot,
        segment_starts,
        gain,
        jnp.swapaxes(slot_down_factors, 1, 2),
        query_weight,
        pltpu.with_memory_space_constraint(weight, pltpu.VMEM),
        *blocks,
    )

    downs = [down] + [send_x(down, k) for k in range(1, n_x)]

    dtypes = [f32] + [bf16] * (groups - 1)
    made = pl.pallas_call(
        functools.partial(second_kernel, n_x, groups, step, offset),
        out_shape=[jax.ShapeDtypeStruct((rows_here, columns + LANES), t) for t in dtypes],
        in_specs=[SMEM] + [VMEM] * (5 + n_x),
        out_specs=[VMEM] * groups,
        scratch_shapes=[pltpu.VMEM((rows, columns + LANES), f32)],
        cost_estimate=cost(2 * rows * depth * rest, 2 * depth * rest),
        compiler_params=params(16),
        name="last_columns",
    )(
        segment_starts,
        x,
        square,
        base,
        pltpu.with_memory_space_constraint(weight_rest, pltpu.VMEM),
        adapter_up_factors,
        *downs,
    )
    parts = [made[0]] + [send_g(made[k], k) for k in range(1, groups)]

    return pl.pallas_call(
        final_kernel,
        out_shape=jax.ShapeDtypeStruct((rows_here, columns), bf16),
        in_specs=[VMEM] * groups,
        out_specs=VMEM,
        compiler_params=params(12),
        name="query_rows",
    )(*parts)


def solution(mesh):
    return jax.shard_map(
        body,
        mesh=mesh,
        in_specs=(
            P(("rep", "gx"), ("gy", "gz")),
            P(("gy", "gz")),
            P(("gy", "gz"), "gx"),
            P("gx", ("gy", "gz"), None),
            P(None, None, "gx"),
            P("rep"),
            P(),
            P(),
            P("rep"),
        ),
        out_specs=P(("rep", "gy", "gz"), "gx"),
        check_vma=False,
    )
```

time: 48.8 us -> 45.7 us (0.936)
  waiting for transfers between devices: 5 us -> 10.2 us
  starting transfers between devices: 19.9 us -> 14.9 us
  Pallas kernels: 22.7 us -> 19.5 us
    ppermute x15 -> x3, starting transfers between devices: 9.94 us -> 1.93 us  [send_g(): return lax.ppermute(value, ('gy', 'gz'), pairs)]
    ppermute x15 -> x3, waiting for transfers between devices: 2.82 us -> 6.58 us  [send_g(): return lax.ppermute(value, ('gy', 'gz'), pairs)]
    pallas_call x8 -> x4, Pallas kernels: 22.7 us -> 19.5 us  [the longest x1 8.3 us: body(): pl.pallas_call(functools.partial(first_kernel, n_x, step, depth * groups)...]
    ppermute x6, starting transfers between devices: 9.93 us -> 13 us  [send_x(): return lax.ppermute(value, 'gx', [(j, (j + k) % n_x) for j in range(n_x)])]
    ppermute x6, waiting for transfers between devices: 2.17 us -> 3.6 us  [send_x(): return lax.ppermute(value, 'gx', [(j, (j + k) % n_x) for j in range(n_x)])]
    reshape x1 -> x0, local copies, waits for them, and re-layouts: 0.71 us -> none  [body(): attention_norm_gain.reshape(1, depth)]
    unnamed x12 -> x14, local copies, waits for them, and re-layouts: 0.04 us -> 0.72 us
  transfers between devices with their start and end apart: 21 -> 9, of which waited for: 4 -> 4; matrix products, arithmetic and copies ran while one was open for 2% -> 0% of each run, Pallas kernels for 40% -> 16%
where the time goes in v2:
time: 45.7 us; the launch traced here: 45.5 us
  Pallas kernels  19.5 us (43%)
  starting transfers between devices  14.9 us (33%)
  waiting for transfers between devices  10.2 us (22%)
  local copies, waits for them, and re-layouts  0.72 us (2%)
    ppermute x6, starting transfers between devices, send_x(): return lax.ppermute(value, 'gx', [(j, (j + k) % n_x) for j in range(n_x)])  13 us
    pallas_call x1, Pallas kernels, body(): pl.pallas_call(functools.partial(first_kernel, n_x, step, depth * groups)...  8.3 us
    pallas_call x1, Pallas kernels, body(): pl.pallas_call(fetch_kernel, out_shape=(jax.ShapeDtypeStruct((1, depth),...  7.15 us
    ppermute x3, waiting for transfers between devices, send_g(): return lax.ppermute(value, ('gy', 'gz'), pairs)  6.58 us
    ppermute x6, waiting for transfers between devices, send_x(): return lax.ppermute(value, 'gx', [(j, (j + k) % n_x) for j in range(n_x)])  3.6 us
    pallas_call x1, Pallas kernels, body(): pl.pallas_call(functools.partial(second_kernel, n_x, groups, step, offset...  3.27 us
    ppermute x3, starting transfers between devices, send_g(): return lax.ppermute(value, ('gy', 'gz'), pairs)  1.93 us
  transfers between devices with their start and end apart: 9, of which 4 were waited for; matrix products, arithmetic and copies ran while one was open for 0% of the time, Pallas kernels for 16%

profile of v2, /device:TPU:0, one launch (start us, length us, event | category | flops | bytes accessed | tf_op | source)
XLA Modules:
  0.0 45.5 jit_solution(14835193836244881441)
XLA Ops:
  0.0 4.0 %collective-permute-start.1 = (bf16[16,4096]{1,0:T(8,128)(2,1)}, bf16[16,4096]{1,0:T(8,128)(2,1)S(1)}, u32[]{:S(2)}, u32[]{:S(2)}) collective-permute-start(bf16[16,4096]{1,0:T(8,128)(2,1)} %refs_7_.1), channel_id=1, source_target_pairs={{0,8},{4,12},{8,0},{12,4},{1,9},{5,13},{9,1},{13,5},{2,10},{6,14},... | collective-permute-start | bytes 393224 | tf_op jit(solution)/shard_map/ppermute | solution.py:175
  4.0 1.6 %collective-permute-start = (bf16[16,4096]{1,0:T(8,128)(2,1)}, bf16[16,4096]{1,0:T(8,128)(2,1)S(1)}, u32[]{:S(2)}, u32[]{:S(2)}) collective-permute-start(bf16[16,4096]{1,0:T(8,128)(2,1)} %refs_7_.1), channel_id=1, source_target_pairs={{0,4},{4,8},{8,12},{12,0},{1,5},{5,9},{9,13},{13,1},{2,6},{6,10},{... | collective-permute-start | bytes 393224 | tf_op jit(solution)/shard_map/ppermute | solution.py:175
  5.6 2.2 %collective-permute-start.2 = (bf16[16,4096]{1,0:T(8,128)(2,1)}, bf16[16,4096]{1,0:T(8,128)(2,1)S(1)}, u32[]{:S(2)}, u32[]{:S(2)}) collective-permute-start(bf16[16,4096]{1,0:T(8,128)(2,1)} %refs_7_.1), channel_id=1, source_target_pairs={{0,12},{4,0},{8,4},{12,8},{1,13},{5,1},{9,5},{13,9},{2,14},{6,2},{... | collective-permute-start | bytes 393224 | tf_op jit(solution)/shard_map/ppermute | solution.py:175
  7.9 0.7 %copy-done.3 = bf16[4096]{0:T(1024)(128)(2,1)S(1)} copy-done((bf16[4096]{0:T(1024)(128)(2,1)S(1)}, bf16[4096]{0:T(1024)(128)(2,1)}, u32[]{:S(2)}) %copy-start.3) | copy-done | bytes 8216
  8.6 7.1 %fetch_weight.1 = (f32[1,4096]{1,0:T(1,128)S(1)}, bf16[4096,2560]{1,0:T(8,128)(2,1)S(1)}) custom-call(bf16[4096,4096]{1,0:T(8,128)(2,1)} %refs_5_.2, bf16[4096]{0:T(1024)(128)(2,1)S(1)} %copy-done.3), custom_call_target="tpu_custom_call" | custom-call | bytes 20971520 | tf_op jit(solution)/shard_map/fetch_weight/pallas_call | solution.py:191
  15.7 0.0 collective-permute-done.1.refs_9_
  15.7 0.0 collective-permute-done.refs_8_
  15.7 0.0 collective-permute-done.2.refs_10_
  15.8 0.0 copy-start
  15.8 8.3 %first_columns.1 = (bf16[64,4096]{1,0:T(8,128)(2,1)S(1)}, f32[64,128]{1,0:T(8,128)S(1)}, bf16[64,128]{1,0:T(8,128)(2,1)S(1)}, f32[64,2560]{1,0:T(8,128)S(1)}, bf16[4096,1536]{1,0:T(8,128)(2,1)S(1)}) custom-call(s32[4]{0:T(128)S(1)} %copy-done.5, s32[4]{0:T(128)S(1)} %copy-done.6, s32[5]{0:T(128)S(1)} %copy-done.4, f32[1,4096]{1,0:T(1,128)S(1)} %get-tuple-element.16.refs_3_, ...), custom_call_target="tpu_custom_call" | custom-call | flops 1342177280 | bytes 12582912 | tf_op jit(solution)/shard_map/first_columns/pallas_call | solution.py:205
  24.1 1.3 %collective-permute-start.5 = (bf16[64,128]{1,0:T(8,128)(2,1)S(1)}, bf16[64,128]{1,0:T(8,128)(2,1)S(1)}, u32[]{:S(2)}, u32[]{:S(2)}) collective-permute-start(bf16[64,128]{1,0:T(8,128)(2,1)S(1)} %get-tuple-element.22.refs_6_), channel_id=1, source_target_pairs={{0,12},{4,0},{8,4},{12,8},{1,13},{5,1},{9,5},{13,9},{2,14},{6,2},{... | collective-permute-start | bytes 49160 | tf_op jit(solution)/shard_map/ppermute | solution.py:175
  25.4 1.9 %collective-permute-start.4 = (bf16[64,128]{1,0:T(8,128)(2,1)S(1)}, bf16[64,128]{1,0:T(8,128)(2,1)S(1)}, u32[]{:S(2)}, u32[]{:S(2)}) collective-permute-start(bf16[64,128]{1,0:T(8,128)(2,1)S(1)} %get-tuple-element.22.refs_6_), channel_id=1, source_target_pairs={{0,8},{4,12},{8,0},{12,4},{1,9},{5,13},{9,1},{13,5},{2,10},{6,14},... | collective-permute-start | bytes 49160 | tf_op jit(solution)/shard_map/ppermute | solution.py:175
  27.3 1.9 %collective-permute-start.3 = (bf16[64,128]{1,0:T(8,128)(2,1)S(1)}, bf16[64,128]{1,0:T(8,128)(2,1)S(1)}, u32[]{:S(2)}, u32[]{:S(2)}) collective-permute-start(bf16[64,128]{1,0:T(8,128)(2,1)S(1)} %get-tuple-element.22.refs_6_), channel_id=1, source_target_pairs={{0,4},{4,8},{8,12},{12,0},{1,5},{5,9},{9,13},{13,1},{2,6},{6,10},{... | collective-permute-start | bytes 49160 | tf_op jit(solution)/shard_map/ppermute | solution.py:175
  29.3 0.0 collective-permute-done.5.refs_9_
  29.3 0.8 %collective-permute-done.4.refs_8_ = bf16[64,128]{1,0:T(8,128)(2,1)S(1)} collective-permute-done((bf16[64,128]{1,0:T(8,128)(2,1)S(1)}, bf16[64,128]{1,0:T(8,128)(2,1)S(1)}, u32[]{:S(2)}, u32[]{:S(2)}) %collective-permute-start.4) | collective-permute-done | bytes 16416 | tf_op jit(solution)/shard_map/ppermute | solution.py:175
  30.1 2.8 %collective-permute-done.3.refs_7_ = bf16[64,128]{1,0:T(8,128)(2,1)S(1)} collective-permute-done((bf16[64,128]{1,0:T(8,128)(2,1)S(1)}, bf16[64,128]{1,0:T(8,128)(2,1)S(1)}, u32[]{:S(2)}, u32[]{:S(2)}) %collective-permute-start.3) | collective-permute-done | bytes 16416 | tf_op jit(solution)/shard_map/ppermute | solution.py:175
  32.8 3.3 %last_columns.1 = (f32[16,4224]{1,0:T(8,128)S(1)}, bf16[16,4224]{1,0:T(8,128)(2,1)S(1)}, bf16[16,4224]{1,0:T(8,128)(2,1)S(1)}, bf16[16,4224]{1,0:T(8,128)(2,1)S(1)}) custom-call(s32[5]{0:T(128)S(1)} %copy-done.4, bf16[64,4096]{1,0:T(8,128)(2,1)S(1)} %get-tuple-element.18.refs_1_, f32[64,128]{1,0:T(8,128)S(1)} %get-tuple-element.19.refs_2_, ...), custom_call_target="tpu_custom_call" | custom-call | flops 805306368 | bytes 12582912 | tf_op jit(solution)/shard_map/last_columns/pallas_call | solution.py:234
  36.1 0.1 collective-permute-start.6
  36.2 1.6 %collective-permute-start.7 = (bf16[16,4224]{1,0:T(8,128)(2,1)S(1)}, bf16[16,4224]{1,0:T(8,128)(2,1)S(1)}, u32[]{:S(2)}, u32[]{:S(2)}) collective-permute-start(bf16[16,4224]{1,0:T(8,128)(2,1)S(1)} %get-tuple-element.25), channel_id=1, source_target_pairs={{0,2},{1,3},{2,0},{3,1},{4,6},{5,7},{6,4},{7,5},{8,10},{9,11},{10,... | collective-permute-start | bytes 405512 | tf_op jit(solution)/shard_map/ppermute | solution.py:182
  37.8 0.3 collective-permute-start.8
  38.1 0.0 collective-permute-done.6.refs_1_
  38.1 4.6 %collective-permute-done.7.refs_2_ = bf16[16,4224]{1,0:T(8,128)(2,1)S(1)} collective-permute-done((bf16[16,4224]{1,0:T(8,128)(2,1)S(1)}, bf16[16,4224]{1,0:T(8,128)(2,1)S(1)}, u32[]{:S(2)}, u32[]{:S(2)}) %collective-permute-start.7) | collective-permute-done | bytes 135200 | tf_op jit(solution)/shard_map/ppermute | solution.py:182
  42.7 2.0 %collective-permute-done.8.refs_3_ = bf16[16,4224]{1,0:T(8,128)(2,1)S(1)} collective-permute-done((bf16[16,4224]{1,0:T(8,128)(2,1)S(1)}, bf16[16,4224]{1,0:T(8,128)(2,1)S(1)}, u32[]{:S(2)}, u32[]{:S(2)}) %collective-permute-start.8) | collective-permute-done | bytes 135200 | tf_op jit(solution)/shard_map/ppermute | solution.py:182
  44.6 0.8 %query_rows.1 = bf16[16,4096]{1,0:T(8,128)(2,1)} custom-call(f32[16,4224]{1,0:T(8,128)S(1)} %get-tuple-element.23.refs_0_, bf16[16,4224]{1,0:T(8,128)(2,1)S(1)} %collective-permute-done.6.refs_1_, bf16[16,4224]{1,0:T(8,128)(2,1)S(1)} %collective-permute-done.7.refs_2_, bf16[16,4224]{1,0:T(8,128)(2,1)S(1)} %collective-permute-done.8.refs_3_), custom_call_target="tpu_custom_call" | custom-call | tf_op jit(solution)/shard_map/query_rows/pallas_call | solution.py:254
  (12 shorter events, 0.0 us)
Async XLA Ops:
  0.0 15.8 %copy-start.2 = (bf16[16,4096]{1,0:T(8,128)(2,1)S(1)}, bf16[16,4096]{1,0:T(8,128)(2,1)}, u32[]{:S(2)}) copy-start(bf16[16,4096]{1,0:T(8,128)(2,1)} %refs_7_.1) | copy-start | bytes 393220
  0.0 15.8 %copy-start.1 = (bf16[1,4096,64]{1,2,0:T(8,128)(2,1)S(1)}, bf16[1,4096,64]{1,2,0:T(8,128)(2,1)}, u32[]{:S(2)}) copy-start(bf16[1,4096,64]{1,2,0:T(8,128)(2,1)} %param.12) | copy-start | bytes 1572868
  0.0 15.7 %collective-permute-start.1 = (bf16[16,4096]{1,0:T(8,128)(2,1)}, bf16[16,4096]{1,0:T(8,128)(2,1)S(1)}, u32[]{:S(2)}, u32[]{:S(2)}) collective-permute-start(bf16[16,4096]{1,0:T(8,128)(2,1)} %refs_7_.1), channel_id=1, source_target_pairs={{0,8},{4,12},{8,0},{12,4},{1,9},{5,13},{9,1},{13,5},{2,10},{6,14},... | collective-permute-start | bytes 393224 | tf_op jit(solution)/shard_map/ppermute | solution.py:175
  4.0 11.7 %collective-permute-start = (bf16[16,4096]{1,0:T(8,128)(2,1)}, bf16[16,4096]{1,0:T(8,128)(2,1)S(1)}, u32[]{:S(2)}, u32[]{:S(2)}) collective-permute-start(bf16[16,4096]{1,0:T(8,128)(2,1)} %refs_7_.1), channel_id=1, source_target_pairs={{0,4},{4,8},{8,12},{12,0},{1,5},{5,9},{9,13},{13,1},{2,6},{6,10},{... | collective-permute-start | bytes 393224 | tf_op jit(solution)/shard_map/ppermute | solution.py:175
  5.6 10.1 %collective-permute-start.2 = (bf16[16,4096]{1,0:T(8,128)(2,1)}, bf16[16,4096]{1,0:T(8,128)(2,1)S(1)}, u32[]{:S(2)}, u32[]{:S(2)}) collective-permute-start(bf16[16,4096]{1,0:T(8,128)(2,1)} %refs_7_.1), channel_id=1, source_target_pairs={{0,12},{4,0},{8,4},{12,8},{1,13},{5,1},{9,5},{13,9},{2,14},{6,2},{... | collective-permute-start | bytes 393224 | tf_op jit(solution)/shard_map/ppermute | solution.py:175
  7.9 0.7 %copy-start.3 = (bf16[4096]{0:T(1024)(128)(2,1)S(1)}, bf16[4096]{0:T(1024)(128)(2,1)}, u32[]{:S(2)}) copy-start(bf16[4096]{0:T(1024)(128)(2,1)} %gain_ref.1) | copy-start | bytes 24580
  8.6 7.2 %copy-start.4 = (s32[5]{0:T(128)S(1)}, s32[5]{0:T(128)}, u32[]{:S(2)}) copy-start(s32[5]{0:T(128)} %refs_0_.3) | copy-start | bytes 64
  8.6 7.2 %copy-start.5 = (s32[4]{0:T(128)S(1)}, s32[4]{0:T(128)}, u32[]{:S(2)}) copy-start(s32[4]{0:T(128)} %refs_0_.2) | copy-start | bytes 52
  8.6 7.2 %copy-start.6 = (s32[4]{0:T(128)S(1)}, s32[4]{0:T(128)}, u32[]{:S(2)}) copy-start(s32[4]{0:T(128)} %refs_1_.1) | copy-start | bytes 52
  15.8 17.0 %copy-start = (bf16[4,64,4096]{2,1,0:T(8,128)(2,1)S(1)}, bf16[4,64,4096]{2,1,0:T(8,128)(2,1)}, u32[]{:S(2)}) copy-start(bf16[4,64,4096]{2,1,0:T(8,128)(2,1)} %refs_5_.3) | copy-start | bytes 6291460
  24.1 5.1 %collective-permute-start.5 = (bf16[64,128]{1,0:T(8,128)(2,1)S(1)}, bf16[64,128]{1,0:T(8,128)(2,1)S(1)}, u32[]{:S(2)}, u32[]{:S(2)}) collective-permute-start(bf16[64,128]{1,0:T(8,128)(2,1)S(1)} %get-tuple-element.22.refs_6_), channel_id=1, source_target_pairs={{0,12},{4,0},{8,4},{12,8},{1,13},{5,1},{9,5},{13,9},{2,14},{6,2},{... | collective-permute-start | bytes 49160 | tf_op jit(solution)/shard_map/ppermute | solution.py:175
  25.4 4.6 %collective-permute-start.4 = (bf16[64,128]{1,0:T(8,128)(2,1)S(1)}, bf16[64,128]{1,0:T(8,128)(2,1)S(1)}, u32[]{:S(2)}, u32[]{:S(2)}) collective-permute-start(bf16[64,128]{1,0:T(8,128)(2,1)S(1)} %get-tuple-element.22.refs_6_), channel_id=1, source_target_pairs={{0,8},{4,12},{8,0},{12,4},{1,9},{5,13},{9,1},{13,5},{2,10},{6,14},... | collective-permute-start | bytes 49160 | tf_op jit(solution)/shard_map/ppermute | solution.py:175
  27.3 5.5 %collective-permute-start.3 = (bf16[64,128]{1,0:T(8,128)(2,1)S(1)}, bf16[64,128]{1,0:T(8,128)(2,1)S(1)}, u32[]{:S(2)}, u32[]{:S(2)}) collective-permute-start(bf16[64,128]{1,0:T(8,128)(2,1)S(1)} %get-tuple-element.22.refs_6_), channel_id=1, source_target_pairs={{0,4},{4,8},{8,12},{12,0},{1,5},{5,9},{9,13},{13,1},{2,6},{6,10},{... | collective-permute-start | bytes 49160 | tf_op jit(solution)/shard_map/ppermute | solution.py:175
  36.1 1.9 %collective-permute-start.6 = (bf16[16,4224]{1,0:T(8,128)(2,1)S(1)}, bf16[16,4224]{1,0:T(8,128)(2,1)S(1)}, u32[]{:S(2)}, u32[]{:S(2)}) collective-permute-start(bf16[16,4224]{1,0:T(8,128)(2,1)S(1)} %get-tuple-element.24), channel_id=1, source_target_pairs={{0,1},{1,0},{2,3},{3,2},{4,5},{5,4},{6,7},{7,6},{8,9},{9,8},{10,11... | collective-permute-start | bytes 405512 | tf_op jit(solution)/shard_map/ppermute | solution.py:182
  36.2 6.5 %collective-permute-start.7 = (bf16[16,4224]{1,0:T(8,128)(2,1)S(1)}, bf16[16,4224]{1,0:T(8,128)(2,1)S(1)}, u32[]{:S(2)}, u32[]{:S(2)}) collective-permute-start(bf16[16,4224]{1,0:T(8,128)(2,1)S(1)} %get-tuple-element.25), channel_id=1, source_target_pairs={{0,2},{1,3},{2,0},{3,1},{4,6},{5,7},{6,4},{7,5},{8,10},{9,11},{10,... | collective-permute-start | bytes 405512 | tf_op jit(solution)/shard_map/ppermute | solution.py:182
  37.8 6.9 %collective-permute-start.8 = (bf16[16,4224]{1,0:T(8,128)(2,1)S(1)}, bf16[16,4224]{1,0:T(8,128)(2,1)S(1)}, u32[]{:S(2)}, u32[]{:S(2)}) collective-permute-start(bf16[16,4224]{1,0:T(8,128)(2,1)S(1)} %get-tuple-element.26), channel_id=1, source_target_pairs={{0,3},{1,2},{2,1},{3,0},{4,7},{5,6},{6,5},{7,4},{8,11},{9,10},{10,... | collective-permute-start | bytes 405512 | tf_op jit(solution)/shard_map/ppermute | solution.py:182

commit v3 on v2

--- a/solution.py
+++ b/solution.py
@@ -39,34 +39,28 @@
     ]
 
 
-def fetch_kernel(w_hbm, gain_ref, gain_out, w_vmem, sems):
-    copies = weight_copies(w_hbm, 0, w_vmem, sems)
+def fetch_kernel(n, w_hbm, token_ref, *refs):
+    weights, sems = refs[:n], refs[n]
+    copies = []
+    first = 0
+    for j, w_vmem in enumerate(weights):
+        copies += weight_copies(w_hbm, first, w_vmem, sems.at[j])
+        first += w_vmem.shape[1]
     for copy in copies:
         copy.start()
-    gain_out[...] = gain_ref[...].astype(jnp.float32).reshape(gain_out.shape)
+    token_ref[...] = jnp.zeros(token_ref.shape, token_ref.dtype)
     for copy in copies:
         copy.wait()
 
 
-def multiply(x_ref, w_ref, out_ref, first, step):
-    width = w_ref.shape[1]
-    for c in range(0, width, step):
-        out_ref[:, first + c : first + c + step] = jnp.dot(
-            x_ref[...], w_ref[:, c : c + step], preferred_element_type=jnp.float32
-        )
-
-
-def first_kernel(n, step, width, *refs):
-    rank_ref, slot_ref, start_ref, gain_ref, down_ref, w_hbm, w_ref = refs[:7]
-    blocks = refs[7 : 7 + n]
-    x_ref, square_ref, down_out, base_ref, rest_ref, sems = refs[7 + n :]
-    copies = weight_copies(w_hbm, w_ref.shape[1], rest_ref, sems)
-    for copy in copies:
-        copy.start()
+def rows_kernel(n, width, *refs):
+    rank_ref, slot_ref, start_ref, gain_ref, down_ref, _ = refs[:6]
+    blocks = refs[6 : 6 + n]
+    x_ref, square_ref, down_out = refs[6 + n :]
     home = lax.axis_index("gx")
     block_rows = blocks[0].shape[0]
     rows = n * block_rows
-    gain = gain_ref[...]
+    gain = gain_ref[...].astype(jnp.float32).reshape(1, gain_ref.shape[0])
     for k in range(n):
         source = lax.rem(home - k + n, n)
         begin = pl.multiple_of(source * block_rows, block_rows)
@@ -89,18 +83,15 @@
         total = total + jnp.where(live, projected * scale, 0.0)
     down_out[...] = jnp.zeros(down_out.shape, down_out.dtype)
     down_out[:, :rank_columns] = total.astype(down_out.dtype)
-    multiply(x_ref, w_ref, base_ref, 0, step)
-    for copy in copies:
-        copy.wait()
-
-
-def second_kernel(n_x, groups, step, offset, *refs):
-    start_ref, x_ref, square_ref, base_ref, w_ref, up_ref = refs[:6]
-    downs = refs[6 : 6 + n_x]
-    outs, acc = refs[6 + n_x : -1], refs[-1]
+
+
+def product_kernel(n_x, n_w, groups, step, offset, *refs):
+    start_ref, x_ref, square_ref, up_ref = refs[:4]
+    downs, refs = refs[4 : 4 + n_x], refs[4 + n_x :]
+    weights, outs, acc = refs[:n_w], refs[n_w:-1], refs[-1]
     rows = x_ref.shape[0]
-    done = base_ref.shape[1]
-    columns = done + w_ref.shape[1]
+    width = weights[0].shape[1]
+    columns = width * n_w
     adapters, rank_columns, _ = up_ref.shape
     down = downs[0][:, :rank_columns]
     for other in downs[1:]:
@@ -116,14 +107,13 @@
     for c in range(0, columns, step):
         here = slice(c, c + step)
         up = up_ref[:, :, here].reshape(adapters * rank_columns, step)
-        delta = jnp.dot(spread, up, preferred_element_type=jnp.float32)
-        if c < done:
-            base = base_ref[:, here]
-        else:
-            base = jnp.dot(
-                x_ref[...], w_ref[:, c - done : c - done + step], preferred_element_type=jnp.float32
-            )
-        acc[:, here] = base + delta
+        inner = c % width
+        base = jnp.dot(
+            x_ref[...],
+            weights[c // width][:, inner : inner + step],
+            preferred_element_type=jnp.float32,
+        )
+        acc[:, here] = base + jnp.dot(spread, up, preferred_element_type=jnp.float32)
     square = square_ref[...]
     high = square.astype(jnp.bfloat16).astype(jnp.float32)
     low = jnp.where(high < jnp.inf, square - high, 0.0)
@@ -184,47 +174,38 @@
     blocks = [hidden] + [send_x(hidden, k) for k in range(1, n_x)]
 
     step = min(512, columns // 4)
-    first = columns * 5 // 8 // step * step
-    rest = columns - first
-    pieces = 8
+    n_w, pieces = 4, 4
     f32, bf16 = jnp.float32, jnp.bfloat16
-    gain, weight = pl.pallas_call(
-        fetch_kernel,
-        out_shape=(
-            jax.ShapeDtypeStruct((1, depth), f32),
-            pltpu.VMEM((depth, first), query_weight.dtype),
-        ),
-        in_specs=[ANY, VMEM],
-        out_specs=(VMEM, VMEM),
-        scratch_shapes=[pltpu.SemaphoreType.DMA((pieces,))],
-        cost_estimate=cost(0, 2 * depth * first),
-        compiler_params=params(12),
+    token, *weights = pl.pallas_call(
+        functools.partial(fetch_kernel, n_w),
+        out_shape=[jax.ShapeDtypeStruct((8, LANES), f32)]
+        + [pltpu.VMEM((depth, columns // n_w), query_weight.dtype)] * n_w,
+        in_specs=[ANY],
+        out_specs=[VMEM] * (1 + n_w),
+        scratch_shapes=[pltpu.SemaphoreType.DMA((n_w, pieces))],
+        cost_estimate=cost(0, 2 * query_weight.size),
+        compiler_params=params(4),
         name="fetch_weight",
-    )(query_weight, attention_norm_gain)
-
-    x, square, down, base, weight_rest = pl.pallas_call(
-        functools.partial(first_kernel, n_x, step, depth * groups),
+    )(query_weight)
+
+    x, square, down = pl.pallas_call(
+        functools.partial(rows_kernel, n_x, depth * groups),
         out_shape=(
             jax.ShapeDtypeStruct((rows, depth), bf16),
             jax.ShapeDtypeStruct((rows, LANES), f32),
             jax.ShapeDtypeStruct((rows, LANES), bf16),
-            jax.ShapeDtypeStruct((rows, first), f32),
-            pltpu.VMEM((depth, rest), query_weight.dtype),
         ),
-        in_specs=[SMEM] * 3 + [VMEM] * 2 + [ANY] + [VMEM] * (1 + n_x),
-        out_specs=(VMEM,) * 5,
-        scratch_shapes=[pltpu.SemaphoreType.DMA((pieces,))],
-        cost_estimate=cost(2 * rows * depth * first, 2 * depth * rest),
-        compiler_params=params(16),
-        name="first_columns",
+        in_specs=[SMEM] * 3 + [VMEM] * 2 + [ANY] + [VMEM] * n_x,
+        out_specs=(VMEM,) * 3,
+        compiler_params=params(4 + (rows * depth >> 16)),
+        name="scaled_rows",
     )(
         padded_adapter_rank,
         adapter_in_slot,
         segment_starts,
-        gain,
+        attention_norm_gain,
         jnp.swapaxes(slot_down_factors, 1, 2),
-        query_weight,
-        pltpu.with_memory_space_constraint(weight, pltpu.VMEM),
+        token,
         *blocks,
     )
 
@@ -232,22 +213,21 @@
 
     dtypes = [f32] + [bf16] * (groups - 1)
     made = pl.pallas_call(
-        functools.partial(second_kernel, n_x, groups, step, offset),
+        functools.partial(product_kernel, n_x, n_w, groups, step, offset),
         out_shape=[jax.ShapeDtypeStruct((rows_here, columns + LANES), t) for t in dtypes],
-        in_specs=[SMEM] + [VMEM] * (5 + n_x),
+        in_specs=[SMEM] + [VMEM] * (3 + n_x + n_w),
         out_specs=[VMEM] * groups,
         scratch_shapes=[pltpu.VMEM((rows, columns + LANES), f32)],
-        cost_estimate=cost(2 * rows * depth * rest, 2 * depth * rest),
-        compiler_params=params(16),
-        name="last_columns",
+        cost_estimate=cost(2 * rows * depth * columns, 2 * depth * columns),
+        compiler_params=params(4 + (rows * depth >> 16)),
+        name="product",
     )(
         segment_starts,
         x,
         square,
-        base,
-        pltpu.with_memory_space_constraint(weight_rest, pltpu.VMEM),
         adapter_up_factors,
         *downs,
+        *[pltpu.with_memory_space_constraint(w, pltpu.VMEM) for w in weights],
     )
     parts = [made[0]] + [send_g(made[k], k) for k in range(1, groups)]
 
@@ -256,7 +236,7 @@
         out_shape=jax.ShapeDtypeStruct((rows_here, columns), bf16),
         in_specs=[VMEM] * groups,
         out_specs=VMEM,
-        compiler_params=params(12),
+        compiler_params=params(4 + (rows * depth >> 16)),
         name="query_rows",
     )(*parts)
 

time: 45.7 us -> 43.2 us (0.945)
  starting transfers between devices: 14.9 us -> 11.9 us
  waiting for transfers between devices: 10.2 us -> 11.3 us
  local copies, waits for them, and re-layouts: 0.72 us -> 0.03 us
    ppermute x6, starting transfers between devices: 13 us -> 10 us  [send_x(): return lax.ppermute(value, 'gx', [(j, (j + k) % n_x) for j in range(n_x)])]
    ppermute x6, waiting for transfers between devices: 3.6 us -> 4.75 us  [send_x(): return lax.ppermute(value, 'gx', [(j, (j + k) % n_x) for j in range(n_x)])]
    unnamed x14, local copies, waits for them, and re-layouts: 0.72 us -> 0.03 us
  transfers between devices with their start and end apart: 9 -> 9, of which waited for: 4 -> 5; matrix products, arithmetic and copies ran while one was open for 0% -> 0% of each run, Pallas kernels for 16% -> 25%
where the time goes in v3:
time: 43.2 us; the launch traced here: 43.1 us
  Pallas kernels  19.7 us (46%)
  starting transfers between devices  11.9 us (28%)
  waiting for transfers between devices  11.3 us (26%)
    pallas_call x1, Pallas kernels, body(): pl.pallas_call(functools.partial(fetch_kernel, n_w), out_shape=[jax.Shape...  10.9 us
    ppermute x6, starting transfers between devices, send_x(): return lax.ppermute(value, 'gx', [(j, (j + k) % n_x) for j in range(n_x)])  10 us
    pallas_call x1, Pallas kernels, body(): pl.pallas_call(functools.partial(product_kernel, n_x, n_w, groups, step,...  6.92 us
    ppermute x3, waiting for transfers between devices, send_g(): return lax.ppermute(value, ('gy', 'gz'), pairs)  6.58 us
    ppermute x6, waiting for transfers between devices, send_x(): return lax.ppermute(value, 'gx', [(j, (j + k) % n_x) for j in range(n_x)])  4.75 us
    ppermute x3, starting transfers between devices, send_g(): return lax.ppermute(value, ('gy', 'gz'), pairs)  1.93 us
    pallas_call x1, Pallas kernels, body(): pl.pallas_call(functools.partial(rows_kernel, n_x, depth * groups), out_s...  1.03 us
  transfers between devices with their start and end apart: 9, of which 5 were waited for; matrix products, arithmetic and copies ran while one was open for 0% of the time, Pallas kernels for 25%

profile of v3, /device:TPU:0, one launch (start us, length us, event | category | flops | bytes accessed | tf_op | source)
XLA Modules:
  0.0 43.1 jit_solution(2403975473777027805)
XLA Ops:
  0.0 0.0 copy-start.3
  0.0 4.1 %collective-permute-start.1 = (bf16[16,4096]{1,0:T(8,128)(2,1)}, bf16[16,4096]{1,0:T(8,128)(2,1)S(1)}, u32[]{:S(2)}, u32[]{:S(2)}) collective-permute-start(bf16[16,4096]{1,0:T(8,128)(2,1)} %refs_6_.1), channel_id=1, source_target_pairs={{0,8},{4,12},{8,0},{12,4},{1,9},{5,13},{9,1},{13,5},{2,10},{6,14},... | collective-permute-start | bytes 393224 | tf_op jit(solution)/shard_map/ppermute | solution.py:165
  4.2 1.6 %collective-permute-start = (bf16[16,4096]{1,0:T(8,128)(2,1)}, bf16[16,4096]{1,0:T(8,128)(2,1)S(1)}, u32[]{:S(2)}, u32[]{:S(2)}) collective-permute-start(bf16[16,4096]{1,0:T(8,128)(2,1)} %refs_6_.1), channel_id=1, source_target_pairs={{0,4},{4,8},{8,12},{12,0},{1,5},{5,9},{9,13},{13,1},{2,6},{6,10},{... | collective-permute-start | bytes 393224 | tf_op jit(solution)/shard_map/ppermute | solution.py:165
  5.7 2.2 %collective-permute-start.2 = (bf16[16,4096]{1,0:T(8,128)(2,1)}, bf16[16,4096]{1,0:T(8,128)(2,1)S(1)}, u32[]{:S(2)}, u32[]{:S(2)}) collective-permute-start(bf16[16,4096]{1,0:T(8,128)(2,1)} %refs_6_.1), channel_id=1, source_target_pairs={{0,12},{4,0},{8,4},{12,8},{1,13},{5,1},{9,5},{13,9},{2,14},{6,2},{... | collective-permute-start | bytes 393224 | tf_op jit(solution)/shard_map/ppermute | solution.py:165
  8.0 10.9 %fetch_weight.1 = (f32[8,128]{1,0:T(8,128)S(1)}, bf16[4096,1024]{1,0:T(8,128)(2,1)S(1)}, bf16[4096,1024]{1,0:T(8,128)(2,1)S(1)}, bf16[4096,1024]{1,0:T(8,128)(2,1)S(1)}, bf16[4096,1024]{1,0:T(8,128)(2,1)S(1)}) custom-call(bf16[4096,4096]{1,0:T(8,128)(2,1)} %w_hbm.1), custom_call_target="tpu_custom_call" | custom-call | bytes 33554432 | tf_op jit(solution)/shard_map/fetch_weight/pallas_call | solution.py:179
  18.9 0.0 collective-permute-done.1.refs_8_
  18.9 0.0 collective-permute-done.refs_7_
  18.9 0.0 collective-permute-done.2.refs_9_
  19.0 1.0 %scaled_rows.1 = (bf16[64,4096]{1,0:T(8,128)(2,1)S(1)}, f32[64,128]{1,0:T(8,128)S(1)}, bf16[64,128]{1,0:T(8,128)(2,1)S(1)}) custom-call(s32[4]{0:T(128)S(1)} %copy-done.5, s32[4]{0:T(128)S(1)} %copy-done.6, s32[5]{0:T(128)S(1)} %copy-done.4, bf16[4096]{0:T(1024)(128)(2,1)S(1)} %copy-done.3, bf16[1,64,4096]{2,1,0:T(8,128)(2,1)S(1)} %bitcast.1, ...), custom_call_target="tpu_custom_call" | custom-call | tf_op jit(solution)/shard_map/scaled_rows/pallas_call | solution.py:191
  20.0 0.1 collective-permute-start.5
  20.1 1.2 %collective-permute-start.4 = (bf16[64,128]{1,0:T(8,128)(2,1)S(1)}, bf16[64,128]{1,0:T(8,128)(2,1)S(1)}, u32[]{:S(2)}, u32[]{:S(2)}) collective-permute-start(bf16[64,128]{1,0:T(8,128)(2,1)S(1)} %get-tuple-element.20.refs_4_), channel_id=1, source_target_pairs={{0,8},{4,12},{8,0},{12,4},{1,9},{5,13},{9,1},{13,5},{2,10},{6,14},... | collective-permute-start | bytes 49160 | tf_op jit(solution)/shard_map/ppermute | solution.py:165
  21.3 0.8 %collective-permute-start.3 = (bf16[64,128]{1,0:T(8,128)(2,1)S(1)}, bf16[64,128]{1,0:T(8,128)(2,1)S(1)}, u32[]{:S(2)}, u32[]{:S(2)}) collective-permute-start(bf16[64,128]{1,0:T(8,128)(2,1)S(1)} %get-tuple-element.20.refs_4_), channel_id=1, source_target_pairs={{0,4},{4,8},{8,12},{12,0},{1,5},{5,9},{9,13},{13,1},{2,6},{6,10},{... | collective-permute-start | bytes 49160 | tf_op jit(solution)/shard_map/ppermute | solution.py:165
  22.1 1.7 %collective-permute-done.5.refs_7_ = bf16[64,128]{1,0:T(8,128)(2,1)S(1)} collective-permute-done((bf16[64,128]{1,0:T(8,128)(2,1)S(1)}, bf16[64,128]{1,0:T(8,128)(2,1)S(1)}, u32[]{:S(2)}, u32[]{:S(2)}) %collective-permute-start.5) | collective-permute-done | bytes 16416 | tf_op jit(solution)/shard_map/ppermute | solution.py:165
  23.8 1.0 %collective-permute-done.4.refs_6_ = bf16[64,128]{1,0:T(8,128)(2,1)S(1)} collective-permute-done((bf16[64,128]{1,0:T(8,128)(2,1)S(1)}, bf16[64,128]{1,0:T(8,128)(2,1)S(1)}, u32[]{:S(2)}, u32[]{:S(2)}) %collective-permute-start.4) | collective-permute-done | bytes 16416 | tf_op jit(solution)/shard_map/ppermute | solution.py:165
  24.8 2.1 %collective-permute-done.3.refs_5_ = bf16[64,128]{1,0:T(8,128)(2,1)S(1)} collective-permute-done((bf16[64,128]{1,0:T(8,128)(2,1)S(1)}, bf16[64,128]{1,0:T(8,128)(2,1)S(1)}, u32[]{:S(2)}, u32[]{:S(2)}) %collective-permute-start.3) | collective-permute-done | bytes 16416 | tf_op jit(solution)/shard_map/ppermute | solution.py:165
  26.8 0.0 copy-done
  26.8 6.9 %product.1 = (f32[16,4224]{1,0:T(8,128)S(1)}, bf16[16,4224]{1,0:T(8,128)(2,1)S(1)}, bf16[16,4224]{1,0:T(8,128)(2,1)S(1)}, bf16[16,4224]{1,0:T(8,128)(2,1)S(1)}) custom-call(s32[5]{0:T(128)S(1)} %copy-done.4, bf16[64,4096]{1,0:T(8,128)(2,1)S(1)} %get-tuple-element.18.refs_1_, f32[64,128]{1,0:T(8,128)S(1)} %get-tuple-element.19.refs_2_, ...), custom_call_target="tpu_custom_call" | custom-call | flops 2147483648 | bytes 33554432 | tf_op jit(solution)/shard_map/product/pallas_call | solution.py:215
  33.8 0.1 collective-permute-start.6
  33.8 1.6 %collective-permute-start.7 = (bf16[16,4224]{1,0:T(8,128)(2,1)S(1)}, bf16[16,4224]{1,0:T(8,128)(2,1)S(1)}, u32[]{:S(2)}, u32[]{:S(2)}) collective-permute-start(bf16[16,4224]{1,0:T(8,128)(2,1)S(1)} %get-tuple-element.27), channel_id=1, source_target_pairs={{0,2},{1,3},{2,0},{3,1},{4,6},{5,7},{6,4},{7,5},{8,10},{9,11},{10,... | collective-permute-start | bytes 405512 | tf_op jit(solution)/shard_map/ppermute | solution.py:172
  35.4 0.3 collective-permute-start.8
  35.7 0.0 collective-permute-done.6.refs_1_
  35.7 4.6 %collective-permute-done.7.refs_2_ = bf16[16,4224]{1,0:T(8,128)(2,1)S(1)} collective-permute-done((bf16[16,4224]{1,0:T(8,128)(2,1)S(1)}, bf16[16,4224]{1,0:T(8,128)(2,1)S(1)}, u32[]{:S(2)}, u32[]{:S(2)}) %collective-permute-start.7) | collective-permute-done | bytes 135200 | tf_op jit(solution)/shard_map/ppermute | solution.py:172
  40.3 2.0 %collective-permute-done.8.refs_3_ = bf16[16,4224]{1,0:T(8,128)(2,1)S(1)} collective-permute-done((bf16[16,4224]{1,0:T(8,128)(2,1)S(1)}, bf16[16,4224]{1,0:T(8,128)(2,1)S(1)}, u32[]{:S(2)}, u32[]{:S(2)}) %collective-permute-start.8) | collective-permute-done | bytes 135200 | tf_op jit(solution)/shard_map/ppermute | solution.py:172
  42.3 0.8 %query_rows.1 = bf16[16,4096]{1,0:T(8,128)(2,1)} custom-call(f32[16,4224]{1,0:T(8,128)S(1)} %get-tuple-element.25.refs_0_, bf16[16,4224]{1,0:T(8,128)(2,1)S(1)} %collective-permute-done.6.refs_1_, bf16[16,4224]{1,0:T(8,128)(2,1)S(1)} %collective-permute-done.7.refs_2_, bf16[16,4224]{1,0:T(8,128)(2,1)S(1)} %collective-permute-done.8.refs_3_), custom_call_target="tpu_custom_call" | custom-call | tf_op jit(solution)/shard_map/query_rows/pallas_call | solution.py:234
  (12 shorter events, 0.0 us)
Async XLA Ops:
  0.0 18.9 %copy-start.2 = (bf16[16,4096]{1,0:T(8,128)(2,1)S(1)}, bf16[16,4096]{1,0:T(8,128)(2,1)}, u32[]{:S(2)}) copy-start(bf16[16,4096]{1,0:T(8,128)(2,1)} %refs_6_.1) | copy-start | bytes 393220
  0.0 18.9 %copy-start.4 = (s32[5]{0:T(128)S(1)}, s32[5]{0:T(128)}, u32[]{:S(2)}) copy-start(s32[5]{0:T(128)} %refs_0_.3) | copy-start | bytes 64
  0.0 18.9 %copy-start.6 = (s32[4]{0:T(128)S(1)}, s32[4]{0:T(128)}, u32[]{:S(2)}) copy-start(s32[4]{0:T(128)} %refs_1_.1) | copy-start | bytes 52
  0.0 18.9 %copy-start.5 = (s32[4]{0:T(128)S(1)}, s32[4]{0:T(128)}, u32[]{:S(2)}) copy-start(s32[4]{0:T(128)} %refs_0_.2) | copy-start | bytes 52
  0.0 18.9 %copy-start.1 = (bf16[1,4096,64]{1,2,0:T(8,128)(2,1)S(1)}, bf16[1,4096,64]{1,2,0:T(8,128)(2,1)}, u32[]{:S(2)}) copy-start(bf16[1,4096,64]{1,2,0:T(8,128)(2,1)} %param.12) | copy-start | bytes 1572868
  0.0 18.9 %copy-start.3 = (bf16[4096]{0:T(1024)(128)(2,1)S(1)}, bf16[4096]{0:T(1024)(128)(2,1)}, u32[]{:S(2)}) copy-start(bf16[4096]{0:T(1024)(128)(2,1)} %refs_3_.2) | copy-start | bytes 24580
  0.0 26.8 %copy-start = (bf16[4,64,4096]{2,1,0:T(8,128)(2,1)S(1)}, bf16[4,64,4096]{2,1,0:T(8,128)(2,1)}, u32[]{:S(2)}) copy-start(bf16[4,64,4096]{2,1,0:T(8,128)(2,1)} %refs_3_.3) | copy-start | bytes 6291460
  0.0 18.8 %collective-permute-start.1 = (bf16[16,4096]{1,0:T(8,128)(2,1)}, bf16[16,4096]{1,0:T(8,128)(2,1)S(1)}, u32[]{:S(2)}, u32[]{:S(2)}) collective-permute-start(bf16[16,4096]{1,0:T(8,128)(2,1)} %refs_6_.1), channel_id=1, source_target_pairs={{0,8},{4,12},{8,0},{12,4},{1,9},{5,13},{9,1},{13,5},{2,10},{6,14},... | collective-permute-start | bytes 393224 | tf_op jit(solution)/shard_map/ppermute | solution.py:165
  4.2 14.7 %collective-permute-start = (bf16[16,4096]{1,0:T(8,128)(2,1)}, bf16[16,4096]{1,0:T(8,128)(2,1)S(1)}, u32[]{:S(2)}, u32[]{:S(2)}) collective-permute-start(bf16[16,4096]{1,0:T(8,128)(2,1)} %refs_6_.1), channel_id=1, source_target_pairs={{0,4},{4,8},{8,12},{12,0},{1,5},{5,9},{9,13},{13,1},{2,6},{6,10},{... | collective-permute-start | bytes 393224 | tf_op jit(solution)/shard_map/ppermute | solution.py:165
  5.7 13.2 %collective-permute-start.2 = (bf16[16,4096]{1,0:T(8,128)(2,1)}, bf16[16,4096]{1,0:T(8,128)(2,1)S(1)}, u32[]{:S(2)}, u32[]{:S(2)}) collective-permute-start(bf16[16,4096]{1,0:T(8,128)(2,1)} %refs_6_.1), channel_id=1, source_target_pairs={{0,12},{4,0},{8,4},{12,8},{1,13},{5,1},{9,5},{13,9},{2,14},{6,2},{... | collective-permute-start | bytes 393224 | tf_op jit(solution)/shard_map/ppermute | solution.py:165
  20.0 3.8 %collective-permute-start.5 = (bf16[64,128]{1,0:T(8,128)(2,1)S(1)}, bf16[64,128]{1,0:T(8,128)(2,1)S(1)}, u32[]{:S(2)}, u32[]{:S(2)}) collective-permute-start(bf16[64,128]{1,0:T(8,128)(2,1)S(1)} %get-tuple-element.20.refs_4_), channel_id=1, source_target_pairs={{0,12},{4,0},{8,4},{12,8},{1,13},{5,1},{9,5},{13,9},{2,14},{6,2},{... | collective-permute-start | bytes 49160 | tf_op jit(solution)/shard_map/ppermute | solution.py:165
  20.1 4.7 %collective-permute-start.4 = (bf16[64,128]{1,0:T(8,128)(2,1)S(1)}, bf16[64,128]{1,0:T(8,128)(2,1)S(1)}, u32[]{:S(2)}, u32[]{:S(2)}) collective-permute-start(bf16[64,128]{1,0:T(8,128)(2,1)S(1)} %get-tuple-element.20.refs_4_), channel_id=1, source_target_pairs={{0,8},{4,12},{8,0},{12,4},{1,9},{5,13},{9,1},{13,5},{2,10},{6,14},... | collective-permute-start | bytes 49160 | tf_op jit(solution)/shard_map/ppermute | solution.py:165
  21.3 5.5 %collective-permute-start.3 = (bf16[64,128]{1,0:T(8,128)(2,1)S(1)}, bf16[64,128]{1,0:T(8,128)(2,1)S(1)}, u32[]{:S(2)}, u32[]{:S(2)}) collective-permute-start(bf16[64,128]{1,0:T(8,128)(2,1)S(1)} %get-tuple-element.20.refs_4_), channel_id=1, source_target_pairs={{0,4},{4,8},{8,12},{12,0},{1,5},{5,9},{9,13},{13,1},{2,6},{6,10},{... | collective-permute-start | bytes 49160 | tf_op jit(solution)/shard_map/ppermute | solution.py:165
  33.8 1.9 %collective-permute-start.6 = (bf16[16,4224]{1,0:T(8,128)(2,1)S(1)}, bf16[16,4224]{1,0:T(8,128)(2,1)S(1)}, u32[]{:S(2)}, u32[]{:S(2)}) collective-permute-start(bf16[16,4224]{1,0:T(8,128)(2,1)S(1)} %get-tuple-element.26), channel_id=1, source_target_pairs={{0,1},{1,0},{2,3},{3,2},{4,5},{5,4},{6,7},{7,6},{8,9},{9,8},{10,11... | collective-permute-start | bytes 405512 | tf_op jit(solution)/shard_map/ppermute | solution.py:172
  33.8 6.5 %collective-permute-start.7 = (bf16[16,4224]{1,0:T(8,128)(2,1)S(1)}, bf16[16,4224]{1,0:T(8,128)(2,1)S(1)}, u32[]{:S(2)}, u32[]{:S(2)}) collective-permute-start(bf16[16,4224]{1,0:T(8,128)(2,1)S(1)} %get-tuple-element.27), channel_id=1, source_target_pairs={{0,2},{1,3},{2,0},{3,1},{4,6},{5,7},{6,4},{7,5},{8,10},{9,11},{10,... | collective-permute-start | bytes 405512 | tf_op jit(solution)/shard_map/ppermute | solution.py:172
  35.4 6.9 %collective-permute-start.8 = (bf16[16,4224]{1,0:T(8,128)(2,1)S(1)}, bf16[16,4224]{1,0:T(8,128)(2,1)S(1)}, u32[]{:S(2)}, u32[]{:S(2)}) collective-permute-start(bf16[16,4224]{1,0:T(8,128)(2,1)S(1)} %get-tuple-element.28), channel_id=1, source_target_pairs={{0,3},{1,2},{2,1},{3,0},{4,7},{5,6},{6,5},{7,4},{8,11},{9,10},{10,... | collective-permute-start | bytes 405512 | tf_op jit(solution)/shard_map/ppermute | solution.py:172

commit v4 on v3

--- a/solution.py
+++ b/solution.py
@@ -82,20 +82,21 @@
         scale = ADAPTER_ALPHA / jnp.full((rows, rank_columns), rank, jnp.int32).astype(jnp.float32)
         total = total + jnp.where(live, projected * scale, 0.0)
     down_out[...] = jnp.zeros(down_out.shape, down_out.dtype)
-    down_out[:, :rank_columns] = total.astype(down_out.dtype)
-
-
-def product_kernel(n_x, n_w, groups, step, offset, *refs):
-    start_ref, x_ref, square_ref, up_ref = refs[:4]
-    downs, refs = refs[4 : 4 + n_x], refs[4 + n_x :]
-    weights, outs, acc = refs[:n_w], refs[n_w:-1], refs[-1]
+    for k in range(n):
+        down_out[k, :, :rank_columns] = total.astype(down_out.dtype)
+
+
+def product_kernel(n_w, step, *refs):
+    start_ref, x_ref, square_ref, up_ref, downs = refs[:5]
+    weights, out_ref = refs[5 : 5 + n_w], refs[5 + n_w]
     rows = x_ref.shape[0]
     width = weights[0].shape[1]
     columns = width * n_w
     adapters, rank_columns, _ = up_ref.shape
-    down = downs[0][:, :rank_columns]
-    for other in downs[1:]:
-        down = down + other[:, :rank_columns]
+    down = downs[0, :, :rank_columns]
+    for k in range(1, downs.shape[0]):
+        down = down + downs[k, :, :rank_columns]
+    groups, rows_here, _ = out_ref.shape
     row = lax.broadcasted_iota(jnp.int32, (rows, rank_columns), 0)
     spread = jnp.concatenate(
         [
@@ -113,25 +114,21 @@
             weights[c // width][:, inner : inner + step],
             preferred_element_type=jnp.float32,
         )
-        acc[:, here] = base + jnp.dot(spread, up, preferred_element_type=jnp.float32)
+        total = base + jnp.dot(spread, up, preferred_element_type=jnp.float32)
+        out_ref[:, :, here] = total.reshape(groups, rows_here, step).astype(out_ref.dtype)
     square = square_ref[...]
     high = square.astype(jnp.bfloat16).astype(jnp.float32)
     low = jnp.where(high < jnp.inf, square - high, 0.0)
     lane = lax.broadcasted_iota(jnp.int32, square.shape, 1)
-    acc[:, columns:] = jnp.where(lane < LANES // 2, high, low)
-    g = lax.axis_index(("gy", "gz"))
-    rows_here = outs[0].shape[0]
-    for k in range(groups):
-        begin = pl.multiple_of(offset(g, k) * rows_here, rows_here)
-        outs[k][...] = acc[pl.ds(begin, rows_here), :].astype(outs[k].dtype)
-
-
-def final_kernel(*refs):
-    parts, out_ref = refs[:-1], refs[-1]
+    both = jnp.where(lane < LANES // 2, high, low)
+    out_ref[:, :, columns:] = both.reshape(groups, rows_here, LANES).astype(out_ref.dtype)
+
+
+def final_kernel(parts, out_ref):
     columns = out_ref.shape[1]
-    total = parts[0][...]
-    for other in parts[1:]:
-        total = total + other[...].astype(jnp.float32)
+    total = parts[0].astype(jnp.float32)
+    for k in range(1, parts.shape[0]):
+        total = total + parts[k].astype(jnp.float32)
     mean_sq = total[:, columns : columns + 1] + total[:, columns + LANES - 1 :]
     scale = lax.rsqrt(mean_sq + EPSILON)
     value = jnp.where(mean_sq < jnp.inf, total[:, :columns] * scale, 0.0)
@@ -156,20 +153,8 @@
     rows = n_x * block_rows
     rows_here = rows // groups
 
-    def offset(g, k):
-        y = lax.rem(g // n_z + k // n_z, n_y)
-        z = lax.rem(lax.rem(g, n_z) + k % n_z, n_z)
-        return y * n_z + z
-
     def send_x(value, k):
         return lax.ppermute(value, "gx", [(j, (j + k) % n_x) for j in range(n_x)])
-
-    def send_g(value, k):
-        pairs = []
-        for g in range(groups):
-            y, z = (g // n_z + k // n_z) % n_y, (g % n_z + k % n_z) % n_z
-            pairs.append((g, y * n_z + z))
-        return lax.ppermute(value, ("gy", "gz"), pairs)
 
     blocks = [hidden] + [send_x(hidden, k) for k in range(1, n_x)]
 
@@ -193,7 +178,7 @@
         out_shape=(
             jax.ShapeDtypeStruct((rows, depth), bf16),
             jax.ShapeDtypeStruct((rows, LANES), f32),
-            jax.ShapeDtypeStruct((rows, LANES), bf16),
+            jax.ShapeDtypeStruct((n_x, rows, LANES), bf16),
         ),
         in_specs=[SMEM] * 3 + [VMEM] * 2 + [ANY] + [VMEM] * n_x,
         out_specs=(VMEM,) * 3,
@@ -209,15 +194,13 @@
         *blocks,
     )
 
-    downs = [down] + [send_x(down, k) for k in range(1, n_x)]
-
-    dtypes = [f32] + [bf16] * (groups - 1)
+    downs = lax.all_to_all(down, "gx", 0, 0)
+
     made = pl.pallas_call(
-        functools.partial(product_kernel, n_x, n_w, groups, step, offset),
-        out_shape=[jax.ShapeDtypeStruct((rows_here, columns + LANES), t) for t in dtypes],
-        in_specs=[SMEM] + [VMEM] * (3 + n_x + n_w),
-        out_specs=[VMEM] * groups,
-        scratch_shapes=[pltpu.VMEM((rows, columns + LANES), f32)],
+        functools.partial(product_kernel, n_w, step),
+        out_shape=jax.ShapeDtypeStruct((groups, rows_here, columns + LANES), bf16),
+        in_specs=[SMEM] + [VMEM] * (4 + n_w),
+        out_specs=VMEM,
         cost_estimate=cost(2 * rows * depth * columns, 2 * depth * columns),
         compiler_params=params(4 + (rows * depth >> 16)),
         name="product",
@@ -226,19 +209,19 @@
         x,
         square,
         adapter_up_factors,
-        *downs,
+        downs,
         *[pltpu.with_memory_space_constraint(w, pltpu.VMEM) for w in weights],
     )
-    parts = [made[0]] + [send_g(made[k], k) for k in range(1, groups)]
+    parts = lax.all_to_all(made, ("gy", "gz"), 0, 0)
 
     return pl.pallas_call(
         final_kernel,
         out_shape=jax.ShapeDtypeStruct((rows_here, columns), bf16),
-        in_specs=[VMEM] * groups,
+        in_specs=[VMEM],
         out_specs=VMEM,
         compiler_params=params(4 + (rows * depth >> 16)),
         name="query_rows",
-    )(*parts)
+    )(parts)
 
 
 def solution(mesh):

time: 43.2 us -> 47.6 us (1.10)
  blocking collectives: 0 us -> 19.7 us
  waiting for transfers between devices: 11.3 us -> 0.01 us
  starting transfers between devices: 11.9 us -> 7.94 us
    all_to_all x0 -> x2, blocking collectives: none -> 19.7 us  [the longest x1 11.6 us: body(): parts = lax.all_to_all(made, ('gy', 'gz'), 0, 0)]
    ppermute x3 -> x0, waiting for transfers between devices: 6.58 us -> none  [send_g(): return lax.ppermute(value, ('gy', 'gz'), pairs)]
    ppermute x6 -> x3, waiting for transfers between devices: 4.75 us -> 0.01 us  [send_x(): return lax.ppermute(value, 'gx', [(j, (j + k) % n_x) for j in range(n_x)])]
    ppermute x6 -> x3, starting transfers between devices: 10 us -> 7.94 us  [send_x(): return lax.ppermute(value, 'gx', [(j, (j + k) % n_x) for j in range(n_x)])]
    ppermute x3 -> x0, starting transfers between devices: 1.93 us -> none  [send_g(): return lax.ppermute(value, ('gy', 'gz'), pairs)]
  transfers between devices with their start and end apart: 9 -> 3, of which waited for: 5 -> 0; matrix products, arithmetic and copies ran while one was open for 0% -> 0% of each run, Pallas kernels for 25% -> 23%
where the time goes in v4:
time: 47.6 us; the launch traced here: 47.4 us
  Pallas kernels  19.7 us (41%)
  blocking collectives  19.7 us (41%)
  starting transfers between devices  7.94 us (17%)
    all_to_all x1, blocking collectives, body(): parts = lax.all_to_all(made, ('gy', 'gz'), 0, 0)  11.6 us
    pallas_call x1, Pallas kernels, body(): pl.pallas_call(functools.partial(fetch_kernel, n_w), out_shape=[jax.Shape...  10.9 us
    all_to_all x1, blocking collectives, body(): downs = lax.all_to_all(down, 'gx', 0, 0)  8.11 us
    ppermute x3, starting transfers between devices, send_x(): return lax.ppermute(value, 'gx', [(j, (j + k) % n_x) for j in range(n_x)])  7.94 us
    pallas_call x1, Pallas kernels, body(): pl.pallas_call(functools.partial(product_kernel, n_w, step), out_shape=ja...  6.91 us
    pallas_call x1, Pallas kernels, body(): pl.pallas_call(functools.partial(rows_kernel, n_x, depth * groups), out_s...  1.03 us
  transfers between devices with their start and end apart: 3, of which 0 were waited for; matrix products, arithmetic and copies ran while one was open for 0% of the time, Pallas kernels for 23%

profile of v4, /device:TPU:0, one launch (start us, length us, event | category | flops | bytes accessed | tf_op | source)
XLA Modules:
  0.0 47.4 jit_solution(550445900512868376)
XLA Ops:
  0.0 0.0 copy-start.2
  0.0 0.0 copy-start.4
  0.0 0.0 copy-start.6
  0.0 0.0 copy-start.3
  0.0 0.0 copy-start
  0.0 4.1 %collective-permute-start.1 = (bf16[16,4096]{1,0:T(8,128)(2,1)}, bf16[16,4096]{1,0:T(8,128)(2,1)S(1)}, u32[]{:S(2)}, u32[]{:S(2)}) collective-permute-start(bf16[16,4096]{1,0:T(8,128)(2,1)} %refs_6_.1), channel_id=1, source_target_pairs={{0,8},{4,12},{8,0},{12,4},{1,9},{5,13},{9,1},{13,5},{2,10},{6,14},... | collective-permute-start | bytes 393224 | tf_op jit(solution)/shard_map/ppermute | solution.py:157
  4.2 1.6 %collective-permute-start = (bf16[16,4096]{1,0:T(8,128)(2,1)}, bf16[16,4096]{1,0:T(8,128)(2,1)S(1)}, u32[]{:S(2)}, u32[]{:S(2)}) collective-permute-start(bf16[16,4096]{1,0:T(8,128)(2,1)} %refs_6_.1), channel_id=1, source_target_pairs={{0,4},{4,8},{8,12},{12,0},{1,5},{5,9},{9,13},{13,1},{2,6},{6,10},{... | collective-permute-start | bytes 393224 | tf_op jit(solution)/shard_map/ppermute | solution.py:157
  5.7 2.2 %collective-permute-start.2 = (bf16[16,4096]{1,0:T(8,128)(2,1)}, bf16[16,4096]{1,0:T(8,128)(2,1)S(1)}, u32[]{:S(2)}, u32[]{:S(2)}) collective-permute-start(bf16[16,4096]{1,0:T(8,128)(2,1)} %refs_6_.1), channel_id=1, source_target_pairs={{0,12},{4,0},{8,4},{12,8},{1,13},{5,1},{9,5},{13,9},{2,14},{6,2},{... | collective-permute-start | bytes 393224 | tf_op jit(solution)/shard_map/ppermute | solution.py:157
  8.0 10.9 %fetch_weight.1 = (f32[8,128]{1,0:T(8,128)S(1)}, bf16[4096,1024]{1,0:T(8,128)(2,1)S(1)}, bf16[4096,1024]{1,0:T(8,128)(2,1)S(1)}, bf16[4096,1024]{1,0:T(8,128)(2,1)S(1)}, bf16[4096,1024]{1,0:T(8,128)(2,1)S(1)}) custom-call(bf16[4096,4096]{1,0:T(8,128)(2,1)} %w_hbm.1), custom_call_target="tpu_custom_call" | custom-call | bytes 33554432 | tf_op jit(solution)/shard_map/fetch_weight/pallas_call | solution.py:164
  18.9 0.0 collective-permute-done.1.refs_8_
  18.9 0.0 collective-permute-done.refs_7_
  18.9 0.0 collective-permute-done.2.refs_9_
  18.9 0.0 copy-done.2
  18.9 0.0 copy-done.4
  18.9 0.0 copy-done.6
  18.9 0.0 copy-done.5
  18.9 0.0 copy-done.1
  19.0 0.0 copy-done.3
  19.0 1.0 %scaled_rows.1 = (bf16[64,4096]{1,0:T(8,128)(2,1)S(1)}, f32[64,128]{1,0:T(8,128)S(1)}, bf16[4,64,128]{2,1,0:T(8,128)(2,1)S(1)}) custom-call(s32[4]{0:T(128)S(1)} %copy-done.5, s32[4]{0:T(128)S(1)} %copy-done.6, s32[5]{0:T(128)S(1)} %copy-done.4, bf16[4096]{0:T(1024)(128)(2,1)S(1)} %copy-done.3, bf16[1,64,4096]{2,1,0:T(8,128)(2,1)S(1)} %bitcast.1, ...), custom_call_target="tpu_custom_call" | custom-call | tf_op jit(solution)/shard_map/scaled_rows/pallas_call | solution.py:176
  20.0 8.1 %all_to_all.10.refs_4_ = bf16[4,64,128]{2,1,0:T(8,128)(2,1)S(1)} all-to-all(bf16[4,64,128]{2,1,0:T(8,128)(2,1)S(1)} %get-tuple-element.16), channel_id=1, replica_groups=mesh['rep'=2,'gx'=4,'gy'=2,'gz'=2] {'gx'}, dimensions={0} | all-to-all | bytes 131072 | tf_op jit(solution)/shard_map/all_to_all | solution.py:197
  28.1 0.0 copy-done
  28.1 6.9 %product.1 = bf16[4,16,4224]{2,1,0:T(8,128)(2,1)S(1)} custom-call(s32[5]{0:T(128)S(1)} %copy-done.4, bf16[64,4096]{1,0:T(8,128)(2,1)S(1)} %get-tuple-element.14.refs_1_, f32[64,128]{1,0:T(8,128)S(1)} %get-tuple-element.15.refs_2_, bf16[4,64,4096]{2,1,0:T(8,128)(2,1)S(1)} %copy-done, bf16[4,64,128]{2,1,0:T(8,128)(2,1)S(1)} %all_to_all.10.refs_4_, ...), custom_call_target="tpu_custom_call" | custom-call | flops 2147483648 | bytes 33554432 | tf_op jit(solution)/shard_map/product/pallas_call | solution.py:199
  35.0 11.6 %all_to_all.11.parts = bf16[4,16,4224]{2,1,0:T(8,128)(2,1)S(1)} all-to-all(bf16[4,16,4224]{2,1,0:T(8,128)(2,1)S(1)} %product.1), channel_id=1, replica_groups=mesh['rep'=2,'gx'=4,'gy'=2,'gz'=2] {'gy','gz'}, dimensions={0} | all-to-all | bytes 1081344 | tf_op jit(solution)/shard_map/all_to_all | solution.py:215
  46.6 0.8 %query_rows.1 = bf16[16,4096]{1,0:T(8,128)(2,1)} custom-call(bf16[4,16,4224]{2,1,0:T(8,128)(2,1)S(1)} %all_to_all.11.parts), custom_call_target="tpu_custom_call" | custom-call | tf_op jit(solution)/shard_map/query_rows/pallas_call | solution.py:217
  (2 shorter events, 0.0 us)
Async XLA Ops:
  0.0 18.9 %copy-start.2 = (bf16[16,4096]{1,0:T(8,128)(2,1)S(1)}, bf16[16,4096]{1,0:T(8,128)(2,1)}, u32[]{:S(2)}) copy-start(bf16[16,4096]{1,0:T(8,128)(2,1)} %refs_6_.1) | copy-start | bytes 393220
  0.0 18.9 %copy-start.4 = (s32[5]{0:T(128)S(1)}, s32[5]{0:T(128)}, u32[]{:S(2)}) copy-start(s32[5]{0:T(128)} %refs_0_.3) | copy-start | bytes 64
  0.0 18.9 %copy-start.6 = (s32[4]{0:T(128)S(1)}, s32[4]{0:T(128)}, u32[]{:S(2)}) copy-start(s32[4]{0:T(128)} %refs_1_.1) | copy-start | bytes 52
  0.0 18.9 %copy-start.5 = (s32[4]{0:T(128)S(1)}, s32[4]{0:T(128)}, u32[]{:S(2)}) copy-start(s32[4]{0:T(128)} %refs_0_.2) | copy-start | bytes 52
  0.0 18.9 %copy-start.1 = (bf16[1,4096,64]{1,2,0:T(8,128)(2,1)S(1)}, bf16[1,4096,64]{1,2,0:T(8,128)(2,1)}, u32[]{:S(2)}) copy-start(bf16[1,4096,64]{1,2,0:T(8,128)(2,1)} %param.12) | copy-start | bytes 1572868
  0.0 18.9 %copy-start.3 = (bf16[4096]{0:T(1024)(128)(2,1)S(1)}, bf16[4096]{0:T(1024)(128)(2,1)}, u32[]{:S(2)}) copy-start(bf16[4096]{0:T(1024)(128)(2,1)} %refs_3_.2) | copy-start | bytes 24580
  0.0 28.1 %copy-start = (bf16[4,64,4096]{2,1,0:T(8,128)(2,1)S(1)}, bf16[4,64,4096]{2,1,0:T(8,128)(2,1)}, u32[]{:S(2)}) copy-start(bf16[4,64,4096]{2,1,0:T(8,128)(2,1)} %refs_3_.3) | copy-start | bytes 6291460
  0.0 18.8 %collective-permute-start.1 = (bf16[16,4096]{1,0:T(8,128)(2,1)}, bf16[16,4096]{1,0:T(8,128)(2,1)S(1)}, u32[]{:S(2)}, u32[]{:S(2)}) collective-permute-start(bf16[16,4096]{1,0:T(8,128)(2,1)} %refs_6_.1), channel_id=1, source_target_pairs={{0,8},{4,12},{8,0},{12,4},{1,9},{5,13},{9,1},{13,5},{2,10},{6,14},... | collective-permute-start | bytes 393224 | tf_op jit(solution)/shard_map/ppermute | solution.py:157
  4.2 14.7 %collective-permute-start = (bf16[16,4096]{1,0:T(8,128)(2,1)}, bf16[16,4096]{1,0:T(8,128)(2,1)S(1)}, u32[]{:S(2)}, u32[]{:S(2)}) collective-permute-start(bf16[16,4096]{1,0:T(8,128)(2,1)} %refs_6_.1), channel_id=1, source_target_pairs={{0,4},{4,8},{8,12},{12,0},{1,5},{5,9},{9,13},{13,1},{2,6},{6,10},{... | collective-permute-start | bytes 393224 | tf_op jit(solution)/shard_map/ppermute | solution.py:157
  5.7 13.2 %collective-permute-start.2 = (bf16[16,4096]{1,0:T(8,128)(2,1)}, bf16[16,4096]{1,0:T(8,128)(2,1)S(1)}, u32[]{:S(2)}, u32[]{:S(2)}) collective-permute-start(bf16[16,4096]{1,0:T(8,128)(2,1)} %refs_6_.1), channel_id=1, source_target_pairs={{0,12},{4,0},{8,4},{12,8},{1,13},{5,1},{9,5},{13,9},{2,14},{6,2},{... | collective-permute-start | bytes 393224 | tf_op jit(solution)/shard_map/ppermute | solution.py:157

commit v5 on v3

--- a/solution.py
+++ b/solution.py
@@ -85,13 +85,26 @@
     down_out[:, :rank_columns] = total.astype(down_out.dtype)
 
 
+def base_kernel(n_w, step, x_ref, *refs):
+    weights, out_ref = refs[:n_w], refs[n_w]
+    width = weights[0].shape[1]
+    for c in range(0, out_ref.shape[1], step):
+        inner = c % width
+        out_ref[:, c : c + step] = jnp.dot(
+            x_ref[...],
+            weights[c // width][:, inner : inner + step],
+            preferred_element_type=jnp.float32,
+        )
+
+
 def product_kernel(n_x, n_w, groups, step, offset, *refs):
-    start_ref, x_ref, square_ref, up_ref = refs[:4]
-    downs, refs = refs[4 : 4 + n_x], refs[4 + n_x :]
+    start_ref, x_ref, square_ref, up_ref, base_ref = refs[:5]
+    downs, refs = refs[5 : 5 + n_x], refs[5 + n_x :]
     weights, outs, acc = refs[:n_w], refs[n_w:-1], refs[-1]
     rows = x_ref.shape[0]
     width = weights[0].shape[1]
-    columns = width * n_w
+    done = base_ref.shape[1]
+    columns = done + width * n_w
     adapters, rank_columns, _ = up_ref.shape
     down = downs[0][:, :rank_columns]
     for other in downs[1:]:
@@ -107,12 +120,15 @@
     for c in range(0, columns, step):
         here = slice(c, c + step)
         up = up_ref[:, :, here].reshape(adapters * rank_columns, step)
-        inner = c % width
-        base = jnp.dot(
-            x_ref[...],
-            weights[c // width][:, inner : inner + step],
-            preferred_element_type=jnp.float32,
-        )
+        if c < done:
+            base = base_ref[:, here]
+        else:
+            inner = (c - done) % width
+            base = jnp.dot(
+                x_ref[...],
+                weights[(c - done) // width][:, inner : inner + step],
+                preferred_element_type=jnp.float32,
+            )
         acc[:, here] = base + jnp.dot(spread, up, preferred_element_type=jnp.float32)
     square = square_ref[...]
     high = square.astype(jnp.bfloat16).astype(jnp.float32)
@@ -211,25 +227,33 @@
 
     downs = [down] + [send_x(down, k) for k in range(1, n_x)]
 
+    weights = [pltpu.with_memory_space_constraint(w, pltpu.VMEM) for w in weights]
+    early = n_w // 2
+    base_columns = early * (columns // n_w)
+    base = pl.pallas_call(
+        functools.partial(base_kernel, early, step),
+        out_shape=jax.ShapeDtypeStruct((rows, base_columns), f32),
+        in_specs=[VMEM] * (1 + early),
+        out_specs=VMEM,
+        cost_estimate=cost(2 * rows * depth * base_columns, 2 * depth * base_columns),
+        compiler_params=params(4 + (rows * depth >> 16)),
+        name="first_columns",
+    )(x, *weights[:early])
+
+    late = n_w - early
+    late_columns = columns - base_columns
     dtypes = [f32] + [bf16] * (groups - 1)
     made = pl.pallas_call(
-        functools.partial(product_kernel, n_x, n_w, groups, step, offset),
+        functools.partial(product_kernel, n_x, late, groups, step, offset),
         out_shape=[jax.ShapeDtypeStruct((rows_here, columns + LANES), t) for t in dtypes],
-        in_specs=[SMEM] + [VMEM] * (3 + n_x + n_w),
+        in_specs=[SMEM] + [VMEM] * (4 + n_x + late),
         out_specs=[VMEM] * groups,
         scratch_shapes=[pltpu.VMEM((rows, columns + LANES), f32)],
-        cost_estimate=cost(2 * rows * depth * columns, 2 * depth * columns),
-        compiler_params=params(4 + (rows * depth >> 16)),
-        name="product",
-    )(
-        segment_starts,
-        x,
-        square,
-        adapter_up_factors,
-        *downs,
-        *[pltpu.with_memory_space_constraint(w, pltpu.VMEM) for w in weights],
-    )
-    parts = [made[0]] + [send_g(made[k], k) for k in range(1, groups)]
+        cost_estimate=cost(2 * rows * depth * late_columns, 2 * depth * late_columns),
+        compiler_params=params(4 + (rows * depth >> 16)),
+        name="last_columns",
+    )(segment_starts, x, square, adapter_up_factors, base, *downs, *weights[early:])
+    parts = [made[0]] + [send_g(made[k], k) for k in range(groups - 1, 0, -1)]
 
     return pl.pallas_call(
         final_kernel,

time: 43.2 us -> 40.7 us (0.942)
  waiting for transfers between devices: 11.3 us -> 8.61 us
    ppermute x6, waiting for transfers between devices: 4.75 us -> 1.69 us  [send_x(): return lax.ppermute(value, 'gx', [(j, (j + k) % n_x) for j in range(n_x)])]
    pallas_call x1 -> x2, Pallas kernels: 6.92 us -> 7.08 us  [the longest x1 4.04 us: body(): pl.pallas_call(functools.partial(product_kernel, n_x, late, groups, step,...]
  transfers between devices with their start and end apart: 9 -> 9, of which waited for: 5 -> 3; matrix products, arithmetic and copies ran while one was open for 0% -> 0% of each run, Pallas kernels for 25% -> 34%
where the time goes in v5:
time: 40.7 us; the launch traced here: 40.5 us
  Pallas kernels  19.8 us (49%)
  starting transfers between devices  11.9 us (29%)
  waiting for transfers between devices  8.61 us (21%)
    pallas_call x1, Pallas kernels, body(): pl.pallas_call(functools.partial(fetch_kernel, n_w), out_shape=[jax.Shape...  10.9 us
    ppermute x6, starting transfers between devices, send_x(): return lax.ppermute(value, 'gx', [(j, (j + k) % n_x) for j in range(n_x)])  10 us
    ppermute x3, waiting for transfers between devices, send_g(): return lax.ppermute(value, ('gy', 'gz'), pairs)  6.92 us
    pallas_call x1, Pallas kernels, body(): pl.pallas_call(functools.partial(product_kernel, n_x, late, groups, step,...  4.04 us
    pallas_call x1, Pallas kernels, body(): pl.pallas_call(functools.partial(base_kernel, early, step), out_shape=jax...  3.04 us
    ppermute x3, starting transfers between devices, send_g(): return lax.ppermute(value, ('gy', 'gz'), pairs)  1.92 us
    ppermute x6, waiting for transfers between devices, send_x(): return lax.ppermute(value, 'gx', [(j, (j + k) % n_x) for j in range(n_x)])  1.69 us
    pallas_call x1, Pallas kernels, body(): pl.pallas_call(functools.partial(rows_kernel, n_x, depth * groups), out_s...  1.02 us
  transfers between devices with their start and end apart: 9, of which 3 were waited for; matrix products, arithmetic and copies ran while one was open for 0% of the time, Pallas kernels for 34%

profile of v5, /device:TPU:0, one launch (start us, length us, event | category | flops | bytes accessed | tf_op | source)
XLA Modules:
  0.0 40.5 jit_solution(11828726143495896168)
XLA Ops:
  0.0 0.0 copy-start.3
  0.0 4.1 %collective-permute-start.1 = (bf16[16,4096]{1,0:T(8,128)(2,1)}, bf16[16,4096]{1,0:T(8,128)(2,1)S(1)}, u32[]{:S(2)}, u32[]{:S(2)}) collective-permute-start(bf16[16,4096]{1,0:T(8,128)(2,1)} %refs_6_.1), channel_id=1, source_target_pairs={{0,8},{4,12},{8,0},{12,4},{1,9},{5,13},{9,1},{13,5},{2,10},{6,14},... | collective-permute-start | bytes 393224 | tf_op jit(solution)/shard_map/ppermute | solution.py:181
  4.1 1.6 %collective-permute-start = (bf16[16,4096]{1,0:T(8,128)(2,1)}, bf16[16,4096]{1,0:T(8,128)(2,1)S(1)}, u32[]{:S(2)}, u32[]{:S(2)}) collective-permute-start(bf16[16,4096]{1,0:T(8,128)(2,1)} %refs_6_.1), channel_id=1, source_target_pairs={{0,4},{4,8},{8,12},{12,0},{1,5},{5,9},{9,13},{13,1},{2,6},{6,10},{... | collective-permute-start | bytes 393224 | tf_op jit(solution)/shard_map/ppermute | solution.py:181
  5.7 2.2 %collective-permute-start.2 = (bf16[16,4096]{1,0:T(8,128)(2,1)}, bf16[16,4096]{1,0:T(8,128)(2,1)S(1)}, u32[]{:S(2)}, u32[]{:S(2)}) collective-permute-start(bf16[16,4096]{1,0:T(8,128)(2,1)} %refs_6_.1), channel_id=1, source_target_pairs={{0,12},{4,0},{8,4},{12,8},{1,13},{5,1},{9,5},{13,9},{2,14},{6,2},{... | collective-permute-start | bytes 393224 | tf_op jit(solution)/shard_map/ppermute | solution.py:181
  8.0 10.9 %fetch_weight.1 = (f32[8,128]{1,0:T(8,128)S(1)}, bf16[4096,1024]{1,0:T(8,128)(2,1)S(1)}, bf16[4096,1024]{1,0:T(8,128)(2,1)S(1)}, bf16[4096,1024]{1,0:T(8,128)(2,1)S(1)}, bf16[4096,1024]{1,0:T(8,128)(2,1)S(1)}) custom-call(bf16[4096,4096]{1,0:T(8,128)(2,1)} %w_hbm.1), custom_call_target="tpu_custom_call" | custom-call | bytes 33554432 | tf_op jit(solution)/shard_map/fetch_weight/pallas_call | solution.py:195
  18.9 0.0 collective-permute-done.1.refs_8_
  18.9 0.0 collective-permute-done.refs_7_
  18.9 0.0 collective-permute-done.2.refs_9_
  19.0 1.0 %scaled_rows.1 = (bf16[64,4096]{1,0:T(8,128)(2,1)S(1)}, f32[64,128]{1,0:T(8,128)S(1)}, bf16[64,128]{1,0:T(8,128)(2,1)S(1)}) custom-call(s32[4]{0:T(128)S(1)} %copy-done.5, s32[4]{0:T(128)S(1)} %copy-done.6, s32[5]{0:T(128)S(1)} %copy-done.4, bf16[4096]{0:T(1024)(128)(2,1)S(1)} %copy-done.3, bf16[1,64,4096]{2,1,0:T(8,128)(2,1)S(1)} %bitcast.1, ...), custom_call_target="tpu_custom_call" | custom-call | tf_op jit(solution)/shard_map/scaled_rows/pallas_call | solution.py:207
  20.0 0.1 collective-permute-start.5
  20.0 1.2 %collective-permute-start.4 = (bf16[64,128]{1,0:T(8,128)(2,1)S(1)}, bf16[64,128]{1,0:T(8,128)(2,1)S(1)}, u32[]{:S(2)}, u32[]{:S(2)}) collective-permute-start(bf16[64,128]{1,0:T(8,128)(2,1)S(1)} %get-tuple-element.22.refs_5_), channel_id=1, source_target_pairs={{0,8},{4,12},{8,0},{12,4},{1,9},{5,13},{9,1},{13,5},{2,10},{6,14},... | collective-permute-start | bytes 49160 | tf_op jit(solution)/shard_map/ppermute | solution.py:181
  21.3 0.8 %collective-permute-start.3 = (bf16[64,128]{1,0:T(8,128)(2,1)S(1)}, bf16[64,128]{1,0:T(8,128)(2,1)S(1)}, u32[]{:S(2)}, u32[]{:S(2)}) collective-permute-start(bf16[64,128]{1,0:T(8,128)(2,1)S(1)} %get-tuple-element.22.refs_5_), channel_id=1, source_target_pairs={{0,4},{4,8},{8,12},{12,0},{1,5},{5,9},{9,13},{13,1},{2,6},{6,10},{... | collective-permute-start | bytes 49160 | tf_op jit(solution)/shard_map/ppermute | solution.py:181
  22.1 3.0 %first_columns.1.refs_4_ = f32[64,2048]{1,0:T(8,128)S(1)} custom-call(bf16[64,4096]{1,0:T(8,128)(2,1)S(1)} %get-tuple-element.18.x_ref.refs_1_, bf16[4096,1024]{1,0:T(8,128)(2,1)S(1)} %get-tuple-element.20.refs_0_, bf16[4096,1024]{1,0:T(8,128)(2,1)S(1)} %get-tuple-element.21.refs_1_), custom_call_target="tpu_custom_call" | custom-call | flops 1073741824 | bytes 16777216 | tf_op jit(solution)/shard_map/first_columns/pallas_call | solution.py:233
  25.1 0.0 collective-permute-done.5.refs_8_
  25.1 0.0 collective-permute-done.4.refs_7_
  25.1 1.7 %collective-permute-done.3.refs_6_ = bf16[64,128]{1,0:T(8,128)(2,1)S(1)} collective-permute-done((bf16[64,128]{1,0:T(8,128)(2,1)S(1)}, bf16[64,128]{1,0:T(8,128)(2,1)S(1)}, u32[]{:S(2)}, u32[]{:S(2)}) %collective-permute-start.3) | collective-permute-done | bytes 16416 | tf_op jit(solution)/shard_map/ppermute | solution.py:181
  26.8 4.0 %last_columns.1 = (f32[16,4224]{1,0:T(8,128)S(1)}, bf16[16,4224]{1,0:T(8,128)(2,1)S(1)}, bf16[16,4224]{1,0:T(8,128)(2,1)S(1)}, bf16[16,4224]{1,0:T(8,128)(2,1)S(1)}) custom-call(s32[5]{0:T(128)S(1)} %copy-done.4, bf16[64,4096]{1,0:T(8,128)(2,1)S(1)} %get-tuple-element.18.x_ref.refs_1_, f32[64,128]{1,0:T(8,128)S(1)} %get-tuple-element.19.refs_2_, ...), custom_call_target="tpu_custom_call" | custom-call | flops 1073741824 | bytes 16777216 | tf_op jit(solution)/shard_map/last_columns/pallas_call | solution.py:246
  30.9 0.1 collective-permute-start.6
  30.9 1.6 %collective-permute-start.7 = (bf16[16,4224]{1,0:T(8,128)(2,1)S(1)}, bf16[16,4224]{1,0:T(8,128)(2,1)S(1)}, u32[]{:S(2)}, u32[]{:S(2)}) collective-permute-start(bf16[16,4224]{1,0:T(8,128)(2,1)S(1)} %get-tuple-element.27), channel_id=1, source_target_pairs={{0,2},{1,3},{2,0},{3,1},{4,6},{5,7},{6,4},{7,5},{8,10},{9,11},{10,... | collective-permute-start | bytes 405512 | tf_op jit(solution)/shard_map/ppermute | solution.py:188
  32.5 0.3 collective-permute-start.8
  32.8 4.0 %collective-permute-done.6.refs_1_ = bf16[16,4224]{1,0:T(8,128)(2,1)S(1)} collective-permute-done((bf16[16,4224]{1,0:T(8,128)(2,1)S(1)}, bf16[16,4224]{1,0:T(8,128)(2,1)S(1)}, u32[]{:S(2)}, u32[]{:S(2)}) %collective-permute-start.6) | collective-permute-done | bytes 135200 | tf_op jit(solution)/shard_map/ppermute | solution.py:188
  36.8 2.9 %collective-permute-done.7.refs_2_ = bf16[16,4224]{1,0:T(8,128)(2,1)S(1)} collective-permute-done((bf16[16,4224]{1,0:T(8,128)(2,1)S(1)}, bf16[16,4224]{1,0:T(8,128)(2,1)S(1)}, u32[]{:S(2)}, u32[]{:S(2)}) %collective-permute-start.7) | collective-permute-done | bytes 135200 | tf_op jit(solution)/shard_map/ppermute | solution.py:188
  39.7 0.0 collective-permute-done.8.refs_3_
  39.7 0.8 %query_rows.1 = bf16[16,4096]{1,0:T(8,128)(2,1)} custom-call(f32[16,4224]{1,0:T(8,128)S(1)} %get-tuple-element.25.refs_0_, bf16[16,4224]{1,0:T(8,128)(2,1)S(1)} %collective-permute-done.6.refs_1_, bf16[16,4224]{1,0:T(8,128)(2,1)S(1)} %collective-permute-done.7.refs_2_, bf16[16,4224]{1,0:T(8,128)(2,1)S(1)} %collective-permute-done.8.refs_3_), custom_call_target="tpu_custom_call" | custom-call | tf_op jit(solution)/shard_map/query_rows/pallas_call | solution.py:258
  (13 shorter events, 0.0 us)
Async XLA Ops:
  0.0 18.9 %copy-start.2 = (bf16[16,4096]{1,0:T(8,128)(2,1)S(1)}, bf16[16,4096]{1,0:T(8,128)(2,1)}, u32[]{:S(2)}) copy-start(bf16[16,4096]{1,0:T(8,128)(2,1)} %refs_6_.1) | copy-start | bytes 393220
  0.0 18.9 %copy-start.4 = (s32[5]{0:T(128)S(1)}, s32[5]{0:T(128)}, u32[]{:S(2)}) copy-start(s32[5]{0:T(128)} %refs_0_.3) | copy-start | bytes 64
  0.0 18.9 %copy-start.6 = (s32[4]{0:T(128)S(1)}, s32[4]{0:T(128)}, u32[]{:S(2)}) copy-start(s32[4]{0:T(128)} %refs_1_.1) | copy-start | bytes 52
  0.0 18.9 %copy-start.5 = (s32[4]{0:T(128)S(1)}, s32[4]{0:T(128)}, u32[]{:S(2)}) copy-start(s32[4]{0:T(128)} %refs_0_.2) | copy-start | bytes 52
  0.0 18.9 %copy-start.1 = (bf16[1,4096,64]{1,2,0:T(8,128)(2,1)S(1)}, bf16[1,4096,64]{1,2,0:T(8,128)(2,1)}, u32[]{:S(2)}) copy-start(bf16[1,4096,64]{1,2,0:T(8,128)(2,1)} %param.12) | copy-start | bytes 1572868
  0.0 18.9 %copy-start.3 = (bf16[4096]{0:T(1024)(128)(2,1)S(1)}, bf16[4096]{0:T(1024)(128)(2,1)}, u32[]{:S(2)}) copy-start(bf16[4096]{0:T(1024)(128)(2,1)} %refs_3_.2) | copy-start | bytes 24580
  0.0 18.8 %collective-permute-start.1 = (bf16[16,4096]{1,0:T(8,128)(2,1)}, bf16[16,4096]{1,0:T(8,128)(2,1)S(1)}, u32[]{:S(2)}, u32[]{:S(2)}) collective-permute-start(bf16[16,4096]{1,0:T(8,128)(2,1)} %refs_6_.1), channel_id=1, source_target_pairs={{0,8},{4,12},{8,0},{12,4},{1,9},{5,13},{9,1},{13,5},{2,10},{6,14},... | collective-permute-start | bytes 393224 | tf_op jit(solution)/shard_map/ppermute | solution.py:181
  4.1 14.7 %collective-permute-start = (bf16[16,4096]{1,0:T(8,128)(2,1)}, bf16[16,4096]{1,0:T(8,128)(2,1)S(1)}, u32[]{:S(2)}, u32[]{:S(2)}) collective-permute-start(bf16[16,4096]{1,0:T(8,128)(2,1)} %refs_6_.1), channel_id=1, source_target_pairs={{0,4},{4,8},{8,12},{12,0},{1,5},{5,9},{9,13},{13,1},{2,6},{6,10},{... | collective-permute-start | bytes 393224 | tf_op jit(solution)/shard_map/ppermute | solution.py:181
  5.7 13.2 %collective-permute-start.2 = (bf16[16,4096]{1,0:T(8,128)(2,1)}, bf16[16,4096]{1,0:T(8,128)(2,1)S(1)}, u32[]{:S(2)}, u32[]{:S(2)}) collective-permute-start(bf16[16,4096]{1,0:T(8,128)(2,1)} %refs_6_.1), channel_id=1, source_target_pairs={{0,12},{4,0},{8,4},{12,8},{1,13},{5,1},{9,5},{13,9},{2,14},{6,2},{... | collective-permute-start | bytes 393224 | tf_op jit(solution)/shard_map/ppermute | solution.py:181
  20.0 5.1 %collective-permute-start.5 = (bf16[64,128]{1,0:T(8,128)(2,1)S(1)}, bf16[64,128]{1,0:T(8,128)(2,1)S(1)}, u32[]{:S(2)}, u32[]{:S(2)}) collective-permute-start(bf16[64,128]{1,0:T(8,128)(2,1)S(1)} %get-tuple-element.22.refs_5_), channel_id=1, source_target_pairs={{0,12},{4,0},{8,4},{12,8},{1,13},{5,1},{9,5},{13,9},{2,14},{6,2},{... | collective-permute-start | bytes 49160 | tf_op jit(solution)/shard_map/ppermute | solution.py:181
  20.0 5.1 %collective-permute-start.4 = (bf16[64,128]{1,0:T(8,128)(2,1)S(1)}, bf16[64,128]{1,0:T(8,128)(2,1)S(1)}, u32[]{:S(2)}, u32[]{:S(2)}) collective-permute-start(bf16[64,128]{1,0:T(8,128)(2,1)S(1)} %get-tuple-element.22.refs_5_), channel_id=1, source_target_pairs={{0,8},{4,12},{8,0},{12,4},{1,9},{5,13},{9,1},{13,5},{2,10},{6,14},... | collective-permute-start | bytes 49160 | tf_op jit(solution)/shard_map/ppermute | solution.py:181
  21.3 5.5 %collective-permute-start.3 = (bf16[64,128]{1,0:T(8,128)(2,1)S(1)}, bf16[64,128]{1,0:T(8,128)(2,1)S(1)}, u32[]{:S(2)}, u32[]{:S(2)}) collective-permute-start(bf16[64,128]{1,0:T(8,128)(2,1)S(1)} %get-tuple-element.22.refs_5_), channel_id=1, source_target_pairs={{0,4},{4,8},{8,12},{12,0},{1,5},{5,9},{9,13},{13,1},{2,6},{6,10},{... | collective-permute-start | bytes 49160 | tf_op jit(solution)/shard_map/ppermute | solution.py:181
  22.1 4.8 %copy-start = (bf16[4,64,4096]{2,1,0:T(8,128)(2,1)S(1)}, bf16[4,64,4096]{2,1,0:T(8,128)(2,1)}, u32[]{:S(2)}) copy-start(bf16[4,64,4096]{2,1,0:T(8,128)(2,1)} %refs_3_.3) | copy-start | bytes 6291460
  30.9 5.9 %collective-permute-start.6 = (bf16[16,4224]{1,0:T(8,128)(2,1)S(1)}, bf16[16,4224]{1,0:T(8,128)(2,1)S(1)}, u32[]{:S(2)}, u32[]{:S(2)}) collective-permute-start(bf16[16,4224]{1,0:T(8,128)(2,1)S(1)} %get-tuple-element.26), channel_id=1, source_target_pairs={{0,3},{1,2},{2,1},{3,0},{4,7},{5,6},{6,5},{7,4},{8,11},{9,10},{10,... | collective-permute-start | bytes 405512 | tf_op jit(solution)/shard_map/ppermute | solution.py:188
  30.9 8.8 %collective-permute-start.7 = (bf16[16,4224]{1,0:T(8,128)(2,1)S(1)}, bf16[16,4224]{1,0:T(8,128)(2,1)S(1)}, u32[]{:S(2)}, u32[]{:S(2)}) collective-permute-start(bf16[16,4224]{1,0:T(8,128)(2,1)S(1)} %get-tuple-element.27), channel_id=1, source_target_pairs={{0,2},{1,3},{2,0},{3,1},{4,6},{5,7},{6,4},{7,5},{8,10},{9,11},{10,... | collective-permute-start | bytes 405512 | tf_op jit(solution)/shard_map/ppermute | solution.py:188
  32.5 7.2 %collective-permute-start.8 = (bf16[16,4224]{1,0:T(8,128)(2,1)S(1)}, bf16[16,4224]{1,0:T(8,128)(2,1)S(1)}, u32[]{:S(2)}, u32[]{:S(2)}) collective-permute-start(bf16[16,4224]{1,0:T(8,128)(2,1)S(1)} %get-tuple-element.28), channel_id=1, source_target_pairs={{0,1},{1,0},{2,3},{3,2},{4,5},{5,4},{6,7},{7,6},{8,9},{9,8},{10,11... | collective-permute-start | bytes 405512 | tf_op jit(solution)/shard_map/ppermute | solution.py:188

commit v6 on v5

--- a/solution.py
+++ b/solution.py
@@ -193,12 +193,12 @@
     n_w, pieces = 4, 4
     f32, bf16 = jnp.float32, jnp.bfloat16
     token, *weights = pl.pallas_call(
-        functools.partial(fetch_kernel, n_w),
+        functools.partial(fetch_kernel, n_w - 1),
         out_shape=[jax.ShapeDtypeStruct((8, LANES), f32)]
-        + [pltpu.VMEM((depth, columns // n_w), query_weight.dtype)] * n_w,
+        + [pltpu.VMEM((depth, columns // n_w), query_weight.dtype)] * (n_w - 1),
         in_specs=[ANY],
-        out_specs=[VMEM] * (1 + n_w),
-        scratch_shapes=[pltpu.SemaphoreType.DMA((n_w, pieces))],
+        out_specs=[VMEM] * n_w,
+        scratch_shapes=[pltpu.SemaphoreType.DMA((n_w - 1, pieces))],
         cost_estimate=cost(0, 2 * query_weight.size),
         compiler_params=params(4),
         name="fetch_weight",
@@ -227,6 +227,7 @@
 
     downs = [down] + [send_x(down, k) for k in range(1, n_x)]
 
+    weights.append(query_weight[:, columns - columns // n_w :])
     weights = [pltpu.with_memory_space_constraint(w, pltpu.VMEM) for w in weights]
     early = n_w // 2
     base_columns = early * (columns // n_w)

time: 40.7 us -> 63.8 us (1.57)
  local copies, waits for them, and re-layouts: 0.03 us -> 26.4 us
  Pallas kernels: 19.8 us -> 17.4 us
  waiting for transfers between devices: 8.61 us -> 6.94 us
  starting transfers between devices: 11.9 us -> 12.8 us
    unnamed x14 -> x30, local copies, waits for them, and re-layouts: 0.03 us -> 18.7 us
    slice x0 -> x1, local copies, waits for them, and re-layouts: none -> 7.65 us  [body(): weights.append(query_weight[:, columns - columns // n_w:])]
    pallas_call x1, Pallas kernels: 10.9 us -> 8.43 us  [body(): pl.pallas_call(functools.partial(fetch_kernel, n_w - 1), out_shape=[jax.S...]
    ppermute x6, waiting for transfers between devices: 1.69 us -> 0.02 us  [send_x(): return lax.ppermute(value, 'gx', [(j, (j + k) % n_x) for j in range(n_x)])]
    ppermute x6, starting transfers between devices: 10 us -> 10.8 us  [send_x(): return lax.ppermute(value, 'gx', [(j, (j + k) % n_x) for j in range(n_x)])]
  transfers between devices with their start and end apart: 9 -> 9, of which waited for: 3 -> 2; matrix products, arithmetic and copies ran while one was open for 0% -> 12% of each run, Pallas kernels for 34% -> 18%
where the time goes in v6:
time: 63.8 us; the launch traced here: 63.6 us
  local copies, waits for them, and re-layouts  26.4 us (41%)
  Pallas kernels  17.4 us (27%)
  starting transfers between devices  12.8 us (20%)
  waiting for transfers between devices  6.94 us (11%)
    unnamed x30, local copies, waits for them, and re-layouts  18.7 us
    ppermute x6, starting transfers between devices, send_x(): return lax.ppermute(value, 'gx', [(j, (j + k) % n_x) for j in range(n_x)])  10.8 us
    pallas_call x1, Pallas kernels, body(): pl.pallas_call(functools.partial(fetch_kernel, n_w - 1), out_shape=[jax.S...  8.43 us
    slice x1, local copies, waits for them, and re-layouts, body(): weights.append(query_weight[:, columns - columns // n_w:])  7.65 us
    ppermute x3, waiting for transfers between devices, send_g(): return lax.ppermute(value, ('gy', 'gz'), pairs)  6.92 us
    pallas_call x1, Pallas kernels, body(): pl.pallas_call(functools.partial(product_kernel, n_x, late, groups, step,...  4.03 us
    pallas_call x1, Pallas kernels, body(): pl.pallas_call(functools.partial(base_kernel, early, step), out_shape=jax...  3.06 us
    ppermute x3, starting transfers between devices, send_g(): return lax.ppermute(value, ('gy', 'gz'), pairs)  1.92 us
  transfers between devices with their start and end apart: 9, of which 2 were waited for; matrix products, arithmetic and copies ran while one was open for 12% of the time, Pallas kernels for 18%

profile of v6, /device:TPU:0, one launch (start us, length us, event | category | flops | bytes accessed | tf_op | source)
XLA Modules:
  0.0 63.6 jit_solution(5942089819697916956)
XLA Ops:
  0.0 3.0 %collective-permute-start = (bf16[16,4096]{1,0:T(8,128)(2,1)}, bf16[16,4096]{1,0:T(8,128)(2,1)S(1)}, u32[]{:S(2)}, u32[]{:S(2)}) collective-permute-start(bf16[16,4096]{1,0:T(8,128)(2,1)} %refs_6_.1), channel_id=1, source_target_pairs={{0,4},{4,8},{8,12},{12,0},{1,5},{5,9},{9,13},{13,1},{2,6},{6,10},{... | collective-permute-start | bytes 393224 | tf_op jit(solution)/shard_map/ppermute | solution.py:181
  3.0 2.6 %collective-permute-start.1 = (bf16[16,4096]{1,0:T(8,128)(2,1)}, bf16[16,4096]{1,0:T(8,128)(2,1)S(1)}, u32[]{:S(2)}, u32[]{:S(2)}) collective-permute-start(bf16[16,4096]{1,0:T(8,128)(2,1)} %refs_6_.1), channel_id=1, source_target_pairs={{0,8},{4,12},{8,0},{12,4},{1,9},{5,13},{9,1},{13,5},{2,10},{6,14},... | collective-permute-start | bytes 393224 | tf_op jit(solution)/shard_map/ppermute | solution.py:181
  5.6 1.3 %collective-permute-start.2 = (bf16[16,4096]{1,0:T(8,128)(2,1)}, bf16[16,4096]{1,0:T(8,128)(2,1)S(1)}, u32[]{:S(2)}, u32[]{:S(2)}) collective-permute-start(bf16[16,4096]{1,0:T(8,128)(2,1)} %refs_6_.1), channel_id=1, source_target_pairs={{0,12},{4,0},{8,4},{12,8},{1,13},{5,1},{9,5},{13,9},{2,14},{6,2},{... | collective-permute-start | bytes 393224 | tf_op jit(solution)/shard_map/ppermute | solution.py:181
  7.0 8.4 %fetch_weight.1 = (f32[8,128]{1,0:T(8,128)S(1)}, bf16[4096,1024]{1,0:T(8,128)(2,1)S(1)}, bf16[4096,1024]{1,0:T(8,128)(2,1)S(1)}, bf16[4096,1024]{1,0:T(8,128)(2,1)S(1)}) custom-call(bf16[4096,4096]{1,0:T(8,128)(2,1)} %w_hbm.1), custom_call_target="tpu_custom_call" | custom-call | bytes 33554432 | tf_op jit(solution)/shard_map/fetch_weight/pallas_call | solution.py:195
  15.4 3.3 %copy-done = bf16[4096,1024]{1,0:T(8,128)(2,1)} copy-done((bf16[4096,1024]{1,0:T(8,128)(2,1)}, bf16[4096,1024]{1,0:T(8,128)(2,1)S(1)}, u32[]{:S(2)}) %copy-start) | copy-done | bytes 8388632
  18.7 3.2 %copy-done.2 = bf16[4096,1024]{1,0:T(8,128)(2,1)} copy-done((bf16[4096,1024]{1,0:T(8,128)(2,1)}, bf16[4096,1024]{1,0:T(8,128)(2,1)S(1)}, u32[]{:S(2)}) %copy-start.2) | copy-done | bytes 8388632
  21.9 3.3 %copy-done.4 = bf16[4096,1024]{1,0:T(8,128)(2,1)} copy-done((bf16[4096,1024]{1,0:T(8,128)(2,1)}, bf16[4096,1024]{1,0:T(8,128)(2,1)S(1)}, u32[]{:S(2)}) %copy-start.4) | copy-done | bytes 8388632
  25.2 7.7 %slice.3.refs_10_ = bf16[4096,1024]{1,0:T(8,128)(2,1)} slice(bf16[4096,4096]{1,0:T(8,128)(2,1)} %w_hbm.1), slice={[0:4096], [3072:4096]} | slice | bytes 16777216 | tf_op jit(solution)/shard_map/slice | solution.py:230
  33.0 1.0 %scaled_rows.1 = (bf16[64,4096]{1,0:T(8,128)(2,1)S(1)}, f32[64,128]{1,0:T(8,128)S(1)}, bf16[64,128]{1,0:T(8,128)(2,1)S(1)}) custom-call(s32[4]{0:T(128)S(1)} %copy-done.11, s32[4]{0:T(128)S(1)} %copy-done.12, s32[5]{0:T(128)S(1)} %copy-done.10, bf16[4096]{0:T(1024)(128)(2,1)S(1)} %copy-done.9, bf16[1,64,4096]{2,1,0:T(8,128)(2,1)S(1)} %bitcast.3, ...), custom_call_target="tpu_custom_call" | custom-call | tf_op jit(solution)/shard_map/scaled_rows/pallas_call | solution.py:207
  34.0 0.7 %collective-permute-start.3 = (bf16[64,128]{1,0:T(8,128)(2,1)S(1)}, bf16[64,128]{1,0:T(8,128)(2,1)S(1)}, u32[]{:S(2)}, u32[]{:S(2)}) collective-permute-start(bf16[64,128]{1,0:T(8,128)(2,1)S(1)} %get-tuple-element.21.refs_5_), channel_id=1, source_target_pairs={{0,4},{4,8},{8,12},{12,0},{1,5},{5,9},{9,13},{13,1},{2,6},{6,10},{... | collective-permute-start | bytes 49160 | tf_op jit(solution)/shard_map/ppermute | solution.py:181
  34.7 0.3 collective-permute-start.4
  35.1 2.8 %collective-permute-start.5 = (bf16[64,128]{1,0:T(8,128)(2,1)S(1)}, bf16[64,128]{1,0:T(8,128)(2,1)S(1)}, u32[]{:S(2)}, u32[]{:S(2)}) collective-permute-start(bf16[64,128]{1,0:T(8,128)(2,1)S(1)} %get-tuple-element.21.refs_5_), channel_id=1, source_target_pairs={{0,12},{4,0},{8,4},{12,8},{1,13},{5,1},{9,5},{13,9},{2,14},{6,2},{... | collective-permute-start | bytes 49160 | tf_op jit(solution)/shard_map/ppermute | solution.py:181
  37.9 3.4 %copy-done.3 = bf16[4096,1024]{1,0:T(8,128)(2,1)S(1)} copy-done((bf16[4096,1024]{1,0:T(8,128)(2,1)S(1)}, bf16[4096,1024]{1,0:T(8,128)(2,1)}, u32[]{:S(2)}) %copy-start.3) | copy-done | bytes 8388632
  41.3 3.4 %copy-done.5 = bf16[4096,1024]{1,0:T(8,128)(2,1)S(1)} copy-done((bf16[4096,1024]{1,0:T(8,128)(2,1)S(1)}, bf16[4096,1024]{1,0:T(8,128)(2,1)}, u32[]{:S(2)}) %copy-start.5) | copy-done | bytes 8388632
  44.6 3.1 %first_columns.1.refs_4_ = f32[64,2048]{1,0:T(8,128)S(1)} custom-call(bf16[64,4096]{1,0:T(8,128)(2,1)S(1)} %get-tuple-element.17.x_ref.refs_1_, bf16[4096,1024]{1,0:T(8,128)(2,1)S(1)} %copy-done.3, bf16[4096,1024]{1,0:T(8,128)(2,1)S(1)} %copy-done.5), custom_call_target="tpu_custom_call" | custom-call | flops 1073741824 | bytes 16777216 | tf_op jit(solution)/shard_map/first_columns/pallas_call | solution.py:234
  47.8 1.5 %copy-done.1 = bf16[4096,1024]{1,0:T(8,128)(2,1)S(1)} copy-done((bf16[4096,1024]{1,0:T(8,128)(2,1)S(1)}, bf16[4096,1024]{1,0:T(8,128)(2,1)}, u32[]{:S(2)}) %copy-start.1) | copy-done | bytes 8388632
  49.3 0.6 copy-done.6
  49.9 4.0 %last_columns.1 = (f32[16,4224]{1,0:T(8,128)S(1)}, bf16[16,4224]{1,0:T(8,128)(2,1)S(1)}, bf16[16,4224]{1,0:T(8,128)(2,1)S(1)}, bf16[16,4224]{1,0:T(8,128)(2,1)S(1)}) custom-call(s32[5]{0:T(128)S(1)} %copy-done.10, bf16[64,4096]{1,0:T(8,128)(2,1)S(1)} %get-tuple-element.17.x_ref.refs_1_, f32[64,128]{1,0:T(8,128)S(1)} %get-tuple-element.18.refs_2_, ...), custom_call_target="tpu_custom_call" | custom-call | flops 1073741824 | bytes 16777216 | tf_op jit(solution)/shard_map/last_columns/pallas_call | solution.py:247
  53.9 0.1 collective-permute-start.6
  54.0 1.6 %collective-permute-start.7 = (bf16[16,4224]{1,0:T(8,128)(2,1)S(1)}, bf16[16,4224]{1,0:T(8,128)(2,1)S(1)}, u32[]{:S(2)}, u32[]{:S(2)}) collective-permute-start(bf16[16,4224]{1,0:T(8,128)(2,1)S(1)} %get-tuple-element.25), channel_id=1, source_target_pairs={{0,2},{1,3},{2,0},{3,1},{4,6},{5,7},{6,4},{7,5},{8,10},{9,11},{10,... | collective-permute-start | bytes 405512 | tf_op jit(solution)/shard_map/ppermute | solution.py:188
  55.6 0.3 collective-permute-start.8
  55.9 4.0 %collective-permute-done.6.refs_1_ = bf16[16,4224]{1,0:T(8,128)(2,1)S(1)} collective-permute-done((bf16[16,4224]{1,0:T(8,128)(2,1)S(1)}, bf16[16,4224]{1,0:T(8,128)(2,1)S(1)}, u32[]{:S(2)}, u32[]{:S(2)}) %collective-permute-start.6) | collective-permute-done | bytes 135200 | tf_op jit(solution)/shard_map/ppermute | solution.py:188
  59.8 3.0 %collective-permute-done.7.refs_2_ = bf16[16,4224]{1,0:T(8,128)(2,1)S(1)} collective-permute-done((bf16[16,4224]{1,0:T(8,128)(2,1)S(1)}, bf16[16,4224]{1,0:T(8,128)(2,1)S(1)}, u32[]{:S(2)}, u32[]{:S(2)}) %collective-permute-start.7) | collective-permute-done | bytes 135200 | tf_op jit(solution)/shard_map/ppermute | solution.py:188
  62.8 0.8 %query_rows.1 = bf16[16,4096]{1,0:T(8,128)(2,1)} custom-call(f32[16,4224]{1,0:T(8,128)S(1)} %get-tuple-element.23.refs_0_, bf16[16,4224]{1,0:T(8,128)(2,1)S(1)} %collective-permute-done.6.refs_1_, bf16[16,4224]{1,0:T(8,128)(2,1)S(1)} %collective-permute-done.7.refs_2_, bf16[16,4224]{1,0:T(8,128)(2,1)S(1)} %collective-permute-done.8.refs_3_), custom_call_target="tpu_custom_call" | custom-call | tf_op jit(solution)/shard_map/query_rows/pallas_call | solution.py:259
  (31 shorter events, 0.1 us)
Async XLA Ops:
  0.0 32.9 %collective-permute-start = (bf16[16,4096]{1,0:T(8,128)(2,1)}, bf16[16,4096]{1,0:T(8,128)(2,1)S(1)}, u32[]{:S(2)}, u32[]{:S(2)}) collective-permute-start(bf16[16,4096]{1,0:T(8,128)(2,1)} %refs_6_.1), channel_id=1, source_target_pairs={{0,4},{4,8},{8,12},{12,0},{1,5},{5,9},{9,13},{13,1},{2,6},{6,10},{... | collective-permute-start | bytes 393224 | tf_op jit(solution)/shard_map/ppermute | solution.py:181
  3.0 29.9 %collective-permute-start.1 = (bf16[16,4096]{1,0:T(8,128)(2,1)}, bf16[16,4096]{1,0:T(8,128)(2,1)S(1)}, u32[]{:S(2)}, u32[]{:S(2)}) collective-permute-start(bf16[16,4096]{1,0:T(8,128)(2,1)} %refs_6_.1), channel_id=1, source_target_pairs={{0,8},{4,12},{8,0},{12,4},{1,9},{5,13},{9,1},{13,5},{2,10},{6,14},... | collective-permute-start | bytes 393224 | tf_op jit(solution)/shard_map/ppermute | solution.py:181
  5.6 27.3 %collective-permute-start.2 = (bf16[16,4096]{1,0:T(8,128)(2,1)}, bf16[16,4096]{1,0:T(8,128)(2,1)S(1)}, u32[]{:S(2)}, u32[]{:S(2)}) collective-permute-start(bf16[16,4096]{1,0:T(8,128)(2,1)} %refs_6_.1), channel_id=1, source_target_pairs={{0,12},{4,0},{8,4},{12,8},{1,13},{5,1},{9,5},{13,9},{2,14},{6,2},{... | collective-permute-start | bytes 393224 | tf_op jit(solution)/shard_map/ppermute | solution.py:181
  15.4 3.3 %copy-start = (bf16[4096,1024]{1,0:T(8,128)(2,1)}, bf16[4096,1024]{1,0:T(8,128)(2,1)S(1)}, u32[]{:S(2)}) copy-start(bf16[4096,1024]{1,0:T(8,128)(2,1)S(1)} %get-tuple-element.22.refs_9_) | copy-start | bytes 25165828
  18.7 3.2 %copy-start.2 = (bf16[4096,1024]{1,0:T(8,128)(2,1)}, bf16[4096,1024]{1,0:T(8,128)(2,1)S(1)}, u32[]{:S(2)}) copy-start(bf16[4096,1024]{1,0:T(8,128)(2,1)S(1)} %get-tuple-element.19.refs_0_) | copy-start | bytes 25165828
  21.9 3.3 %copy-start.4 = (bf16[4096,1024]{1,0:T(8,128)(2,1)}, bf16[4096,1024]{1,0:T(8,128)(2,1)S(1)}, u32[]{:S(2)}) copy-start(bf16[4096,1024]{1,0:T(8,128)(2,1)S(1)} %get-tuple-element.20.refs_1_) | copy-start | bytes 25165828
  25.2 7.7 %copy-start.7 = (bf16[1,4096,64]{1,2,0:T(8,128)(2,1)S(1)}, bf16[1,4096,64]{1,2,0:T(8,128)(2,1)}, u32[]{:S(2)}) copy-start(bf16[1,4096,64]{1,2,0:T(8,128)(2,1)} %param.12) | copy-start | bytes 1572868
  25.2 7.7 %copy-start.8 = (bf16[16,4096]{1,0:T(8,128)(2,1)S(1)}, bf16[16,4096]{1,0:T(8,128)(2,1)}, u32[]{:S(2)}) copy-start(bf16[16,4096]{1,0:T(8,128)(2,1)} %refs_6_.1) | copy-start | bytes 393220
  25.2 7.7 %copy-start.9 = (bf16[4096]{0:T(1024)(128)(2,1)S(1)}, bf16[4096]{0:T(1024)(128)(2,1)}, u32[]{:S(2)}) copy-start(bf16[4096]{0:T(1024)(128)(2,1)} %refs_3_.2) | copy-start | bytes 24580
  25.2 7.7 %copy-start.10 = (s32[5]{0:T(128)S(1)}, s32[5]{0:T(128)}, u32[]{:S(2)}) copy-start(s32[5]{0:T(128)} %refs_0_.3) | copy-start | bytes 64
  25.2 7.7 %copy-start.11 = (s32[4]{0:T(128)S(1)}, s32[4]{0:T(128)}, u32[]{:S(2)}) copy-start(s32[4]{0:T(128)} %refs_0_.2) | copy-start | bytes 52
  25.2 7.7 %copy-start.12 = (s32[4]{0:T(128)S(1)}, s32[4]{0:T(128)}, u32[]{:S(2)}) copy-start(s32[4]{0:T(128)} %refs_1_.1) | copy-start | bytes 52
  33.0 14.8 %slice-start = ((s8[8388608]{0:T(1024)(128)(4,1)}), s8[4194304]{0:T(1024)(128)(4,1)S(1)}, s32[]{:S(2)}) async-start(s8[8388608]{0:T(1024)(128)(4,1)} %bitcast.1), calls=%async_computation | async-start | bytes 8388608
  34.0 13.7 %collective-permute-start.3 = (bf16[64,128]{1,0:T(8,128)(2,1)S(1)}, bf16[64,128]{1,0:T(8,128)(2,1)S(1)}, u32[]{:S(2)}, u32[]{:S(2)}) collective-permute-start(bf16[64,128]{1,0:T(8,128)(2,1)S(1)} %get-tuple-element.21.refs_5_), channel_id=1, source_target_pairs={{0,4},{4,8},{8,12},{12,0},{1,5},{5,9},{9,13},{13,1},{2,6},{6,10},{... | collective-permute-start | bytes 49160 | tf_op jit(solution)/shard_map/ppermute | solution.py:181
  34.7 13.0 %collective-permute-start.4 = (bf16[64,128]{1,0:T(8,128)(2,1)S(1)}, bf16[64,128]{1,0:T(8,128)(2,1)S(1)}, u32[]{:S(2)}, u32[]{:S(2)}) collective-permute-start(bf16[64,128]{1,0:T(8,128)(2,1)S(1)} %get-tuple-element.21.refs_5_), channel_id=1, source_target_pairs={{0,8},{4,12},{8,0},{12,4},{1,9},{5,13},{9,1},{13,5},{2,10},{6,14},... | collective-permute-start | bytes 49160 | tf_op jit(solution)/shard_map/ppermute | solution.py:181
  35.1 12.7 %collective-permute-start.5 = (bf16[64,128]{1,0:T(8,128)(2,1)S(1)}, bf16[64,128]{1,0:T(8,128)(2,1)S(1)}, u32[]{:S(2)}, u32[]{:S(2)}) collective-permute-start(bf16[64,128]{1,0:T(8,128)(2,1)S(1)} %get-tuple-element.21.refs_5_), channel_id=1, source_target_pairs={{0,12},{4,0},{8,4},{12,8},{1,13},{5,1},{9,5},{13,9},{2,14},{6,2},{... | collective-permute-start | bytes 49160 | tf_op jit(solution)/shard_map/ppermute | solution.py:181
  37.9 3.4 %copy-start.3 = (bf16[4096,1024]{1,0:T(8,128)(2,1)S(1)}, bf16[4096,1024]{1,0:T(8,128)(2,1)}, u32[]{:S(2)}) copy-start(bf16[4096,1024]{1,0:T(8,128)(2,1)} %copy-done.2) | copy-start | bytes 25165828
  41.3 3.4 %copy-start.5 = (bf16[4096,1024]{1,0:T(8,128)(2,1)S(1)}, bf16[4096,1024]{1,0:T(8,128)(2,1)}, u32[]{:S(2)}) copy-start(bf16[4096,1024]{1,0:T(8,128)(2,1)} %copy-done.4) | copy-start | bytes 25165828
  44.6 3.1 %slice-start.1 = ((s8[8388608]{0:T(1024)(128)(4,1)}), s8[4194304]{0:T(1024)(128)(4,1)S(1)}, s32[]{:S(2)}) async-start(s8[8388608]{0:T(1024)(128)(4,1)} %bitcast.1), calls=%async_computation.1 | async-start | bytes 8388608
  44.6 4.7 %copy-start.1 = (bf16[4096,1024]{1,0:T(8,128)(2,1)S(1)}, bf16[4096,1024]{1,0:T(8,128)(2,1)}, u32[]{:S(2)}) copy-start(bf16[4096,1024]{1,0:T(8,128)(2,1)} %copy-done) | copy-start | bytes 25165828
  44.6 5.3 %copy-start.6 = (bf16[4,64,4096]{2,1,0:T(8,128)(2,1)S(1)}, bf16[4,64,4096]{2,1,0:T(8,128)(2,1)}, u32[]{:S(2)}) copy-start(bf16[4,64,4096]{2,1,0:T(8,128)(2,1)} %refs_3_.3) | copy-start | bytes 6291460
  53.9 5.9 %collective-permute-start.6 = (bf16[16,4224]{1,0:T(8,128)(2,1)S(1)}, bf16[16,4224]{1,0:T(8,128)(2,1)S(1)}, u32[]{:S(2)}, u32[]{:S(2)}) collective-permute-start(bf16[16,4224]{1,0:T(8,128)(2,1)S(1)} %get-tuple-element.24), channel_id=1, source_target_pairs={{0,3},{1,2},{2,1},{3,0},{4,7},{5,6},{6,5},{7,4},{8,11},{9,10},{10,... | collective-permute-start | bytes 405512 | tf_op jit(solution)/shard_map/ppermute | solution.py:188
  54.0 8.8 %collective-permute-start.7 = (bf16[16,4224]{1,0:T(8,128)(2,1)S(1)}, bf16[16,4224]{1,0:T(8,128)(2,1)S(1)}, u32[]{:S(2)}, u32[]{:S(2)}) collective-permute-start(bf16[16,4224]{1,0:T(8,128)(2,1)S(1)} %get-tuple-element.25), channel_id=1, source_target_pairs={{0,2},{1,3},{2,0},{3,1},{4,6},{5,7},{6,4},{7,5},{8,10},{9,11},{10,... | collective-permute-start | bytes 405512 | tf_op jit(solution)/shard_map/ppermute | solution.py:188
  55.6 7.2 %collective-permute-start.8 = (bf16[16,4224]{1,0:T(8,128)(2,1)S(1)}, bf16[16,4224]{1,0:T(8,128)(2,1)S(1)}, u32[]{:S(2)}, u32[]{:S(2)}) collective-permute-start(bf16[16,4224]{1,0:T(8,128)(2,1)S(1)} %get-tuple-element.26), channel_id=1, source_target_pairs={{0,1},{1,0},{2,3},{3,2},{4,5},{5,4},{6,7},{7,6},{8,9},{9,8},{10,11... | collective-permute-start | bytes 405512 | tf_op jit(solution)/shard_map/ppermute | solution.py:188

commit v7 on v5

--- a/solution.py
+++ b/solution.py
@@ -85,31 +85,81 @@
     down_out[:, :rank_columns] = total.astype(down_out.dtype)
 
 
-def base_kernel(n_w, step, x_ref, *refs):
-    weights, out_ref = refs[:n_w], refs[n_w]
+def split_wide(value):
+    high = value.astype(jnp.bfloat16).astype(jnp.float32)
+    low = jnp.where(high < jnp.inf, value - high, 0.0)
+    lane = lax.broadcasted_iota(jnp.int32, value.shape, 1)
+    return jnp.where(lane < LANES // 2, high, low)
+
+
+def join_wide(value):
+    return value[:, :1] + value[:, LANES - 1 :]
+
+
+def write_rows(acc, outs, n_y, n_z):
+    z = lax.axis_index("gz")
+    rows_here = outs[0].shape[0] // n_y
+    for k in range(n_z):
+        for y in range(n_y):
+            owner = y * n_z + lax.rem(z + k, n_z)
+            begin = pl.multiple_of(owner * rows_here, rows_here)
+            outs[k][y * rows_here : (y + 1) * rows_here, :] = acc[
+                pl.ds(begin, rows_here), :
+            ].astype(outs[k].dtype)
+
+
+def multiply(x_ref, weights, step, acc):
     width = weights[0].shape[1]
-    for c in range(0, out_ref.shape[1], step):
+    for c in range(0, width * len(weights), step):
         inner = c % width
-        out_ref[:, c : c + step] = jnp.dot(
+        acc[:, c : c + step] = jnp.dot(
             x_ref[...],
             weights[c // width][:, inner : inner + step],
             preferred_element_type=jnp.float32,
         )
 
 
-def product_kernel(n_x, n_w, groups, step, offset, *refs):
-    start_ref, x_ref, square_ref, up_ref, base_ref = refs[:5]
-    downs, refs = refs[5 : 5 + n_x], refs[5 + n_x :]
+def first_kernel(n_w, n_y, n_z, step, x_ref, *refs):
     weights, outs, acc = refs[:n_w], refs[n_w:-1], refs[-1]
-    rows = x_ref.shape[0]
-    width = weights[0].shape[1]
-    done = base_ref.shape[1]
-    columns = done + width * n_w
+    multiply(x_ref, weights, step, acc)
+    write_rows(acc, outs, n_y, n_z)
+
+
+def last_kernel(n_w, n_x, n_y, n_z, step, x_ref, square_ref, *refs):
+    downs, refs = refs[:n_x], refs[n_x:]
+    weights, outs, acc = refs[:n_w], refs[n_w:-1], refs[-1]
+    multiply(x_ref, weights, step, acc)
+    columns = weights[0].shape[1] * n_w
+    down = downs[0][...].astype(jnp.float32)
+    for other in downs[1:]:
+        down = down + other[...].astype(jnp.float32)
+    acc[:, columns : columns + LANES] = down
+    acc[:, columns + LANES :] = split_wide(square_ref[...])
+    write_rows(acc, outs, n_y, n_z)
+
+
+def pair_kernel(n_y, n_z, step, start_ref, up_ref, *refs):
+    firsts, lasts = refs[:n_z], refs[n_z : 2 * n_z]
+    outs, acc = refs[2 * n_z : -1], refs[-1]
+    rows, done = firsts[0].shape
+    rows_here = rows // n_y
+    columns = done + lasts[0].shape[1] - 2 * LANES
     adapters, rank_columns, _ = up_ref.shape
-    down = downs[0][:, :rank_columns]
-    for other in downs[1:]:
-        down = down + other[:, :rank_columns]
+    z = lax.axis_index("gz")
+
+    def added(parts, here):
+        total = parts[0][:, here]
+        for part in parts[1:]:
+            total = total + part[:, here].astype(jnp.float32)
+        return total
+
+    late = columns - done
+    square = join_wide(lasts[0][:, late + LANES :])
+    for part in lasts[1:]:
+        square = square + join_wide(part[:, late + LANES :].astype(jnp.float32))
+    down = added(lasts, slice(late, late + rank_columns)).astype(jnp.bfloat16)
     row = lax.broadcasted_iota(jnp.int32, (rows, rank_columns), 0)
+    row = (row // rows_here * n_z + z) * rows_here + lax.rem(row, rows_here)
     spread = jnp.concatenate(
         [
             jnp.where((row >= start_ref[a]) & (row < start_ref[a + 1]), down, jnp.zeros_like(down))
@@ -118,27 +168,16 @@
         axis=1,
     )
     for c in range(0, columns, step):
-        here = slice(c, c + step)
-        up = up_ref[:, :, here].reshape(adapters * rank_columns, step)
         if c < done:
-            base = base_ref[:, here]
+            base = added(firsts, slice(c, c + step))
         else:
-            inner = (c - done) % width
-            base = jnp.dot(
-                x_ref[...],
-                weights[(c - done) // width][:, inner : inner + step],
-                preferred_element_type=jnp.float32,
-            )
-        acc[:, here] = base + jnp.dot(spread, up, preferred_element_type=jnp.float32)
-    square = square_ref[...]
-    high = square.astype(jnp.bfloat16).astype(jnp.float32)
-    low = jnp.where(high < jnp.inf, square - high, 0.0)
-    lane = lax.broadcasted_iota(jnp.int32, square.shape, 1)
-    acc[:, columns:] = jnp.where(lane < LANES // 2, high, low)
-    g = lax.axis_index(("gy", "gz"))
-    rows_here = outs[0].shape[0]
-    for k in range(groups):
-        begin = pl.multiple_of(offset(g, k) * rows_here, rows_here)
+            base = added(lasts, slice(c - done, c - done + step))
+        up = up_ref[:, :, c : c + step].reshape(adapters * rank_columns, step)
+        acc[:, c : c + step] = base + jnp.dot(spread, up, preferred_element_type=jnp.float32)
+    acc[:, columns:] = split_wide(jnp.broadcast_to(square, (rows, LANES)))
+    y = lax.axis_index("gy")
+    for k in range(n_y):
+        begin = pl.multiple_of(lax.rem(y + k, n_y) * rows_here, rows_here)
         outs[k][...] = acc[pl.ds(begin, rows_here), :].astype(outs[k].dtype)
 
 
@@ -148,7 +187,7 @@
     total = parts[0][...]
     for other in parts[1:]:
         total = total + other[...].astype(jnp.float32)
-    mean_sq = total[:, columns : columns + 1] + total[:, columns + LANES - 1 :]
+    mean_sq = join_wide(total[:, columns:])
     scale = lax.rsqrt(mean_sq + EPSILON)
     value = jnp.where(mean_sq < jnp.inf, total[:, :columns] * scale, 0.0)
     out_ref[...] = value.astype(out_ref.dtype)
@@ -172,22 +211,13 @@
     rows = n_x * block_rows
     rows_here = rows // groups
 
-    def offset(g, k):
-        y = lax.rem(g // n_z + k // n_z, n_y)
-        z = lax.rem(lax.rem(g, n_z) + k % n_z, n_z)
-        return y * n_z + z
-
-    def send_x(value, k):
-        return lax.ppermute(value, "gx", [(j, (j + k) % n_x) for j in range(n_x)])
-
-    def send_g(value, k):
-        pairs = []
-        for g in range(groups):
-            y, z = (g // n_z + k // n_z) % n_y, (g % n_z + k % n_z) % n_z
-            pairs.append((g, y * n_z + z))
-        return lax.ppermute(value, ("gy", "gz"), pairs)
-
-    blocks = [hidden] + [send_x(hidden, k) for k in range(1, n_x)]
+    def send(value, axis, n, k):
+        return lax.ppermute(value, axis, [(j, (j + k) % n) for j in range(n)])
+
+    def spread_out(made, axis, n):
+        return [made[0]] + [send(made[k], axis, n, k) for k in range(1, n)]
+
+    blocks = [hidden] + [send(hidden, "gx", n_x, k) for k in range(1, n_x)]
 
     step = min(512, columns // 4)
     n_w, pieces = 4, 4
@@ -225,40 +255,55 @@
         *blocks,
     )
 
-    downs = [down] + [send_x(down, k) for k in range(1, n_x)]
+    downs = [down] + [send(down, "gx", n_x, k) for k in range(1, n_x)]
 
     weights = [pltpu.with_memory_space_constraint(w, pltpu.VMEM) for w in weights]
-    early = n_w // 2
-    base_columns = early * (columns // n_w)
-    base = pl.pallas_call(
-        functools.partial(base_kernel, early, step),
-        out_shape=jax.ShapeDtypeStruct((rows, base_columns), f32),
+    early, late = n_w - 1, 1
+    early_columns, late_columns = (n * (columns // n_w) for n in (early, late))
+    kept = n_y * rows_here
+
+    def shapes(n, shape):
+        return [jax.ShapeDtypeStruct(shape, f32 if k == 0 else bf16) for k in range(n)]
+
+    made = pl.pallas_call(
+        functools.partial(first_kernel, early, n_y, n_z, step),
+        out_shape=shapes(n_z, (kept, early_columns)),
         in_specs=[VMEM] * (1 + early),
-        out_specs=VMEM,
-        cost_estimate=cost(2 * rows * depth * base_columns, 2 * depth * base_columns),
+        out_specs=[VMEM] * n_z,
+        scratch_shapes=[pltpu.VMEM((rows, early_columns), f32)],
+        cost_estimate=cost(2 * rows * depth * early_columns, 2 * depth * early_columns),
         compiler_params=params(4 + (rows * depth >> 16)),
         name="first_columns",
     )(x, *weights[:early])
-
-    late = n_w - early
-    late_columns = columns - base_columns
-    dtypes = [f32] + [bf16] * (groups - 1)
+    firsts = spread_out(made, "gz", n_z)
+
     made = pl.pallas_call(
-        functools.partial(product_kernel, n_x, late, groups, step, offset),
-        out_shape=[jax.ShapeDtypeStruct((rows_here, columns + LANES), t) for t in dtypes],
-        in_specs=[SMEM] + [VMEM] * (4 + n_x + late),
-        out_specs=[VMEM] * groups,
-        scratch_shapes=[pltpu.VMEM((rows, columns + LANES), f32)],
-        cost_estimate=cost(2 * rows * depth * late_columns, 2 * depth * late_columns),
+        functools.partial(last_kernel, late, n_x, n_y, n_z, step),
+        out_shape=shapes(n_z, (kept, late_columns + 2 * LANES)),
+        in_specs=[VMEM] * (2 + n_x + late),
+        out_specs=[VMEM] * n_z,
+        scratch_shapes=[pltpu.VMEM((rows, late_columns + 2 * LANES), f32)],
+        cost_estimate=cost(2 * rows * depth * columns, 4 * depth * columns),
         compiler_params=params(4 + (rows * depth >> 16)),
         name="last_columns",
-    )(segment_starts, x, square, adapter_up_factors, base, *downs, *weights[early:])
-    parts = [made[0]] + [send_g(made[k], k) for k in range(groups - 1, 0, -1)]
+    )(x, square, *downs, *weights[early:])
+    lasts = spread_out(made, "gz", n_z)
+
+    made = pl.pallas_call(
+        functools.partial(pair_kernel, n_y, n_z, step),
+        out_shape=shapes(n_y, (rows_here, columns + LANES)),
+        in_specs=[SMEM] + [VMEM] * (1 + 2 * n_z),
+        out_specs=[VMEM] * n_y,
+        scratch_shapes=[pltpu.VMEM((kept, columns + LANES), f32)],
+        compiler_params=params(4 + (rows * depth >> 16)),
+        name="chip_sums",
+    )(segment_starts, adapter_up_factors, *firsts, *lasts)
+    parts = spread_out(made, "gy", n_y)
 
     return pl.pallas_call(
         final_kernel,
         out_shape=jax.ShapeDtypeStruct((rows_here, columns), bf16),
-        in_specs=[VMEM] * groups,
+        in_specs=[VMEM] * n_y,
         out_specs=VMEM,
         compiler_params=params(4 + (rows * depth >> 16)),
         name="query_rows",

time: 40.7 us -> 38.7 us (0.951)
  waiting for transfers between devices: 8.61 us -> 5.3 us
  starting transfers between devices: 11.9 us -> 13.1 us
    ppermute x9, waiting for transfers between devices: 8.61 us -> 5.3 us  [send(): return lax.ppermute(value, axis, [(j, (j + k) % n) for j in range(n)])]
    ppermute x9, starting transfers between devices: 11.9 us -> 13.1 us  [send(): return lax.ppermute(value, axis, [(j, (j + k) % n) for j in range(n)])]
    pallas_call x2 -> x3, Pallas kernels: 7.08 us -> 7.29 us  [the longest x1 4.56 us: body(): pl.pallas_call(functools.partial(first_kernel, early, n_y, n_z, step), ou...]
  transfers between devices with their start and end apart: 9 -> 9, of which waited for: 3 -> 2; matrix products, arithmetic and copies ran while one was open for 0% -> 0% of each run, Pallas kernels for 34% -> 44%
where the time goes in v7:
time: 38.7 us; the launch traced here: 38.6 us
  Pallas kernels  20 us (52%)
  starting transfers between devices  13.1 us (34%)
  waiting for transfers between devices  5.3 us (14%)
    ppermute x9, starting transfers between devices, send(): return lax.ppermute(value, axis, [(j, (j + k) % n) for j in range(n)])  13.1 us
    pallas_call x1, Pallas kernels, body(): pl.pallas_call(functools.partial(fetch_kernel, n_w), out_shape=[jax.Shape...  10.9 us
    ppermute x9, waiting for transfers between devices, send(): return lax.ppermute(value, axis, [(j, (j + k) % n) for j in range(n)])  5.3 us
    pallas_call x1, Pallas kernels, body(): pl.pallas_call(functools.partial(first_kernel, early, n_y, n_z, step), ou...  4.56 us
    pallas_call x1, Pallas kernels, body(): pl.pallas_call(functools.partial(last_kernel, late, n_x, n_y, n_z, step),...  1.64 us
    pallas_call x1, Pallas kernels, body(): pl.pallas_call(functools.partial(pair_kernel, n_y, n_z, step), out_shape=...  1.09 us
    pallas_call x1, Pallas kernels, body(): pl.pallas_call(functools.partial(rows_kernel, n_x, depth * groups), out_s...  1.02 us
    pallas_call x1, Pallas kernels, body(): pl.pallas_call(final_kernel, out_shape=jax.ShapeDtypeStruct((rows_here, c...  0.83 us
  transfers between devices with their start and end apart: 9, of which 2 were waited for; matrix products, arithmetic and copies ran while one was open for 0% of the time, Pallas kernels for 44%

profile of v7, /device:TPU:0, one launch (start us, length us, event | category | flops | bytes accessed | tf_op | source)
XLA Modules:
  0.0 38.6 jit_solution(14690762640299564817)
XLA Ops:
  0.0 3.1 %collective-permute-start = (bf16[16,4096]{1,0:T(8,128)(2,1)}, bf16[16,4096]{1,0:T(8,128)(2,1)S(1)}, u32[]{:S(2)}, u32[]{:S(2)}) collective-permute-start(bf16[16,4096]{1,0:T(8,128)(2,1)} %refs_6_.1), channel_id=1, source_target_pairs={{0,4},{4,8},{8,12},{12,0},{1,5},{5,9},{9,13},{13,1},{2,6},{6,10},{... | collective-permute-start | bytes 393224 | tf_op jit(solution)/shard_map/ppermute | solution.py:215
  3.1 2.6 %collective-permute-start.1 = (bf16[16,4096]{1,0:T(8,128)(2,1)}, bf16[16,4096]{1,0:T(8,128)(2,1)S(1)}, u32[]{:S(2)}, u32[]{:S(2)}) collective-permute-start(bf16[16,4096]{1,0:T(8,128)(2,1)} %refs_6_.1), channel_id=1, source_target_pairs={{0,8},{4,12},{8,0},{12,4},{1,9},{5,13},{9,1},{13,5},{2,10},{6,14},... | collective-permute-start | bytes 393224 | tf_op jit(solution)/shard_map/ppermute | solution.py:215
  5.7 1.3 %collective-permute-start.2 = (bf16[16,4096]{1,0:T(8,128)(2,1)}, bf16[16,4096]{1,0:T(8,128)(2,1)S(1)}, u32[]{:S(2)}, u32[]{:S(2)}) collective-permute-start(bf16[16,4096]{1,0:T(8,128)(2,1)} %refs_6_.1), channel_id=1, source_target_pairs={{0,12},{4,0},{8,4},{12,8},{1,13},{5,1},{9,5},{13,9},{2,14},{6,2},{... | collective-permute-start | bytes 393224 | tf_op jit(solution)/shard_map/ppermute | solution.py:215
  7.1 10.9 %fetch_weight.1 = (f32[8,128]{1,0:T(8,128)S(1)}, bf16[4096,1024]{1,0:T(8,128)(2,1)S(1)}, bf16[4096,1024]{1,0:T(8,128)(2,1)S(1)}, bf16[4096,1024]{1,0:T(8,128)(2,1)S(1)}, bf16[4096,1024]{1,0:T(8,128)(2,1)S(1)}) custom-call(bf16[4096,4096]{1,0:T(8,128)(2,1)} %w_hbm.1), custom_call_target="tpu_custom_call" | custom-call | bytes 33554432 | tf_op jit(solution)/shard_map/fetch_weight/pallas_call | solution.py:225
  18.0 0.0 collective-permute-done.refs_7_
  18.0 0.0 collective-permute-done.1.refs_8_
  18.0 0.0 collective-permute-done.2.refs_9_
  18.0 1.0 %scaled_rows.1 = (bf16[64,4096]{1,0:T(8,128)(2,1)S(1)}, f32[64,128]{1,0:T(8,128)S(1)}, bf16[64,128]{1,0:T(8,128)(2,1)S(1)}) custom-call(s32[4]{0:T(128)S(1)} %copy-done.5, s32[4]{0:T(128)S(1)} %copy-done.6, s32[5]{0:T(128)S(1)} %copy-done.4, bf16[4096]{0:T(1024)(128)(2,1)S(1)} %copy-done.3, bf16[1,64,4096]{2,1,0:T(8,128)(2,1)S(1)} %bitcast.1, ...), custom_call_target="tpu_custom_call" | custom-call | tf_op jit(solution)/shard_map/scaled_rows/pallas_call | solution.py:237
  19.1 0.7 %collective-permute-start.4 = (bf16[64,128]{1,0:T(8,128)(2,1)S(1)}, bf16[64,128]{1,0:T(8,128)(2,1)S(1)}, u32[]{:S(2)}, u32[]{:S(2)}) collective-permute-start(bf16[64,128]{1,0:T(8,128)(2,1)S(1)} %get-tuple-element.27.refs_0_), channel_id=1, source_target_pairs={{0,4},{4,8},{8,12},{12,0},{1,5},{5,9},{9,13},{13,1},{2,6},{6,10},{... | collective-permute-start | bytes 49160 | tf_op jit(solution)/shard_map/ppermute | solution.py:215
  19.8 0.8 %collective-permute-start.5 = (bf16[64,128]{1,0:T(8,128)(2,1)S(1)}, bf16[64,128]{1,0:T(8,128)(2,1)S(1)}, u32[]{:S(2)}, u32[]{:S(2)}) collective-permute-start(bf16[64,128]{1,0:T(8,128)(2,1)S(1)} %get-tuple-element.27.refs_0_), channel_id=1, source_target_pairs={{0,8},{4,12},{8,0},{12,4},{1,9},{5,13},{9,1},{13,5},{2,10},{6,14},... | collective-permute-start | bytes 49160 | tf_op jit(solution)/shard_map/ppermute | solution.py:215
  20.6 2.4 %collective-permute-start.6 = (bf16[64,128]{1,0:T(8,128)(2,1)S(1)}, bf16[64,128]{1,0:T(8,128)(2,1)S(1)}, u32[]{:S(2)}, u32[]{:S(2)}) collective-permute-start(bf16[64,128]{1,0:T(8,128)(2,1)S(1)} %get-tuple-element.27.refs_0_), channel_id=1, source_target_pairs={{0,12},{4,0},{8,4},{12,8},{1,13},{5,1},{9,5},{13,9},{2,14},{6,2},{... | collective-permute-start | bytes 49160 | tf_op jit(solution)/shard_map/ppermute | solution.py:215
  22.9 4.6 %first_columns.1 = (f32[32,3072]{1,0:T(8,128)S(1)}, bf16[32,3072]{1,0:T(8,128)(2,1)S(1)}) custom-call(bf16[64,4096]{1,0:T(8,128)(2,1)S(1)} %get-tuple-element.20.x_ref, bf16[4096,1024]{1,0:T(8,128)(2,1)S(1)} %get-tuple-element.21.refs_0_, bf16[4096,1024]{1,0:T(8,128)(2,1)S(1)} %get-tuple-element.22.refs_1_, bf16[4096,1024]{1,0:T(8,128)(2,1)S(1)} %get-tuple-element.23.refs_2_), custom_call_target="tpu_custom_call" | custom-call | flops 1610612736 | bytes 25165824 | tf_op jit(solution)/shard_map/first_columns/pallas_call | solution.py:268
  27.5 0.0 copy-start
  27.5 0.1 collective-permute-start.3
  27.6 0.0 collective-permute-done.5.refs_2_
  27.6 0.0 collective-permute-done.6.refs_3_
  27.6 1.6 %last_columns.1 = (f32[32,1280]{1,0:T(8,128)S(1)}, bf16[32,1280]{1,0:T(8,128)(2,1)S(1)}) custom-call(bf16[64,4096]{1,0:T(8,128)(2,1)S(1)} %get-tuple-element.20.x_ref, f32[64,128]{1,0:T(8,128)S(1)} %get-tuple-element.26.square_ref, bf16[64,128]{1,0:T(8,128)(2,1)S(1)} %get-tuple-element.27.refs_0_, bf16[64,128]{1,0:T(8,128)(2,1)S(1)} %collective-permute-done.4.refs_1_, ...), custom_call_target="tpu_custom_call" | custom-call | flops 2147483648 | bytes 67108864 | tf_op jit(solution)/shard_map/last_columns/pallas_call | solution.py:280
  29.3 0.5 %collective-permute-start.7 = (bf16[32,1280]{1,0:T(8,128)(2,1)S(1)}, bf16[32,1280]{1,0:T(8,128)(2,1)S(1)}, u32[]{:S(2)}, u32[]{:S(2)}) collective-permute-start(bf16[32,1280]{1,0:T(8,128)(2,1)S(1)} %get-tuple-element.30), channel_id=1, source_target_pairs={{0,1},{1,0},{2,3},{3,2},{4,5},{5,4},{6,7},{7,6},{8,9},{9,8},{10,11... | collective-permute-start | bytes 245768 | tf_op jit(solution)/shard_map/ppermute | solution.py:215
  29.8 0.9 %collective-permute-done.7.refs_3_ = bf16[32,1280]{1,0:T(8,128)(2,1)S(1)} collective-permute-done((bf16[32,1280]{1,0:T(8,128)(2,1)S(1)}, bf16[32,1280]{1,0:T(8,128)(2,1)S(1)}, u32[]{:S(2)}, u32[]{:S(2)}) %collective-permute-start.7) | collective-permute-done | bytes 81952 | tf_op jit(solution)/shard_map/ppermute | solution.py:215
  30.7 0.0 collective-permute-done.3.refs_1_
  30.8 1.1 %chip_sums.1 = (f32[16,4224]{1,0:T(8,128)S(1)}, bf16[16,4224]{1,0:T(8,128)(2,1)S(1)}) custom-call(s32[5]{0:T(128)S(1)} %copy-done.4, bf16[4,64,4096]{2,1,0:T(8,128)(2,1)S(1)} %copy-done, f32[32,3072]{1,0:T(8,128)S(1)} %get-tuple-element.24.refs_0_, bf16[32,3072]{1,0:T(8,128)(2,1)S(1)} %collective-permute-done.3.refs_1_, ...), custom_call_target="tpu_custom_call" | custom-call | tf_op jit(solution)/shard_map/chip_sums/pallas_call | solution.py:292
  31.8 1.6 %collective-permute-start.8 = (bf16[16,4224]{1,0:T(8,128)(2,1)S(1)}, bf16[16,4224]{1,0:T(8,128)(2,1)S(1)}, u32[]{:S(2)}, u32[]{:S(2)}) collective-permute-start(bf16[16,4224]{1,0:T(8,128)(2,1)S(1)} %get-tuple-element.32), channel_id=1, source_target_pairs={{0,2},{2,0},{1,3},{3,1},{4,6},{6,4},{5,7},{7,5},{8,10},{10,8},{9,1... | collective-permute-start | bytes 405512 | tf_op jit(solution)/shard_map/ppermute | solution.py:215
  33.4 4.4 %collective-permute-done.8.refs_1_ = bf16[16,4224]{1,0:T(8,128)(2,1)S(1)} collective-permute-done((bf16[16,4224]{1,0:T(8,128)(2,1)S(1)}, bf16[16,4224]{1,0:T(8,128)(2,1)S(1)}, u32[]{:S(2)}, u32[]{:S(2)}) %collective-permute-start.8) | collective-permute-done | bytes 135200 | tf_op jit(solution)/shard_map/ppermute | solution.py:215
  37.8 0.8 %query_rows.1 = bf16[16,4096]{1,0:T(8,128)(2,1)} custom-call(f32[16,4224]{1,0:T(8,128)S(1)} %get-tuple-element.31.refs_0_, bf16[16,4224]{1,0:T(8,128)(2,1)S(1)} %collective-permute-done.8.refs_1_), custom_call_target="tpu_custom_call" | custom-call | tf_op jit(solution)/shard_map/query_rows/pallas_call | solution.py:303
  (14 shorter events, 0.0 us)
Async XLA Ops:
  0.0 18.0 %copy-start.2 = (bf16[16,4096]{1,0:T(8,128)(2,1)S(1)}, bf16[16,4096]{1,0:T(8,128)(2,1)}, u32[]{:S(2)}) copy-start(bf16[16,4096]{1,0:T(8,128)(2,1)} %refs_6_.1) | copy-start | bytes 393220
  0.0 18.0 %copy-start.1 = (bf16[1,4096,64]{1,2,0:T(8,128)(2,1)S(1)}, bf16[1,4096,64]{1,2,0:T(8,128)(2,1)}, u32[]{:S(2)}) copy-start(bf16[1,4096,64]{1,2,0:T(8,128)(2,1)} %param.12) | copy-start | bytes 1572868
  0.0 18.0 %copy-start.3 = (bf16[4096]{0:T(1024)(128)(2,1)S(1)}, bf16[4096]{0:T(1024)(128)(2,1)}, u32[]{:S(2)}) copy-start(bf16[4096]{0:T(1024)(128)(2,1)} %refs_3_.1) | copy-start | bytes 24580
  0.0 18.0 %copy-start.5 = (s32[4]{0:T(128)S(1)}, s32[4]{0:T(128)}, u32[]{:S(2)}) copy-start(s32[4]{0:T(128)} %refs_0_.1) | copy-start | bytes 52
  0.0 18.0 %copy-start.6 = (s32[4]{0:T(128)S(1)}, s32[4]{0:T(128)}, u32[]{:S(2)}) copy-start(s32[4]{0:T(128)} %refs_1_.1) | copy-start | bytes 52
  0.0 18.0 %copy-start.4 = (s32[5]{0:T(128)S(1)}, s32[5]{0:T(128)}, u32[]{:S(2)}) copy-start(s32[5]{0:T(128)} %start_ref.1) | copy-start | bytes 64
  0.0 17.9 %collective-permute-start = (bf16[16,4096]{1,0:T(8,128)(2,1)}, bf16[16,4096]{1,0:T(8,128)(2,1)S(1)}, u32[]{:S(2)}, u32[]{:S(2)}) collective-permute-start(bf16[16,4096]{1,0:T(8,128)(2,1)} %refs_6_.1), channel_id=1, source_target_pairs={{0,4},{4,8},{8,12},{12,0},{1,5},{5,9},{9,13},{13,1},{2,6},{6,10},{... | collective-permute-start | bytes 393224 | tf_op jit(solution)/shard_map/ppermute | solution.py:215
  3.1 14.8 %collective-permute-start.1 = (bf16[16,4096]{1,0:T(8,128)(2,1)}, bf16[16,4096]{1,0:T(8,128)(2,1)S(1)}, u32[]{:S(2)}, u32[]{:S(2)}) collective-permute-start(bf16[16,4096]{1,0:T(8,128)(2,1)} %refs_6_.1), channel_id=1, source_target_pairs={{0,8},{4,12},{8,0},{12,4},{1,9},{5,13},{9,1},{13,5},{2,10},{6,14},... | collective-permute-start | bytes 393224 | tf_op jit(solution)/shard_map/ppermute | solution.py:215
  5.7 12.3 %collective-permute-start.2 = (bf16[16,4096]{1,0:T(8,128)(2,1)}, bf16[16,4096]{1,0:T(8,128)(2,1)S(1)}, u32[]{:S(2)}, u32[]{:S(2)}) collective-permute-start(bf16[16,4096]{1,0:T(8,128)(2,1)} %refs_6_.1), channel_id=1, source_target_pairs={{0,12},{4,0},{8,4},{12,8},{1,13},{5,1},{9,5},{13,9},{2,14},{6,2},{... | collective-permute-start | bytes 393224 | tf_op jit(solution)/shard_map/ppermute | solution.py:215
  19.1 8.5 %collective-permute-start.4 = (bf16[64,128]{1,0:T(8,128)(2,1)S(1)}, bf16[64,128]{1,0:T(8,128)(2,1)S(1)}, u32[]{:S(2)}, u32[]{:S(2)}) collective-permute-start(bf16[64,128]{1,0:T(8,128)(2,1)S(1)} %get-tuple-element.27.refs_0_), channel_id=1, source_target_pairs={{0,4},{4,8},{8,12},{12,0},{1,5},{5,9},{9,13},{13,1},{2,6},{6,10},{... | collective-permute-start | bytes 49160 | tf_op jit(solution)/shard_map/ppermute | solution.py:215
  19.8 7.8 %collective-permute-start.5 = (bf16[64,128]{1,0:T(8,128)(2,1)S(1)}, bf16[64,128]{1,0:T(8,128)(2,1)S(1)}, u32[]{:S(2)}, u32[]{:S(2)}) collective-permute-start(bf16[64,128]{1,0:T(8,128)(2,1)S(1)} %get-tuple-element.27.refs_0_), channel_id=1, source_target_pairs={{0,8},{4,12},{8,0},{12,4},{1,9},{5,13},{9,1},{13,5},{2,10},{6,14},... | collective-permute-start | bytes 49160 | tf_op jit(solution)/shard_map/ppermute | solution.py:215
  20.6 7.0 %collective-permute-start.6 = (bf16[64,128]{1,0:T(8,128)(2,1)S(1)}, bf16[64,128]{1,0:T(8,128)(2,1)S(1)}, u32[]{:S(2)}, u32[]{:S(2)}) collective-permute-start(bf16[64,128]{1,0:T(8,128)(2,1)S(1)} %get-tuple-element.27.refs_0_), channel_id=1, source_target_pairs={{0,12},{4,0},{8,4},{12,8},{1,13},{5,1},{9,5},{13,9},{2,14},{6,2},{... | collective-permute-start | bytes 49160 | tf_op jit(solution)/shard_map/ppermute | solution.py:215
  27.5 3.2 %copy-start = (bf16[4,64,4096]{2,1,0:T(8,128)(2,1)S(1)}, bf16[4,64,4096]{2,1,0:T(8,128)(2,1)}, u32[]{:S(2)}) copy-start(bf16[4,64,4096]{2,1,0:T(8,128)(2,1)} %up_ref.1) | copy-start | bytes 6291460
  27.5 3.2 %collective-permute-start.3 = (bf16[32,3072]{1,0:T(8,128)(2,1)S(1)}, bf16[32,3072]{1,0:T(8,128)(2,1)S(1)}, u32[]{:S(2)}, u32[]{:S(2)}) collective-permute-start(bf16[32,3072]{1,0:T(8,128)(2,1)S(1)} %get-tuple-element.25), channel_id=1, source_target_pairs={{0,1},{1,0},{2,3},{3,2},{4,5},{5,4},{6,7},{7,6},{8,9},{9,8},{10,11... | collective-permute-start | bytes 589832 | tf_op jit(solution)/shard_map/ppermute | solution.py:215
  29.3 1.5 %collective-permute-start.7 = (bf16[32,1280]{1,0:T(8,128)(2,1)S(1)}, bf16[32,1280]{1,0:T(8,128)(2,1)S(1)}, u32[]{:S(2)}, u32[]{:S(2)}) collective-permute-start(bf16[32,1280]{1,0:T(8,128)(2,1)S(1)} %get-tuple-element.30), channel_id=1, source_target_pairs={{0,1},{1,0},{2,3},{3,2},{4,5},{5,4},{6,7},{7,6},{8,9},{9,8},{10,11... | collective-permute-start | bytes 245768 | tf_op jit(solution)/shard_map/ppermute | solution.py:215
  31.8 5.9 %collective-permute-start.8 = (bf16[16,4224]{1,0:T(8,128)(2,1)S(1)}, bf16[16,4224]{1,0:T(8,128)(2,1)S(1)}, u32[]{:S(2)}, u32[]{:S(2)}) collective-permute-start(bf16[16,4224]{1,0:T(8,128)(2,1)S(1)} %get-tuple-element.32), channel_id=1, source_target_pairs={{0,2},{2,0},{1,3},{3,1},{4,6},{6,4},{5,7},{7,5},{8,10},{10,8},{9,1... | collective-permute-start | bytes 405512 | tf_op jit(solution)/shard_map/ppermute | solution.py:215

commit v8 on v7

--- a/solution.py
+++ b/solution.py
@@ -53,21 +53,34 @@
         copy.wait()
 
 
+def split_wide(value):
+    high = value.astype(jnp.bfloat16).astype(jnp.float32)
+    low = jnp.where(high < jnp.inf, value - high, 0.0)
+    lane = lax.broadcasted_iota(jnp.int32, value.shape, 1)
+    return jnp.where(lane < LANES // 2, high, low)
+
+
+def join_wide(value):
+    return value[:, :1] + value[:, LANES - 1 :]
+
+
 def rows_kernel(n, width, *refs):
     rank_ref, slot_ref, start_ref, gain_ref, down_ref, _ = refs[:6]
     blocks = refs[6 : 6 + n]
-    x_ref, square_ref, down_out = refs[6 + n :]
+    x_ref, small_ref = refs[6 + n :]
     home = lax.axis_index("gx")
     block_rows = blocks[0].shape[0]
     rows = n * block_rows
     gain = gain_ref[...].astype(jnp.float32).reshape(1, gain_ref.shape[0])
+    small_ref[...] = jnp.zeros(small_ref.shape, small_ref.dtype)
     for k in range(n):
-        source = lax.rem(home - k + n, n)
-        begin = pl.multiple_of(source * block_rows, block_rows)
+        begin = pl.multiple_of(jnp.bitwise_xor(home, k) * block_rows, block_rows)
         values = blocks[k][...].astype(jnp.float32)
-        squares = jnp.sum(values * values, axis=1, keepdims=True) / width
         x_ref[pl.ds(begin, block_rows), :] = (values * gain).astype(jnp.bfloat16)
-        square_ref[pl.ds(begin, block_rows), :] = jnp.broadcast_to(squares, (block_rows, LANES))
+        if k == 0:
+            squares = jnp.sum(values * values, axis=1, keepdims=True) / width
+            squares = split_wide(jnp.broadcast_to(squares, (block_rows, LANES)))
+            small_ref[pl.ds(begin, block_rows), LANES:] = squares.astype(jnp.bfloat16)
     slots, rank_columns = down_ref.shape[0], down_ref.shape[1]
     row = lax.broadcasted_iota(jnp.int32, (rows, rank_columns), 0)
     col = lax.broadcasted_iota(jnp.int32, (rows, rank_columns), 1)
@@ -81,19 +94,7 @@
         )
         scale = ADAPTER_ALPHA / jnp.full((rows, rank_columns), rank, jnp.int32).astype(jnp.float32)
         total = total + jnp.where(live, projected * scale, 0.0)
-    down_out[...] = jnp.zeros(down_out.shape, down_out.dtype)
-    down_out[:, :rank_columns] = total.astype(down_out.dtype)
-
-
-def split_wide(value):
-    high = value.astype(jnp.bfloat16).astype(jnp.float32)
-    low = jnp.where(high < jnp.inf, value - high, 0.0)
-    lane = lax.broadcasted_iota(jnp.int32, value.shape, 1)
-    return jnp.where(lane < LANES // 2, high, low)
-
-
-def join_wide(value):
-    return value[:, :1] + value[:, LANES - 1 :]
+    small_ref[:, :rank_columns] = total.astype(small_ref.dtype)
 
 
 def write_rows(acc, outs, n_y, n_z):
@@ -101,7 +102,7 @@
     rows_here = outs[0].shape[0] // n_y
     for k in range(n_z):
         for y in range(n_y):
-            owner = y * n_z + lax.rem(z + k, n_z)
+            owner = y * n_z + jnp.bitwise_xor(z, k)
             begin = pl.multiple_of(owner * rows_here, rows_here)
             outs[k][y * rows_here : (y + 1) * rows_here, :] = acc[
                 pl.ds(begin, rows_here), :
@@ -119,31 +120,19 @@
         )
 
 
-def first_kernel(n_w, n_y, n_z, step, x_ref, *refs):
+def product_kernel(n_w, n_y, n_z, step, _, x_ref, *refs):
     weights, outs, acc = refs[:n_w], refs[n_w:-1], refs[-1]
     multiply(x_ref, weights, step, acc)
     write_rows(acc, outs, n_y, n_z)
 
 
-def last_kernel(n_w, n_x, n_y, n_z, step, x_ref, square_ref, *refs):
-    downs, refs = refs[:n_x], refs[n_x:]
-    weights, outs, acc = refs[:n_w], refs[n_w:-1], refs[-1]
-    multiply(x_ref, weights, step, acc)
-    columns = weights[0].shape[1] * n_w
-    down = downs[0][...].astype(jnp.float32)
-    for other in downs[1:]:
-        down = down + other[...].astype(jnp.float32)
-    acc[:, columns : columns + LANES] = down
-    acc[:, columns + LANES :] = split_wide(square_ref[...])
-    write_rows(acc, outs, n_y, n_z)
-
-
 def pair_kernel(n_y, n_z, step, start_ref, up_ref, *refs):
+    smalls, refs = refs[:n_z], refs[n_z:]
     firsts, lasts = refs[:n_z], refs[n_z : 2 * n_z]
     outs, acc = refs[2 * n_z : -1], refs[-1]
     rows, done = firsts[0].shape
     rows_here = rows // n_y
-    columns = done + lasts[0].shape[1] - 2 * LANES
+    columns = done + lasts[0].shape[1]
     adapters, rank_columns, _ = up_ref.shape
     z = lax.axis_index("gz")
 
@@ -153,11 +142,15 @@
             total = total + part[:, here].astype(jnp.float32)
         return total
 
-    late = columns - done
-    square = join_wide(lasts[0][:, late + LANES :])
-    for part in lasts[1:]:
-        square = square + join_wide(part[:, late + LANES :].astype(jnp.float32))
-    down = added(lasts, slice(late, late + rank_columns)).astype(jnp.bfloat16)
+    small = jnp.zeros((rows, 2 * LANES), jnp.float32)
+    for part in smalls:
+        blocks = []
+        for y in range(n_y):
+            begin = pl.multiple_of((y * n_z + z) * rows_here, rows_here)
+            blocks.append(part[pl.ds(begin, rows_here), :].astype(jnp.float32))
+        small = small + jnp.concatenate(blocks, axis=0)
+    square = join_wide(small[:, LANES:])
+    down = small[:, :rank_columns].astype(jnp.bfloat16)
     row = lax.broadcasted_iota(jnp.int32, (rows, rank_columns), 0)
     row = (row // rows_here * n_z + z) * rows_here + lax.rem(row, rows_here)
     spread = jnp.concatenate(
@@ -177,7 +170,7 @@
     acc[:, columns:] = split_wide(jnp.broadcast_to(square, (rows, LANES)))
     y = lax.axis_index("gy")
     for k in range(n_y):
-        begin = pl.multiple_of(lax.rem(y + k, n_y) * rows_here, rows_here)
+        begin = pl.multiple_of(jnp.bitwise_xor(y, k) * rows_here, rows_here)
         outs[k][...] = acc[pl.ds(begin, rows_here), :].astype(outs[k].dtype)
 
 
@@ -212,7 +205,7 @@
     rows_here = rows // groups
 
     def send(value, axis, n, k):
-        return lax.ppermute(value, axis, [(j, (j + k) % n) for j in range(n)])
+        return lax.ppermute(value, axis, [(j, j ^ k) for j in range(n)])
 
     def spread_out(made, axis, n):
         return [made[0]] + [send(made[k], axis, n, k) for k in range(1, n)]
@@ -234,15 +227,14 @@
         name="fetch_weight",
     )(query_weight)
 
-    x, square, down = pl.pallas_call(
+    x, small = pl.pallas_call(
         functools.partial(rows_kernel, n_x, depth * groups),
         out_shape=(
             jax.ShapeDtypeStruct((rows, depth), bf16),
-            jax.ShapeDtypeStruct((rows, LANES), f32),
-            jax.ShapeDtypeStruct((rows, LANES), bf16),
+            jax.ShapeDtypeStruct((rows, 2 * LANES), bf16),
         ),
         in_specs=[SMEM] * 3 + [VMEM] * 2 + [ANY] + [VMEM] * n_x,
-        out_specs=(VMEM,) * 3,
+        out_specs=(VMEM,) * 2,
         compiler_params=params(4 + (rows * depth >> 16)),
         name="scaled_rows",
     )(
@@ -255,49 +247,46 @@
         *blocks,
     )
 
-    downs = [down] + [send(down, "gx", n_x, k) for k in range(1, n_x)]
+    half = small + send(small, "gx", n_x, 1)
+    hop = 2
+    small = half
+    while hop < n_x:
+        small = small + send(small, "gx", n_x, hop)
+        hop *= 2
+    smalls = [small] + [send(small, "gz", n_z, k) for k in range(1, n_z)]
 
     weights = [pltpu.with_memory_space_constraint(w, pltpu.VMEM) for w in weights]
-    early, late = n_w - 1, 1
-    early_columns, late_columns = (n * (columns // n_w) for n in (early, late))
     kept = n_y * rows_here
 
     def shapes(n, shape):
         return [jax.ShapeDtypeStruct(shape, f32 if k == 0 else bf16) for k in range(n)]
 
-    made = pl.pallas_call(
-        functools.partial(first_kernel, early, n_y, n_z, step),
-        out_shape=shapes(n_z, (kept, early_columns)),
-        in_specs=[VMEM] * (1 + early),
-        out_specs=[VMEM] * n_z,
-        scratch_shapes=[pltpu.VMEM((rows, early_columns), f32)],
-        cost_estimate=cost(2 * rows * depth * early_columns, 2 * depth * early_columns),
-        compiler_params=params(4 + (rows * depth >> 16)),
-        name="first_columns",
-    )(x, *weights[:early])
-    firsts = spread_out(made, "gz", n_z)
-
-    made = pl.pallas_call(
-        functools.partial(last_kernel, late, n_x, n_y, n_z, step),
-        out_shape=shapes(n_z, (kept, late_columns + 2 * LANES)),
-        in_specs=[VMEM] * (2 + n_x + late),
-        out_specs=[VMEM] * n_z,
-        scratch_shapes=[pltpu.VMEM((rows, late_columns + 2 * LANES), f32)],
-        cost_estimate=cost(2 * rows * depth * columns, 4 * depth * columns),
-        compiler_params=params(4 + (rows * depth >> 16)),
-        name="last_columns",
-    )(x, square, *downs, *weights[early:])
-    lasts = spread_out(made, "gz", n_z)
+    def product(some, after, weight_of_time):
+        wide = len(some) * (columns // n_w)
+        made = pl.pallas_call(
+            functools.partial(product_kernel, len(some), n_y, n_z, step),
+            out_shape=shapes(n_z, (kept, wide)),
+            in_specs=[ANY] + [VMEM] * (1 + len(some)),
+            out_specs=[VMEM] * n_z,
+            scratch_shapes=[pltpu.VMEM((rows, wide), f32)],
+            cost_estimate=cost(2 * rows * depth * wide * weight_of_time, 2 * depth * wide),
+            compiler_params=params(4 + (rows * depth >> 16)),
+            name="product",
+        )(after, x, *some)
+        return spread_out(made, "gz", n_z)
+
+    firsts = product(weights[:-1], token, 1)
+    lasts = product(weights[-1:], half, 8)
 
     made = pl.pallas_call(
         functools.partial(pair_kernel, n_y, n_z, step),
         out_shape=shapes(n_y, (rows_here, columns + LANES)),
-        in_specs=[SMEM] + [VMEM] * (1 + 2 * n_z),
+        in_specs=[SMEM] + [VMEM] * (1 + 3 * n_z),
         out_specs=[VMEM] * n_y,
         scratch_shapes=[pltpu.VMEM((kept, columns + LANES), f32)],
         compiler_params=params(4 + (rows * depth >> 16)),
         name="chip_sums",
-    )(segment_starts, adapter_up_factors, *firsts, *lasts)
+    )(segment_starts, adapter_up_factors, *smalls, *firsts, *lasts)
     parts = spread_out(made, "gy", n_y)
 
     return pl.pallas_call(

time: 38.7 us -> 38.4 us (level)
  starting transfers between devices: 13.1 us -> 12.4 us
  waiting for transfers between devices: 5.3 us -> 5.72 us
    ppermute x9, starting transfers between devices: 13.1 us -> 12.4 us  [send(): return lax.ppermute(value, axis, [(j, j ^ k) for j in range(n)])]
    ppermute x9, waiting for transfers between devices: 5.3 us -> 5.72 us  [send(): return lax.ppermute(value, axis, [(j, j ^ k) for j in range(n)])]
  transfers between devices with their start and end apart: 9 -> 9, of which waited for: 2 -> 3; matrix products, arithmetic and copies ran while one was open for 0% -> 0% of each run, Pallas kernels for 44% -> 45%
where the time goes in v8:
time: 38.4 us; the launch traced here: 38.3 us
  Pallas kernels  19.9 us (52%)
  starting transfers between devices  12.4 us (32%)
  waiting for transfers between devices  5.72 us (15%)
    ppermute x9, starting transfers between devices, send(): return lax.ppermute(value, axis, [(j, j ^ k) for j in range(n)])  12.4 us
    pallas_call x1, Pallas kernels, body(): pl.pallas_call(functools.partial(fetch_kernel, n_w), out_shape=[jax.Shape...  10.9 us
    pallas_call x2, Pallas kernels, product(): pl.pallas_call(functools.partial(product_kernel, len(some), n_y, n_z, ste...  6.15 us
    ppermute x9, waiting for transfers between devices, send(): return lax.ppermute(value, axis, [(j, j ^ k) for j in range(n)])  5.72 us
    pallas_call x1, Pallas kernels, body(): pl.pallas_call(functools.partial(pair_kernel, n_y, n_z, step), out_shape=...  1.09 us
    pallas_call x1, Pallas kernels, body(): pl.pallas_call(functools.partial(rows_kernel, n_x, depth * groups), out_s...  0.97 us
    pallas_call x1, Pallas kernels, body(): pl.pallas_call(final_kernel, out_shape=jax.ShapeDtypeStruct((rows_here, c...  0.83 us
  transfers between devices with their start and end apart: 9, of which 3 were waited for; matrix products, arithmetic and copies ran while one was open for 0% of the time, Pallas kernels for 45%

profile of v8, /device:TPU:0, one launch (start us, length us, event | category | flops | bytes accessed | tf_op | source)
XLA Modules:
  0.0 38.3 jit_solution(52905662835409038)
XLA Ops:
  0.0 3.1 %collective-permute-start = (bf16[16,4096]{1,0:T(8,128)(2,1)}, bf16[16,4096]{1,0:T(8,128)(2,1)S(1)}, u32[]{:S(2)}, u32[]{:S(2)}) collective-permute-start(bf16[16,4096]{1,0:T(8,128)(2,1)} %refs_6_.1), channel_id=1, source_target_pairs={{0,4},{4,0},{8,12},{12,8},{1,5},{5,1},{9,13},{13,9},{2,6},{6,2},{1... | collective-permute-start | bytes 393224 | tf_op jit(solution)/shard_map/ppermute | solution.py:208
  3.1 2.6 %collective-permute-start.1 = (bf16[16,4096]{1,0:T(8,128)(2,1)}, bf16[16,4096]{1,0:T(8,128)(2,1)S(1)}, u32[]{:S(2)}, u32[]{:S(2)}) collective-permute-start(bf16[16,4096]{1,0:T(8,128)(2,1)} %refs_6_.1), channel_id=1, source_target_pairs={{0,8},{4,12},{8,0},{12,4},{1,9},{5,13},{9,1},{13,5},{2,10},{6,14},... | collective-permute-start | bytes 393224 | tf_op jit(solution)/shard_map/ppermute | solution.py:208
  5.7 0.0 collective-permute-start.2
  5.7 10.9 %fetch_weight.1 = (f32[8,128]{1,0:T(8,128)S(1)}, bf16[4096,1024]{1,0:T(8,128)(2,1)S(1)}, bf16[4096,1024]{1,0:T(8,128)(2,1)S(1)}, bf16[4096,1024]{1,0:T(8,128)(2,1)S(1)}, bf16[4096,1024]{1,0:T(8,128)(2,1)S(1)}) custom-call(bf16[4096,4096]{1,0:T(8,128)(2,1)} %w_hbm.1), custom_call_target="tpu_custom_call" | custom-call | bytes 33554432 | tf_op jit(solution)/shard_map/fetch_weight/pallas_call | solution.py:218
  16.6 0.0 collective-permute-done.1.refs_8_
  16.6 0.0 collective-permute-done.2.refs_9_
  16.7 1.0 %scaled_rows.1 = (bf16[64,4096]{1,0:T(8,128)(2,1)S(1)}, bf16[64,256]{1,0:T(8,128)(2,1)S(1)}) custom-call(s32[4]{0:T(128)S(1)} %copy-done.5, s32[4]{0:T(128)S(1)} %copy-done.6, s32[5]{0:T(128)S(1)} %copy-done.4, bf16[4096]{0:T(1024)(128)(2,1)S(1)} %copy-done.3, bf16[1,64,4096]{2,1,0:T(8,128)(2,1)S(1)} %bitcast.1, f32[8,128]{1,0:T(8,128)S(1)} %get-tuple-element.18.refs_5_._, ...), custom_call_target="tpu_custom_call" | custom-call | tf_op jit(solution)/shard_map/scaled_rows/pallas_call | solution.py:230
  17.7 1.6 %collective-permute-start.3 = (bf16[64,256]{1,0:T(8,128)(2,1)S(1)}, bf16[64,256]{1,0:T(8,128)(2,1)S(1)}, u32[]{:S(2)}, u32[]{:S(2)}) collective-permute-start(bf16[64,256]{1,0:T(8,128)(2,1)S(1)} %get-tuple-element.19), channel_id=1, source_target_pairs={{0,4},{4,0},{8,12},{12,8},{1,5},{5,1},{9,13},{13,9},{2,6},{6,2},{1... | collective-permute-start | bytes 98312 | tf_op jit(solution)/shard_map/ppermute | solution.py:208
  19.3 4.6 %product.2 = (f32[32,3072]{1,0:T(8,128)S(1)}, bf16[32,3072]{1,0:T(8,128)(2,1)S(1)}) custom-call(f32[8,128]{1,0:T(8,128)S(1)} %get-tuple-element.18.refs_5_._, bf16[64,4096]{1,0:T(8,128)(2,1)S(1)} %get-tuple-element.20.x_ref, bf16[4096,1024]{1,0:T(8,128)(2,1)S(1)} %get-tuple-element.21.refs_0_, bf16[4096,1024]{1,0:T(8,128)(2,1)S(1)} %get-tuple-element.22.refs_1_, ...), custom_call_target="tpu_custom_call" | custom-call | flops 1610612736 | bytes 25165824 | tf_op jit(solution)/shard_map/product/pallas_call | solution.py:266
  23.9 0.0 copy-start
  23.9 0.1 collective-permute-start.6
  24.0 0.0 collective-permute-done.3
  24.0 2.9 %collective-permute-start.4 = (bf16[64,256]{1,0:T(8,128)(2,1)S(1)}, bf16[64,256]{1,0:T(8,128)(2,1)S(1)}, u32[]{:S(2)}, u32[]{:S(2)}) collective-permute-start(bf16[64,256]{1,0:T(8,128)(2,1)S(1)} %add.6._), channel_id=1, source_target_pairs={{0,8},{4,12},{8,0},{12,4},{1,9},{5,13},{9,1},{13,5},{2,10},{6,14},... | collective-permute-start | bytes 98312 | tf_op jit(solution)/shard_map/ppermute | solution.py:208
  26.9 1.6 %product.3 = (f32[32,1024]{1,0:T(8,128)S(1)}, bf16[32,1024]{1,0:T(8,128)(2,1)S(1)}) custom-call(bf16[64,256]{1,0:T(8,128)(2,1)S(1)} %add.6._, bf16[64,4096]{1,0:T(8,128)(2,1)S(1)} %get-tuple-element.20.x_ref, bf16[4096,1024]{1,0:T(8,128)(2,1)S(1)} %get-tuple-element.26.refs_0_), custom_call_target="tpu_custom_call" | custom-call | flops 4294967296 | bytes 8388608 | tf_op jit(solution)/shard_map/product/pallas_call | solution.py:266
  28.5 0.3 collective-permute-start.7
  28.8 0.6 %collective-permute-done.4 = bf16[64,256]{1,0:T(8,128)(2,1)S(1)} collective-permute-done((bf16[64,256]{1,0:T(8,128)(2,1)S(1)}, bf16[64,256]{1,0:T(8,128)(2,1)S(1)}, u32[]{:S(2)}, u32[]{:S(2)}) %collective-permute-start.4) | collective-permute-done | bytes 32800 | tf_op jit(solution)/shard_map/ppermute | solution.py:208
  29.4 0.1 collective-permute-start.5
  29.4 1.2 %collective-permute-done.5.refs_1_ = bf16[64,256]{1,0:T(8,128)(2,1)S(1)} collective-permute-done((bf16[64,256]{1,0:T(8,128)(2,1)S(1)}, bf16[64,256]{1,0:T(8,128)(2,1)S(1)}, u32[]{:S(2)}, u32[]{:S(2)}) %collective-permute-start.5) | collective-permute-done | bytes 32800 | tf_op jit(solution)/shard_map/ppermute | solution.py:208
  30.6 0.0 collective-permute-done.7.refs_5_
  30.6 0.0 collective-permute-done.6.refs_3_
  30.7 1.1 %chip_sums.1 = (f32[16,4224]{1,0:T(8,128)S(1)}, bf16[16,4224]{1,0:T(8,128)(2,1)S(1)}) custom-call(s32[5]{0:T(128)S(1)} %copy-done.4, bf16[4,64,4096]{2,1,0:T(8,128)(2,1)S(1)} %copy-done, bf16[64,256]{1,0:T(8,128)(2,1)S(1)} %add.7.refs_0_, bf16[64,256]{1,0:T(8,128)(2,1)S(1)} %collective-permute-done.5.refs_1_, f32[32,3072]{1,0:T(8,128)S(1)} %get-tuple-element.24.refs_2_, ...), custom_call_target="tpu_custom_call" | custom-call | tf_op jit(solution)/shard_map/chip_sums/pallas_call | solution.py:281
  31.7 1.8 %collective-permute-start.8 = (bf16[16,4224]{1,0:T(8,128)(2,1)S(1)}, bf16[16,4224]{1,0:T(8,128)(2,1)S(1)}, u32[]{:S(2)}, u32[]{:S(2)}) collective-permute-start(bf16[16,4224]{1,0:T(8,128)(2,1)S(1)} %get-tuple-element.30), channel_id=1, source_target_pairs={{0,2},{2,0},{1,3},{3,1},{4,6},{6,4},{5,7},{7,5},{8,10},{10,8},{9,1... | collective-permute-start | bytes 405512 | tf_op jit(solution)/shard_map/ppermute | solution.py:208
  33.5 3.9 %collective-permute-done.8.refs_1_ = bf16[16,4224]{1,0:T(8,128)(2,1)S(1)} collective-permute-done((bf16[16,4224]{1,0:T(8,128)(2,1)S(1)}, bf16[16,4224]{1,0:T(8,128)(2,1)S(1)}, u32[]{:S(2)}, u32[]{:S(2)}) %collective-permute-start.8) | collective-permute-done | bytes 135200 | tf_op jit(solution)/shard_map/ppermute | solution.py:208
  37.5 0.8 %query_rows.1 = bf16[16,4096]{1,0:T(8,128)(2,1)} custom-call(f32[16,4224]{1,0:T(8,128)S(1)} %get-tuple-element.29.refs_0_, bf16[16,4224]{1,0:T(8,128)(2,1)S(1)} %collective-permute-done.8.refs_1_), custom_call_target="tpu_custom_call" | custom-call | tf_op jit(solution)/shard_map/query_rows/pallas_call | solution.py:292
  (16 shorter events, 0.1 us)
Async XLA Ops:
  0.0 16.7 %copy-start.2 = (bf16[16,4096]{1,0:T(8,128)(2,1)S(1)}, bf16[16,4096]{1,0:T(8,128)(2,1)}, u32[]{:S(2)}) copy-start(bf16[16,4096]{1,0:T(8,128)(2,1)} %refs_6_.1) | copy-start | bytes 393220
  0.0 16.7 %copy-start.1 = (bf16[1,4096,64]{1,2,0:T(8,128)(2,1)S(1)}, bf16[1,4096,64]{1,2,0:T(8,128)(2,1)}, u32[]{:S(2)}) copy-start(bf16[1,4096,64]{1,2,0:T(8,128)(2,1)} %param.12) | copy-start | bytes 1572868
  0.0 16.7 %copy-start.3 = (bf16[4096]{0:T(1024)(128)(2,1)S(1)}, bf16[4096]{0:T(1024)(128)(2,1)}, u32[]{:S(2)}) copy-start(bf16[4096]{0:T(1024)(128)(2,1)} %refs_3_.1) | copy-start | bytes 24580
  0.0 16.7 %copy-start.5 = (s32[4]{0:T(128)S(1)}, s32[4]{0:T(128)}, u32[]{:S(2)}) copy-start(s32[4]{0:T(128)} %refs_0_.1) | copy-start | bytes 52
  0.0 16.7 %copy-start.6 = (s32[4]{0:T(128)S(1)}, s32[4]{0:T(128)}, u32[]{:S(2)}) copy-start(s32[4]{0:T(128)} %refs_1_.1) | copy-start | bytes 52
  0.0 16.7 %copy-start.4 = (s32[5]{0:T(128)S(1)}, s32[5]{0:T(128)}, u32[]{:S(2)}) copy-start(s32[5]{0:T(128)} %start_ref.1) | copy-start | bytes 64
  0.0 16.6 %collective-permute-start = (bf16[16,4096]{1,0:T(8,128)(2,1)}, bf16[16,4096]{1,0:T(8,128)(2,1)S(1)}, u32[]{:S(2)}, u32[]{:S(2)}) collective-permute-start(bf16[16,4096]{1,0:T(8,128)(2,1)} %refs_6_.1), channel_id=1, source_target_pairs={{0,4},{4,0},{8,12},{12,8},{1,5},{5,1},{9,13},{13,9},{2,6},{6,2},{1... | collective-permute-start | bytes 393224 | tf_op jit(solution)/shard_map/ppermute | solution.py:208
  3.1 13.5 %collective-permute-start.1 = (bf16[16,4096]{1,0:T(8,128)(2,1)}, bf16[16,4096]{1,0:T(8,128)(2,1)S(1)}, u32[]{:S(2)}, u32[]{:S(2)}) collective-permute-start(bf16[16,4096]{1,0:T(8,128)(2,1)} %refs_6_.1), channel_id=1, source_target_pairs={{0,8},{4,12},{8,0},{12,4},{1,9},{5,13},{9,1},{13,5},{2,10},{6,14},... | collective-permute-start | bytes 393224 | tf_op jit(solution)/shard_map/ppermute | solution.py:208
  5.7 10.9 %collective-permute-start.2 = (bf16[16,4096]{1,0:T(8,128)(2,1)}, bf16[16,4096]{1,0:T(8,128)(2,1)S(1)}, u32[]{:S(2)}, u32[]{:S(2)}) collective-permute-start(bf16[16,4096]{1,0:T(8,128)(2,1)} %refs_6_.1), channel_id=1, source_target_pairs={{0,12},{4,8},{8,4},{12,0},{1,13},{5,9},{9,5},{13,1},{2,14},{6,10},... | collective-permute-start | bytes 393224 | tf_op jit(solution)/shard_map/ppermute | solution.py:208
  17.7 6.3 %collective-permute-start.3 = (bf16[64,256]{1,0:T(8,128)(2,1)S(1)}, bf16[64,256]{1,0:T(8,128)(2,1)S(1)}, u32[]{:S(2)}, u32[]{:S(2)}) collective-permute-start(bf16[64,256]{1,0:T(8,128)(2,1)S(1)} %get-tuple-element.19), channel_id=1, source_target_pairs={{0,4},{4,0},{8,12},{12,8},{1,5},{5,1},{9,13},{13,9},{2,6},{6,2},{1... | collective-permute-start | bytes 98312 | tf_op jit(solution)/shard_map/ppermute | solution.py:208
  23.9 6.7 %copy-start = (bf16[4,64,4096]{2,1,0:T(8,128)(2,1)S(1)}, bf16[4,64,4096]{2,1,0:T(8,128)(2,1)}, u32[]{:S(2)}) copy-start(bf16[4,64,4096]{2,1,0:T(8,128)(2,1)} %up_ref.1) | copy-start | bytes 6291460
  23.9 6.7 %collective-permute-start.6 = (bf16[32,3072]{1,0:T(8,128)(2,1)S(1)}, bf16[32,3072]{1,0:T(8,128)(2,1)S(1)}, u32[]{:S(2)}, u32[]{:S(2)}) collective-permute-start(bf16[32,3072]{1,0:T(8,128)(2,1)S(1)} %get-tuple-element.25), channel_id=1, source_target_pairs={{0,1},{1,0},{2,3},{3,2},{4,5},{5,4},{6,7},{7,6},{8,9},{9,8},{10,11... | collective-permute-start | bytes 589832 | tf_op jit(solution)/shard_map/ppermute | solution.py:208
  24.0 5.3 %collective-permute-start.4 = (bf16[64,256]{1,0:T(8,128)(2,1)S(1)}, bf16[64,256]{1,0:T(8,128)(2,1)S(1)}, u32[]{:S(2)}, u32[]{:S(2)}) collective-permute-start(bf16[64,256]{1,0:T(8,128)(2,1)S(1)} %add.6._), channel_id=1, source_target_pairs={{0,8},{4,12},{8,0},{12,4},{1,9},{5,13},{9,1},{13,5},{2,10},{6,14},... | collective-permute-start | bytes 98312 | tf_op jit(solution)/shard_map/ppermute | solution.py:208
  28.5 2.1 %collective-permute-start.7 = (bf16[32,1024]{1,0:T(8,128)(2,1)S(1)}, bf16[32,1024]{1,0:T(8,128)(2,1)S(1)}, u32[]{:S(2)}, u32[]{:S(2)}) collective-permute-start(bf16[32,1024]{1,0:T(8,128)(2,1)S(1)} %get-tuple-element.28), channel_id=1, source_target_pairs={{0,1},{1,0},{2,3},{3,2},{4,5},{5,4},{6,7},{7,6},{8,9},{9,8},{10,11... | collective-permute-start | bytes 196616 | tf_op jit(solution)/shard_map/ppermute | solution.py:208
  29.4 1.3 %collective-permute-start.5 = (bf16[64,256]{1,0:T(8,128)(2,1)S(1)}, bf16[64,256]{1,0:T(8,128)(2,1)S(1)}, u32[]{:S(2)}, u32[]{:S(2)}) collective-permute-start(bf16[64,256]{1,0:T(8,128)(2,1)S(1)} %add.7.refs_0_), channel_id=1, source_target_pairs={{0,1},{1,0},{2,3},{3,2},{4,5},{5,4},{6,7},{7,6},{8,9},{9,8},{10,11... | collective-permute-start | bytes 98312 | tf_op jit(solution)/shard_map/ppermute | solution.py:208
  31.7 5.7 %collective-permute-start.8 = (bf16[16,4224]{1,0:T(8,128)(2,1)S(1)}, bf16[16,4224]{1,0:T(8,128)(2,1)S(1)}, u32[]{:S(2)}, u32[]{:S(2)}) collective-permute-start(bf16[16,4224]{1,0:T(8,128)(2,1)S(1)} %get-tuple-element.30), channel_id=1, source_target_pairs={{0,2},{2,0},{1,3},{3,1},{4,6},{6,4},{5,7},{7,5},{8,10},{10,8},{9,1... | collective-permute-start | bytes 405512 | tf_op jit(solution)/shard_map/ppermute | solution.py:208

commit v9 on v8

--- a/solution.py
+++ b/solution.py
@@ -109,30 +109,37 @@
             ].astype(outs[k].dtype)
 
 
-def multiply(x_ref, weights, step, acc):
+def multiply(x_ref, weights, step, out, first):
     width = weights[0].shape[1]
     for c in range(0, width * len(weights), step):
         inner = c % width
-        acc[:, c : c + step] = jnp.dot(
+        out[:, first + c : first + c + step] = jnp.dot(
             x_ref[...],
             weights[c // width][:, inner : inner + step],
             preferred_element_type=jnp.float32,
         )
 
 
-def product_kernel(n_w, n_y, n_z, step, _, x_ref, *refs):
+def base_kernel(n_w, step, _, x_ref, *refs):
+    multiply(x_ref, refs[:n_w], step, refs[n_w], 0)
+
+
+def product_kernel(n_w, n_y, n_z, step, first, x_ref, side_ref, *refs):
     weights, outs, acc = refs[:n_w], refs[n_w:-1], refs[-1]
-    multiply(x_ref, weights, step, acc)
+    wide = weights[0].shape[1] * n_w
+    multiply(x_ref, weights, step, acc, first)
+    begin = 0 if first else wide
+    acc[:, begin : begin + side_ref.shape[1]] = side_ref[...].astype(jnp.float32)
     write_rows(acc, outs, n_y, n_z)
 
 
 def pair_kernel(n_y, n_z, step, start_ref, up_ref, *refs):
-    smalls, refs = refs[:n_z], refs[n_z:]
     firsts, lasts = refs[:n_z], refs[n_z : 2 * n_z]
     outs, acc = refs[2 * n_z : -1], refs[-1]
     rows, done = firsts[0].shape
     rows_here = rows // n_y
-    columns = done + lasts[0].shape[1]
+    late = lasts[0].shape[1] - 2 * LANES
+    columns = done + late
     adapters, rank_columns, _ = up_ref.shape
     z = lax.axis_index("gz")
 
@@ -142,15 +149,10 @@
             total = total + part[:, here].astype(jnp.float32)
         return total
 
-    small = jnp.zeros((rows, 2 * LANES), jnp.float32)
-    for part in smalls:
-        blocks = []
-        for y in range(n_y):
-            begin = pl.multiple_of((y * n_z + z) * rows_here, rows_here)
-            blocks.append(part[pl.ds(begin, rows_here), :].astype(jnp.float32))
-        small = small + jnp.concatenate(blocks, axis=0)
-    square = join_wide(small[:, LANES:])
-    down = small[:, :rank_columns].astype(jnp.bfloat16)
+    square = join_wide(lasts[0][:, late + LANES :])
+    for part in lasts[1:]:
+        square = square + join_wide(part[:, late + LANES :].astype(jnp.float32))
+    down = added(lasts, slice(late, late + rank_columns)).astype(jnp.bfloat16)
     row = lax.broadcasted_iota(jnp.int32, (rows, rank_columns), 0)
     row = (row // rows_here * n_z + z) * rows_here + lax.rem(row, rows_here)
     spread = jnp.concatenate(
@@ -213,7 +215,7 @@
     blocks = [hidden] + [send(hidden, "gx", n_x, k) for k in range(1, n_x)]
 
     step = min(512, columns // 4)
-    n_w, pieces = 4, 4
+    n_w, pieces = 4, 8
     f32, bf16 = jnp.float32, jnp.bfloat16
     token, *weights = pl.pallas_call(
         functools.partial(fetch_kernel, n_w),
@@ -247,13 +249,10 @@
         *blocks,
     )
 
-    half = small + send(small, "gx", n_x, 1)
-    hop = 2
-    small = half
+    hop = 1
     while hop < n_x:
         small = small + send(small, "gx", n_x, hop)
         hop *= 2
-    smalls = [small] + [send(small, "gz", n_z, k) for k in range(1, n_z)]
 
     weights = [pltpu.with_memory_space_constraint(w, pltpu.VMEM) for w in weights]
     kept = n_y * rows_here
@@ -261,32 +260,43 @@
     def shapes(n, shape):
         return [jax.ShapeDtypeStruct(shape, f32 if k == 0 else bf16) for k in range(n)]
 
-    def product(some, after, weight_of_time):
-        wide = len(some) * (columns // n_w)
+    quarter = columns // n_w
+    base = pl.pallas_call(
+        functools.partial(base_kernel, 1, step),
+        out_shape=jax.ShapeDtypeStruct((rows, quarter), f32),
+        in_specs=[ANY] + [VMEM] * 2,
+        out_specs=VMEM,
+        cost_estimate=cost(2 * rows * depth * quarter, 2 * depth * quarter),
+        compiler_params=params(4 + (rows * depth >> 16)),
+        name="first_columns",
+    )(token, x, weights[0])
+
+    def product(some, first, side, times, name):
+        wide = first + len(some) * quarter + (0 if first else side.shape[1])
         made = pl.pallas_call(
-            functools.partial(product_kernel, len(some), n_y, n_z, step),
+            functools.partial(product_kernel, len(some), n_y, n_z, step, first),
             out_shape=shapes(n_z, (kept, wide)),
-            in_specs=[ANY] + [VMEM] * (1 + len(some)),
+            in_specs=[VMEM] * (2 + len(some)),
             out_specs=[VMEM] * n_z,
             scratch_shapes=[pltpu.VMEM((rows, wide), f32)],
-            cost_estimate=cost(2 * rows * depth * wide * weight_of_time, 2 * depth * wide),
+            cost_estimate=cost(2 * rows * depth * wide * times, 2 * depth * wide),
             compiler_params=params(4 + (rows * depth >> 16)),
-            name="product",
-        )(after, x, *some)
+            name=name,
+        )(x, side, *some)
         return spread_out(made, "gz", n_z)
 
-    firsts = product(weights[:-1], token, 1)
-    lasts = product(weights[-1:], half, 8)
+    firsts = product(weights[1:-1], quarter, base, 4, "middle_columns")
+    lasts = product(weights[-1:], 0, small, 8, "last_columns")
 
     made = pl.pallas_call(
         functools.partial(pair_kernel, n_y, n_z, step),
         out_shape=shapes(n_y, (rows_here, columns + LANES)),
-        in_specs=[SMEM] + [VMEM] * (1 + 3 * n_z),
+        in_specs=[SMEM] + [VMEM] * (1 + 2 * n_z),
         out_specs=[VMEM] * n_y,
         scratch_shapes=[pltpu.VMEM((kept, columns + LANES), f32)],
         compiler_params=params(4 + (rows * depth >> 16)),
         name="chip_sums",
-    )(segment_starts, adapter_up_factors, *smalls, *firsts, *lasts)
+    )(segment_starts, adapter_up_factors, *firsts, *lasts)
     parts = spread_out(made, "gy", n_y)
 
     return pl.pallas_call(

time: 38.4 us -> 38.5 us (level)
  starting transfers between devices: 12.4 us -> 11.3 us
  waiting for transfers between devices: 5.72 us -> 6.71 us
    pallas_call x0 -> x1, Pallas kernels: none -> 1.58 us  [body(): pl.pallas_call(functools.partial(base_kernel, 1, step), out_shape=jax.Sha...]
    pallas_call x2, Pallas kernels: 6.15 us -> 4.71 us  [product(): pl.pallas_call(functools.partial(product_kernel, len(some), n_y, n_z, ste...]
    ppermute x9 -> x8, starting transfers between devices: 12.4 us -> 11.3 us  [send(): return lax.ppermute(value, axis, [(j, j ^ k) for j in range(n)])]
    ppermute x9 -> x8, waiting for transfers between devices: 5.72 us -> 6.71 us  [send(): return lax.ppermute(value, axis, [(j, j ^ k) for j in range(n)])]
  transfers between devices with their start and end apart: 9 -> 8, of which waited for: 3 -> 3; matrix products, arithmetic and copies ran while one was open for 0% -> 0% of each run, Pallas kernels for 45% -> 45%
where the time goes in v9:
time: 38.5 us; the launch traced here: 38.3 us
  Pallas kernels  20.1 us (52%)
  starting transfers between devices  11.3 us (29%)
  waiting for transfers between devices  6.71 us (17%)
    ppermute x8, starting transfers between devices, send(): return lax.ppermute(value, axis, [(j, j ^ k) for j in range(n)])  11.3 us
    pallas_call x1, Pallas kernels, body(): pl.pallas_call(functools.partial(fetch_kernel, n_w), out_shape=[jax.Shape...  11 us
    ppermute x8, waiting for transfers between devices, send(): return lax.ppermute(value, axis, [(j, j ^ k) for j in range(n)])  6.71 us
    pallas_call x2, Pallas kernels, product(): pl.pallas_call(functools.partial(product_kernel, len(some), n_y, n_z, ste...  4.71 us
    pallas_call x1, Pallas kernels, body(): pl.pallas_call(functools.partial(base_kernel, 1, step), out_shape=jax.Sha...  1.58 us
    pallas_call x1, Pallas kernels, body(): pl.pallas_call(functools.partial(pair_kernel, n_y, n_z, step), out_shape=...  1.08 us
    pallas_call x1, Pallas kernels, body(): pl.pallas_call(functools.partial(rows_kernel, n_x, depth * groups), out_s...  0.97 us
    pallas_call x1, Pallas kernels, body(): pl.pallas_call(final_kernel, out_shape=jax.ShapeDtypeStruct((rows_here, c...  0.83 us
  transfers between devices with their start and end apart: 8, of which 3 were waited for; matrix products, arithmetic and copies ran while one was open for 0% of the time, Pallas kernels for 45%

profile of v9, /device:TPU:0, one launch (start us, length us, event | category | flops | bytes accessed | tf_op | source)
XLA Modules:
  0.0 38.3 jit_solution(8734283641107545021)
XLA Ops:
  0.0 4.1 %collective-permute-start.1 = (bf16[16,4096]{1,0:T(8,128)(2,1)}, bf16[16,4096]{1,0:T(8,128)(2,1)S(1)}, u32[]{:S(2)}, u32[]{:S(2)}) collective-permute-start(bf16[16,4096]{1,0:T(8,128)(2,1)} %refs_6_.1), channel_id=1, source_target_pairs={{0,8},{4,12},{8,0},{12,4},{1,9},{5,13},{9,1},{13,5},{2,10},{6,14},... | collective-permute-start | bytes 393224 | tf_op jit(solution)/shard_map/ppermute | solution.py:210
  4.1 1.6 %collective-permute-start = (bf16[16,4096]{1,0:T(8,128)(2,1)}, bf16[16,4096]{1,0:T(8,128)(2,1)S(1)}, u32[]{:S(2)}, u32[]{:S(2)}) collective-permute-start(bf16[16,4096]{1,0:T(8,128)(2,1)} %refs_6_.1), channel_id=1, source_target_pairs={{0,4},{4,0},{8,12},{12,8},{1,5},{5,1},{9,13},{13,9},{2,6},{6,2},{1... | collective-permute-start | bytes 393224 | tf_op jit(solution)/shard_map/ppermute | solution.py:210
  5.7 0.0 collective-permute-start.2
  5.7 11.0 %fetch_weight.1 = (f32[8,128]{1,0:T(8,128)S(1)}, bf16[4096,1024]{1,0:T(8,128)(2,1)S(1)}, bf16[4096,1024]{1,0:T(8,128)(2,1)S(1)}, bf16[4096,1024]{1,0:T(8,128)(2,1)S(1)}, bf16[4096,1024]{1,0:T(8,128)(2,1)S(1)}) custom-call(bf16[4096,4096]{1,0:T(8,128)(2,1)} %w_hbm.1), custom_call_target="tpu_custom_call" | custom-call | bytes 33554432 | tf_op jit(solution)/shard_map/fetch_weight/pallas_call | solution.py:220
  16.7 0.0 collective-permute-done.1.refs_8_
  16.7 0.0 collective-permute-done.refs_7_
  16.7 0.0 collective-permute-done.2.refs_9_
  16.8 1.0 %scaled_rows.1 = (bf16[64,4096]{1,0:T(8,128)(2,1)S(1)}, bf16[64,256]{1,0:T(8,128)(2,1)S(1)}) custom-call(s32[4]{0:T(128)S(1)} %copy-done.5, s32[4]{0:T(128)S(1)} %copy-done.6, s32[5]{0:T(128)S(1)} %copy-done.4, bf16[4096]{0:T(1024)(128)(2,1)S(1)} %copy-done.3, bf16[1,64,4096]{2,1,0:T(8,128)(2,1)S(1)} %bitcast.1, f32[8,128]{1,0:T(8,128)S(1)} %get-tuple-element.18.refs_5_._, ...), custom_call_target="tpu_custom_call" | custom-call | tf_op jit(solution)/shard_map/scaled_rows/pallas_call | solution.py:232
  17.8 1.0 %collective-permute-start.4 = (bf16[64,256]{1,0:T(8,128)(2,1)S(1)}, bf16[64,256]{1,0:T(8,128)(2,1)S(1)}, u32[]{:S(2)}, u32[]{:S(2)}) collective-permute-start(bf16[64,256]{1,0:T(8,128)(2,1)S(1)} %get-tuple-element.25), channel_id=1, source_target_pairs={{0,4},{4,0},{8,12},{12,8},{1,5},{5,1},{9,13},{13,9},{2,6},{6,2},{1... | collective-permute-start | bytes 98312 | tf_op jit(solution)/shard_map/ppermute | solution.py:210
  18.7 1.6 %first_columns.1.side_ref = f32[64,1024]{1,0:T(8,128)S(1)} custom-call(f32[8,128]{1,0:T(8,128)S(1)} %get-tuple-element.18.refs_5_._, bf16[64,4096]{1,0:T(8,128)(2,1)S(1)} %get-tuple-element.19.x_ref, bf16[4096,1024]{1,0:T(8,128)(2,1)S(1)} %get-tuple-element.20.refs_0_), custom_call_target="tpu_custom_call" | custom-call | flops 536870912 | bytes 8388608 | tf_op jit(solution)/shard_map/first_columns/pallas_call | solution.py:264
  20.3 1.4 %collective-permute-done.4 = bf16[64,256]{1,0:T(8,128)(2,1)S(1)} collective-permute-done((bf16[64,256]{1,0:T(8,128)(2,1)S(1)}, bf16[64,256]{1,0:T(8,128)(2,1)S(1)}, u32[]{:S(2)}, u32[]{:S(2)}) %collective-permute-start.4) | collective-permute-done | bytes 32800 | tf_op jit(solution)/shard_map/ppermute | solution.py:210
  21.8 2.4 %collective-permute-start.5 = (bf16[64,256]{1,0:T(8,128)(2,1)S(1)}, bf16[64,256]{1,0:T(8,128)(2,1)S(1)}, u32[]{:S(2)}, u32[]{:S(2)}) collective-permute-start(bf16[64,256]{1,0:T(8,128)(2,1)S(1)} %add.6), channel_id=1, source_target_pairs={{0,8},{4,12},{8,0},{12,4},{1,9},{5,13},{9,1},{13,5},{2,10},{6,14},... | collective-permute-start | bytes 98312 | tf_op jit(solution)/shard_map/ppermute | solution.py:210
  24.2 3.1 %middle_columns.1 = (f32[32,3072]{1,0:T(8,128)S(1)}, bf16[32,3072]{1,0:T(8,128)(2,1)S(1)}) custom-call(bf16[64,4096]{1,0:T(8,128)(2,1)S(1)} %get-tuple-element.19.x_ref, f32[64,1024]{1,0:T(8,128)S(1)} %first_columns.1.side_ref, bf16[4096,1024]{1,0:T(8,128)(2,1)S(1)} %get-tuple-element.21.refs_0_, bf16[4096,1024]{1,0:T(8,128)(2,1)S(1)} %get-tuple-element.22.refs_1_), custom_call_target="tpu_custom_call" | custom-call | flops 6442450944 | bytes 25165824 | tf_op jit(solution)/shard_map/middle_columns/pallas_call | solution.py:276
  27.3 0.1 collective-permute-start.3
  27.4 0.0 collective-permute-done.5
  27.4 0.0 copy-start
  27.4 1.6 %last_columns.1 = (f32[32,1280]{1,0:T(8,128)S(1)}, bf16[32,1280]{1,0:T(8,128)(2,1)S(1)}) custom-call(bf16[64,4096]{1,0:T(8,128)(2,1)S(1)} %get-tuple-element.19.x_ref, bf16[64,256]{1,0:T(8,128)(2,1)S(1)} %add.7.side_ref, bf16[4096,1024]{1,0:T(8,128)(2,1)S(1)} %get-tuple-element.26.refs_0_), custom_call_target="tpu_custom_call" | custom-call | flops 5368709120 | bytes 10485760 | tf_op jit(solution)/shard_map/last_columns/pallas_call | solution.py:276
  29.0 0.6 %collective-permute-start.6 = (bf16[32,1280]{1,0:T(8,128)(2,1)S(1)}, bf16[32,1280]{1,0:T(8,128)(2,1)S(1)}, u32[]{:S(2)}, u32[]{:S(2)}) collective-permute-start(bf16[32,1280]{1,0:T(8,128)(2,1)S(1)} %get-tuple-element.28), channel_id=1, source_target_pairs={{0,1},{1,0},{2,3},{3,2},{4,5},{5,4},{6,7},{7,6},{8,9},{9,8},{10,11... | collective-permute-start | bytes 245768 | tf_op jit(solution)/shard_map/ppermute | solution.py:210
  29.6 0.9 %collective-permute-done.6.refs_3_ = bf16[32,1280]{1,0:T(8,128)(2,1)S(1)} collective-permute-done((bf16[32,1280]{1,0:T(8,128)(2,1)S(1)}, bf16[32,1280]{1,0:T(8,128)(2,1)S(1)}, u32[]{:S(2)}, u32[]{:S(2)}) %collective-permute-start.6) | collective-permute-done | bytes 81952 | tf_op jit(solution)/shard_map/ppermute | solution.py:210
  30.5 0.0 collective-permute-done.3.refs_1_
  30.5 1.1 %chip_sums.1 = (f32[16,4224]{1,0:T(8,128)S(1)}, bf16[16,4224]{1,0:T(8,128)(2,1)S(1)}) custom-call(s32[5]{0:T(128)S(1)} %copy-done.4, bf16[4,64,4096]{2,1,0:T(8,128)(2,1)S(1)} %copy-done, f32[32,3072]{1,0:T(8,128)S(1)} %get-tuple-element.23.refs_0_, bf16[32,3072]{1,0:T(8,128)(2,1)S(1)} %collective-permute-done.3.refs_1_, ...), custom_call_target="tpu_custom_call" | custom-call | tf_op jit(solution)/shard_map/chip_sums/pallas_call | solution.py:291
  31.6 1.6 %collective-permute-start.7 = (bf16[16,4224]{1,0:T(8,128)(2,1)S(1)}, bf16[16,4224]{1,0:T(8,128)(2,1)S(1)}, u32[]{:S(2)}, u32[]{:S(2)}) collective-permute-start(bf16[16,4224]{1,0:T(8,128)(2,1)S(1)} %get-tuple-element.30), channel_id=1, source_target_pairs={{0,2},{2,0},{1,3},{3,1},{4,6},{6,4},{5,7},{7,5},{8,10},{10,8},{9,1... | collective-permute-start | bytes 405512 | tf_op jit(solution)/shard_map/ppermute | solution.py:210
  33.2 4.3 %collective-permute-done.7.refs_1_ = bf16[16,4224]{1,0:T(8,128)(2,1)S(1)} collective-permute-done((bf16[16,4224]{1,0:T(8,128)(2,1)S(1)}, bf16[16,4224]{1,0:T(8,128)(2,1)S(1)}, u32[]{:S(2)}, u32[]{:S(2)}) %collective-permute-start.7) | collective-permute-done | bytes 135200 | tf_op jit(solution)/shard_map/ppermute | solution.py:210
  37.5 0.8 %query_rows.1 = bf16[16,4096]{1,0:T(8,128)(2,1)} custom-call(f32[16,4224]{1,0:T(8,128)S(1)} %get-tuple-element.29.refs_0_, bf16[16,4224]{1,0:T(8,128)(2,1)S(1)} %collective-permute-done.7.refs_1_), custom_call_target="tpu_custom_call" | custom-call | tf_op jit(solution)/shard_map/query_rows/pallas_call | solution.py:302
  (15 shorter events, 0.0 us)
Async XLA Ops:
  0.0 16.7 %copy-start.2 = (bf16[16,4096]{1,0:T(8,128)(2,1)S(1)}, bf16[16,4096]{1,0:T(8,128)(2,1)}, u32[]{:S(2)}) copy-start(bf16[16,4096]{1,0:T(8,128)(2,1)} %refs_6_.1) | copy-start | bytes 393220
  0.0 16.7 %copy-start.4 = (s32[5]{0:T(128)S(1)}, s32[5]{0:T(128)}, u32[]{:S(2)}) copy-start(s32[5]{0:T(128)} %start_ref.1) | copy-start | bytes 64
  0.0 16.8 %copy-start.6 = (s32[4]{0:T(128)S(1)}, s32[4]{0:T(128)}, u32[]{:S(2)}) copy-start(s32[4]{0:T(128)} %refs_1_.1) | copy-start | bytes 52
  0.0 16.8 %copy-start.5 = (s32[4]{0:T(128)S(1)}, s32[4]{0:T(128)}, u32[]{:S(2)}) copy-start(s32[4]{0:T(128)} %refs_0_.1) | copy-start | bytes 52
  0.0 16.8 %copy-start.1 = (bf16[1,4096,64]{1,2,0:T(8,128)(2,1)S(1)}, bf16[1,4096,64]{1,2,0:T(8,128)(2,1)}, u32[]{:S(2)}) copy-start(bf16[1,4096,64]{1,2,0:T(8,128)(2,1)} %param.12) | copy-start | bytes 1572868
  0.0 16.8 %copy-start.3 = (bf16[4096]{0:T(1024)(128)(2,1)S(1)}, bf16[4096]{0:T(1024)(128)(2,1)}, u32[]{:S(2)}) copy-start(bf16[4096]{0:T(1024)(128)(2,1)} %refs_3_.1) | copy-start | bytes 24580
  0.0 16.7 %collective-permute-start.1 = (bf16[16,4096]{1,0:T(8,128)(2,1)}, bf16[16,4096]{1,0:T(8,128)(2,1)S(1)}, u32[]{:S(2)}, u32[]{:S(2)}) collective-permute-start(bf16[16,4096]{1,0:T(8,128)(2,1)} %refs_6_.1), channel_id=1, source_target_pairs={{0,8},{4,12},{8,0},{12,4},{1,9},{5,13},{9,1},{13,5},{2,10},{6,14},... | collective-permute-start | bytes 393224 | tf_op jit(solution)/shard_map/ppermute | solution.py:210
  4.1 12.6 %collective-permute-start = (bf16[16,4096]{1,0:T(8,128)(2,1)}, bf16[16,4096]{1,0:T(8,128)(2,1)S(1)}, u32[]{:S(2)}, u32[]{:S(2)}) collective-permute-start(bf16[16,4096]{1,0:T(8,128)(2,1)} %refs_6_.1), channel_id=1, source_target_pairs={{0,4},{4,0},{8,12},{12,8},{1,5},{5,1},{9,13},{13,9},{2,6},{6,2},{1... | collective-permute-start | bytes 393224 | tf_op jit(solution)/shard_map/ppermute | solution.py:210
  5.7 11.0 %collective-permute-start.2 = (bf16[16,4096]{1,0:T(8,128)(2,1)}, bf16[16,4096]{1,0:T(8,128)(2,1)S(1)}, u32[]{:S(2)}, u32[]{:S(2)}) collective-permute-start(bf16[16,4096]{1,0:T(8,128)(2,1)} %refs_6_.1), channel_id=1, source_target_pairs={{0,12},{4,8},{8,4},{12,0},{1,13},{5,9},{9,5},{13,1},{2,14},{6,10},... | collective-permute-start | bytes 393224 | tf_op jit(solution)/shard_map/ppermute | solution.py:210
  17.8 4.0 %collective-permute-start.4 = (bf16[64,256]{1,0:T(8,128)(2,1)S(1)}, bf16[64,256]{1,0:T(8,128)(2,1)S(1)}, u32[]{:S(2)}, u32[]{:S(2)}) collective-permute-start(bf16[64,256]{1,0:T(8,128)(2,1)S(1)} %get-tuple-element.25), channel_id=1, source_target_pairs={{0,4},{4,0},{8,12},{12,8},{1,5},{5,1},{9,13},{13,9},{2,6},{6,2},{1... | collective-permute-start | bytes 98312 | tf_op jit(solution)/shard_map/ppermute | solution.py:210
  21.8 5.6 %collective-permute-start.5 = (bf16[64,256]{1,0:T(8,128)(2,1)S(1)}, bf16[64,256]{1,0:T(8,128)(2,1)S(1)}, u32[]{:S(2)}, u32[]{:S(2)}) collective-permute-start(bf16[64,256]{1,0:T(8,128)(2,1)S(1)} %add.6), channel_id=1, source_target_pairs={{0,8},{4,12},{8,0},{12,4},{1,9},{5,13},{9,1},{13,5},{2,10},{6,14},... | collective-permute-start | bytes 98312 | tf_op jit(solution)/shard_map/ppermute | solution.py:210
  27.3 3.2 %collective-permute-start.3 = (bf16[32,3072]{1,0:T(8,128)(2,1)S(1)}, bf16[32,3072]{1,0:T(8,128)(2,1)S(1)}, u32[]{:S(2)}, u32[]{:S(2)}) collective-permute-start(bf16[32,3072]{1,0:T(8,128)(2,1)S(1)} %get-tuple-element.24), channel_id=1, source_target_pairs={{0,1},{1,0},{2,3},{3,2},{4,5},{5,4},{6,7},{7,6},{8,9},{9,8},{10,11... | collective-permute-start | bytes 589832 | tf_op jit(solution)/shard_map/ppermute | solution.py:210
  27.4 3.1 %copy-start = (bf16[4,64,4096]{2,1,0:T(8,128)(2,1)S(1)}, bf16[4,64,4096]{2,1,0:T(8,128)(2,1)}, u32[]{:S(2)}) copy-start(bf16[4,64,4096]{2,1,0:T(8,128)(2,1)} %up_ref.1) | copy-start | bytes 6291460
  29.0 1.5 %collective-permute-start.6 = (bf16[32,1280]{1,0:T(8,128)(2,1)S(1)}, bf16[32,1280]{1,0:T(8,128)(2,1)S(1)}, u32[]{:S(2)}, u32[]{:S(2)}) collective-permute-start(bf16[32,1280]{1,0:T(8,128)(2,1)S(1)} %get-tuple-element.28), channel_id=1, source_target_pairs={{0,1},{1,0},{2,3},{3,2},{4,5},{5,4},{6,7},{7,6},{8,9},{9,8},{10,11... | collective-permute-start | bytes 245768 | tf_op jit(solution)/shard_map/ppermute | solution.py:210
  31.6 5.9 %collective-permute-start.7 = (bf16[16,4224]{1,0:T(8,128)(2,1)S(1)}, bf16[16,4224]{1,0:T(8,128)(2,1)S(1)}, u32[]{:S(2)}, u32[]{:S(2)}) collective-permute-start(bf16[16,4224]{1,0:T(8,128)(2,1)S(1)} %get-tuple-element.30), channel_id=1, source_target_pairs={{0,2},{2,0},{1,3},{3,1},{4,6},{6,4},{5,7},{7,5},{8,10},{10,8},{9,1... | collective-permute-start | bytes 405512 | tf_op jit(solution)/shard_map/ppermute | solution.py:210

commit v10 on v9

--- a/solution.py
+++ b/solution.py
@@ -64,7 +64,8 @@
     return value[:, :1] + value[:, LANES - 1 :]
 
 
-def rows_kernel(n, width, *refs):
+def rows_kernel(order, width, *refs):
+    n = len(order)
     rank_ref, slot_ref, start_ref, gain_ref, down_ref, _ = refs[:6]
     blocks = refs[6 : 6 + n]
     x_ref, small_ref = refs[6 + n :]
@@ -73,9 +74,9 @@
     rows = n * block_rows
     gain = gain_ref[...].astype(jnp.float32).reshape(1, gain_ref.shape[0])
     small_ref[...] = jnp.zeros(small_ref.shape, small_ref.dtype)
-    for k in range(n):
+    for k, block in zip(order, blocks):
         begin = pl.multiple_of(jnp.bitwise_xor(home, k) * block_rows, block_rows)
-        values = blocks[k][...].astype(jnp.float32)
+        values = block[...].astype(jnp.float32)
         x_ref[pl.ds(begin, block_rows), :] = (values * gain).astype(jnp.bfloat16)
         if k == 0:
             squares = jnp.sum(values * values, axis=1, keepdims=True) / width
@@ -133,28 +134,46 @@
     write_rows(acc, outs, n_y, n_z)
 
 
-def pair_kernel(n_y, n_z, step, start_ref, up_ref, *refs):
-    firsts, lasts = refs[:n_z], refs[n_z : 2 * n_z]
-    outs, acc = refs[2 * n_z : -1], refs[-1]
-    rows, done = firsts[0].shape
-    rows_here = rows // n_y
-    late = lasts[0].shape[1] - 2 * LANES
-    columns = done + late
+def pair_kernel(n_y, side, *refs):
+    parts, outs = refs[:-n_y], refs[-n_y:]
+    rows_here, columns = outs[0].shape
+    y = lax.axis_index("gy")
+    for k in range(n_y):
+        begin = pl.multiple_of(jnp.bitwise_xor(y, k) * rows_here, rows_here)
+        here = pl.ds(begin, rows_here)
+        total = parts[0][here, :]
+        for part in parts[1:]:
+            total = total + part[here, :].astype(jnp.float32)
+        if side:
+            late = columns - LANES
+            square = join_wide(total[:, late:])
+            outs[k][:, late:] = split_wide(jnp.broadcast_to(square, (rows_here, LANES))).astype(
+                outs[k].dtype
+            )
+            outs[k][:, :late] = total[:, :late].astype(outs[k].dtype)
+        else:
+            outs[k][...] = total.astype(outs[k].dtype)
+
+
+def final_kernel(n, n_z, step, start_ref, up_ref, *refs):
+    firsts, lasts, out_ref = refs[:n], refs[n : 2 * n], refs[2 * n]
+    rows_here, columns = out_ref.shape
+    done = firsts[0].shape[1]
+    late = columns - done
     adapters, rank_columns, _ = up_ref.shape
-    z = lax.axis_index("gz")
-
-    def added(parts, here):
-        total = parts[0][:, here]
+
+    def added(parts, begin, end):
+        total = parts[0][:, begin:end]
         for part in parts[1:]:
-            total = total + part[:, here].astype(jnp.float32)
+            total = total + part[:, begin:end].astype(jnp.float32)
         return total
 
-    square = join_wide(lasts[0][:, late + LANES :])
-    for part in lasts[1:]:
-        square = square + join_wide(part[:, late + LANES :].astype(jnp.float32))
-    down = added(lasts, slice(late, late + rank_columns)).astype(jnp.bfloat16)
-    row = lax.broadcasted_iota(jnp.int32, (rows, rank_columns), 0)
-    row = (row // rows_here * n_z + z) * rows_here + lax.rem(row, rows_here)
+    side = added(lasts, late, late + 2 * LANES)
+    mean_sq = join_wide(side[:, LANES:])
+    scale = lax.rsqrt(mean_sq + EPSILON)
+    down = side[:, :rank_columns].astype(jnp.bfloat16)
+    first_row = (lax.axis_index("gy") * n_z + lax.axis_index("gz")) * rows_here
+    row = lax.broadcasted_iota(jnp.int32, (rows_here, rank_columns), 0) + first_row
     spread = jnp.concatenate(
         [
             jnp.where((row >= start_ref[a]) & (row < start_ref[a + 1]), down, jnp.zeros_like(down))
@@ -164,28 +183,13 @@
     )
     for c in range(0, columns, step):
         if c < done:
-            base = added(firsts, slice(c, c + step))
+            base = added(firsts, c, c + step)
         else:
-            base = added(lasts, slice(c - done, c - done + step))
+            base = added(lasts, c - done, c - done + step)
         up = up_ref[:, :, c : c + step].reshape(adapters * rank_columns, step)
-        acc[:, c : c + step] = base + jnp.dot(spread, up, preferred_element_type=jnp.float32)
-    acc[:, columns:] = split_wide(jnp.broadcast_to(square, (rows, LANES)))
-    y = lax.axis_index("gy")
-    for k in range(n_y):
-        begin = pl.multiple_of(jnp.bitwise_xor(y, k) * rows_here, rows_here)
-        outs[k][...] = acc[pl.ds(begin, rows_here), :].astype(outs[k].dtype)
-
-
-def final_kernel(*refs):
-    parts, out_ref = refs[:-1], refs[-1]
-    columns = out_ref.shape[1]
-    total = parts[0][...]
-    for other in parts[1:]:
-        total = total + other[...].astype(jnp.float32)
-    mean_sq = join_wide(total[:, columns:])
-    scale = lax.rsqrt(mean_sq + EPSILON)
-    value = jnp.where(mean_sq < jnp.inf, total[:, :columns] * scale, 0.0)
-    out_ref[...] = value.astype(out_ref.dtype)
+        total = base + jnp.dot(spread, up, preferred_element_type=jnp.float32)
+        value = jnp.where(mean_sq < jnp.inf, total * scale, 0.0)
+        out_ref[:, c : c + step] = value.astype(out_ref.dtype)
 
 
 def body(
@@ -212,7 +216,8 @@
     def spread_out(made, axis, n):
         return [made[0]] + [send(made[k], axis, n, k) for k in range(1, n)]
 
-    blocks = [hidden] + [send(hidden, "gx", n_x, k) for k in range(1, n_x)]
+    near_last = [0] + sorted(range(1, n_x), reverse=True)
+    blocks = [hidden] + [send(hidden, "gx", n_x, k) for k in near_last[1:]]
 
     step = min(512, columns // 4)
     n_w, pieces = 4, 8
@@ -230,7 +235,7 @@
     )(query_weight)
 
     x, small = pl.pallas_call(
-        functools.partial(rows_kernel, n_x, depth * groups),
+        functools.partial(rows_kernel, near_last, depth * groups),
         out_shape=(
             jax.ShapeDtypeStruct((rows, depth), bf16),
             jax.ShapeDtypeStruct((rows, 2 * LANES), bf16),
@@ -288,25 +293,30 @@
     firsts = product(weights[1:-1], quarter, base, 4, "middle_columns")
     lasts = product(weights[-1:], 0, small, 8, "last_columns")
 
-    made = pl.pallas_call(
-        functools.partial(pair_kernel, n_y, n_z, step),
-        out_shape=shapes(n_y, (rows_here, columns + LANES)),
-        in_specs=[SMEM] + [VMEM] * (1 + 2 * n_z),
-        out_specs=[VMEM] * n_y,
-        scratch_shapes=[pltpu.VMEM((kept, columns + LANES), f32)],
-        compiler_params=params(4 + (rows * depth >> 16)),
-        name="chip_sums",
-    )(segment_starts, adapter_up_factors, *firsts, *lasts)
-    parts = spread_out(made, "gy", n_y)
+    def chip_sums(parts, side, name):
+        wide = parts[0].shape[1]
+        made = pl.pallas_call(
+            functools.partial(pair_kernel, n_y, side),
+            out_shape=shapes(n_y, (rows_here, wide)),
+            in_specs=[VMEM] * n_z,
+            out_specs=[VMEM] * n_y,
+            cost_estimate=cost(2 * rows * depth * quarter, 2 * depth * quarter),
+            compiler_params=params(4 + (rows * depth >> 16)),
+            name=name,
+        )(*parts)
+        return spread_out(made, "gy", n_y)
+
+    first_parts = chip_sums(firsts, False, "first_sums")
+    last_parts = chip_sums(lasts, True, "last_sums")
 
     return pl.pallas_call(
-        final_kernel,
+        functools.partial(final_kernel, n_y, n_z, step),
         out_shape=jax.ShapeDtypeStruct((rows_here, columns), bf16),
-        in_specs=[VMEM] * n_y,
+        in_specs=[SMEM] + [VMEM] * (1 + 2 * n_y),
         out_specs=VMEM,
         compiler_params=params(4 + (rows * depth >> 16)),
         name="query_rows",
-    )(*parts)
+    )(segment_starts, adapter_up_factors, *first_parts, *last_parts)
 
 
 def solution(mesh):

time: 38.5 us -> 37.6 us (0.977)
  waiting for transfers between devices: 6.71 us -> 3.73 us
  starting transfers between devices: 11.3 us -> 13.5 us
    ppermute x8 -> x9, waiting for transfers between devices: 6.71 us -> 3.73 us  [send(): return lax.ppermute(value, axis, [(j, j ^ k) for j in range(n)])]
    ppermute x8 -> x9, starting transfers between devices: 11.3 us -> 13.5 us  [send(): return lax.ppermute(value, axis, [(j, j ^ k) for j in range(n)])]
    pallas_call x3 -> x4, Pallas kernels: 2.87 us -> 2.8 us  [the longest x1 1.64 us: body(): pl.pallas_call(functools.partial(final_kernel, n_y, n_z, step), out_shape...]
  transfers between devices with their start and end apart: 8 -> 9, of which waited for: 3 -> 2; matrix products, arithmetic and copies ran while one was open for 0% -> 0% of each run, Pallas kernels for 45% -> 47%
where the time goes in v10:
time: 37.6 us; the launch traced here: 37.5 us
  Pallas kernels  20.1 us (53%)
  starting transfers between devices  13.5 us (36%)
  waiting for transfers between devices  3.73 us (10%)
    ppermute x9, starting transfers between devices, send(): return lax.ppermute(value, axis, [(j, j ^ k) for j in range(n)])  13.5 us
    pallas_call x1, Pallas kernels, body(): pl.pallas_call(functools.partial(fetch_kernel, n_w), out_shape=[jax.Shape...  11 us
    pallas_call x2, Pallas kernels, product(): pl.pallas_call(functools.partial(product_kernel, len(some), n_y, n_z, ste...  4.71 us
    ppermute x9, waiting for transfers between devices, send(): return lax.ppermute(value, axis, [(j, j ^ k) for j in range(n)])  3.73 us
    pallas_call x1, Pallas kernels, body(): pl.pallas_call(functools.partial(final_kernel, n_y, n_z, step), out_shape...  1.64 us
    pallas_call x1, Pallas kernels, body(): pl.pallas_call(functools.partial(base_kernel, 1, step), out_shape=jax.Sha...  1.58 us
    pallas_call x1, Pallas kernels, body(): pl.pallas_call(functools.partial(rows_kernel, near_last, depth * groups),...  0.97 us
  transfers between devices with their start and end apart: 9, of which 2 were waited for; matrix products, arithmetic and copies ran while one was open for 0% of the time, Pallas kernels for 47%

profile of v10, /device:TPU:0, one launch (start us, length us, event | category | flops | bytes accessed | tf_op | source)
XLA Modules:
  0.0 37.5 jit_solution(1748717006842959596)
XLA Ops:
  0.0 4.1 %collective-permute-start.1 = (bf16[16,4096]{1,0:T(8,128)(2,1)}, bf16[16,4096]{1,0:T(8,128)(2,1)S(1)}, u32[]{:S(2)}, u32[]{:S(2)}) collective-permute-start(bf16[16,4096]{1,0:T(8,128)(2,1)} %refs_6_.1), channel_id=1, source_target_pairs={{0,8},{4,12},{8,0},{12,4},{1,9},{5,13},{9,1},{13,5},{2,10},{6,14},... | collective-permute-start | bytes 393224 | tf_op jit(solution)/shard_map/ppermute | solution.py:214
  4.1 1.3 %collective-permute-start = (bf16[16,4096]{1,0:T(8,128)(2,1)}, bf16[16,4096]{1,0:T(8,128)(2,1)S(1)}, u32[]{:S(2)}, u32[]{:S(2)}) collective-permute-start(bf16[16,4096]{1,0:T(8,128)(2,1)} %refs_6_.1), channel_id=1, source_target_pairs={{0,12},{4,8},{8,4},{12,0},{1,13},{5,9},{9,5},{13,1},{2,14},{6,10},... | collective-permute-start | bytes 393224 | tf_op jit(solution)/shard_map/ppermute | solution.py:214
  5.5 0.2 collective-permute-start.2
  5.7 11.0 %fetch_weight.1 = (f32[8,128]{1,0:T(8,128)S(1)}, bf16[4096,1024]{1,0:T(8,128)(2,1)S(1)}, bf16[4096,1024]{1,0:T(8,128)(2,1)S(1)}, bf16[4096,1024]{1,0:T(8,128)(2,1)S(1)}, bf16[4096,1024]{1,0:T(8,128)(2,1)S(1)}) custom-call(bf16[4096,4096]{1,0:T(8,128)(2,1)} %w_hbm.1), custom_call_target="tpu_custom_call" | custom-call | bytes 33554432 | tf_op jit(solution)/shard_map/fetch_weight/pallas_call | solution.py:225
  16.7 0.0 collective-permute-done.1.refs_8_
  16.7 0.0 collective-permute-done.refs_7_
  16.7 0.0 collective-permute-done.2.refs_9_
  16.8 1.0 %scaled_rows.1 = (bf16[64,4096]{1,0:T(8,128)(2,1)S(1)}, bf16[64,256]{1,0:T(8,128)(2,1)S(1)}) custom-call(s32[4]{0:T(128)S(1)} %copy-done.5, s32[4]{0:T(128)S(1)} %copy-done.6, s32[5]{0:T(128)S(1)} %copy-done.4, bf16[4096]{0:T(1024)(128)(2,1)S(1)} %copy-done.3, bf16[1,64,4096]{2,1,0:T(8,128)(2,1)S(1)} %bitcast.1, f32[8,128]{1,0:T(8,128)S(1)} %get-tuple-element.20.refs_5_._, ...), custom_call_target="tpu_custom_call" | custom-call | tf_op jit(solution)/shard_map/scaled_rows/pallas_call | solution.py:237
  17.8 1.9 %collective-permute-start.5 = (bf16[64,256]{1,0:T(8,128)(2,1)S(1)}, bf16[64,256]{1,0:T(8,128)(2,1)S(1)}, u32[]{:S(2)}, u32[]{:S(2)}) collective-permute-start(bf16[64,256]{1,0:T(8,128)(2,1)S(1)} %get-tuple-element.29), channel_id=1, source_target_pairs={{0,4},{4,0},{8,12},{12,8},{1,5},{5,1},{9,13},{13,9},{2,6},{6,2},{1... | collective-permute-start | bytes 98312 | tf_op jit(solution)/shard_map/ppermute | solution.py:214
  19.6 1.6 %first_columns.1.side_ref = f32[64,1024]{1,0:T(8,128)S(1)} custom-call(f32[8,128]{1,0:T(8,128)S(1)} %get-tuple-element.20.refs_5_._, bf16[64,4096]{1,0:T(8,128)(2,1)S(1)} %get-tuple-element.21.x_ref, bf16[4096,1024]{1,0:T(8,128)(2,1)S(1)} %get-tuple-element.22.refs_0_), custom_call_target="tpu_custom_call" | custom-call | flops 536870912 | bytes 8388608 | tf_op jit(solution)/shard_map/first_columns/pallas_call | solution.py:269
  21.2 0.5 %collective-permute-done.5 = bf16[64,256]{1,0:T(8,128)(2,1)S(1)} collective-permute-done((bf16[64,256]{1,0:T(8,128)(2,1)S(1)}, bf16[64,256]{1,0:T(8,128)(2,1)S(1)}, u32[]{:S(2)}, u32[]{:S(2)}) %collective-permute-start.5) | collective-permute-done | bytes 32800 | tf_op jit(solution)/shard_map/ppermute | solution.py:214
  21.8 2.9 %collective-permute-start.6 = (bf16[64,256]{1,0:T(8,128)(2,1)S(1)}, bf16[64,256]{1,0:T(8,128)(2,1)S(1)}, u32[]{:S(2)}, u32[]{:S(2)}) collective-permute-start(bf16[64,256]{1,0:T(8,128)(2,1)S(1)} %add.6), channel_id=1, source_target_pairs={{0,8},{4,12},{8,0},{12,4},{1,9},{5,13},{9,1},{13,5},{2,10},{6,14},... | collective-permute-start | bytes 98312 | tf_op jit(solution)/shard_map/ppermute | solution.py:214
  24.6 3.1 %middle_columns.1 = (f32[32,3072]{1,0:T(8,128)S(1)}, bf16[32,3072]{1,0:T(8,128)(2,1)S(1)}) custom-call(bf16[64,4096]{1,0:T(8,128)(2,1)S(1)} %get-tuple-element.21.x_ref, f32[64,1024]{1,0:T(8,128)S(1)} %first_columns.1.side_ref, bf16[4096,1024]{1,0:T(8,128)(2,1)S(1)} %get-tuple-element.23.refs_0_, bf16[4096,1024]{1,0:T(8,128)(2,1)S(1)} %get-tuple-element.24.refs_1_), custom_call_target="tpu_custom_call" | custom-call | flops 6442450944 | bytes 25165824 | tf_op jit(solution)/shard_map/middle_columns/pallas_call | solution.py:281
  27.7 0.1 collective-permute-start.3
  27.8 0.0 collective-permute-done.6
  27.8 0.0 copy-start
  27.9 1.6 %last_columns.1 = (f32[32,1280]{1,0:T(8,128)S(1)}, bf16[32,1280]{1,0:T(8,128)(2,1)S(1)}) custom-call(bf16[64,4096]{1,0:T(8,128)(2,1)S(1)} %get-tuple-element.21.x_ref, bf16[64,256]{1,0:T(8,128)(2,1)S(1)} %add.7.side_ref, bf16[4096,1024]{1,0:T(8,128)(2,1)S(1)} %get-tuple-element.30.refs_0_), custom_call_target="tpu_custom_call" | custom-call | flops 5368709120 | bytes 10485760 | tf_op jit(solution)/shard_map/last_columns/pallas_call | solution.py:281
  29.5 0.6 %collective-permute-start.7 = (bf16[32,1280]{1,0:T(8,128)(2,1)S(1)}, bf16[32,1280]{1,0:T(8,128)(2,1)S(1)}, u32[]{:S(2)}, u32[]{:S(2)}) collective-permute-start(bf16[32,1280]{1,0:T(8,128)(2,1)S(1)} %get-tuple-element.32), channel_id=1, source_target_pairs={{0,1},{1,0},{2,3},{3,2},{4,5},{5,4},{6,7},{7,6},{8,9},{9,8},{10,11... | collective-permute-start | bytes 245768 | tf_op jit(solution)/shard_map/ppermute | solution.py:214
  30.1 1.6 %collective-permute-start.4 = (bf16[16,3072]{1,0:T(8,128)(2,1)S(1)}, bf16[16,3072]{1,0:T(8,128)(2,1)S(1)}, u32[]{:S(2)}, u32[]{:S(2)}) collective-permute-start(bf16[16,3072]{1,0:T(8,128)(2,1)S(1)} %get-tuple-element.28), channel_id=1, source_target_pairs={{0,2},{2,0},{1,3},{3,1},{4,6},{6,4},{5,7},{7,5},{8,10},{10,8},{9,1... | collective-permute-start | bytes 294920 | tf_op jit(solution)/shard_map/ppermute | solution.py:214
  31.6 0.0 collective-permute-done.7.refs_1_
  31.6 0.1 last_sums.1
  31.8 0.9 %collective-permute-start.8 = (bf16[16,1280]{1,0:T(8,128)(2,1)S(1)}, bf16[16,1280]{1,0:T(8,128)(2,1)S(1)}, u32[]{:S(2)}, u32[]{:S(2)}) collective-permute-start(bf16[16,1280]{1,0:T(8,128)(2,1)S(1)} %get-tuple-element.34), channel_id=1, source_target_pairs={{0,2},{2,0},{1,3},{3,1},{4,6},{6,4},{5,7},{7,5},{8,10},{10,8},{9,1... | collective-permute-start | bytes 122888 | tf_op jit(solution)/shard_map/ppermute | solution.py:214
  32.6 3.2 %collective-permute-done.8.refs_3_ = bf16[16,1280]{1,0:T(8,128)(2,1)S(1)} collective-permute-done((bf16[16,1280]{1,0:T(8,128)(2,1)S(1)}, bf16[16,1280]{1,0:T(8,128)(2,1)S(1)}, u32[]{:S(2)}, u32[]{:S(2)}) %collective-permute-start.8) | collective-permute-done | bytes 40992 | tf_op jit(solution)/shard_map/ppermute | solution.py:214
  35.8 1.6 %query_rows.1 = bf16[16,4096]{1,0:T(8,128)(2,1)} custom-call(s32[5]{0:T(128)S(1)} %copy-done.4, bf16[4,64,4096]{2,1,0:T(8,128)(2,1)S(1)} %copy-done, f32[16,3072]{1,0:T(8,128)S(1)} %get-tuple-element.27.refs_0_, bf16[16,3072]{1,0:T(8,128)(2,1)S(1)} %collective-permute-done.4.refs_1_, f32[16,1280]{1,0:T(8,128)S(1)} %get-tuple-element.33.refs_2_, ...), custom_call_target="tpu_custom_call" | custom-call | tf_op jit(solution)/shard_map/query_rows/pallas_call | solution.py:312
  (18 shorter events, 0.1 us)
Async XLA Ops:
  0.0 16.7 %copy-start.2 = (bf16[16,4096]{1,0:T(8,128)(2,1)S(1)}, bf16[16,4096]{1,0:T(8,128)(2,1)}, u32[]{:S(2)}) copy-start(bf16[16,4096]{1,0:T(8,128)(2,1)} %refs_6_.1) | copy-start | bytes 393220
  0.0 16.7 %copy-start.4 = (s32[5]{0:T(128)S(1)}, s32[5]{0:T(128)}, u32[]{:S(2)}) copy-start(s32[5]{0:T(128)} %start_ref.1) | copy-start | bytes 64
  0.0 16.8 %copy-start.6 = (s32[4]{0:T(128)S(1)}, s32[4]{0:T(128)}, u32[]{:S(2)}) copy-start(s32[4]{0:T(128)} %refs_1_.1) | copy-start | bytes 52
  0.0 16.8 %copy-start.5 = (s32[4]{0:T(128)S(1)}, s32[4]{0:T(128)}, u32[]{:S(2)}) copy-start(s32[4]{0:T(128)} %refs_0_.1) | copy-start | bytes 52
  0.0 16.8 %copy-start.1 = (bf16[1,4096,64]{1,2,0:T(8,128)(2,1)S(1)}, bf16[1,4096,64]{1,2,0:T(8,128)(2,1)}, u32[]{:S(2)}) copy-start(bf16[1,4096,64]{1,2,0:T(8,128)(2,1)} %param.12) | copy-start | bytes 1572868
  0.0 16.8 %copy-start.3 = (bf16[4096]{0:T(1024)(128)(2,1)S(1)}, bf16[4096]{0:T(1024)(128)(2,1)}, u32[]{:S(2)}) copy-start(bf16[4096]{0:T(1024)(128)(2,1)} %refs_3_.1) | copy-start | bytes 24580
  0.0 16.7 %collective-permute-start.1 = (bf16[16,4096]{1,0:T(8,128)(2,1)}, bf16[16,4096]{1,0:T(8,128)(2,1)S(1)}, u32[]{:S(2)}, u32[]{:S(2)}) collective-permute-start(bf16[16,4096]{1,0:T(8,128)(2,1)} %refs_6_.1), channel_id=1, source_target_pairs={{0,8},{4,12},{8,0},{12,4},{1,9},{5,13},{9,1},{13,5},{2,10},{6,14},... | collective-permute-start | bytes 393224 | tf_op jit(solution)/shard_map/ppermute | solution.py:214
  4.1 12.6 %collective-permute-start = (bf16[16,4096]{1,0:T(8,128)(2,1)}, bf16[16,4096]{1,0:T(8,128)(2,1)S(1)}, u32[]{:S(2)}, u32[]{:S(2)}) collective-permute-start(bf16[16,4096]{1,0:T(8,128)(2,1)} %refs_6_.1), channel_id=1, source_target_pairs={{0,12},{4,8},{8,4},{12,0},{1,13},{5,9},{9,5},{13,1},{2,14},{6,10},... | collective-permute-start | bytes 393224 | tf_op jit(solution)/shard_map/ppermute | solution.py:214
  5.5 11.2 %collective-permute-start.2 = (bf16[16,4096]{1,0:T(8,128)(2,1)}, bf16[16,4096]{1,0:T(8,128)(2,1)S(1)}, u32[]{:S(2)}, u32[]{:S(2)}) collective-permute-start(bf16[16,4096]{1,0:T(8,128)(2,1)} %refs_6_.1), channel_id=1, source_target_pairs={{0,4},{4,0},{8,12},{12,8},{1,5},{5,1},{9,13},{13,9},{2,6},{6,2},{1... | collective-permute-start | bytes 393224 | tf_op jit(solution)/shard_map/ppermute | solution.py:214
  17.8 4.0 %collective-permute-start.5 = (bf16[64,256]{1,0:T(8,128)(2,1)S(1)}, bf16[64,256]{1,0:T(8,128)(2,1)S(1)}, u32[]{:S(2)}, u32[]{:S(2)}) collective-permute-start(bf16[64,256]{1,0:T(8,128)(2,1)S(1)} %get-tuple-element.29), channel_id=1, source_target_pairs={{0,4},{4,0},{8,12},{12,8},{1,5},{5,1},{9,13},{13,9},{2,6},{6,2},{1... | collective-permute-start | bytes 98312 | tf_op jit(solution)/shard_map/ppermute | solution.py:214
  21.8 6.1 %collective-permute-start.6 = (bf16[64,256]{1,0:T(8,128)(2,1)S(1)}, bf16[64,256]{1,0:T(8,128)(2,1)S(1)}, u32[]{:S(2)}, u32[]{:S(2)}) collective-permute-start(bf16[64,256]{1,0:T(8,128)(2,1)S(1)} %add.6), channel_id=1, source_target_pairs={{0,8},{4,12},{8,0},{12,4},{1,9},{5,13},{9,1},{13,5},{2,10},{6,14},... | collective-permute-start | bytes 98312 | tf_op jit(solution)/shard_map/ppermute | solution.py:214
  27.7 2.3 %collective-permute-start.3 = (bf16[32,3072]{1,0:T(8,128)(2,1)S(1)}, bf16[32,3072]{1,0:T(8,128)(2,1)S(1)}, u32[]{:S(2)}, u32[]{:S(2)}) collective-permute-start(bf16[32,3072]{1,0:T(8,128)(2,1)S(1)} %get-tuple-element.26), channel_id=1, source_target_pairs={{0,1},{1,0},{2,3},{3,2},{4,5},{5,4},{6,7},{7,6},{8,9},{9,8},{10,11... | collective-permute-start | bytes 589832 | tf_op jit(solution)/shard_map/ppermute | solution.py:214
  27.8 8.0 %copy-start = (bf16[4,64,4096]{2,1,0:T(8,128)(2,1)S(1)}, bf16[4,64,4096]{2,1,0:T(8,128)(2,1)}, u32[]{:S(2)}) copy-start(bf16[4,64,4096]{2,1,0:T(8,128)(2,1)} %up_ref.1) | copy-start | bytes 6291460
  29.5 2.2 %collective-permute-start.7 = (bf16[32,1280]{1,0:T(8,128)(2,1)S(1)}, bf16[32,1280]{1,0:T(8,128)(2,1)S(1)}, u32[]{:S(2)}, u32[]{:S(2)}) collective-permute-start(bf16[32,1280]{1,0:T(8,128)(2,1)S(1)} %get-tuple-element.32), channel_id=1, source_target_pairs={{0,1},{1,0},{2,3},{3,2},{4,5},{5,4},{6,7},{7,6},{8,9},{9,8},{10,11... | collective-permute-start | bytes 245768 | tf_op jit(solution)/shard_map/ppermute | solution.py:214
  30.1 5.8 %collective-permute-start.4 = (bf16[16,3072]{1,0:T(8,128)(2,1)S(1)}, bf16[16,3072]{1,0:T(8,128)(2,1)S(1)}, u32[]{:S(2)}, u32[]{:S(2)}) collective-permute-start(bf16[16,3072]{1,0:T(8,128)(2,1)S(1)} %get-tuple-element.28), channel_id=1, source_target_pairs={{0,2},{2,0},{1,3},{3,1},{4,6},{6,4},{5,7},{7,5},{8,10},{10,8},{9,1... | collective-permute-start | bytes 294920 | tf_op jit(solution)/shard_map/ppermute | solution.py:214
  31.8 4.0 %collective-permute-start.8 = (bf16[16,1280]{1,0:T(8,128)(2,1)S(1)}, bf16[16,1280]{1,0:T(8,128)(2,1)S(1)}, u32[]{:S(2)}, u32[]{:S(2)}) collective-permute-start(bf16[16,1280]{1,0:T(8,128)(2,1)S(1)} %get-tuple-element.34), channel_id=1, source_target_pairs={{0,2},{2,0},{1,3},{3,1},{4,6},{6,4},{5,7},{7,5},{8,10},{10,8},{9,1... | collective-permute-start | bytes 122888 | tf_op jit(solution)/shard_map/ppermute | solution.py:214

commit v11 on v10

v11 whole, which is shorter than its diff:
```python
import functools

import jax
import jax.numpy as jnp
from jax import lax
from jax.experimental import pallas as pl
from jax.experimental.pallas import tpu as pltpu
from jax.sharding import PartitionSpec as P

EPSILON = 1e-05
ADAPTER_ALPHA = 32.0
LANES = 128
MIB = 1 << 20

VMEM = pl.BlockSpec(memory_space=pltpu.VMEM)
HBM = pl.BlockSpec(memory_space=pltpu.HBM)
ANY = pl.BlockSpec(memory_space=pl.ANY)


def params(mib):
    return pltpu.CompilerParams(vmem_limit_bytes=mib * MIB)


def cost(flops, moved):
    return pl.CostEstimate(flops=flops, bytes_accessed=moved, transcendentals=0)


def weight_copies(w_hbm, first, w_vmem, sems):
    pieces = sems.shape[0]
    depth, width = w_vmem.shape
    step = depth // pieces
    return [
        pltpu.make_async_copy(
            w_hbm.at[pl.ds(p * step, step), pl.ds(first, width)],
            w_vmem.at[pl.ds(p * step, step)],
            sems.at[p],
        )
        for p in range(pieces)
    ]


def fetch_kernel(n, w_hbm, rank_hbm, slot_hbm, start_hbm, factor_ref, spread_ref, *refs):
    weights, sems, scalar_sems = refs[:n], refs[n], refs[n + 1]
    rank_ref, slot_ref, start_ref = refs[n + 2 :]
    scalars = [
        pltpu.make_async_copy(source, target, scalar_sems.at[j])
        for j, (source, target) in enumerate(
            ((rank_hbm, rank_ref), (slot_hbm, slot_ref), (start_hbm, start_ref))
        )
    ]
    for copy in scalars:
        copy.start()
    copies = []
    first = 0
    for j, w_vmem in enumerate(weights):
        copies += weight_copies(w_hbm, first, w_vmem, sems.at[j])
        first += w_vmem.shape[1]
    for copy in copies:
        copy.start()
    for copy in scalars:
        copy.wait()
    slots, rows, rank_columns = factor_ref.shape
    home = lax.axis_index("gx")
    row = lax.broadcasted_iota(jnp.int32, (rows, rank_columns), 0)
    col = lax.broadcasted_iota(jnp.int32, (rows, rank_columns), 1)
    for s in range(slots):
        adapter = slot_ref[home * slots + s]
        rank = rank_ref[adapter]
        live = (row >= start_ref[adapter]) & (row < start_ref[adapter + 1]) & (col < rank)
        scale = ADAPTER_ALPHA / jnp.full((rows, rank_columns), rank, jnp.int32).astype(jnp.float32)
        factor_ref[s] = jnp.where(live, scale, 0.0)
    adapters = spread_ref.shape[1] // rank_columns
    for a in range(adapters):
        live = (row >= start_ref[a]) & (row < start_ref[a + 1])
        spread_ref[:, a * rank_columns : (a + 1) * rank_columns] = jnp.where(live, 1.0, 0.0)
    for copy in copies:
        copy.wait()


def split_wide(value):
    high = value.astype(jnp.bfloat16).astype(jnp.float32)
    low = jnp.where(high < jnp.inf, value - high, 0.0)
    lane = lax.broadcasted_iota(jnp.int32, value.shape, 1)
    return jnp.where(lane < LANES // 2, high, low)


def join_wide(value):
    return value[:, :1] + value[:, LANES - 1 :]


def rows_kernel(order, width, gain_ref, down_ref, factor_ref, *refs):
    n = len(order)
    blocks = refs[:n]
    x_ref, small_ref = refs[n:]
    home = lax.axis_index("gx")
    block_rows = blocks[0].shape[0]
    gain = gain_ref[...].astype(jnp.float32).reshape(1, gain_ref.shape[0])
    small_ref[...] = jnp.zeros(small_ref.shape, small_ref.dtype)
    for k, block in zip(order, blocks):
        begin = pl.multiple_of(jnp.bitwise_xor(home, k) * block_rows, block_rows)
        values = block[...].astype(jnp.float32)
        x_ref[pl.ds(begin, block_rows), :] = (values * gain).astype(jnp.bfloat16)
        if k == 0:
            squares = jnp.sum(values * values, axis=1, keepdims=True) / width
            squares = split_wide(jnp.broadcast_to(squares, (block_rows, LANES)))
            small_ref[pl.ds(begin, block_rows), LANES:] = squares.astype(jnp.bfloat16)
    slots, rows, rank_columns = factor_ref.shape
    total = jnp.zeros((rows, rank_columns), jnp.float32)
    for s in range(slots):
        projected = lax.dot_general(
            x_ref[...], down_ref[s], (((1,), (1,)), ((), ())), preferred_element_type=jnp.float32
        )
        factor = factor_ref[s]
        total = total + jnp.where(factor > 0, projected * factor, 0.0)
    small_ref[:, :rank_columns] = total.astype(small_ref.dtype)


def write_rows(acc, outs, n_y, n_z):
    z = lax.axis_index("gz")
    rows_here = outs[0].shape[0] // n_y
    for k in range(n_z):
        for y in range(n_y):
            owner = y * n_z + jnp.bitwise_xor(z, k)
            begin = pl.multiple_of(owner * rows_here, rows_here)
            outs[k][y * rows_here : (y + 1) * rows_here, :] = acc[
                pl.ds(begin, rows_here), :
            ].astype(outs[k].dtype)


def multiply(x_ref, weights, step, out, first):
    width = weights[0].shape[1]
    for c in range(0, width * len(weights), step):
        inner = c % width
        out[:, first + c : first + c + step] = jnp.dot(
            x_ref[...],
            weights[c // width][:, inner : inner + step],
            preferred_element_type=jnp.float32,
        )


def base_kernel(n_w, step, x_ref, *refs):
    multiply(x_ref, refs[:n_w], step, refs[n_w], 0)


def product_kernel(n_w, n_y, n_z, step, first, x_ref, *refs):
    if first:
        base_ref, refs = refs[0], refs[2:]
    weights, outs, acc = refs[:n_w], refs[n_w:-1], refs[-1]
    if first:
        acc[:, :first] = base_ref[...]
    multiply(x_ref, weights, step, acc, first)
    write_rows(acc, outs, n_y, n_z)


def chip_rows(parts, here):
    total = parts[0][here, :].astype(jnp.float32)
    for part in parts[1:]:
        total = total + part[here, :].astype(jnp.float32)
    return total


def pair_kernel(n_y, n_z, *refs):
    parts, smalls, outs = refs[:n_z], refs[n_z:-n_y], refs[-n_y:]
    rows_here = outs[0].shape[0]
    columns = parts[0].shape[1]
    y, z = lax.axis_index("gy"), lax.axis_index("gz")
    for k in range(n_y):
        other = jnp.bitwise_xor(y, k)
        here = pl.ds(pl.multiple_of(other * rows_here, rows_here), rows_here)
        outs[k][:, :columns] = chip_rows(parts, here).astype(outs[k].dtype)
        if smalls:
            owner = other * n_z + z
            here = pl.ds(pl.multiple_of(owner * rows_here, rows_here), rows_here)
            small = chip_rows(smalls, here)
            square = jnp.broadcast_to(join_wide(small[:, LANES:]), (rows_here, LANES))
            outs[k][:, columns : columns + LANES] = small[:, :LANES].astype(outs[k].dtype)
            outs[k][:, columns + LANES :] = split_wide(square).astype(outs[k].dtype)


def final_kernel(n, n_z, step, spread_ref, up_ref, *refs):
    firsts, lasts, out_ref = refs[:n], refs[n : 2 * n], refs[2 * n]
    rows_here, columns = out_ref.shape
    done = firsts[0].shape[1]
    late = columns - done
    adapters, rank_columns, _ = up_ref.shape

    def added(parts, begin, end):
        total = parts[0][:, begin:end]
        for part in parts[1:]:
            total = total + part[:, begin:end].astype(jnp.float32)
        return total

    side = added(lasts, late, late + 2 * LANES)
    mean_sq = join_wide(side[:, LANES:])
    scale = lax.rsqrt(mean_sq + EPSILON)
    owner = lax.axis_index("gy") * n_z + lax.axis_index("gz")
    live = spread_ref[pl.ds(pl.multiple_of(owner * rows_here, rows_here), rows_here), :]
    spread = jnp.concatenate([side[:, :rank_columns]] * adapters, axis=1)
    spread = jnp.where(live > 0, spread, 0.0).astype(jnp.bfloat16)
    for c in range(0, columns, step):
        if c < done:
            base = added(firsts, c, c + step)
        else:
            base = added(lasts, c - done, c - done + step)
        up = up_ref[:, :, c : c + step].reshape(adapters * rank_columns, step)
        total = base + jnp.dot(spread, up, preferred_element_type=jnp.float32)
        value = jnp.where(mean_sq < jnp.inf, total * scale, 0.0)
        out_ref[:, c : c + step] = value.astype(out_ref.dtype)


def body(
    hidden,
    attention_norm_gain,
    query_weight,
    slot_down_factors,
    adapter_up_factors,
    adapter_of_row,
    padded_adapter_rank,
    adapter_in_slot,
    segment_starts,
):
    n_x, n_y, n_z = lax.axis_size("gx"), lax.axis_size("gy"), lax.axis_size("gz")
    groups = n_y * n_z
    block_rows, depth = hidden.shape
    columns = query_weight.shape[1]
    rows = n_x * block_rows
    rows_here = rows // groups

    def send(value, axis, n, k):
        return lax.ppermute(value, axis, [(j, j ^ k) for j in range(n)])

    def spread_out(made, axis, n):
        return [made[0]] + [send(made[k], axis, n, k) for k in range(1, n)]

    half = n_x // 2
    order = [0, *range(half, n_x), *range(half - 1, 0, -1)]
    blocks = [hidden] + [send(hidden, "gx", n_x, k) for k in order[1:]]

    step = min(512, columns // 4)
    n_w, pieces = 4, 8
    f32, bf16 = jnp.float32, jnp.bfloat16
    slots, rank_columns = slot_down_factors.shape[0], slot_down_factors.shape[2]
    adapters = adapter_up_factors.shape[0]
    quarter = columns // n_w
    kept = n_y * rows_here
    roomy = params(4 + (rows * depth >> 16))

    scalars = (padded_adapter_rank, adapter_in_slot, segment_starts)
    factor, spread, *weights = pl.pallas_call(
        functools.partial(fetch_kernel, n_w),
        out_shape=[
            jax.ShapeDtypeStruct((slots, rows, rank_columns), f32),
            jax.ShapeDtypeStruct((rows, adapters * rank_columns), f32),
        ]
        + [pltpu.VMEM((depth, quarter), query_weight.dtype)] * n_w,
        in_specs=[ANY] + [HBM] * 3,
        out_specs=[VMEM] * (2 + n_w),
        scratch_shapes=[
            pltpu.SemaphoreType.DMA((n_w, pieces)),
            pltpu.SemaphoreType.DMA((len(scalars),)),
            *[pltpu.SMEM(value.shape, value.dtype) for value in scalars],
        ],
        cost_estimate=cost(0, 2 * query_weight.size),
        compiler_params=roomy,
        name="fetch_weight",
    )(query_weight, *[pltpu.with_memory_space_constraint(v, pltpu.HBM) for v in scalars])
    weights = [pltpu.with_memory_space_constraint(w, pltpu.VMEM) for w in weights]

    x, small = pl.pallas_call(
        functools.partial(rows_kernel, order, depth * groups),
        out_shape=(
            jax.ShapeDtypeStruct((rows, depth), bf16),
            jax.ShapeDtypeStruct((rows, 2 * LANES), bf16),
        ),
        in_specs=[VMEM] * (3 + n_x),
        out_specs=(VMEM,) * 2,
        compiler_params=roomy,
        name="scaled_rows",
    )(attention_norm_gain, jnp.swapaxes(slot_down_factors, 1, 2), factor, *blocks)

    one_hop = small = small + send(small, "gx", n_x, 1)
    hop = 2
    while hop < n_x:
        small = small + send(small, "gx", n_x, hop)
        hop *= 2

    def shapes(n, shape):
        return [jax.ShapeDtypeStruct(shape, f32 if k == 0 else bf16) for k in range(n)]

    early = n_w // 2
    base_columns = early * quarter
    base = pl.pallas_call(
        functools.partial(base_kernel, early, step),
        out_shape=jax.ShapeDtypeStruct((rows, base_columns), f32),
        in_specs=[VMEM] * (1 + early),
        out_specs=VMEM,
        cost_estimate=cost(2 * rows * depth * base_columns, 2 * depth * base_columns),
        compiler_params=roomy,
        name="first_columns",
    )(x, *weights[:early])

    def product(some, bases, times, name):
        first = sum(part.shape[1] for part in bases[:1])
        wide = first + len(some) * quarter
        made = pl.pallas_call(
            functools.partial(product_kernel, len(some), n_y, n_z, step, first),
            out_shape=shapes(n_z, (kept, wide)),
            in_specs=[VMEM] * (1 + len(bases) + len(some)),
            out_specs=[VMEM] * n_z,
            scratch_shapes=[pltpu.VMEM((rows, wide), f32)],
            cost_estimate=cost(2 * rows * depth * wide * times, 2 * depth * wide),
            compiler_params=roomy,
            name=name,
        )(x, *bases, *some)
        return spread_out(made, "gz", n_z)

    firsts = product(weights[early:-1], [base, one_hop], 4, "middle_columns")
    lasts = product(weights[-1:], [], 8, "last_columns")
    smalls = spread_out([small] * n_z, "gz", n_z)

    def chip_sums(parts, sides, name):
        wide = parts[0].shape[1] + (2 * LANES if sides else 0)
        made = pl.pallas_call(
            functools.partial(pair_kernel, n_y, n_z),
            out_shape=shapes(n_y, (rows_here, wide)),
            in_specs=[VMEM] * (n_z + len(sides)),
            out_specs=[VMEM] * n_y,
            cost_estimate=cost(2 * rows * depth * quarter, 2 * depth * quarter),
            compiler_params=roomy,
            name=name,
        )(*parts, *sides)
        return spread_out(made, "gy", n_y)

    first_parts = chip_sums(firsts, [], "first_sums")
    last_parts = chip_sums(lasts, smalls, "last_sums")

    return pl.pallas_call(
        functools.partial(final_kernel, n_y, n_z, step),
        out_shape=jax.ShapeDtypeStruct((rows_here, columns), bf16),
        in_specs=[VMEM] * (2 + 2 * n_y),
        out_specs=VMEM,
        compiler_params=roomy,
        name="query_rows",
    )(spread, adapter_up_factors, *first_parts, *last_parts)


def solution(mesh):
    return jax.shard_map(
        body,
        mesh=mesh,
        in_specs=(
            P(("rep", "gx"), ("gy", "gz")),
            P(("gy", "gz")),
            P(("gy", "gz"), "gx"),
            P("gx", ("gy", "gz"), None),
            P(None, None, "gx"),
            P("rep"),
            P(),
            P(),
            P("rep"),
        ),
        out_specs=P(("rep", "gy", "gz"), "gx"),
        check_vma=False,
    )
```

time: 37.6 us -> 35.4 us (0.941)
  Pallas kernels: 20.1 us -> 19 us
  starting transfers between devices: 13.5 us -> 12.8 us
  waiting for transfers between devices: 3.73 us -> 3.32 us
    pallas_call x2, Pallas kernels: 4.71 us -> 3.21 us  [product(): pl.pallas_call(functools.partial(product_kernel, len(some), n_y, n_z, ste...]
    pallas_call x4, Pallas kernels: 2.74 us -> 3.65 us  [the longest x1 3.04 us: body(): pl.pallas_call(functools.partial(base_kernel, early, step), out_shape=jax...]
    ppermute x9 -> x10, starting transfers between devices: 13.5 us -> 12.8 us  [send(): return lax.ppermute(value, axis, [(j, j ^ k) for j in range(n)])]
    pallas_call x1, Pallas kernels: 1.64 us -> 1.09 us  [body(): pl.pallas_call(functools.partial(final_kernel, n_y, n_z, step), out_shape...]
    ppermute x9 -> x10, waiting for transfers between devices: 3.73 us -> 3.32 us  [send(): return lax.ppermute(value, axis, [(j, j ^ k) for j in range(n)])]
  transfers between devices with their start and end apart: 9 -> 10, of which waited for: 2 -> 1; matrix products, arithmetic and copies ran while one was open for 0% -> 0% of each run, Pallas kernels for 47% -> 49%
where the time goes in v11:
time: 35.4 us; the launch traced here: 35.3 us
  Pallas kernels  19 us (54%)
  starting transfers between devices  12.8 us (36%)
  waiting for transfers between devices  3.32 us (9%)
    ppermute x10, starting transfers between devices, send(): return lax.ppermute(value, axis, [(j, j ^ k) for j in range(n)])  12.8 us
    pallas_call x1, Pallas kernels, body(): pl.pallas_call(functools.partial(fetch_kernel, n_w), out_shape=[jax.Shape...  11 us
    ppermute x10, waiting for transfers between devices, send(): return lax.ppermute(value, axis, [(j, j ^ k) for j in range(n)])  3.32 us
    pallas_call x2, Pallas kernels, product(): pl.pallas_call(functools.partial(product_kernel, len(some), n_y, n_z, ste...  3.21 us
    pallas_call x1, Pallas kernels, body(): pl.pallas_call(functools.partial(base_kernel, early, step), out_shape=jax...  3.04 us
    pallas_call x1, Pallas kernels, body(): pl.pallas_call(functools.partial(final_kernel, n_y, n_z, step), out_shape...  1.09 us
  transfers between devices with their start and end apart: 10, of which 1 were waited for; matrix products, arithmetic and copies ran while one was open for 0% of the time, Pallas kernels for 49%

profile of v11, /device:TPU:0, one launch (start us, length us, event | category | flops | bytes accessed | tf_op | source)
XLA Modules:
  0.0 35.3 jit_solution(3059461486976235685)
XLA Ops:
  0.0 4.1 %collective-permute-start = (bf16[16,4096]{1,0:T(8,128)(2,1)}, bf16[16,4096]{1,0:T(8,128)(2,1)S(1)}, u32[]{:S(2)}, u32[]{:S(2)}) collective-permute-start(bf16[16,4096]{1,0:T(8,128)(2,1)} %refs_0_.1), channel_id=1, source_target_pairs={{0,8},{4,12},{8,0},{12,4},{1,9},{5,13},{9,1},{13,5},{2,10},{6,14},... | collective-permute-start | bytes 393224 | tf_op jit(solution)/shard_map/ppermute | solution.py:230
  4.1 1.3 %collective-permute-start.1 = (bf16[16,4096]{1,0:T(8,128)(2,1)}, bf16[16,4096]{1,0:T(8,128)(2,1)S(1)}, u32[]{:S(2)}, u32[]{:S(2)}) collective-permute-start(bf16[16,4096]{1,0:T(8,128)(2,1)} %refs_0_.1), channel_id=1, source_target_pairs={{0,12},{4,8},{8,4},{12,0},{1,13},{5,9},{9,5},{13,1},{2,14},{6,10},... | collective-permute-start | bytes 393224 | tf_op jit(solution)/shard_map/ppermute | solution.py:230
  5.5 0.2 collective-permute-start.2
  5.7 11.0 %fetch_weight.1 = (f32[1,64,64]{2,1,0:T(8,128)S(1)}, f32[64,256]{1,0:T(8,128)S(1)}, bf16[4096,1024]{1,0:T(8,128)(2,1)S(1)}, bf16[4096,1024]{1,0:T(8,128)(2,1)S(1...) custom-call(bf16[4096,4096]{1,0:T(8,128)(2,1)} %w_hbm.1, s32[4]{0:T(128)} %rank_hbm.1, s32[4]{0:T(128)} %slot_hbm.1, ...), custom_call_target="tpu_custom_call" | custom-call | bytes 33554432 | tf_op jit(solution)/shard_map/fetch_weight/pallas_call | solution.py:249
  16.7 0.0 collective-permute-done.2.refs_3_
  16.8 0.4 %scaled_rows.1 = (bf16[64,4096]{1,0:T(8,128)(2,1)S(1)}, bf16[64,256]{1,0:T(8,128)(2,1)S(1)}) custom-call(bf16[4096]{0:T(1024)(128)(2,1)S(1)} %copy-done.3, bf16[1,64,4096]{2,1,0:T(8,128)(2,1)S(1)} %bitcast.1, f32[1,64,64]{2,1,0:T(8,128)S(1)} %get-tuple-element.22.factor_ref, bf16[16,4096]{1,0:T(8,128)(2,1)S(1)} %copy-done.2, ...), custom_call_target="tpu_custom_call" | custom-call | tf_op jit(solution)/shard_map/scaled_rows/pallas_call | solution.py:269
  17.2 1.9 %collective-permute-start.3 = (bf16[64,256]{1,0:T(8,128)(2,1)S(1)}, bf16[64,256]{1,0:T(8,128)(2,1)S(1)}, u32[]{:S(2)}, u32[]{:S(2)}) collective-permute-start(bf16[64,256]{1,0:T(8,128)(2,1)S(1)} %get-tuple-element.26), channel_id=1, source_target_pairs={{0,4},{4,0},{8,12},{12,8},{1,5},{5,1},{9,13},{13,9},{2,6},{6,2},{1... | collective-permute-start | bytes 98312 | tf_op jit(solution)/shard_map/ppermute | solution.py:230
  19.0 3.0 %first_columns.1.refs_0_ = f32[64,2048]{1,0:T(8,128)S(1)} custom-call(bf16[64,4096]{1,0:T(8,128)(2,1)S(1)} %get-tuple-element.23.x_ref, bf16[4096,1024]{1,0:T(8,128)(2,1)S(1)} %get-tuple-element.24.refs_0_, bf16[4096,1024]{1,0:T(8,128)(2,1)S(1)} %get-tuple-element.25.refs_1_), custom_call_target="tpu_custom_call" | custom-call | flops 1073741824 | bytes 16777216 | tf_op jit(solution)/shard_map/first_columns/pallas_call | solution.py:292
  22.1 0.0 collective-permute-done.3
  22.1 1.9 %collective-permute-start.7 = (bf16[64,256]{1,0:T(8,128)(2,1)S(1)}, bf16[64,256]{1,0:T(8,128)(2,1)S(1)}, u32[]{:S(2)}, u32[]{:S(2)}) collective-permute-start(bf16[64,256]{1,0:T(8,128)(2,1)S(1)} %add.6.refs_1_), channel_id=1, source_target_pairs={{0,8},{4,12},{8,0},{12,4},{1,9},{5,13},{9,1},{13,5},{2,10},{6,14},... | collective-permute-start | bytes 98312 | tf_op jit(solution)/shard_map/ppermute | solution.py:230
  24.1 1.6 %middle_columns.1 = (f32[32,3072]{1,0:T(8,128)S(1)}, bf16[32,3072]{1,0:T(8,128)(2,1)S(1)}) custom-call(bf16[64,4096]{1,0:T(8,128)(2,1)S(1)} %get-tuple-element.23.x_ref, f32[64,2048]{1,0:T(8,128)S(1)} %first_columns.1.refs_0_, bf16[64,256]{1,0:T(8,128)(2,1)S(1)} %add.6.refs_1_, bf16[4096,1024]{1,0:T(8,128)(2,1)S(1)} %get-tuple-element.27.refs_2_), custom_call_target="tpu_custom_call" | custom-call | flops 6442450944 | bytes 25165824 | tf_op jit(solution)/shard_map/middle_columns/pallas_call | solution.py:305
  25.7 0.1 collective-permute-start.4
  25.8 0.0 copy-start
  25.8 1.6 %last_columns.1 = (f32[32,1024]{1,0:T(8,128)S(1)}, bf16[32,1024]{1,0:T(8,128)(2,1)S(1)}) custom-call(bf16[64,4096]{1,0:T(8,128)(2,1)S(1)} %get-tuple-element.23.x_ref, bf16[4096,1024]{1,0:T(8,128)(2,1)S(1)} %get-tuple-element.32.refs_0_), custom_call_target="tpu_custom_call" | custom-call | flops 4294967296 | bytes 8388608 | tf_op jit(solution)/shard_map/last_columns/pallas_call | solution.py:305
  27.4 0.6 %collective-permute-start.6 = (bf16[32,1024]{1,0:T(8,128)(2,1)S(1)}, bf16[32,1024]{1,0:T(8,128)(2,1)S(1)}, u32[]{:S(2)}, u32[]{:S(2)}) collective-permute-start(bf16[32,1024]{1,0:T(8,128)(2,1)S(1)} %get-tuple-element.34), channel_id=1, source_target_pairs={{0,1},{1,0},{2,3},{3,2},{4,5},{5,4},{6,7},{7,6},{8,9},{9,8},{10,11... | collective-permute-start | bytes 196616 | tf_op jit(solution)/shard_map/ppermute | solution.py:230
  27.9 0.0 collective-permute-done.7
  27.9 0.1 collective-permute-start.8
  28.0 0.0 collective-permute-done.4.refs_1_
  28.1 1.6 %collective-permute-start.5 = (bf16[16,3072]{1,0:T(8,128)(2,1)S(1)}, bf16[16,3072]{1,0:T(8,128)(2,1)S(1)}, u32[]{:S(2)}, u32[]{:S(2)}) collective-permute-start(bf16[16,3072]{1,0:T(8,128)(2,1)S(1)} %get-tuple-element.31), channel_id=1, source_target_pairs={{0,2},{2,0},{1,3},{3,1},{4,6},{6,4},{5,7},{7,5},{8,10},{10,8},{9,1... | collective-permute-start | bytes 294920 | tf_op jit(solution)/shard_map/ppermute | solution.py:230
  29.6 0.0 collective-permute-done.6.refs_1_
  29.7 0.2 last_sums.1
  29.8 1.1 %collective-permute-start.9 = (bf16[16,1280]{1,0:T(8,128)(2,1)S(1)}, bf16[16,1280]{1,0:T(8,128)(2,1)S(1)}, u32[]{:S(2)}, u32[]{:S(2)}) collective-permute-start(bf16[16,1280]{1,0:T(8,128)(2,1)S(1)} %get-tuple-element.36), channel_id=1, source_target_pairs={{0,2},{2,0},{1,3},{3,1},{4,6},{6,4},{5,7},{7,5},{8,10},{10,8},{9,1... | collective-permute-start | bytes 122888 | tf_op jit(solution)/shard_map/ppermute | solution.py:230
  30.9 3.3 %collective-permute-done.9.refs_3_ = bf16[16,1280]{1,0:T(8,128)(2,1)S(1)} collective-permute-done((bf16[16,1280]{1,0:T(8,128)(2,1)S(1)}, bf16[16,1280]{1,0:T(8,128)(2,1)S(1)}, u32[]{:S(2)}, u32[]{:S(2)}) %collective-permute-start.9) | collective-permute-done | bytes 40992 | tf_op jit(solution)/shard_map/ppermute | solution.py:230
  34.2 1.1 %query_rows.1 = bf16[16,4096]{1,0:T(8,128)(2,1)} custom-call(f32[64,256]{1,0:T(8,128)S(1)} %get-tuple-element.21.spread_ref, bf16[4,64,4096]{2,1,0:T(8,128)(2,1)S(1)} %copy-done, f32[16,3072]{1,0:T(8,128)S(1)} %get-tuple-element.30.refs_0_, bf16[16,3072]{1,0:T(8,128)(2,1)S(1)} %collective-permute-done.5.refs_1_, f32[16,1280]{1,0:T(8,128)S(1)} %get-tuple-element.35.refs_2_, ...), custom_call_target="tpu_custom_call" | custom-call | tf_op jit(solution)/shard_map/query_rows/pallas_call | solution.py:337
  (14 shorter events, 0.1 us)
Async XLA Ops:
  0.0 16.7 %copy-start.2 = (bf16[16,4096]{1,0:T(8,128)(2,1)S(1)}, bf16[16,4096]{1,0:T(8,128)(2,1)}, u32[]{:S(2)}) copy-start(bf16[16,4096]{1,0:T(8,128)(2,1)} %refs_0_.1) | copy-start | bytes 393220
  0.0 16.7 %copy-start.1 = (bf16[1,4096,64]{1,2,0:T(8,128)(2,1)S(1)}, bf16[1,4096,64]{1,2,0:T(8,128)(2,1)}, u32[]{:S(2)}) copy-start(bf16[1,4096,64]{1,2,0:T(8,128)(2,1)} %param.12) | copy-start | bytes 1572868
  0.0 16.7 %copy-start.3 = (bf16[4096]{0:T(1024)(128)(2,1)S(1)}, bf16[4096]{0:T(1024)(128)(2,1)}, u32[]{:S(2)}) copy-start(bf16[4096]{0:T(1024)(128)(2,1)} %gain_ref.1) | copy-start | bytes 24580
  0.0 16.7 %collective-permute-start = (bf16[16,4096]{1,0:T(8,128)(2,1)}, bf16[16,4096]{1,0:T(8,128)(2,1)S(1)}, u32[]{:S(2)}, u32[]{:S(2)}) collective-permute-start(bf16[16,4096]{1,0:T(8,128)(2,1)} %refs_0_.1), channel_id=1, source_target_pairs={{0,8},{4,12},{8,0},{12,4},{1,9},{5,13},{9,1},{13,5},{2,10},{6,14},... | collective-permute-start | bytes 393224 | tf_op jit(solution)/shard_map/ppermute | solution.py:230
  4.1 12.6 %collective-permute-start.1 = (bf16[16,4096]{1,0:T(8,128)(2,1)}, bf16[16,4096]{1,0:T(8,128)(2,1)S(1)}, u32[]{:S(2)}, u32[]{:S(2)}) collective-permute-start(bf16[16,4096]{1,0:T(8,128)(2,1)} %refs_0_.1), channel_id=1, source_target_pairs={{0,12},{4,8},{8,4},{12,0},{1,13},{5,9},{9,5},{13,1},{2,14},{6,10},... | collective-permute-start | bytes 393224 | tf_op jit(solution)/shard_map/ppermute | solution.py:230
  5.5 11.3 %collective-permute-start.2 = (bf16[16,4096]{1,0:T(8,128)(2,1)}, bf16[16,4096]{1,0:T(8,128)(2,1)S(1)}, u32[]{:S(2)}, u32[]{:S(2)}) collective-permute-start(bf16[16,4096]{1,0:T(8,128)(2,1)} %refs_0_.1), channel_id=1, source_target_pairs={{0,4},{4,0},{8,12},{12,8},{1,5},{5,1},{9,13},{13,9},{2,6},{6,2},{1... | collective-permute-start | bytes 393224 | tf_op jit(solution)/shard_map/ppermute | solution.py:230
  17.2 4.9 %collective-permute-start.3 = (bf16[64,256]{1,0:T(8,128)(2,1)S(1)}, bf16[64,256]{1,0:T(8,128)(2,1)S(1)}, u32[]{:S(2)}, u32[]{:S(2)}) collective-permute-start(bf16[64,256]{1,0:T(8,128)(2,1)S(1)} %get-tuple-element.26), channel_id=1, source_target_pairs={{0,4},{4,0},{8,12},{12,8},{1,5},{5,1},{9,13},{13,9},{2,6},{6,2},{1... | collective-permute-start | bytes 98312 | tf_op jit(solution)/shard_map/ppermute | solution.py:230
  22.1 5.8 %collective-permute-start.7 = (bf16[64,256]{1,0:T(8,128)(2,1)S(1)}, bf16[64,256]{1,0:T(8,128)(2,1)S(1)}, u32[]{:S(2)}, u32[]{:S(2)}) collective-permute-start(bf16[64,256]{1,0:T(8,128)(2,1)S(1)} %add.6.refs_1_), channel_id=1, source_target_pairs={{0,8},{4,12},{8,0},{12,4},{1,9},{5,13},{9,1},{13,5},{2,10},{6,14},... | collective-permute-start | bytes 98312 | tf_op jit(solution)/shard_map/ppermute | solution.py:230
  25.7 2.4 %collective-permute-start.4 = (bf16[32,3072]{1,0:T(8,128)(2,1)S(1)}, bf16[32,3072]{1,0:T(8,128)(2,1)S(1)}, u32[]{:S(2)}, u32[]{:S(2)}) collective-permute-start(bf16[32,3072]{1,0:T(8,128)(2,1)S(1)} %get-tuple-element.29), channel_id=1, source_target_pairs={{0,1},{1,0},{2,3},{3,2},{4,5},{5,4},{6,7},{7,6},{8,9},{9,8},{10,11... | collective-permute-start | bytes 589832 | tf_op jit(solution)/shard_map/ppermute | solution.py:230
  25.8 8.5 %copy-start = (bf16[4,64,4096]{2,1,0:T(8,128)(2,1)S(1)}, bf16[4,64,4096]{2,1,0:T(8,128)(2,1)}, u32[]{:S(2)}) copy-start(bf16[4,64,4096]{2,1,0:T(8,128)(2,1)} %up_ref.1) | copy-start | bytes 6291460
  27.4 2.3 %collective-permute-start.6 = (bf16[32,1024]{1,0:T(8,128)(2,1)S(1)}, bf16[32,1024]{1,0:T(8,128)(2,1)S(1)}, u32[]{:S(2)}, u32[]{:S(2)}) collective-permute-start(bf16[32,1024]{1,0:T(8,128)(2,1)S(1)} %get-tuple-element.34), channel_id=1, source_target_pairs={{0,1},{1,0},{2,3},{3,2},{4,5},{5,4},{6,7},{7,6},{8,9},{9,8},{10,11... | collective-permute-start | bytes 196616 | tf_op jit(solution)/shard_map/ppermute | solution.py:230
  27.9 1.7 %collective-permute-start.8 = (bf16[64,256]{1,0:T(8,128)(2,1)S(1)}, bf16[64,256]{1,0:T(8,128)(2,1)S(1)}, u32[]{:S(2)}, u32[]{:S(2)}) collective-permute-start(bf16[64,256]{1,0:T(8,128)(2,1)S(1)} %add.7.refs_2_), channel_id=1, source_target_pairs={{0,1},{1,0},{2,3},{3,2},{4,5},{5,4},{6,7},{7,6},{8,9},{9,8},{10,11... | collective-permute-start | bytes 98312 | tf_op jit(solution)/shard_map/ppermute | solution.py:230
  28.1 6.1 %collective-permute-start.5 = (bf16[16,3072]{1,0:T(8,128)(2,1)S(1)}, bf16[16,3072]{1,0:T(8,128)(2,1)S(1)}, u32[]{:S(2)}, u32[]{:S(2)}) collective-permute-start(bf16[16,3072]{1,0:T(8,128)(2,1)S(1)} %get-tuple-element.31), channel_id=1, source_target_pairs={{0,2},{2,0},{1,3},{3,1},{4,6},{6,4},{5,7},{7,5},{8,10},{10,8},{9,1... | collective-permute-start | bytes 294920 | tf_op jit(solution)/shard_map/ppermute | solution.py:230
  29.8 4.4 %collective-permute-start.9 = (bf16[16,1280]{1,0:T(8,128)(2,1)S(1)}, bf16[16,1280]{1,0:T(8,128)(2,1)S(1)}, u32[]{:S(2)}, u32[]{:S(2)}) collective-permute-start(bf16[16,1280]{1,0:T(8,128)(2,1)S(1)} %get-tuple-element.36), channel_id=1, source_target_pairs={{0,2},{2,0},{1,3},{3,1},{4,6},{6,4},{5,7},{7,5},{8,10},{10,8},{9,1... | collective-permute-start | bytes 122888 | tf_op jit(solution)/shard_map/ppermute | solution.py:230

commit v12 on v11

--- a/solution.py
+++ b/solution.py
@@ -39,42 +39,52 @@
     ]
 
 
-def fetch_kernel(n, w_hbm, rank_hbm, slot_hbm, start_hbm, factor_ref, spread_ref, *refs):
-    weights, sems, scalar_sems = refs[:n], refs[n], refs[n + 1]
-    rank_ref, slot_ref, start_ref = refs[n + 2 :]
-    scalars = [
-        pltpu.make_async_copy(source, target, scalar_sems.at[j])
-        for j, (source, target) in enumerate(
-            ((rank_hbm, rank_ref), (slot_hbm, slot_ref), (start_hbm, start_ref))
-        )
-    ]
-    for copy in scalars:
-        copy.start()
+def load(w_hbm, first, weights, sems, meanwhile):
     copies = []
-    first = 0
     for j, w_vmem in enumerate(weights):
         copies += weight_copies(w_hbm, first, w_vmem, sems.at[j])
         first += w_vmem.shape[1]
     for copy in copies:
         copy.start()
-    for copy in scalars:
-        copy.wait()
-    slots, rows, rank_columns = factor_ref.shape
-    home = lax.axis_index("gx")
-    row = lax.broadcasted_iota(jnp.int32, (rows, rank_columns), 0)
-    col = lax.broadcasted_iota(jnp.int32, (rows, rank_columns), 1)
-    for s in range(slots):
-        adapter = slot_ref[home * slots + s]
-        rank = rank_ref[adapter]
-        live = (row >= start_ref[adapter]) & (row < start_ref[adapter + 1]) & (col < rank)
-        scale = ADAPTER_ALPHA / jnp.full((rows, rank_columns), rank, jnp.int32).astype(jnp.float32)
-        factor_ref[s] = jnp.where(live, scale, 0.0)
-    adapters = spread_ref.shape[1] // rank_columns
-    for a in range(adapters):
-        live = (row >= start_ref[a]) & (row < start_ref[a + 1])
-        spread_ref[:, a * rank_columns : (a + 1) * rank_columns] = jnp.where(live, 1.0, 0.0)
+    meanwhile()
     for copy in copies:
         copy.wait()
+
+
+def first_load_kernel(n, w_hbm, rank_hbm, slot_hbm, start_hbm, factor_ref, spread_ref, *refs):
+    weights, sems, scalar_sems = refs[:n], refs[n], refs[n + 1]
+    rank_ref, slot_ref, start_ref = refs[n + 2 :]
+
+    def masks():
+        pairs = ((rank_hbm, rank_ref), (slot_hbm, slot_ref), (start_hbm, start_ref))
+        scalars = [
+            pltpu.make_async_copy(source, target, scalar_sems.at[j])
+            for j, (source, target) in enumerate(pairs)
+        ]
+        for copy in scalars:
+            copy.start()
+        for copy in scalars:
+            copy.wait()
+        slots, rows, rank_columns = factor_ref.shape
+        home = lax.axis_index("gx")
+        row = lax.broadcasted_iota(jnp.int32, (rows, rank_columns), 0)
+        col = lax.broadcasted_iota(jnp.int32, (rows, rank_columns), 1)
+        for s in range(slots):
+            adapter = slot_ref[home * slots + s]
+            rank = rank_ref[adapter]
+            live = (row >= start_ref[adapter]) & (row < start_ref[adapter + 1]) & (col < rank)
+            ranks = jnp.full((rows, rank_columns), rank, jnp.int32).astype(jnp.float32)
+            factor_ref[s] = jnp.where(live, ADAPTER_ALPHA / ranks, 0.0)
+        adapters = spread_ref.shape[1] // rank_columns
+        for a in range(adapters):
+            live = (row >= start_ref[a]) & (row < start_ref[a + 1])
+            spread_ref[:, a * rank_columns : (a + 1) * rank_columns] = jnp.where(live, 1.0, 0.0)
+
+    load(w_hbm, 0, weights, sems, masks)
+
+
+def last_load_kernel(n, first, w_hbm, _, __, *refs):
+    load(w_hbm, first, refs[:n], refs[n], lambda: None)
 
 
 def split_wide(value):
@@ -232,9 +242,11 @@
     def spread_out(made, axis, n):
         return [made[0]] + [send(made[k], axis, n, k) for k in range(1, n)]
 
-    half = n_x // 2
-    order = [0, *range(half, n_x), *range(half - 1, 0, -1)]
-    blocks = [hidden] + [send(hidden, "gx", n_x, k) for k in order[1:]]
+    sent = {0: hidden}
+    order = [0, *range(2, n_x, 2), 1, *range(3, n_x, 2)]
+    for k in order[1:]:
+        sent[k] = send(sent[k - 1], "gx", n_x, 1) if k % 2 else send(hidden, "gx", n_x, k)
+    blocks = [sent[k] for k in order]
 
     step = min(512, columns // 4)
     n_w, pieces = 4, 8
@@ -246,24 +258,36 @@
     roomy = params(4 + (rows * depth >> 16))
 
     scalars = (padded_adapter_rank, adapter_in_slot, segment_starts)
+    early = n_w // 2
+    load_cost = cost(300 * query_weight.size, query_weight.size)
     factor, spread, *weights = pl.pallas_call(
-        functools.partial(fetch_kernel, n_w),
+        functools.partial(first_load_kernel, early),
         out_shape=[
             jax.ShapeDtypeStruct((slots, rows, rank_columns), f32),
             jax.ShapeDtypeStruct((rows, adapters * rank_columns), f32),
         ]
-        + [pltpu.VMEM((depth, quarter), query_weight.dtype)] * n_w,
+        + [pltpu.VMEM((depth, quarter), query_weight.dtype)] * early,
         in_specs=[ANY] + [HBM] * 3,
-        out_specs=[VMEM] * (2 + n_w),
+        out_specs=[VMEM] * (2 + early),
         scratch_shapes=[
-            pltpu.SemaphoreType.DMA((n_w, pieces)),
+            pltpu.SemaphoreType.DMA((early, pieces)),
             pltpu.SemaphoreType.DMA((len(scalars),)),
             *[pltpu.SMEM(value.shape, value.dtype) for value in scalars],
         ],
-        cost_estimate=cost(0, 2 * query_weight.size),
-        compiler_params=roomy,
-        name="fetch_weight",
+        cost_estimate=load_cost,
+        compiler_params=roomy,
+        name="first_load",
     )(query_weight, *[pltpu.with_memory_space_constraint(v, pltpu.HBM) for v in scalars])
+    weights += pl.pallas_call(
+        functools.partial(last_load_kernel, n_w - early, early * quarter),
+        out_shape=[pltpu.VMEM((depth, quarter), query_weight.dtype)] * (n_w - early),
+        in_specs=[ANY] * 3,
+        out_specs=[VMEM] * (n_w - early),
+        scratch_shapes=[pltpu.SemaphoreType.DMA((n_w - early, pieces))],
+        cost_estimate=load_cost,
+        compiler_params=roomy,
+        name="last_load",
+    )(query_weight, factor, blocks[1])
     weights = [pltpu.with_memory_space_constraint(w, pltpu.VMEM) for w in weights]
 
     x, small = pl.pallas_call(
@@ -287,7 +311,6 @@
     def shapes(n, shape):
         return [jax.ShapeDtypeStruct(shape, f32 if k == 0 else bf16) for k in range(n)]
 
-    early = n_w // 2
     base_columns = early * quarter
     base = pl.pallas_call(
         functools.partial(base_kernel, early, step),

time: 35.4 us -> 36.7 us (1.037)
  Pallas kernels: 19 us -> 20 us
    pallas_call x1 -> x2, Pallas kernels: 11 us -> 12.1 us  [the longest x1 6.05 us: body(): pl.pallas_call(functools.partial(last_load_kernel, n_w - early, early * q...]
  transfers between devices with their start and end apart: 10 -> 10, of which waited for: 1 -> 1; matrix products, arithmetic and copies ran while one was open for 0% -> 0% of each run, Pallas kernels for 49% -> 51%
where the time goes in v12:
time: 36.7 us; the launch traced here: 36.5 us
  Pallas kernels  20 us (54%)
  starting transfers between devices  13 us (35%)
  waiting for transfers between devices  3.32 us (9%)
    ppermute x10, starting transfers between devices, send(): return lax.ppermute(value, axis, [(j, j ^ k) for j in range(n)])  13 us
    pallas_call x1, Pallas kernels, body(): pl.pallas_call(functools.partial(last_load_kernel, n_w - early, early * q...  6.05 us
    pallas_call x1, Pallas kernels, body(): pl.pallas_call(functools.partial(first_load_kernel, early), out_shape=[ja...  6.02 us
    ppermute x10, waiting for transfers between devices, send(): return lax.ppermute(value, axis, [(j, j ^ k) for j in range(n)])  3.32 us
    pallas_call x2, Pallas kernels, product(): pl.pallas_call(functools.partial(product_kernel, len(some), n_y, n_z, ste...  3.21 us
    pallas_call x1, Pallas kernels, body(): pl.pallas_call(functools.partial(base_kernel, early, step), out_shape=jax...  3.03 us
    pallas_call x1, Pallas kernels, body(): pl.pallas_call(functools.partial(final_kernel, n_y, n_z, step), out_shape...  1.09 us
  transfers between devices with their start and end apart: 10, of which 1 were waited for; matrix products, arithmetic and copies ran while one was open for 0% of the time, Pallas kernels for 51%

profile of v12, /device:TPU:0, one launch (start us, length us, event | category | flops | bytes accessed | tf_op | source)
XLA Modules:
  0.0 36.5 jit_solution(9991927742236451186)
XLA Ops:
  0.0 4.0 %collective-permute-start = (bf16[16,4096]{1,0:T(8,128)(2,1)}, bf16[16,4096]{1,0:T(8,128)(2,1)S(1)}, u32[]{:S(2)}, u32[]{:S(2)}) collective-permute-start(bf16[16,4096]{1,0:T(8,128)(2,1)} %refs_0_.1), channel_id=1, source_target_pairs={{0,8},{4,12},{8,0},{12,4},{1,9},{5,13},{9,1},{13,5},{2,10},{6,14},... | collective-permute-start | bytes 393224 | tf_op jit(solution)/shard_map/ppermute | solution.py:240
  4.0 1.6 %collective-permute-start.1 = (bf16[16,4096]{1,0:T(8,128)(2,1)}, bf16[16,4096]{1,0:T(8,128)(2,1)S(1)}, u32[]{:S(2)}, u32[]{:S(2)}) collective-permute-start(bf16[16,4096]{1,0:T(8,128)(2,1)} %refs_0_.1), channel_id=1, source_target_pairs={{0,4},{4,0},{8,12},{12,8},{1,5},{5,1},{9,13},{13,9},{2,6},{6,2},{1... | collective-permute-start | bytes 393224 | tf_op jit(solution)/shard_map/ppermute | solution.py:240
  5.6 6.0 %first_load.1 = (f32[1,64,64]{2,1,0:T(8,128)S(1)}, f32[64,256]{1,0:T(8,128)S(1)}, bf16[4096,1024]{1,0:T(8,128)(2,1)S(1)}, bf16[4096,1024]{1,0:T(8,128)(2,1)S(1)}) custom-call(bf16[4096,4096]{1,0:T(8,128)(2,1)} %w_hbm.3, s32[4]{0:T(128)} %rank_hbm.1, s32[4]{0:T(128)} %slot_hbm.1, s32[5]{0:T(128)} %start_hbm.1), custom_call_target="tpu_custom_call" | custom-call | flops 5033164800 | bytes 16777216 | tf_op jit(solution)/shard_map/first_load/pallas_call | solution.py:263
  11.6 0.0 collective-permute-done.refs_1_.__
  11.6 0.5 %collective-permute-start.2 = (bf16[16,4096]{1,0:T(8,128)(2,1)S(1)}, bf16[16,4096]{1,0:T(8,128)(2,1)S(1)}, u32[]{:S(2)}, u32[]{:S(2)}) collective-permute-start(bf16[16,4096]{1,0:T(8,128)(2,1)S(1)} %collective-permute-done.refs_1_.__), channel_id=1, source_target_pairs={{0,4},{4,0},{8,12},{12,8},{1,5},{5,1},{9,13},{13,9},{2,6},{6,2},{1... | collective-permute-start | bytes 393224 | tf_op jit(solution)/shard_map/ppermute | solution.py:240
  12.2 6.0 %last_load.1 = (bf16[4096,1024]{1,0:T(8,128)(2,1)S(1)}, bf16[4096,1024]{1,0:T(8,128)(2,1)S(1)}) custom-call(bf16[4096,4096]{1,0:T(8,128)(2,1)} %w_hbm.3, f32[1,64,64]{2,1,0:T(8,128)S(1)} %get-tuple-element.22.factor_ref._, bf16[16,4096]{1,0:T(8,128)(2,1)S(1)} %collective-permute-done.refs_1_.__), custom_call_target="tpu_custom_call" | custom-call | flops 5033164800 | bytes 16777216 | tf_op jit(solution)/shard_map/last_load/pallas_call | solution.py:281
  18.2 0.0 collective-permute-done.2.refs_3_
  18.3 0.4 %scaled_rows.1 = (bf16[64,4096]{1,0:T(8,128)(2,1)S(1)}, bf16[64,256]{1,0:T(8,128)(2,1)S(1)}) custom-call(bf16[4096]{0:T(1024)(128)(2,1)S(1)} %copy-done.3, bf16[1,64,4096]{2,1,0:T(8,128)(2,1)S(1)} %bitcast.1, f32[1,64,64]{2,1,0:T(8,128)S(1)} %get-tuple-element.22.factor_ref._, bf16[16,4096]{1,0:T(8,128)(2,1)S(1)} %copy-done.2, ...), custom_call_target="tpu_custom_call" | custom-call | tf_op jit(solution)/shard_map/scaled_rows/pallas_call | solution.py:293
  18.7 1.6 %collective-permute-start.3 = (bf16[64,256]{1,0:T(8,128)(2,1)S(1)}, bf16[64,256]{1,0:T(8,128)(2,1)S(1)}, u32[]{:S(2)}, u32[]{:S(2)}) collective-permute-start(bf16[64,256]{1,0:T(8,128)(2,1)S(1)} %get-tuple-element.26), channel_id=1, source_target_pairs={{0,4},{4,0},{8,12},{12,8},{1,5},{5,1},{9,13},{13,9},{2,6},{6,2},{1... | collective-permute-start | bytes 98312 | tf_op jit(solution)/shard_map/ppermute | solution.py:240
  20.3 3.0 %first_columns.1.refs_0_ = f32[64,2048]{1,0:T(8,128)S(1)} custom-call(bf16[64,4096]{1,0:T(8,128)(2,1)S(1)} %get-tuple-element.23.x_ref, bf16[4096,1024]{1,0:T(8,128)(2,1)S(1)} %get-tuple-element.24.refs_0_, bf16[4096,1024]{1,0:T(8,128)(2,1)S(1)} %get-tuple-element.25.refs_1_), custom_call_target="tpu_custom_call" | custom-call | flops 1073741824 | bytes 16777216 | tf_op jit(solution)/shard_map/first_columns/pallas_call | solution.py:315
  23.4 1.8 %collective-permute-start.7 = (bf16[64,256]{1,0:T(8,128)(2,1)S(1)}, bf16[64,256]{1,0:T(8,128)(2,1)S(1)}, u32[]{:S(2)}, u32[]{:S(2)}) collective-permute-start(bf16[64,256]{1,0:T(8,128)(2,1)S(1)} %add.6.refs_1_), channel_id=1, source_target_pairs={{0,8},{4,12},{8,0},{12,4},{1,9},{5,13},{9,1},{13,5},{2,10},{6,14},... | collective-permute-start | bytes 98312 | tf_op jit(solution)/shard_map/ppermute | solution.py:240
  25.3 1.6 %middle_columns.1 = (f32[32,3072]{1,0:T(8,128)S(1)}, bf16[32,3072]{1,0:T(8,128)(2,1)S(1)}) custom-call(bf16[64,4096]{1,0:T(8,128)(2,1)S(1)} %get-tuple-element.23.x_ref, f32[64,2048]{1,0:T(8,128)S(1)} %first_columns.1.refs_0_, bf16[64,256]{1,0:T(8,128)(2,1)S(1)} %add.6.refs_1_, bf16[4096,1024]{1,0:T(8,128)(2,1)S(1)} %get-tuple-element.27.refs_2_), custom_call_target="tpu_custom_call" | custom-call | flops 6442450944 | bytes 25165824 | tf_op jit(solution)/shard_map/middle_columns/pallas_call | solution.py:328
  26.9 0.1 collective-permute-start.4
  27.0 0.0 copy-start
  27.0 1.6 %last_columns.1 = (f32[32,1024]{1,0:T(8,128)S(1)}, bf16[32,1024]{1,0:T(8,128)(2,1)S(1)}) custom-call(bf16[64,4096]{1,0:T(8,128)(2,1)S(1)} %get-tuple-element.23.x_ref, bf16[4096,1024]{1,0:T(8,128)(2,1)S(1)} %get-tuple-element.32.refs_0_), custom_call_target="tpu_custom_call" | custom-call | flops 4294967296 | bytes 8388608 | tf_op jit(solution)/shard_map/last_columns/pallas_call | solution.py:328
  28.6 0.6 %collective-permute-start.6 = (bf16[32,1024]{1,0:T(8,128)(2,1)S(1)}, bf16[32,1024]{1,0:T(8,128)(2,1)S(1)}, u32[]{:S(2)}, u32[]{:S(2)}) collective-permute-start(bf16[32,1024]{1,0:T(8,128)(2,1)S(1)} %get-tuple-element.34), channel_id=1, source_target_pairs={{0,1},{1,0},{2,3},{3,2},{4,5},{5,4},{6,7},{7,6},{8,9},{9,8},{10,11... | collective-permute-start | bytes 196616 | tf_op jit(solution)/shard_map/ppermute | solution.py:240
  29.1 0.0 collective-permute-done.7
  29.1 0.1 collective-permute-start.8
  29.3 1.6 %collective-permute-start.5 = (bf16[16,3072]{1,0:T(8,128)(2,1)S(1)}, bf16[16,3072]{1,0:T(8,128)(2,1)S(1)}, u32[]{:S(2)}, u32[]{:S(2)}) collective-permute-start(bf16[16,3072]{1,0:T(8,128)(2,1)S(1)} %get-tuple-element.31), channel_id=1, source_target_pairs={{0,2},{2,0},{1,3},{3,1},{4,6},{6,4},{5,7},{7,5},{8,10},{10,8},{9,1... | collective-permute-start | bytes 294920 | tf_op jit(solution)/shard_map/ppermute | solution.py:240
  30.8 0.0 collective-permute-done.6.refs_1_
  30.9 0.2 last_sums.1
  31.0 1.1 %collective-permute-start.9 = (bf16[16,1280]{1,0:T(8,128)(2,1)S(1)}, bf16[16,1280]{1,0:T(8,128)(2,1)S(1)}, u32[]{:S(2)}, u32[]{:S(2)}) collective-permute-start(bf16[16,1280]{1,0:T(8,128)(2,1)S(1)} %get-tuple-element.36), channel_id=1, source_target_pairs={{0,2},{2,0},{1,3},{3,1},{4,6},{6,4},{5,7},{7,5},{8,10},{10,8},{9,1... | collective-permute-start | bytes 122888 | tf_op jit(solution)/shard_map/ppermute | solution.py:240
  32.1 3.3 %collective-permute-done.9.refs_3_ = bf16[16,1280]{1,0:T(8,128)(2,1)S(1)} collective-permute-done((bf16[16,1280]{1,0:T(8,128)(2,1)S(1)}, bf16[16,1280]{1,0:T(8,128)(2,1)S(1)}, u32[]{:S(2)}, u32[]{:S(2)}) %collective-permute-start.9) | collective-permute-done | bytes 40992 | tf_op jit(solution)/shard_map/ppermute | solution.py:240
  35.4 1.1 %query_rows.1 = bf16[16,4096]{1,0:T(8,128)(2,1)} custom-call(f32[64,256]{1,0:T(8,128)S(1)} %get-tuple-element.21.spread_ref, bf16[4,64,4096]{2,1,0:T(8,128)(2,1)S(1)} %copy-done, f32[16,3072]{1,0:T(8,128)S(1)} %get-tuple-element.30.refs_0_, bf16[16,3072]{1,0:T(8,128)(2,1)S(1)} %collective-permute-done.5.refs_1_, f32[16,1280]{1,0:T(8,128)S(1)} %get-tuple-element.35.refs_2_, ...), custom_call_target="tpu_custom_call" | custom-call | tf_op jit(solution)/shard_map/query_rows/pallas_call | solution.py:360
  (15 shorter events, 0.1 us)
Async XLA Ops:
  0.0 11.6 %collective-permute-start = (bf16[16,4096]{1,0:T(8,128)(2,1)}, bf16[16,4096]{1,0:T(8,128)(2,1)S(1)}, u32[]{:S(2)}, u32[]{:S(2)}) collective-permute-start(bf16[16,4096]{1,0:T(8,128)(2,1)} %refs_0_.1), channel_id=1, source_target_pairs={{0,8},{4,12},{8,0},{12,4},{1,9},{5,13},{9,1},{13,5},{2,10},{6,14},... | collective-permute-start | bytes 393224 | tf_op jit(solution)/shard_map/ppermute | solution.py:240
  4.0 14.2 %collective-permute-start.1 = (bf16[16,4096]{1,0:T(8,128)(2,1)}, bf16[16,4096]{1,0:T(8,128)(2,1)S(1)}, u32[]{:S(2)}, u32[]{:S(2)}) collective-permute-start(bf16[16,4096]{1,0:T(8,128)(2,1)} %refs_0_.1), channel_id=1, source_target_pairs={{0,4},{4,0},{8,12},{12,8},{1,5},{5,1},{9,13},{13,9},{2,6},{6,2},{1... | collective-permute-start | bytes 393224 | tf_op jit(solution)/shard_map/ppermute | solution.py:240
  11.6 6.6 %collective-permute-start.2 = (bf16[16,4096]{1,0:T(8,128)(2,1)S(1)}, bf16[16,4096]{1,0:T(8,128)(2,1)S(1)}, u32[]{:S(2)}, u32[]{:S(2)}) collective-permute-start(bf16[16,4096]{1,0:T(8,128)(2,1)S(1)} %collective-permute-done.refs_1_.__), channel_id=1, source_target_pairs={{0,4},{4,0},{8,12},{12,8},{1,5},{5,1},{9,13},{13,9},{2,6},{6,2},{1... | collective-permute-start | bytes 393224 | tf_op jit(solution)/shard_map/ppermute | solution.py:240
  12.2 6.1 %copy-start.1 = (bf16[1,4096,64]{1,2,0:T(8,128)(2,1)S(1)}, bf16[1,4096,64]{1,2,0:T(8,128)(2,1)}, u32[]{:S(2)}) copy-start(bf16[1,4096,64]{1,2,0:T(8,128)(2,1)} %param.12) | copy-start | bytes 1572868
  12.2 6.1 %copy-start.2 = (bf16[16,4096]{1,0:T(8,128)(2,1)S(1)}, bf16[16,4096]{1,0:T(8,128)(2,1)}, u32[]{:S(2)}) copy-start(bf16[16,4096]{1,0:T(8,128)(2,1)} %refs_0_.1) | copy-start | bytes 393220
  12.2 6.1 %copy-start.3 = (bf16[4096]{0:T(1024)(128)(2,1)S(1)}, bf16[4096]{0:T(1024)(128)(2,1)}, u32[]{:S(2)}) copy-start(bf16[4096]{0:T(1024)(128)(2,1)} %gain_ref.1) | copy-start | bytes 24580
  18.7 4.7 %collective-permute-start.3 = (bf16[64,256]{1,0:T(8,128)(2,1)S(1)}, bf16[64,256]{1,0:T(8,128)(2,1)S(1)}, u32[]{:S(2)}, u32[]{:S(2)}) collective-permute-start(bf16[64,256]{1,0:T(8,128)(2,1)S(1)} %get-tuple-element.26), channel_id=1, source_target_pairs={{0,4},{4,0},{8,12},{12,8},{1,5},{5,1},{9,13},{13,9},{2,6},{6,2},{1... | collective-permute-start | bytes 98312 | tf_op jit(solution)/shard_map/ppermute | solution.py:240
  23.4 5.7 %collective-permute-start.7 = (bf16[64,256]{1,0:T(8,128)(2,1)S(1)}, bf16[64,256]{1,0:T(8,128)(2,1)S(1)}, u32[]{:S(2)}, u32[]{:S(2)}) collective-permute-start(bf16[64,256]{1,0:T(8,128)(2,1)S(1)} %add.6.refs_1_), channel_id=1, source_target_pairs={{0,8},{4,12},{8,0},{12,4},{1,9},{5,13},{9,1},{13,5},{2,10},{6,14},... | collective-permute-start | bytes 98312 | tf_op jit(solution)/shard_map/ppermute | solution.py:240
  26.9 2.4 %collective-permute-start.4 = (bf16[32,3072]{1,0:T(8,128)(2,1)S(1)}, bf16[32,3072]{1,0:T(8,128)(2,1)S(1)}, u32[]{:S(2)}, u32[]{:S(2)}) collective-permute-start(bf16[32,3072]{1,0:T(8,128)(2,1)S(1)} %get-tuple-element.29), channel_id=1, source_target_pairs={{0,1},{1,0},{2,3},{3,2},{4,5},{5,4},{6,7},{7,6},{8,9},{9,8},{10,11... | collective-permute-start | bytes 589832 | tf_op jit(solution)/shard_map/ppermute | solution.py:240
  27.0 8.5 %copy-start = (bf16[4,64,4096]{2,1,0:T(8,128)(2,1)S(1)}, bf16[4,64,4096]{2,1,0:T(8,128)(2,1)}, u32[]{:S(2)}) copy-start(bf16[4,64,4096]{2,1,0:T(8,128)(2,1)} %up_ref.1) | copy-start | bytes 6291460
  28.6 2.3 %collective-permute-start.6 = (bf16[32,1024]{1,0:T(8,128)(2,1)S(1)}, bf16[32,1024]{1,0:T(8,128)(2,1)S(1)}, u32[]{:S(2)}, u32[]{:S(2)}) collective-permute-start(bf16[32,1024]{1,0:T(8,128)(2,1)S(1)} %get-tuple-element.34), channel_id=1, source_target_pairs={{0,1},{1,0},{2,3},{3,2},{4,5},{5,4},{6,7},{7,6},{8,9},{9,8},{10,11... | collective-permute-start | bytes 196616 | tf_op jit(solution)/shard_map/ppermute | solution.py:240
  29.1 1.7 %collective-permute-start.8 = (bf16[64,256]{1,0:T(8,128)(2,1)S(1)}, bf16[64,256]{1,0:T(8,128)(2,1)S(1)}, u32[]{:S(2)}, u32[]{:S(2)}) collective-permute-start(bf16[64,256]{1,0:T(8,128)(2,1)S(1)} %add.7.refs_2_), channel_id=1, source_target_pairs={{0,1},{1,0},{2,3},{3,2},{4,5},{5,4},{6,7},{7,6},{8,9},{9,8},{10,11... | collective-permute-start | bytes 98312 | tf_op jit(solution)/shard_map/ppermute | solution.py:240
  29.3 6.1 %collective-permute-start.5 = (bf16[16,3072]{1,0:T(8,128)(2,1)S(1)}, bf16[16,3072]{1,0:T(8,128)(2,1)S(1)}, u32[]{:S(2)}, u32[]{:S(2)}) collective-permute-start(bf16[16,3072]{1,0:T(8,128)(2,1)S(1)} %get-tuple-element.31), channel_id=1, source_target_pairs={{0,2},{2,0},{1,3},{3,1},{4,6},{6,4},{5,7},{7,5},{8,10},{10,8},{9,1... | collective-permute-start | bytes 294920 | tf_op jit(solution)/shard_map/ppermute | solution.py:240
  31.0 4.4 %collective-permute-start.9 = (bf16[16,1280]{1,0:T(8,128)(2,1)S(1)}, bf16[16,1280]{1,0:T(8,128)(2,1)S(1)}, u32[]{:S(2)}, u32[]{:S(2)}) collective-permute-start(bf16[16,1280]{1,0:T(8,128)(2,1)S(1)} %get-tuple-element.36), channel_id=1, source_target_pairs={{0,2},{2,0},{1,3},{3,1},{4,6},{6,4},{5,7},{7,5},{8,10},{10,8},{9,1... | collective-permute-start | bytes 122888 | tf_op jit(solution)/shard_map/ppermute | solution.py:240

commit v13 on v12

--- a/solution.py
+++ b/solution.py
@@ -138,14 +138,13 @@
 
 
 def multiply(x_ref, weights, step, out, first):
-    width = weights[0].shape[1]
-    for c in range(0, width * len(weights), step):
-        inner = c % width
-        out[:, first + c : first + c + step] = jnp.dot(
-            x_ref[...],
-            weights[c // width][:, inner : inner + step],
-            preferred_element_type=jnp.float32,
-        )
+    for weight in weights:
+        width = weight.shape[1]
+        for c in range(0, width, step):
+            out[:, first + c : first + c + step] = jnp.dot(
+                x_ref[...], weight[:, c : c + step], preferred_element_type=jnp.float32
+            )
+        first += width
 
 
 def base_kernel(n_w, step, x_ref, *refs):
@@ -248,46 +247,50 @@
         sent[k] = send(sent[k - 1], "gx", n_x, 1) if k % 2 else send(hidden, "gx", n_x, k)
     blocks = [sent[k] for k in order]
 
-    step = min(512, columns // 4)
-    n_w, pieces = 4, 8
+    step = min(512, columns // 8 if columns >= 8 * LANES else columns // 4)
+    pieces = 8
     f32, bf16 = jnp.float32, jnp.bfloat16
     slots, rank_columns = slot_down_factors.shape[0], slot_down_factors.shape[2]
     adapters = adapter_up_factors.shape[0]
-    quarter = columns // n_w
+    quarter = columns // 4
+    if quarter % (2 * LANES) == 0:
+        loads = [quarter, quarter, quarter // 2], [quarter // 2, quarter]
+    else:
+        loads = [quarter, quarter], [quarter, quarter]
     kept = n_y * rows_here
     roomy = params(4 + (rows * depth >> 16))
 
     scalars = (padded_adapter_rank, adapter_in_slot, segment_starts)
-    early = n_w // 2
+    weight_hbm = pltpu.with_memory_space_constraint(query_weight, pltpu.HBM)
     load_cost = cost(300 * query_weight.size, query_weight.size)
     factor, spread, *weights = pl.pallas_call(
-        functools.partial(first_load_kernel, early),
+        functools.partial(first_load_kernel, len(loads[0])),
         out_shape=[
             jax.ShapeDtypeStruct((slots, rows, rank_columns), f32),
             jax.ShapeDtypeStruct((rows, adapters * rank_columns), f32),
         ]
-        + [pltpu.VMEM((depth, quarter), query_weight.dtype)] * early,
-        in_specs=[ANY] + [HBM] * 3,
-        out_specs=[VMEM] * (2 + early),
+        + [pltpu.VMEM((depth, wide), query_weight.dtype) for wide in loads[0]],
+        in_specs=[HBM] * 4,
+        out_specs=[VMEM] * (2 + len(loads[0])),
         scratch_shapes=[
-            pltpu.SemaphoreType.DMA((early, pieces)),
+            pltpu.SemaphoreType.DMA((len(loads[0]), pieces)),
             pltpu.SemaphoreType.DMA((len(scalars),)),
             *[pltpu.SMEM(value.shape, value.dtype) for value in scalars],
         ],
         cost_estimate=load_cost,
         compiler_params=roomy,
         name="first_load",
-    )(query_weight, *[pltpu.with_memory_space_constraint(v, pltpu.HBM) for v in scalars])
+    )(weight_hbm, *[pltpu.with_memory_space_constraint(v, pltpu.HBM) for v in scalars])
     weights += pl.pallas_call(
-        functools.partial(last_load_kernel, n_w - early, early * quarter),
-        out_shape=[pltpu.VMEM((depth, quarter), query_weight.dtype)] * (n_w - early),
-        in_specs=[ANY] * 3,
-        out_specs=[VMEM] * (n_w - early),
-        scratch_shapes=[pltpu.SemaphoreType.DMA((n_w - early, pieces))],
+        functools.partial(last_load_kernel, len(loads[1]), sum(loads[0])),
+        out_shape=[pltpu.VMEM((depth, wide), query_weight.dtype) for wide in loads[1]],
+        in_specs=[HBM, ANY, ANY],
+        out_specs=[VMEM] * len(loads[1]),
+        scratch_shapes=[pltpu.SemaphoreType.DMA((len(loads[1]), pieces))],
         cost_estimate=load_cost,
         compiler_params=roomy,
         name="last_load",
-    )(query_weight, factor, blocks[1])
+    )(weight_hbm, factor, blocks[1])
     weights = [pltpu.with_memory_space_constraint(w, pltpu.VMEM) for w in weights]
 
     x, small = pl.pallas_call(
@@ -311,20 +314,20 @@
     def shapes(n, shape):
         return [jax.ShapeDtypeStruct(shape, f32 if k == 0 else bf16) for k in range(n)]
 
-    base_columns = early * quarter
+    base_columns = 2 * quarter
     base = pl.pallas_call(
-        functools.partial(base_kernel, early, step),
+        functools.partial(base_kernel, 2, step),
         out_shape=jax.ShapeDtypeStruct((rows, base_columns), f32),
-        in_specs=[VMEM] * (1 + early),
+        in_specs=[VMEM] * 3,
         out_specs=VMEM,
         cost_estimate=cost(2 * rows * depth * base_columns, 2 * depth * base_columns),
         compiler_params=roomy,
         name="first_columns",
-    )(x, *weights[:early])
+    )(x, *weights[:2])
 
     def product(some, bases, times, name):
         first = sum(part.shape[1] for part in bases[:1])
-        wide = first + len(some) * quarter
+        wide = first + quarter
         made = pl.pallas_call(
             functools.partial(product_kernel, len(some), n_y, n_z, step, first),
             out_shape=shapes(n_z, (kept, wide)),
@@ -337,7 +340,7 @@
         )(x, *bases, *some)
         return spread_out(made, "gz", n_z)
 
-    firsts = product(weights[early:-1], [base, one_hop], 4, "middle_columns")
+    firsts = product(weights[2:-1], [base, one_hop], 4, "middle_columns")
     lasts = product(weights[-1:], [], 8, "last_columns")
     smalls = spread_out([small] * n_z, "gz", n_z)
 

time: 36.7 us -> 35.9 us (0.978)
  starting transfers between devices: 13 us -> 11.7 us
  waiting for transfers between devices: 3.32 us -> 3.79 us
    ppermute x10, starting transfers between devices: 13 us -> 11.7 us  [send(): return lax.ppermute(value, axis, [(j, j ^ k) for j in range(n)])]
    ppermute x10, waiting for transfers between devices: 3.32 us -> 3.79 us  [send(): return lax.ppermute(value, axis, [(j, j ^ k) for j in range(n)])]
  transfers between devices with their start and end apart: 10 -> 10, of which waited for: 1 -> 2; matrix products, arithmetic and copies ran while one was open for 0% -> 0% of each run, Pallas kernels for 51% -> 52%
where the time goes in v13:
time: 35.9 us; the launch traced here: 35.7 us
  Pallas kernels  20 us (56%)
  starting transfers between devices  11.7 us (33%)
  waiting for transfers between devices  3.79 us (11%)
    ppermute x10, starting transfers between devices, send(): return lax.ppermute(value, axis, [(j, j ^ k) for j in range(n)])  11.7 us
    pallas_call x1, Pallas kernels, body(): pl.pallas_call(functools.partial(first_load_kernel, len(loads[0])), out_s...  7.27 us
    pallas_call x1, Pallas kernels, body(): pl.pallas_call(functools.partial(last_load_kernel, len(loads[1]), sum(loa...  4.86 us
    ppermute x10, waiting for transfers between devices, send(): return lax.ppermute(value, axis, [(j, j ^ k) for j in range(n)])  3.79 us
    pallas_call x2, Pallas kernels, product(): pl.pallas_call(functools.partial(product_kernel, len(some), n_y, n_z, ste...  3.17 us
    pallas_call x1, Pallas kernels, body(): pl.pallas_call(functools.partial(base_kernel, 2, step), out_shape=jax.Sha...  3.03 us
    pallas_call x1, Pallas kernels, body(): pl.pallas_call(functools.partial(final_kernel, n_y, n_z, step), out_shape...  1.09 us
  transfers between devices with their start and end apart: 10, of which 2 were waited for; matrix products, arithmetic and copies ran while one was open for 0% of the time, Pallas kernels for 52%

profile of v13, /device:TPU:0, one launch (start us, length us, event | category | flops | bytes accessed | tf_op | source)
XLA Modules:
  0.0 35.7 jit_solution(15841777097067460455)
XLA Ops:
  0.0 4.0 %collective-permute-start = (bf16[16,4096]{1,0:T(8,128)(2,1)}, bf16[16,4096]{1,0:T(8,128)(2,1)S(1)}, u32[]{:S(2)}, u32[]{:S(2)}) collective-permute-start(bf16[16,4096]{1,0:T(8,128)(2,1)} %refs_0_.1), channel_id=1, source_target_pairs={{0,8},{4,12},{8,0},{12,4},{1,9},{5,13},{9,1},{13,5},{2,10},{6,14},... | collective-permute-start | bytes 393224 | tf_op jit(solution)/shard_map/ppermute | solution.py:239
  4.0 1.6 %collective-permute-start.1 = (bf16[16,4096]{1,0:T(8,128)(2,1)}, bf16[16,4096]{1,0:T(8,128)(2,1)S(1)}, u32[]{:S(2)}, u32[]{:S(2)}) collective-permute-start(bf16[16,4096]{1,0:T(8,128)(2,1)} %refs_0_.1), channel_id=1, source_target_pairs={{0,4},{4,0},{8,12},{12,8},{1,5},{5,1},{9,13},{13,9},{2,6},{6,2},{1... | collective-permute-start | bytes 393224 | tf_op jit(solution)/shard_map/ppermute | solution.py:239
  5.6 7.3 %first_load.1 = (f32[1,64,64]{2,1,0:T(8,128)S(1)}, f32[64,256]{1,0:T(8,128)S(1)}, bf16[4096,1024]{1,0:T(8,128)(2,1)S(1)}, bf16[4096,1024]{1,0:T(8,128)(2,1)S(1)}, bf16[4096,512]{1,0:T(8,128)(2,1)S(1)}) custom-call(bf16[4096,4096]{1,0:T(8,128)(2,1)} %w_hbm.3, s32[4]{0:T(128)} %rank_hbm.1, s32[4]{0:T(128)} %slot_hbm.1, s32[5]{0:T(128)} %start_hbm.1), custom_call_target="tpu_custom_call" | custom-call | flops 5033164800 | bytes 16777216 | tf_op jit(solution)/shard_map/first_load/pallas_call | solution.py:266
  12.9 0.0 collective-permute-done.refs_1_.__
  12.9 0.5 %collective-permute-start.2 = (bf16[16,4096]{1,0:T(8,128)(2,1)S(1)}, bf16[16,4096]{1,0:T(8,128)(2,1)S(1)}, u32[]{:S(2)}, u32[]{:S(2)}) collective-permute-start(bf16[16,4096]{1,0:T(8,128)(2,1)S(1)} %collective-permute-done.refs_1_.__), channel_id=1, source_target_pairs={{0,4},{4,0},{8,12},{12,8},{1,5},{5,1},{9,13},{13,9},{2,6},{6,2},{1... | collective-permute-start | bytes 393224 | tf_op jit(solution)/shard_map/ppermute | solution.py:239
  13.4 4.9 %last_load.1 = (bf16[4096,512]{1,0:T(8,128)(2,1)S(1)}, bf16[4096,1024]{1,0:T(8,128)(2,1)S(1)}) custom-call(bf16[4096,4096]{1,0:T(8,128)(2,1)} %w_hbm.3, f32[1,64,64]{2,1,0:T(8,128)S(1)} %get-tuple-element.23.factor_ref._, bf16[16,4096]{1,0:T(8,128)(2,1)S(1)} %collective-permute-done.refs_1_.__), custom_call_target="tpu_custom_call" | custom-call | flops 5033164800 | bytes 16777216 | tf_op jit(solution)/shard_map/last_load/pallas_call | solution.py:284
  18.3 0.4 %scaled_rows.1 = (bf16[64,4096]{1,0:T(8,128)(2,1)S(1)}, bf16[64,256]{1,0:T(8,128)(2,1)S(1)}) custom-call(bf16[4096]{0:T(1024)(128)(2,1)S(1)} %copy-done.3, bf16[1,64,4096]{2,1,0:T(8,128)(2,1)S(1)} %bitcast.1, f32[1,64,64]{2,1,0:T(8,128)S(1)} %get-tuple-element.23.factor_ref._, bf16[16,4096]{1,0:T(8,128)(2,1)S(1)} %copy-done.2, ...), custom_call_target="tpu_custom_call" | custom-call | tf_op jit(solution)/shard_map/scaled_rows/pallas_call | solution.py:296
  18.8 1.6 %collective-permute-start.3 = (bf16[64,256]{1,0:T(8,128)(2,1)S(1)}, bf16[64,256]{1,0:T(8,128)(2,1)S(1)}, u32[]{:S(2)}, u32[]{:S(2)}) collective-permute-start(bf16[64,256]{1,0:T(8,128)(2,1)S(1)} %get-tuple-element.27), channel_id=1, source_target_pairs={{0,4},{4,0},{8,12},{12,8},{1,5},{5,1},{9,13},{13,9},{2,6},{6,2},{1... | collective-permute-start | bytes 98312 | tf_op jit(solution)/shard_map/ppermute | solution.py:239
  20.4 3.0 %first_columns.1.refs_0_ = f32[64,2048]{1,0:T(8,128)S(1)} custom-call(bf16[64,4096]{1,0:T(8,128)(2,1)S(1)} %get-tuple-element.24.x_ref, bf16[4096,1024]{1,0:T(8,128)(2,1)S(1)} %get-tuple-element.25.refs_0_, bf16[4096,1024]{1,0:T(8,128)(2,1)S(1)} %get-tuple-element.26.refs_1_), custom_call_target="tpu_custom_call" | custom-call | flops 1073741824 | bytes 16777216 | tf_op jit(solution)/shard_map/first_columns/pallas_call | solution.py:318
  23.4 0.0 collective-permute-done.3
  23.5 0.6 %collective-permute-start.7 = (bf16[64,256]{1,0:T(8,128)(2,1)S(1)}, bf16[64,256]{1,0:T(8,128)(2,1)S(1)}, u32[]{:S(2)}, u32[]{:S(2)}) collective-permute-start(bf16[64,256]{1,0:T(8,128)(2,1)S(1)} %add.6.refs_1_), channel_id=1, source_target_pairs={{0,8},{4,12},{8,0},{12,4},{1,9},{5,13},{9,1},{13,5},{2,10},{6,14},... | collective-permute-start | bytes 98312 | tf_op jit(solution)/shard_map/ppermute | solution.py:239
  24.1 1.6 %middle_columns.1 = (f32[32,3072]{1,0:T(8,128)S(1)}, bf16[32,3072]{1,0:T(8,128)(2,1)S(1)}) custom-call(bf16[64,4096]{1,0:T(8,128)(2,1)S(1)} %get-tuple-element.24.x_ref, f32[64,2048]{1,0:T(8,128)S(1)} %first_columns.1.refs_0_, bf16[64,256]{1,0:T(8,128)(2,1)S(1)} %add.6.refs_1_, bf16[4096,512]{1,0:T(8,128)(2,1)S(1)} %get-tuple-element.28.refs_2_, ...), custom_call_target="tpu_custom_call" | custom-call | flops 6442450944 | bytes 25165824 | tf_op jit(solution)/shard_map/middle_columns/pallas_call | solution.py:331
  25.6 0.1 collective-permute-start.4
  25.7 0.0 copy-start
  25.7 1.6 %last_columns.1 = (f32[32,1024]{1,0:T(8,128)S(1)}, bf16[32,1024]{1,0:T(8,128)(2,1)S(1)}) custom-call(bf16[64,4096]{1,0:T(8,128)(2,1)S(1)} %get-tuple-element.24.x_ref, bf16[4096,1024]{1,0:T(8,128)(2,1)S(1)} %get-tuple-element.34.refs_0_), custom_call_target="tpu_custom_call" | custom-call | flops 4294967296 | bytes 8388608 | tf_op jit(solution)/shard_map/last_columns/pallas_call | solution.py:331
  27.3 0.6 %collective-permute-start.6 = (bf16[32,1024]{1,0:T(8,128)(2,1)S(1)}, bf16[32,1024]{1,0:T(8,128)(2,1)S(1)}, u32[]{:S(2)}, u32[]{:S(2)}) collective-permute-start(bf16[32,1024]{1,0:T(8,128)(2,1)S(1)} %get-tuple-element.36), channel_id=1, source_target_pairs={{0,1},{1,0},{2,3},{3,2},{4,5},{5,4},{6,7},{7,6},{8,9},{9,8},{10,11... | collective-permute-start | bytes 196616 | tf_op jit(solution)/shard_map/ppermute | solution.py:239
  27.9 0.5 %collective-permute-done.7 = bf16[64,256]{1,0:T(8,128)(2,1)S(1)} collective-permute-done((bf16[64,256]{1,0:T(8,128)(2,1)S(1)}, bf16[64,256]{1,0:T(8,128)(2,1)S(1)}, u32[]{:S(2)}, u32[]{:S(2)}) %collective-permute-start.7) | collective-permute-done | bytes 32800 | tf_op jit(solution)/shard_map/ppermute | solution.py:239
  28.4 0.1 collective-permute-start.8
  28.5 0.1 first_sums.1
  28.5 1.6 %collective-permute-start.5 = (bf16[16,3072]{1,0:T(8,128)(2,1)S(1)}, bf16[16,3072]{1,0:T(8,128)(2,1)S(1)}, u32[]{:S(2)}, u32[]{:S(2)}) collective-permute-start(bf16[16,3072]{1,0:T(8,128)(2,1)S(1)} %get-tuple-element.33), channel_id=1, source_target_pairs={{0,2},{2,0},{1,3},{3,1},{4,6},{6,4},{5,7},{7,5},{8,10},{10,8},{9,1... | collective-permute-start | bytes 294920 | tf_op jit(solution)/shard_map/ppermute | solution.py:239
  30.1 0.2 last_sums.1
  30.2 1.1 %collective-permute-start.9 = (bf16[16,1280]{1,0:T(8,128)(2,1)S(1)}, bf16[16,1280]{1,0:T(8,128)(2,1)S(1)}, u32[]{:S(2)}, u32[]{:S(2)}) collective-permute-start(bf16[16,1280]{1,0:T(8,128)(2,1)S(1)} %get-tuple-element.38), channel_id=1, source_target_pairs={{0,2},{2,0},{1,3},{3,1},{4,6},{6,4},{5,7},{7,5},{8,10},{10,8},{9,1... | collective-permute-start | bytes 122888 | tf_op jit(solution)/shard_map/ppermute | solution.py:239
  31.3 3.3 %collective-permute-done.9.refs_3_ = bf16[16,1280]{1,0:T(8,128)(2,1)S(1)} collective-permute-done((bf16[16,1280]{1,0:T(8,128)(2,1)S(1)}, bf16[16,1280]{1,0:T(8,128)(2,1)S(1)}, u32[]{:S(2)}, u32[]{:S(2)}) %collective-permute-start.9) | collective-permute-done | bytes 40992 | tf_op jit(solution)/shard_map/ppermute | solution.py:239
  34.7 1.1 %query_rows.1 = bf16[16,4096]{1,0:T(8,128)(2,1)} custom-call(f32[64,256]{1,0:T(8,128)S(1)} %get-tuple-element.22.spread_ref, bf16[4,64,4096]{2,1,0:T(8,128)(2,1)S(1)} %copy-done, f32[16,3072]{1,0:T(8,128)S(1)} %get-tuple-element.32.refs_0_, bf16[16,3072]{1,0:T(8,128)(2,1)S(1)} %collective-permute-done.5.refs_1_, f32[16,1280]{1,0:T(8,128)S(1)} %get-tuple-element.37.refs_2_, ...), custom_call_target="tpu_custom_call" | custom-call | tf_op jit(solution)/shard_map/query_rows/pallas_call | solution.py:363
  (15 shorter events, 0.1 us)
Async XLA Ops:
  0.0 12.9 %collective-permute-start = (bf16[16,4096]{1,0:T(8,128)(2,1)}, bf16[16,4096]{1,0:T(8,128)(2,1)S(1)}, u32[]{:S(2)}, u32[]{:S(2)}) collective-permute-start(bf16[16,4096]{1,0:T(8,128)(2,1)} %refs_0_.1), channel_id=1, source_target_pairs={{0,8},{4,12},{8,0},{12,4},{1,9},{5,13},{9,1},{13,5},{2,10},{6,14},... | collective-permute-start | bytes 393224 | tf_op jit(solution)/shard_map/ppermute | solution.py:239
  4.0 14.3 %collective-permute-start.1 = (bf16[16,4096]{1,0:T(8,128)(2,1)}, bf16[16,4096]{1,0:T(8,128)(2,1)S(1)}, u32[]{:S(2)}, u32[]{:S(2)}) collective-permute-start(bf16[16,4096]{1,0:T(8,128)(2,1)} %refs_0_.1), channel_id=1, source_target_pairs={{0,4},{4,0},{8,12},{12,8},{1,5},{5,1},{9,13},{13,9},{2,6},{6,2},{1... | collective-permute-start | bytes 393224 | tf_op jit(solution)/shard_map/ppermute | solution.py:239
  12.9 5.4 %collective-permute-start.2 = (bf16[16,4096]{1,0:T(8,128)(2,1)S(1)}, bf16[16,4096]{1,0:T(8,128)(2,1)S(1)}, u32[]{:S(2)}, u32[]{:S(2)}) collective-permute-start(bf16[16,4096]{1,0:T(8,128)(2,1)S(1)} %collective-permute-done.refs_1_.__), channel_id=1, source_target_pairs={{0,4},{4,0},{8,12},{12,8},{1,5},{5,1},{9,13},{13,9},{2,6},{6,2},{1... | collective-permute-start | bytes 393224 | tf_op jit(solution)/shard_map/ppermute | solution.py:239
  13.4 4.9 %copy-start.1 = (bf16[1,4096,64]{1,2,0:T(8,128)(2,1)S(1)}, bf16[1,4096,64]{1,2,0:T(8,128)(2,1)}, u32[]{:S(2)}) copy-start(bf16[1,4096,64]{1,2,0:T(8,128)(2,1)} %param.12) | copy-start | bytes 1572868
  13.4 4.9 %copy-start.2 = (bf16[16,4096]{1,0:T(8,128)(2,1)S(1)}, bf16[16,4096]{1,0:T(8,128)(2,1)}, u32[]{:S(2)}) copy-start(bf16[16,4096]{1,0:T(8,128)(2,1)} %refs_0_.1) | copy-start | bytes 393220
  13.4 4.9 %copy-start.3 = (bf16[4096]{0:T(1024)(128)(2,1)S(1)}, bf16[4096]{0:T(1024)(128)(2,1)}, u32[]{:S(2)}) copy-start(bf16[4096]{0:T(1024)(128)(2,1)} %gain_ref.1) | copy-start | bytes 24580
  18.8 4.7 %collective-permute-start.3 = (bf16[64,256]{1,0:T(8,128)(2,1)S(1)}, bf16[64,256]{1,0:T(8,128)(2,1)S(1)}, u32[]{:S(2)}, u32[]{:S(2)}) collective-permute-start(bf16[64,256]{1,0:T(8,128)(2,1)S(1)} %get-tuple-element.27), channel_id=1, source_target_pairs={{0,4},{4,0},{8,12},{12,8},{1,5},{5,1},{9,13},{13,9},{2,6},{6,2},{1... | collective-permute-start | bytes 98312 | tf_op jit(solution)/shard_map/ppermute | solution.py:239
  23.5 4.9 %collective-permute-start.7 = (bf16[64,256]{1,0:T(8,128)(2,1)S(1)}, bf16[64,256]{1,0:T(8,128)(2,1)S(1)}, u32[]{:S(2)}, u32[]{:S(2)}) collective-permute-start(bf16[64,256]{1,0:T(8,128)(2,1)S(1)} %add.6.refs_1_), channel_id=1, source_target_pairs={{0,8},{4,12},{8,0},{12,4},{1,9},{5,13},{9,1},{13,5},{2,10},{6,14},... | collective-permute-start | bytes 98312 | tf_op jit(solution)/shard_map/ppermute | solution.py:239
  25.6 2.8 %collective-permute-start.4 = (bf16[32,3072]{1,0:T(8,128)(2,1)S(1)}, bf16[32,3072]{1,0:T(8,128)(2,1)S(1)}, u32[]{:S(2)}, u32[]{:S(2)}) collective-permute-start(bf16[32,3072]{1,0:T(8,128)(2,1)S(1)} %get-tuple-element.31), channel_id=1, source_target_pairs={{0,1},{1,0},{2,3},{3,2},{4,5},{5,4},{6,7},{7,6},{8,9},{9,8},{10,11... | collective-permute-start | bytes 589832 | tf_op jit(solution)/shard_map/ppermute | solution.py:239
  25.7 8.9 %copy-start = (bf16[4,64,4096]{2,1,0:T(8,128)(2,1)S(1)}, bf16[4,64,4096]{2,1,0:T(8,128)(2,1)}, u32[]{:S(2)}) copy-start(bf16[4,64,4096]{2,1,0:T(8,128)(2,1)} %up_ref.1) | copy-start | bytes 6291460
  27.3 2.7 %collective-permute-start.6 = (bf16[32,1024]{1,0:T(8,128)(2,1)S(1)}, bf16[32,1024]{1,0:T(8,128)(2,1)S(1)}, u32[]{:S(2)}, u32[]{:S(2)}) collective-permute-start(bf16[32,1024]{1,0:T(8,128)(2,1)S(1)} %get-tuple-element.36), channel_id=1, source_target_pairs={{0,1},{1,0},{2,3},{3,2},{4,5},{5,4},{6,7},{7,6},{8,9},{9,8},{10,11... | collective-permute-start | bytes 196616 | tf_op jit(solution)/shard_map/ppermute | solution.py:239
  28.4 1.7 %collective-permute-start.8 = (bf16[64,256]{1,0:T(8,128)(2,1)S(1)}, bf16[64,256]{1,0:T(8,128)(2,1)S(1)}, u32[]{:S(2)}, u32[]{:S(2)}) collective-permute-start(bf16[64,256]{1,0:T(8,128)(2,1)S(1)} %add.7.refs_2_), channel_id=1, source_target_pairs={{0,1},{1,0},{2,3},{3,2},{4,5},{5,4},{6,7},{7,6},{8,9},{9,8},{10,11... | collective-permute-start | bytes 98312 | tf_op jit(solution)/shard_map/ppermute | solution.py:239
  28.5 6.1 %collective-permute-start.5 = (bf16[16,3072]{1,0:T(8,128)(2,1)S(1)}, bf16[16,3072]{1,0:T(8,128)(2,1)S(1)}, u32[]{:S(2)}, u32[]{:S(2)}) collective-permute-start(bf16[16,3072]{1,0:T(8,128)(2,1)S(1)} %get-tuple-element.33), channel_id=1, source_target_pairs={{0,2},{2,0},{1,3},{3,1},{4,6},{6,4},{5,7},{7,5},{8,10},{10,8},{9,1... | collective-permute-start | bytes 294920 | tf_op jit(solution)/shard_map/ppermute | solution.py:239
  30.2 4.4 %collective-permute-start.9 = (bf16[16,1280]{1,0:T(8,128)(2,1)S(1)}, bf16[16,1280]{1,0:T(8,128)(2,1)S(1)}, u32[]{:S(2)}, u32[]{:S(2)}) collective-permute-start(bf16[16,1280]{1,0:T(8,128)(2,1)S(1)} %get-tuple-element.38), channel_id=1, source_target_pairs={{0,2},{2,0},{1,3},{3,1},{4,6},{6,4},{5,7},{7,5},{8,10},{10,8},{9,1... | collective-permute-start | bytes 122888 | tf_op jit(solution)/shard_map/ppermute | solution.py:239

commit v14 on v11

--- a/solution.py
+++ b/solution.py
@@ -128,18 +128,23 @@
 
 
 def multiply(x_ref, weights, step, out, first):
-    width = weights[0].shape[1]
-    for c in range(0, width * len(weights), step):
-        inner = c % width
-        out[:, first + c : first + c + step] = jnp.dot(
-            x_ref[...],
-            weights[c // width][:, inner : inner + step],
-            preferred_element_type=jnp.float32,
-        )
-
-
-def base_kernel(n_w, step, x_ref, *refs):
-    multiply(x_ref, refs[:n_w], step, refs[n_w], 0)
+    for weight in weights:
+        width = weight.shape[1]
+        for c in range(0, width, step):
+            out[:, first + c : first + c + step] = jnp.dot(
+                x_ref[...], weight[:, c : c + step], preferred_element_type=jnp.float32
+            )
+        first += width
+
+
+def base_kernel(n_w, first, step, w_hbm, x_ref, *refs):
+    weights, out_ref, rest = refs[:n_w], refs[n_w], refs[n_w + 1 :]
+    copies = weight_copies(w_hbm, first, *rest) if rest else []
+    for copy in copies:
+        copy.start()
+    multiply(x_ref, weights, step, out_ref, 0)
+    for copy in copies:
+        copy.wait()
 
 
 def product_kernel(n_w, n_y, n_z, step, first, x_ref, *refs):
@@ -232,38 +237,40 @@
     def spread_out(made, axis, n):
         return [made[0]] + [send(made[k], axis, n, k) for k in range(1, n)]
 
-    half = n_x // 2
-    order = [0, *range(half, n_x), *range(half - 1, 0, -1)]
+    order = [0, *range(n_x - 1, 0, -1)]
     blocks = [hidden] + [send(hidden, "gx", n_x, k) for k in order[1:]]
 
     step = min(512, columns // 4)
-    n_w, pieces = 4, 8
+    pieces = 8
     f32, bf16 = jnp.float32, jnp.bfloat16
     slots, rank_columns = slot_down_factors.shape[0], slot_down_factors.shape[2]
     adapters = adapter_up_factors.shape[0]
-    quarter = columns // n_w
+    quarter = columns // 4
+    late = quarter // 2 if quarter % (2 * LANES) == 0 else 0
+    loads = [quarter] * 3 + [quarter - late]
+    weight_hbm = pltpu.with_memory_space_constraint(query_weight, pltpu.HBM)
     kept = n_y * rows_here
     roomy = params(4 + (rows * depth >> 16))
 
     scalars = (padded_adapter_rank, adapter_in_slot, segment_starts)
     factor, spread, *weights = pl.pallas_call(
-        functools.partial(fetch_kernel, n_w),
+        functools.partial(fetch_kernel, len(loads)),
         out_shape=[
             jax.ShapeDtypeStruct((slots, rows, rank_columns), f32),
             jax.ShapeDtypeStruct((rows, adapters * rank_columns), f32),
         ]
-        + [pltpu.VMEM((depth, quarter), query_weight.dtype)] * n_w,
-        in_specs=[ANY] + [HBM] * 3,
-        out_specs=[VMEM] * (2 + n_w),
+        + [pltpu.VMEM((depth, wide), query_weight.dtype) for wide in loads],
+        in_specs=[HBM] * 4,
+        out_specs=[VMEM] * (2 + len(loads)),
         scratch_shapes=[
-            pltpu.SemaphoreType.DMA((n_w, pieces)),
+            pltpu.SemaphoreType.DMA((len(loads), pieces)),
             pltpu.SemaphoreType.DMA((len(scalars),)),
             *[pltpu.SMEM(value.shape, value.dtype) for value in scalars],
         ],
         cost_estimate=cost(0, 2 * query_weight.size),
         compiler_params=roomy,
         name="fetch_weight",
-    )(query_weight, *[pltpu.with_memory_space_constraint(v, pltpu.HBM) for v in scalars])
+    )(weight_hbm, *[pltpu.with_memory_space_constraint(v, pltpu.HBM) for v in scalars])
     weights = [pltpu.with_memory_space_constraint(w, pltpu.VMEM) for w in weights]
 
     x, small = pl.pallas_call(
@@ -287,21 +294,22 @@
     def shapes(n, shape):
         return [jax.ShapeDtypeStruct(shape, f32 if k == 0 else bf16) for k in range(n)]
 
-    early = n_w // 2
-    base_columns = early * quarter
-    base = pl.pallas_call(
-        functools.partial(base_kernel, early, step),
-        out_shape=jax.ShapeDtypeStruct((rows, base_columns), f32),
-        in_specs=[VMEM] * (1 + early),
-        out_specs=VMEM,
-        cost_estimate=cost(2 * rows * depth * base_columns, 2 * depth * base_columns),
+    base, *rest = pl.pallas_call(
+        functools.partial(base_kernel, 2, columns - late, step),
+        out_shape=[jax.ShapeDtypeStruct((rows, 2 * quarter), f32)]
+        + ([pltpu.VMEM((depth, late), query_weight.dtype)] if late else []),
+        in_specs=[HBM] + [VMEM] * 3,
+        out_specs=[VMEM] * (2 if late else 1),
+        scratch_shapes=[pltpu.SemaphoreType.DMA((pieces,))] if late else [],
+        cost_estimate=cost(4 * rows * depth * quarter, 4 * depth * quarter),
         compiler_params=roomy,
         name="first_columns",
-    )(x, *weights[:early])
+    )(weight_hbm, x, *weights[:2])
+    weights += [pltpu.with_memory_space_constraint(w, pltpu.VMEM) for w in rest]
 
     def product(some, bases, times, name):
         first = sum(part.shape[1] for part in bases[:1])
-        wide = first + len(some) * quarter
+        wide = first + quarter
         made = pl.pallas_call(
             functools.partial(product_kernel, len(some), n_y, n_z, step, first),
             out_shape=shapes(n_z, (kept, wide)),
@@ -314,8 +322,8 @@
         )(x, *bases, *some)
         return spread_out(made, "gz", n_z)
 
-    firsts = product(weights[early:-1], [base, one_hop], 4, "middle_columns")
-    lasts = product(weights[-1:], [], 8, "last_columns")
+    firsts = product(weights[2:3], [base, one_hop], 4, "middle_columns")
+    lasts = product(weights[3:], [], 8, "last_columns")
     smalls = spread_out([small] * n_z, "gz", n_z)
 
     def chip_sums(parts, sides, name):

time: 35.4 us -> 36.1 us (1.020)
  Pallas kernels: 19 us -> 19.8 us
    pallas_call x2, Pallas kernels: 14 us -> 14.9 us  [the longest x1 9.76 us: body(): pl.pallas_call(functools.partial(fetch_kernel, len(loads)), out_shape=[ja...]
  transfers between devices with their start and end apart: 10 -> 10, of which waited for: 1 -> 1; matrix products, arithmetic and copies ran while one was open for 0% -> 0% of each run, Pallas kernels for 49% -> 51%
where the time goes in v14:
time: 36.1 us; the launch traced here: 36 us
  Pallas kernels  19.8 us (55%)
  starting transfers between devices  12.7 us (35%)
  waiting for transfers between devices  3.32 us (9%)
    ppermute x10, starting transfers between devices, send(): return lax.ppermute(value, axis, [(j, j ^ k) for j in range(n)])  12.7 us
    pallas_call x1, Pallas kernels, body(): pl.pallas_call(functools.partial(fetch_kernel, len(loads)), out_shape=[ja...  9.76 us
    pallas_call x1, Pallas kernels, body(): pl.pallas_call(functools.partial(base_kernel, 2, columns - late, step), o...  5.14 us
    ppermute x10, waiting for transfers between devices, send(): return lax.ppermute(value, axis, [(j, j ^ k) for j in range(n)])  3.32 us
    pallas_call x2, Pallas kernels, product(): pl.pallas_call(functools.partial(product_kernel, len(some), n_y, n_z, ste...  3.19 us
    pallas_call x1, Pallas kernels, body(): pl.pallas_call(functools.partial(final_kernel, n_y, n_z, step), out_shape...  1.09 us
  transfers between devices with their start and end apart: 10, of which 1 were waited for; matrix products, arithmetic and copies ran while one was open for 0% of the time, Pallas kernels for 51%

profile of v14, /device:TPU:0, one launch (start us, length us, event | category | flops | bytes accessed | tf_op | source)
XLA Modules:
  0.0 36.0 jit_solution(18345266381847959279)
XLA Ops:
  0.0 4.1 %collective-permute-start.1 = (bf16[16,4096]{1,0:T(8,128)(2,1)}, bf16[16,4096]{1,0:T(8,128)(2,1)S(1)}, u32[]{:S(2)}, u32[]{:S(2)}) collective-permute-start(bf16[16,4096]{1,0:T(8,128)(2,1)} %refs_0_.1), channel_id=1, source_target_pairs={{0,8},{4,12},{8,0},{12,4},{1,9},{5,13},{9,1},{13,5},{2,10},{6,14},... | collective-permute-start | bytes 393224 | tf_op jit(solution)/shard_map/ppermute | solution.py:235
  4.1 1.3 %collective-permute-start = (bf16[16,4096]{1,0:T(8,128)(2,1)}, bf16[16,4096]{1,0:T(8,128)(2,1)S(1)}, u32[]{:S(2)}, u32[]{:S(2)}) collective-permute-start(bf16[16,4096]{1,0:T(8,128)(2,1)} %refs_0_.1), channel_id=1, source_target_pairs={{0,12},{4,8},{8,4},{12,0},{1,13},{5,9},{9,5},{13,1},{2,14},{6,10},... | collective-permute-start | bytes 393224 | tf_op jit(solution)/shard_map/ppermute | solution.py:235
  5.5 0.2 collective-permute-start.2
  5.7 9.8 %fetch_weight.1 = (f32[1,64,64]{2,1,0:T(8,128)S(1)}, f32[64,256]{1,0:T(8,128)S(1)}, bf16[4096,1024]{1,0:T(8,128)(2,1)S(1)}, bf16[4096,1024]{1,0:T(8,128)(2,1)S(1...) custom-call(bf16[4096,4096]{1,0:T(8,128)(2,1)} %w_hbm.3, s32[4]{0:T(128)} %rank_hbm.1, s32[4]{0:T(128)} %slot_hbm.1, ...), custom_call_target="tpu_custom_call" | custom-call | bytes 33554432 | tf_op jit(solution)/shard_map/fetch_weight/pallas_call | solution.py:256
  15.5 0.0 collective-permute-done.1.refs_2_
  15.5 0.0 collective-permute-done.refs_1_
  15.5 0.0 collective-permute-done.2.refs_3_
  15.5 0.4 %scaled_rows.1 = (bf16[64,4096]{1,0:T(8,128)(2,1)S(1)}, bf16[64,256]{1,0:T(8,128)(2,1)S(1)}) custom-call(bf16[4096]{0:T(1024)(128)(2,1)S(1)} %copy-done.3, bf16[1,64,4096]{2,1,0:T(8,128)(2,1)S(1)} %bitcast.1, f32[1,64,64]{2,1,0:T(8,128)S(1)} %get-tuple-element.24.factor_ref, bf16[16,4096]{1,0:T(8,128)(2,1)S(1)} %copy-done.2, ...), custom_call_target="tpu_custom_call" | custom-call | tf_op jit(solution)/shard_map/scaled_rows/pallas_call | solution.py:276
  16.0 1.9 %collective-permute-start.3 = (bf16[64,256]{1,0:T(8,128)(2,1)S(1)}, bf16[64,256]{1,0:T(8,128)(2,1)S(1)}, u32[]{:S(2)}, u32[]{:S(2)}) collective-permute-start(bf16[64,256]{1,0:T(8,128)(2,1)S(1)} %get-tuple-element.29), channel_id=1, source_target_pairs={{0,4},{4,0},{8,12},{12,8},{1,5},{5,1},{9,13},{13,9},{2,6},{6,2},{1... | collective-permute-start | bytes 98312 | tf_op jit(solution)/shard_map/ppermute | solution.py:235
  17.8 5.1 %first_columns.1 = (f32[64,2048]{1,0:T(8,128)S(1)}, bf16[4096,512]{1,0:T(8,128)(2,1)S(1)}) custom-call(bf16[4096,4096]{1,0:T(8,128)(2,1)} %w_hbm.3, bf16[64,4096]{1,0:T(8,128)(2,1)S(1)} %get-tuple-element.25.x_ref, bf16[4096,1024]{1,0:T(8,128)(2,1)S(1)} %get-tuple-element.26.refs_0_, bf16[4096,1024]{1,0:T(8,128)(2,1)S(1)} %get-tuple-element.27.refs_1_), custom_call_target="tpu_custom_call" | custom-call | flops 1073741824 | bytes 16777216 | tf_op jit(solution)/shard_map/first_columns/pallas_call | solution.py:297
  23.0 0.0 collective-permute-done.3
  23.0 1.8 %collective-permute-start.7 = (bf16[64,256]{1,0:T(8,128)(2,1)S(1)}, bf16[64,256]{1,0:T(8,128)(2,1)S(1)}, u32[]{:S(2)}, u32[]{:S(2)}) collective-permute-start(bf16[64,256]{1,0:T(8,128)(2,1)S(1)} %add.6.refs_1_), channel_id=1, source_target_pairs={{0,8},{4,12},{8,0},{12,4},{1,9},{5,13},{9,1},{13,5},{2,10},{6,14},... | collective-permute-start | bytes 98312 | tf_op jit(solution)/shard_map/ppermute | solution.py:235
  24.8 1.6 %middle_columns.1 = (f32[32,3072]{1,0:T(8,128)S(1)}, bf16[32,3072]{1,0:T(8,128)(2,1)S(1)}) custom-call(bf16[64,4096]{1,0:T(8,128)(2,1)S(1)} %get-tuple-element.25.x_ref, f32[64,2048]{1,0:T(8,128)S(1)} %get-tuple-element.28.refs_0_, bf16[64,256]{1,0:T(8,128)(2,1)S(1)} %add.6.refs_1_, bf16[4096,1024]{1,0:T(8,128)(2,1)S(1)} %get-tuple-element.30.refs_2_), custom_call_target="tpu_custom_call" | custom-call | flops 6442450944 | bytes 25165824 | tf_op jit(solution)/shard_map/middle_columns/pallas_call | solution.py:313
  26.4 0.1 collective-permute-start.4
  26.5 0.0 copy-start
  26.5 1.6 %last_columns.1 = (f32[32,1024]{1,0:T(8,128)S(1)}, bf16[32,1024]{1,0:T(8,128)(2,1)S(1)}) custom-call(bf16[64,4096]{1,0:T(8,128)(2,1)S(1)} %get-tuple-element.25.x_ref, bf16[4096,512]{1,0:T(8,128)(2,1)S(1)} %get-tuple-element.35.refs_0_, bf16[4096,512]{1,0:T(8,128)(2,1)S(1)} %get-tuple-element.36.refs_1_), custom_call_target="tpu_custom_call" | custom-call | flops 4294967296 | bytes 8388608 | tf_op jit(solution)/shard_map/last_columns/pallas_call | solution.py:313
  28.0 0.6 %collective-permute-start.6 = (bf16[32,1024]{1,0:T(8,128)(2,1)S(1)}, bf16[32,1024]{1,0:T(8,128)(2,1)S(1)}, u32[]{:S(2)}, u32[]{:S(2)}) collective-permute-start(bf16[32,1024]{1,0:T(8,128)(2,1)S(1)} %get-tuple-element.38), channel_id=1, source_target_pairs={{0,1},{1,0},{2,3},{3,2},{4,5},{5,4},{6,7},{7,6},{8,9},{9,8},{10,11... | collective-permute-start | bytes 196616 | tf_op jit(solution)/shard_map/ppermute | solution.py:235
  28.6 0.1 collective-permute-start.8
  28.8 1.6 %collective-permute-start.5 = (bf16[16,3072]{1,0:T(8,128)(2,1)S(1)}, bf16[16,3072]{1,0:T(8,128)(2,1)S(1)}, u32[]{:S(2)}, u32[]{:S(2)}) collective-permute-start(bf16[16,3072]{1,0:T(8,128)(2,1)S(1)} %get-tuple-element.34), channel_id=1, source_target_pairs={{0,2},{2,0},{1,3},{3,1},{4,6},{6,4},{5,7},{7,5},{8,10},{10,8},{9,1... | collective-permute-start | bytes 294920 | tf_op jit(solution)/shard_map/ppermute | solution.py:235
  30.3 0.0 collective-permute-done.8.refs_3_
  30.3 0.2 last_sums.1
  30.5 1.1 %collective-permute-start.9 = (bf16[16,1280]{1,0:T(8,128)(2,1)S(1)}, bf16[16,1280]{1,0:T(8,128)(2,1)S(1)}, u32[]{:S(2)}, u32[]{:S(2)}) collective-permute-start(bf16[16,1280]{1,0:T(8,128)(2,1)S(1)} %get-tuple-element.40), channel_id=1, source_target_pairs={{0,2},{2,0},{1,3},{3,1},{4,6},{6,4},{5,7},{7,5},{8,10},{10,8},{9,1... | collective-permute-start | bytes 122888 | tf_op jit(solution)/shard_map/ppermute | solution.py:235
  31.6 3.3 %collective-permute-done.9.refs_3_ = bf16[16,1280]{1,0:T(8,128)(2,1)S(1)} collective-permute-done((bf16[16,1280]{1,0:T(8,128)(2,1)S(1)}, bf16[16,1280]{1,0:T(8,128)(2,1)S(1)}, u32[]{:S(2)}, u32[]{:S(2)}) %collective-permute-start.9) | collective-permute-done | bytes 40992 | tf_op jit(solution)/shard_map/ppermute | solution.py:235
  34.9 1.1 %query_rows.1 = bf16[16,4096]{1,0:T(8,128)(2,1)} custom-call(f32[64,256]{1,0:T(8,128)S(1)} %get-tuple-element.23.spread_ref, bf16[4,64,4096]{2,1,0:T(8,128)(2,1)S(1)} %copy-done, f32[16,3072]{1,0:T(8,128)S(1)} %get-tuple-element.33.refs_0_, bf16[16,3072]{1,0:T(8,128)(2,1)S(1)} %collective-permute-done.5.refs_1_, f32[16,1280]{1,0:T(8,128)S(1)} %get-tuple-element.39.refs_2_, ...), custom_call_target="tpu_custom_call" | custom-call | tf_op jit(solution)/shard_map/query_rows/pallas_call | solution.py:345
  (14 shorter events, 0.1 us)
Async XLA Ops:
  0.0 15.5 %copy-start.2 = (bf16[16,4096]{1,0:T(8,128)(2,1)S(1)}, bf16[16,4096]{1,0:T(8,128)(2,1)}, u32[]{:S(2)}) copy-start(bf16[16,4096]{1,0:T(8,128)(2,1)} %refs_0_.1) | copy-start | bytes 393220
  0.0 15.5 %copy-start.1 = (bf16[1,4096,64]{1,2,0:T(8,128)(2,1)S(1)}, bf16[1,4096,64]{1,2,0:T(8,128)(2,1)}, u32[]{:S(2)}) copy-start(bf16[1,4096,64]{1,2,0:T(8,128)(2,1)} %param.12) | copy-start | bytes 1572868
  0.0 15.5 %copy-start.3 = (bf16[4096]{0:T(1024)(128)(2,1)S(1)}, bf16[4096]{0:T(1024)(128)(2,1)}, u32[]{:S(2)}) copy-start(bf16[4096]{0:T(1024)(128)(2,1)} %gain_ref.1) | copy-start | bytes 24580
  0.0 15.5 %collective-permute-start.1 = (bf16[16,4096]{1,0:T(8,128)(2,1)}, bf16[16,4096]{1,0:T(8,128)(2,1)S(1)}, u32[]{:S(2)}, u32[]{:S(2)}) collective-permute-start(bf16[16,4096]{1,0:T(8,128)(2,1)} %refs_0_.1), channel_id=1, source_target_pairs={{0,8},{4,12},{8,0},{12,4},{1,9},{5,13},{9,1},{13,5},{2,10},{6,14},... | collective-permute-start | bytes 393224 | tf_op jit(solution)/shard_map/ppermute | solution.py:235
  4.1 11.4 %collective-permute-start = (bf16[16,4096]{1,0:T(8,128)(2,1)}, bf16[16,4096]{1,0:T(8,128)(2,1)S(1)}, u32[]{:S(2)}, u32[]{:S(2)}) collective-permute-start(bf16[16,4096]{1,0:T(8,128)(2,1)} %refs_0_.1), channel_id=1, source_target_pairs={{0,12},{4,8},{8,4},{12,0},{1,13},{5,9},{9,5},{13,1},{2,14},{6,10},... | collective-permute-start | bytes 393224 | tf_op jit(solution)/shard_map/ppermute | solution.py:235
  5.5 10.0 %collective-permute-start.2 = (bf16[16,4096]{1,0:T(8,128)(2,1)}, bf16[16,4096]{1,0:T(8,128)(2,1)S(1)}, u32[]{:S(2)}, u32[]{:S(2)}) collective-permute-start(bf16[16,4096]{1,0:T(8,128)(2,1)} %refs_0_.1), channel_id=1, source_target_pairs={{0,4},{4,0},{8,12},{12,8},{1,5},{5,1},{9,13},{13,9},{2,6},{6,2},{1... | collective-permute-start | bytes 393224 | tf_op jit(solution)/shard_map/ppermute | solution.py:235
  16.0 7.0 %collective-permute-start.3 = (bf16[64,256]{1,0:T(8,128)(2,1)S(1)}, bf16[64,256]{1,0:T(8,128)(2,1)S(1)}, u32[]{:S(2)}, u32[]{:S(2)}) collective-permute-start(bf16[64,256]{1,0:T(8,128)(2,1)S(1)} %get-tuple-element.29), channel_id=1, source_target_pairs={{0,4},{4,0},{8,12},{12,8},{1,5},{5,1},{9,13},{13,9},{2,6},{6,2},{1... | collective-permute-start | bytes 98312 | tf_op jit(solution)/shard_map/ppermute | solution.py:235
  23.0 5.6 %collective-permute-start.7 = (bf16[64,256]{1,0:T(8,128)(2,1)S(1)}, bf16[64,256]{1,0:T(8,128)(2,1)S(1)}, u32[]{:S(2)}, u32[]{:S(2)}) collective-permute-start(bf16[64,256]{1,0:T(8,128)(2,1)S(1)} %add.6.refs_1_), channel_id=1, source_target_pairs={{0,8},{4,12},{8,0},{12,4},{1,9},{5,13},{9,1},{13,5},{2,10},{6,14},... | collective-permute-start | bytes 98312 | tf_op jit(solution)/shard_map/ppermute | solution.py:235
  26.4 2.3 %collective-permute-start.4 = (bf16[32,3072]{1,0:T(8,128)(2,1)S(1)}, bf16[32,3072]{1,0:T(8,128)(2,1)S(1)}, u32[]{:S(2)}, u32[]{:S(2)}) collective-permute-start(bf16[32,3072]{1,0:T(8,128)(2,1)S(1)} %get-tuple-element.32), channel_id=1, source_target_pairs={{0,1},{1,0},{2,3},{3,2},{4,5},{5,4},{6,7},{7,6},{8,9},{9,8},{10,11... | collective-permute-start | bytes 589832 | tf_op jit(solution)/shard_map/ppermute | solution.py:235
  26.5 8.4 %copy-start = (bf16[4,64,4096]{2,1,0:T(8,128)(2,1)S(1)}, bf16[4,64,4096]{2,1,0:T(8,128)(2,1)}, u32[]{:S(2)}) copy-start(bf16[4,64,4096]{2,1,0:T(8,128)(2,1)} %up_ref.1) | copy-start | bytes 6291460
  28.0 2.3 %collective-permute-start.6 = (bf16[32,1024]{1,0:T(8,128)(2,1)S(1)}, bf16[32,1024]{1,0:T(8,128)(2,1)S(1)}, u32[]{:S(2)}, u32[]{:S(2)}) collective-permute-start(bf16[32,1024]{1,0:T(8,128)(2,1)S(1)} %get-tuple-element.38), channel_id=1, source_target_pairs={{0,1},{1,0},{2,3},{3,2},{4,5},{5,4},{6,7},{7,6},{8,9},{9,8},{10,11... | collective-permute-start | bytes 196616 | tf_op jit(solution)/shard_map/ppermute | solution.py:235
  28.6 1.7 %collective-permute-start.8 = (bf16[64,256]{1,0:T(8,128)(2,1)S(1)}, bf16[64,256]{1,0:T(8,128)(2,1)S(1)}, u32[]{:S(2)}, u32[]{:S(2)}) collective-permute-start(bf16[64,256]{1,0:T(8,128)(2,1)S(1)} %add.7.refs_2_), channel_id=1, source_target_pairs={{0,1},{1,0},{2,3},{3,2},{4,5},{5,4},{6,7},{7,6},{8,9},{9,8},{10,11... | collective-permute-start | bytes 98312 | tf_op jit(solution)/shard_map/ppermute | solution.py:235
  28.8 6.1 %collective-permute-start.5 = (bf16[16,3072]{1,0:T(8,128)(2,1)S(1)}, bf16[16,3072]{1,0:T(8,128)(2,1)S(1)}, u32[]{:S(2)}, u32[]{:S(2)}) collective-permute-start(bf16[16,3072]{1,0:T(8,128)(2,1)S(1)} %get-tuple-element.34), channel_id=1, source_target_pairs={{0,2},{2,0},{1,3},{3,1},{4,6},{6,4},{5,7},{7,5},{8,10},{10,8},{9,1... | collective-permute-start | bytes 294920 | tf_op jit(solution)/shard_map/ppermute | solution.py:235
  30.5 4.4 %collective-permute-start.9 = (bf16[16,1280]{1,0:T(8,128)(2,1)S(1)}, bf16[16,1280]{1,0:T(8,128)(2,1)S(1)}, u32[]{:S(2)}, u32[]{:S(2)}) collective-permute-start(bf16[16,1280]{1,0:T(8,128)(2,1)S(1)} %get-tuple-element.40), channel_id=1, source_target_pairs={{0,2},{2,0},{1,3},{3,1},{4,6},{6,4},{5,7},{7,5},{8,10},{10,8},{9,1... | collective-permute-start | bytes 122888 | tf_op jit(solution)/shard_map/ppermute | solution.py:235

commit v15 on v14

--- a/solution.py
+++ b/solution.py
@@ -129,12 +129,14 @@
 
 def multiply(x_ref, weights, step, out, first):
     for weight in weights:
-        width = weight.shape[1]
-        for c in range(0, width, step):
-            out[:, first + c : first + c + step] = jnp.dot(
-                x_ref[...], weight[:, c : c + step], preferred_element_type=jnp.float32
-            )
-        first += width
+
+        def columns(j, weight=weight, first=first):
+            here = pl.ds(pl.multiple_of(j * step, step), step)
+            there = pl.ds(pl.multiple_of(first + j * step, step), step)
+            out[:, there] = jnp.dot(x_ref[...], weight[:, here], preferred_element_type=jnp.float32)
+
+        pl.loop(0, weight.shape[1] // step)(columns)
+        first += weight.shape[1]
 
 
 def base_kernel(n_w, first, step, w_hbm, x_ref, *refs):
@@ -240,7 +242,7 @@
     order = [0, *range(n_x - 1, 0, -1)]
     blocks = [hidden] + [send(hidden, "gx", n_x, k) for k in order[1:]]
 
-    step = min(512, columns // 4)
+    step = min(256, columns // 4)
     pieces = 8
     f32, bf16 = jnp.float32, jnp.bfloat16
     slots, rank_columns = slot_down_factors.shape[0], slot_down_factors.shape[2]
@@ -343,7 +345,7 @@
     last_parts = chip_sums(lasts, smalls, "last_sums")
 
     return pl.pallas_call(
-        functools.partial(final_kernel, n_y, n_z, step),
+        functools.partial(final_kernel, n_y, n_z, min(512, columns // 4)),
         out_shape=jax.ShapeDtypeStruct((rows_here, columns), bf16),
         in_specs=[VMEM] * (2 + 2 * n_y),
         out_specs=VMEM,

time: 36.1 us -> 36.1 us (level)
    pallas_call x1, Pallas kernels: 5.14 us -> 4.18 us  [body(): pl.pallas_call(functools.partial(base_kernel, 2, columns - late, step), o...]
    pallas_call x2, Pallas kernels: 3.19 us -> 4.09 us  [product(): pl.pallas_call(functools.partial(product_kernel, len(some), n_y, n_z, ste...]
where the time goes in v15:
time: 36.1 us; the launch traced here: 35.9 us
  Pallas kernels  19.7 us (55%)
  starting transfers between devices  12.7 us (35%)
  waiting for transfers between devices  3.32 us (9%)
    ppermute x10, starting transfers between devices, send(): return lax.ppermute(value, axis, [(j, j ^ k) for j in range(n)])  12.7 us
    pallas_call x1, Pallas kernels, body(): pl.pallas_call(functools.partial(fetch_kernel, len(loads)), out_shape=[ja...  9.76 us
    pallas_call x1, Pallas kernels, body(): pl.pallas_call(functools.partial(base_kernel, 2, columns - late, step), o...  4.18 us
    pallas_call x2, Pallas kernels, product(): pl.pallas_call(functools.partial(product_kernel, len(some), n_y, n_z, ste...  4.09 us
    ppermute x10, waiting for transfers between devices, send(): return lax.ppermute(value, axis, [(j, j ^ k) for j in range(n)])  3.32 us
    pallas_call x1, Pallas kernels, body(): pl.pallas_call(functools.partial(final_kernel, n_y, n_z, min(512, columns...  1.09 us
  transfers between devices with their start and end apart: 10, of which 1 were waited for; matrix products, arithmetic and copies ran while one was open for 0% of the time, Pallas kernels for 51%

profile of v15, /device:TPU:0, one launch (start us, length us, event | category | flops | bytes accessed | tf_op | source)
XLA Modules:
  0.0 35.9 jit_solution(17765692721480909934)
XLA Ops:
  0.0 4.1 %collective-permute-start.1 = (bf16[16,4096]{1,0:T(8,128)(2,1)}, bf16[16,4096]{1,0:T(8,128)(2,1)S(1)}, u32[]{:S(2)}, u32[]{:S(2)}) collective-permute-start(bf16[16,4096]{1,0:T(8,128)(2,1)} %refs_0_.1), channel_id=1, source_target_pairs={{0,8},{4,12},{8,0},{12,4},{1,9},{5,13},{9,1},{13,5},{2,10},{6,14},... | collective-permute-start | bytes 393224 | tf_op jit(solution)/shard_map/ppermute | solution.py:237
  4.1 1.3 %collective-permute-start = (bf16[16,4096]{1,0:T(8,128)(2,1)}, bf16[16,4096]{1,0:T(8,128)(2,1)S(1)}, u32[]{:S(2)}, u32[]{:S(2)}) collective-permute-start(bf16[16,4096]{1,0:T(8,128)(2,1)} %refs_0_.1), channel_id=1, source_target_pairs={{0,12},{4,8},{8,4},{12,0},{1,13},{5,9},{9,5},{13,1},{2,14},{6,10},... | collective-permute-start | bytes 393224 | tf_op jit(solution)/shard_map/ppermute | solution.py:237
  5.5 0.2 collective-permute-start.2
  5.7 9.8 %fetch_weight.1 = (f32[1,64,64]{2,1,0:T(8,128)S(1)}, f32[64,256]{1,0:T(8,128)S(1)}, bf16[4096,1024]{1,0:T(8,128)(2,1)S(1)}, bf16[4096,1024]{1,0:T(8,128)(2,1)S(1...) custom-call(bf16[4096,4096]{1,0:T(8,128)(2,1)} %w_hbm.3, s32[4]{0:T(128)} %rank_hbm.1, s32[4]{0:T(128)} %slot_hbm.1, ...), custom_call_target="tpu_custom_call" | custom-call | bytes 33554432 | tf_op jit(solution)/shard_map/fetch_weight/pallas_call | solution.py:258
  15.5 0.0 collective-permute-done.refs_1_
  15.5 0.0 collective-permute-done.2.refs_3_
  15.5 0.4 %scaled_rows.1 = (bf16[64,4096]{1,0:T(8,128)(2,1)S(1)}, bf16[64,256]{1,0:T(8,128)(2,1)S(1)}) custom-call(bf16[4096]{0:T(1024)(128)(2,1)S(1)} %copy-done.3, bf16[1,64,4096]{2,1,0:T(8,128)(2,1)S(1)} %bitcast.1, f32[1,64,64]{2,1,0:T(8,128)S(1)} %get-tuple-element.24.factor_ref, bf16[16,4096]{1,0:T(8,128)(2,1)S(1)} %copy-done.2, ...), custom_call_target="tpu_custom_call" | custom-call | tf_op jit(solution)/shard_map/scaled_rows/pallas_call | solution.py:278
  16.0 1.9 %collective-permute-start.3 = (bf16[64,256]{1,0:T(8,128)(2,1)S(1)}, bf16[64,256]{1,0:T(8,128)(2,1)S(1)}, u32[]{:S(2)}, u32[]{:S(2)}) collective-permute-start(bf16[64,256]{1,0:T(8,128)(2,1)S(1)} %get-tuple-element.29), channel_id=1, source_target_pairs={{0,4},{4,0},{8,12},{12,8},{1,5},{5,1},{9,13},{13,9},{2,6},{6,2},{1... | collective-permute-start | bytes 98312 | tf_op jit(solution)/shard_map/ppermute | solution.py:237
  17.8 4.2 %first_columns.1 = (f32[64,2048]{1,0:T(8,128)S(1)}, bf16[4096,512]{1,0:T(8,128)(2,1)S(1)}) custom-call(bf16[4096,4096]{1,0:T(8,128)(2,1)} %w_hbm.3, bf16[64,4096]{1,0:T(8,128)(2,1)S(1)} %get-tuple-element.25.x_ref, bf16[4096,1024]{1,0:T(8,128)(2,1)S(1)} %get-tuple-element.26.refs_0_, bf16[4096,1024]{1,0:T(8,128)(2,1)S(1)} %get-tuple-element.27.refs_1_), custom_call_target="tpu_custom_call" | custom-call | flops 1073741824 | bytes 16777216 | tf_op jit(solution)/shard_map/first_columns/pallas_call | solution.py:299
  22.0 0.0 collective-permute-done.3
  22.0 1.8 %collective-permute-start.7 = (bf16[64,256]{1,0:T(8,128)(2,1)S(1)}, bf16[64,256]{1,0:T(8,128)(2,1)S(1)}, u32[]{:S(2)}, u32[]{:S(2)}) collective-permute-start(bf16[64,256]{1,0:T(8,128)(2,1)S(1)} %add.6.refs_1_), channel_id=1, source_target_pairs={{0,8},{4,12},{8,0},{12,4},{1,9},{5,13},{9,1},{13,5},{2,10},{6,14},... | collective-permute-start | bytes 98312 | tf_op jit(solution)/shard_map/ppermute | solution.py:237
  23.8 2.1 %middle_columns.1 = (f32[32,3072]{1,0:T(8,128)S(1)}, bf16[32,3072]{1,0:T(8,128)(2,1)S(1)}) custom-call(bf16[64,4096]{1,0:T(8,128)(2,1)S(1)} %get-tuple-element.25.x_ref, f32[64,2048]{1,0:T(8,128)S(1)} %get-tuple-element.28.refs_0_, bf16[64,256]{1,0:T(8,128)(2,1)S(1)} %add.6.refs_1_, bf16[4096,1024]{1,0:T(8,128)(2,1)S(1)} %get-tuple-element.30.refs_2_), custom_call_target="tpu_custom_call" | custom-call | flops 6442450944 | bytes 25165824 | tf_op jit(solution)/shard_map/middle_columns/pallas_call | solution.py:315
  25.9 0.1 collective-permute-start.4
  26.0 0.0 copy-start
  26.0 2.0 %last_columns.1 = (f32[32,1024]{1,0:T(8,128)S(1)}, bf16[32,1024]{1,0:T(8,128)(2,1)S(1)}) custom-call(bf16[64,4096]{1,0:T(8,128)(2,1)S(1)} %get-tuple-element.25.x_ref, bf16[4096,512]{1,0:T(8,128)(2,1)S(1)} %get-tuple-element.35.refs_0_, bf16[4096,512]{1,0:T(8,128)(2,1)S(1)} %get-tuple-element.36.refs_1_), custom_call_target="tpu_custom_call" | custom-call | flops 4294967296 | bytes 8388608 | tf_op jit(solution)/shard_map/last_columns/pallas_call | solution.py:315
  28.0 0.6 %collective-permute-start.6 = (bf16[32,1024]{1,0:T(8,128)(2,1)S(1)}, bf16[32,1024]{1,0:T(8,128)(2,1)S(1)}, u32[]{:S(2)}, u32[]{:S(2)}) collective-permute-start(bf16[32,1024]{1,0:T(8,128)(2,1)S(1)} %get-tuple-element.38), channel_id=1, source_target_pairs={{0,1},{1,0},{2,3},{3,2},{4,5},{5,4},{6,7},{7,6},{8,9},{9,8},{10,11... | collective-permute-start | bytes 196616 | tf_op jit(solution)/shard_map/ppermute | solution.py:237
  28.5 0.0 collective-permute-done.7
  28.6 0.1 collective-permute-start.8
  28.7 0.0 collective-permute-done.4.refs_1_
  28.7 1.6 %collective-permute-start.5 = (bf16[16,3072]{1,0:T(8,128)(2,1)S(1)}, bf16[16,3072]{1,0:T(8,128)(2,1)S(1)}, u32[]{:S(2)}, u32[]{:S(2)}) collective-permute-start(bf16[16,3072]{1,0:T(8,128)(2,1)S(1)} %get-tuple-element.34), channel_id=1, source_target_pairs={{0,2},{2,0},{1,3},{3,1},{4,6},{6,4},{5,7},{7,5},{8,10},{10,8},{9,1... | collective-permute-start | bytes 294920 | tf_op jit(solution)/shard_map/ppermute | solution.py:237
  30.3 0.2 last_sums.1
  30.4 1.1 %collective-permute-start.9 = (bf16[16,1280]{1,0:T(8,128)(2,1)S(1)}, bf16[16,1280]{1,0:T(8,128)(2,1)S(1)}, u32[]{:S(2)}, u32[]{:S(2)}) collective-permute-start(bf16[16,1280]{1,0:T(8,128)(2,1)S(1)} %get-tuple-element.40), channel_id=1, source_target_pairs={{0,2},{2,0},{1,3},{3,1},{4,6},{6,4},{5,7},{7,5},{8,10},{10,8},{9,1... | collective-permute-start | bytes 122888 | tf_op jit(solution)/shard_map/ppermute | solution.py:237
  31.5 3.3 %collective-permute-done.9.refs_3_ = bf16[16,1280]{1,0:T(8,128)(2,1)S(1)} collective-permute-done((bf16[16,1280]{1,0:T(8,128)(2,1)S(1)}, bf16[16,1280]{1,0:T(8,128)(2,1)S(1)}, u32[]{:S(2)}, u32[]{:S(2)}) %collective-permute-start.9) | collective-permute-done | bytes 40992 | tf_op jit(solution)/shard_map/ppermute | solution.py:237
  34.8 1.1 %query_rows.1 = bf16[16,4096]{1,0:T(8,128)(2,1)} custom-call(f32[64,256]{1,0:T(8,128)S(1)} %get-tuple-element.23.spread_ref, bf16[4,64,4096]{2,1,0:T(8,128)(2,1)S(1)} %copy-done, f32[16,3072]{1,0:T(8,128)S(1)} %get-tuple-element.33.refs_0_, bf16[16,3072]{1,0:T(8,128)(2,1)S(1)} %collective-permute-done.5.refs_1_, f32[16,1280]{1,0:T(8,128)S(1)} %get-tuple-element.39.refs_2_, ...), custom_call_target="tpu_custom_call" | custom-call | tf_op jit(solution)/shard_map/query_rows/pallas_call | solution.py:347
  (14 shorter events, 0.1 us)
Async XLA Ops:
  0.0 15.5 %copy-start.2 = (bf16[16,4096]{1,0:T(8,128)(2,1)S(1)}, bf16[16,4096]{1,0:T(8,128)(2,1)}, u32[]{:S(2)}) copy-start(bf16[16,4096]{1,0:T(8,128)(2,1)} %refs_0_.1) | copy-start | bytes 393220
  0.0 15.5 %copy-start.1 = (bf16[1,4096,64]{1,2,0:T(8,128)(2,1)S(1)}, bf16[1,4096,64]{1,2,0:T(8,128)(2,1)}, u32[]{:S(2)}) copy-start(bf16[1,4096,64]{1,2,0:T(8,128)(2,1)} %param.12) | copy-start | bytes 1572868
  0.0 15.5 %copy-start.3 = (bf16[4096]{0:T(1024)(128)(2,1)S(1)}, bf16[4096]{0:T(1024)(128)(2,1)}, u32[]{:S(2)}) copy-start(bf16[4096]{0:T(1024)(128)(2,1)} %gain_ref.1) | copy-start | bytes 24580
  0.0 15.5 %collective-permute-start.1 = (bf16[16,4096]{1,0:T(8,128)(2,1)}, bf16[16,4096]{1,0:T(8,128)(2,1)S(1)}, u32[]{:S(2)}, u32[]{:S(2)}) collective-permute-start(bf16[16,4096]{1,0:T(8,128)(2,1)} %refs_0_.1), channel_id=1, source_target_pairs={{0,8},{4,12},{8,0},{12,4},{1,9},{5,13},{9,1},{13,5},{2,10},{6,14},... | collective-permute-start | bytes 393224 | tf_op jit(solution)/shard_map/ppermute | solution.py:237
  4.1 11.4 %collective-permute-start = (bf16[16,4096]{1,0:T(8,128)(2,1)}, bf16[16,4096]{1,0:T(8,128)(2,1)S(1)}, u32[]{:S(2)}, u32[]{:S(2)}) collective-permute-start(bf16[16,4096]{1,0:T(8,128)(2,1)} %refs_0_.1), channel_id=1, source_target_pairs={{0,12},{4,8},{8,4},{12,0},{1,13},{5,9},{9,5},{13,1},{2,14},{6,10},... | collective-permute-start | bytes 393224 | tf_op jit(solution)/shard_map/ppermute | solution.py:237
  5.5 10.0 %collective-permute-start.2 = (bf16[16,4096]{1,0:T(8,128)(2,1)}, bf16[16,4096]{1,0:T(8,128)(2,1)S(1)}, u32[]{:S(2)}, u32[]{:S(2)}) collective-permute-start(bf16[16,4096]{1,0:T(8,128)(2,1)} %refs_0_.1), channel_id=1, source_target_pairs={{0,4},{4,0},{8,12},{12,8},{1,5},{5,1},{9,13},{13,9},{2,6},{6,2},{1... | collective-permute-start | bytes 393224 | tf_op jit(solution)/shard_map/ppermute | solution.py:237
  16.0 6.1 %collective-permute-start.3 = (bf16[64,256]{1,0:T(8,128)(2,1)S(1)}, bf16[64,256]{1,0:T(8,128)(2,1)S(1)}, u32[]{:S(2)}, u32[]{:S(2)}) collective-permute-start(bf16[64,256]{1,0:T(8,128)(2,1)S(1)} %get-tuple-element.29), channel_id=1, source_target_pairs={{0,4},{4,0},{8,12},{12,8},{1,5},{5,1},{9,13},{13,9},{2,6},{6,2},{1... | collective-permute-start | bytes 98312 | tf_op jit(solution)/shard_map/ppermute | solution.py:237
  22.0 6.5 %collective-permute-start.7 = (bf16[64,256]{1,0:T(8,128)(2,1)S(1)}, bf16[64,256]{1,0:T(8,128)(2,1)S(1)}, u32[]{:S(2)}, u32[]{:S(2)}) collective-permute-start(bf16[64,256]{1,0:T(8,128)(2,1)S(1)} %add.6.refs_1_), channel_id=1, source_target_pairs={{0,8},{4,12},{8,0},{12,4},{1,9},{5,13},{9,1},{13,5},{2,10},{6,14},... | collective-permute-start | bytes 98312 | tf_op jit(solution)/shard_map/ppermute | solution.py:237
  25.9 2.7 %collective-permute-start.4 = (bf16[32,3072]{1,0:T(8,128)(2,1)S(1)}, bf16[32,3072]{1,0:T(8,128)(2,1)S(1)}, u32[]{:S(2)}, u32[]{:S(2)}) collective-permute-start(bf16[32,3072]{1,0:T(8,128)(2,1)S(1)} %get-tuple-element.32), channel_id=1, source_target_pairs={{0,1},{1,0},{2,3},{3,2},{4,5},{5,4},{6,7},{7,6},{8,9},{9,8},{10,11... | collective-permute-start | bytes 589832 | tf_op jit(solution)/shard_map/ppermute | solution.py:237
  26.0 8.8 %copy-start = (bf16[4,64,4096]{2,1,0:T(8,128)(2,1)S(1)}, bf16[4,64,4096]{2,1,0:T(8,128)(2,1)}, u32[]{:S(2)}) copy-start(bf16[4,64,4096]{2,1,0:T(8,128)(2,1)} %up_ref.1) | copy-start | bytes 6291460
  28.0 2.3 %collective-permute-start.6 = (bf16[32,1024]{1,0:T(8,128)(2,1)S(1)}, bf16[32,1024]{1,0:T(8,128)(2,1)S(1)}, u32[]{:S(2)}, u32[]{:S(2)}) collective-permute-start(bf16[32,1024]{1,0:T(8,128)(2,1)S(1)} %get-tuple-element.38), channel_id=1, source_target_pairs={{0,1},{1,0},{2,3},{3,2},{4,5},{5,4},{6,7},{7,6},{8,9},{9,8},{10,11... | collective-permute-start | bytes 196616 | tf_op jit(solution)/shard_map/ppermute | solution.py:237
  28.6 1.7 %collective-permute-start.8 = (bf16[64,256]{1,0:T(8,128)(2,1)S(1)}, bf16[64,256]{1,0:T(8,128)(2,1)S(1)}, u32[]{:S(2)}, u32[]{:S(2)}) collective-permute-start(bf16[64,256]{1,0:T(8,128)(2,1)S(1)} %add.7.refs_2_), channel_id=1, source_target_pairs={{0,1},{1,0},{2,3},{3,2},{4,5},{5,4},{6,7},{7,6},{8,9},{9,8},{10,11... | collective-permute-start | bytes 98312 | tf_op jit(solution)/shard_map/ppermute | solution.py:237
  28.7 6.1 %collective-permute-start.5 = (bf16[16,3072]{1,0:T(8,128)(2,1)S(1)}, bf16[16,3072]{1,0:T(8,128)(2,1)S(1)}, u32[]{:S(2)}, u32[]{:S(2)}) collective-permute-start(bf16[16,3072]{1,0:T(8,128)(2,1)S(1)} %get-tuple-element.34), channel_id=1, source_target_pairs={{0,2},{2,0},{1,3},{3,1},{4,6},{6,4},{5,7},{7,5},{8,10},{10,8},{9,1... | collective-permute-start | bytes 294920 | tf_op jit(solution)/shard_map/ppermute | solution.py:237
  30.4 4.4 %collective-permute-start.9 = (bf16[16,1280]{1,0:T(8,128)(2,1)S(1)}, bf16[16,1280]{1,0:T(8,128)(2,1)S(1)}, u32[]{:S(2)}, u32[]{:S(2)}) collective-permute-start(bf16[16,1280]{1,0:T(8,128)(2,1)S(1)} %get-tuple-element.40), channel_id=1, source_target_pairs={{0,2},{2,0},{1,3},{3,1},{4,6},{6,4},{5,7},{7,5},{8,10},{10,8},{9,1... | collective-permute-start | bytes 122888 | tf_op jit(solution)/shard_map/ppermute | solution.py:237

commit v16 on v13

--- a/solution.py
+++ b/solution.py
@@ -147,8 +147,18 @@
         first += width
 
 
-def base_kernel(n_w, step, x_ref, *refs):
-    multiply(x_ref, refs[:n_w], step, refs[n_w], 0)
+def base_kernel(n_w, first, step, w_hbm, x_ref, *refs):
+    weights, out_ref, rest = refs[:n_w], refs[n_w], refs[n_w + 1 :]
+    copies = weight_copies(w_hbm, first, *rest) if rest else []
+    for copy in copies:
+        copy.start()
+
+    @pl.when(lax.axis_index("gx") >= 0)
+    def behind_the_copies():
+        multiply(x_ref, weights, step, out_ref, 0)
+
+    for copy in copies:
+        copy.wait()
 
 
 def product_kernel(n_w, n_y, n_z, step, first, x_ref, *refs):
@@ -247,14 +257,15 @@
         sent[k] = send(sent[k - 1], "gx", n_x, 1) if k % 2 else send(hidden, "gx", n_x, k)
     blocks = [sent[k] for k in order]
 
-    step = min(512, columns // 8 if columns >= 8 * LANES else columns // 4)
+    step = min(512, columns // 4)
     pieces = 8
     f32, bf16 = jnp.float32, jnp.bfloat16
     slots, rank_columns = slot_down_factors.shape[0], slot_down_factors.shape[2]
     adapters = adapter_up_factors.shape[0]
     quarter = columns // 4
-    if quarter % (2 * LANES) == 0:
-        loads = [quarter, quarter, quarter // 2], [quarter // 2, quarter]
+    half = quarter // 2 if quarter % (2 * LANES) == 0 else 0
+    if half:
+        loads = [quarter, quarter, half], [half, half]
     else:
         loads = [quarter, quarter], [quarter, quarter]
     kept = n_y * rows_here
@@ -314,16 +325,18 @@
     def shapes(n, shape):
         return [jax.ShapeDtypeStruct(shape, f32 if k == 0 else bf16) for k in range(n)]
 
-    base_columns = 2 * quarter
-    base = pl.pallas_call(
-        functools.partial(base_kernel, 2, step),
-        out_shape=jax.ShapeDtypeStruct((rows, base_columns), f32),
-        in_specs=[VMEM] * 3,
-        out_specs=VMEM,
-        cost_estimate=cost(2 * rows * depth * base_columns, 2 * depth * base_columns),
+    base, *rest = pl.pallas_call(
+        functools.partial(base_kernel, 2, columns - half, step),
+        out_shape=[jax.ShapeDtypeStruct((rows, 2 * quarter), f32)]
+        + ([pltpu.VMEM((depth, half), query_weight.dtype)] if half else []),
+        in_specs=[HBM] + [VMEM] * 3,
+        out_specs=[VMEM] * (2 if half else 1),
+        scratch_shapes=[pltpu.SemaphoreType.DMA((pieces,))] if half else [],
+        cost_estimate=cost(4 * rows * depth * quarter, 4 * depth * quarter),
         compiler_params=roomy,
         name="first_columns",
-    )(x, *weights[:2])
+    )(weight_hbm, x, *weights[:2])
+    weights += [pltpu.with_memory_space_constraint(w, pltpu.VMEM) for w in rest]
 
     def product(some, bases, times, name):
         first = sum(part.shape[1] for part in bases[:1])
@@ -340,8 +353,8 @@
         )(x, *bases, *some)
         return spread_out(made, "gz", n_z)
 
-    firsts = product(weights[2:-1], [base, one_hop], 4, "middle_columns")
-    lasts = product(weights[-1:], [], 8, "last_columns")
+    firsts = product(weights[2 : 4 if half else 3], [base, one_hop], 4, "middle_columns")
+    lasts = product(weights[4 if half else 3 :], [], 8, "last_columns")
     smalls = spread_out([small] * n_z, "gz", n_z)
 
     def chip_sums(parts, sides, name):

time: 35.9 us -> 35.2 us (0.981)
  Pallas kernels: 20 us -> 18.9 us
  waiting for transfers between devices: 3.79 us -> 4.21 us
    pallas_call x1, Pallas kernels: 4.86 us -> 3.63 us  [body(): pl.pallas_call(functools.partial(last_load_kernel, len(loads[1]), sum(loa...]
    ppermute x10, waiting for transfers between devices: 3.79 us -> 4.21 us  [send(): return lax.ppermute(value, axis, [(j, j ^ k) for j in range(n)])]
  transfers between devices with their start and end apart: 10 -> 10, of which waited for: 2 -> 2; matrix products, arithmetic and copies ran while one was open for 0% -> 0% of each run, Pallas kernels for 52% -> 50%
where the time goes in v16:
time: 35.2 us; the launch traced here: 35 us
  Pallas kernels  18.9 us (54%)
  starting transfers between devices  11.8 us (34%)
  waiting for transfers between devices  4.21 us (12%)
    ppermute x10, starting transfers between devices, send(): return lax.ppermute(value, axis, [(j, j ^ k) for j in range(n)])  11.8 us
    pallas_call x1, Pallas kernels, body(): pl.pallas_call(functools.partial(first_load_kernel, len(loads[0])), out_s...  7.27 us
    ppermute x10, waiting for transfers between devices, send(): return lax.ppermute(value, axis, [(j, j ^ k) for j in range(n)])  4.21 us
    pallas_call x1, Pallas kernels, body(): pl.pallas_call(functools.partial(last_load_kernel, len(loads[1]), sum(loa...  3.63 us
    pallas_call x2, Pallas kernels, product(): pl.pallas_call(functools.partial(product_kernel, len(some), n_y, n_z, ste...  3.15 us
    pallas_call x1, Pallas kernels, body(): pl.pallas_call(functools.partial(base_kernel, 2, columns - half, step), o...  3.13 us
    pallas_call x1, Pallas kernels, body(): pl.pallas_call(functools.partial(final_kernel, n_y, n_z, step), out_shape...  1.1 us
  transfers between devices with their start and end apart: 10, of which 2 were waited for; matrix products, arithmetic and copies ran while one was open for 0% of the time, Pallas kernels for 50%

profile of v16, /device:TPU:0, one launch (start us, length us, event | category | flops | bytes accessed | tf_op | source)
XLA Modules:
  0.0 35.0 jit_solution(13692794797688095720)
XLA Ops:
  0.0 4.0 %collective-permute-start = (bf16[16,4096]{1,0:T(8,128)(2,1)}, bf16[16,4096]{1,0:T(8,128)(2,1)S(1)}, u32[]{:S(2)}, u32[]{:S(2)}) collective-permute-start(bf16[16,4096]{1,0:T(8,128)(2,1)} %refs_0_.1), channel_id=1, source_target_pairs={{0,8},{4,12},{8,0},{12,4},{1,9},{5,13},{9,1},{13,5},{2,10},{6,14},... | collective-permute-start | bytes 393224 | tf_op jit(solution)/shard_map/ppermute | solution.py:249
  4.0 1.6 %collective-permute-start.1 = (bf16[16,4096]{1,0:T(8,128)(2,1)}, bf16[16,4096]{1,0:T(8,128)(2,1)S(1)}, u32[]{:S(2)}, u32[]{:S(2)}) collective-permute-start(bf16[16,4096]{1,0:T(8,128)(2,1)} %refs_0_.1), channel_id=1, source_target_pairs={{0,4},{4,0},{8,12},{12,8},{1,5},{5,1},{9,13},{13,9},{2,6},{6,2},{1... | collective-permute-start | bytes 393224 | tf_op jit(solution)/shard_map/ppermute | solution.py:249
  5.6 7.3 %first_load.1 = (f32[1,64,64]{2,1,0:T(8,128)S(1)}, f32[64,256]{1,0:T(8,128)S(1)}, bf16[4096,1024]{1,0:T(8,128)(2,1)S(1)}, bf16[4096,1024]{1,0:T(8,128)(2,1)S(1)}, bf16[4096,512]{1,0:T(8,128)(2,1)S(1)}) custom-call(bf16[4096,4096]{1,0:T(8,128)(2,1)} %w_hbm.5, s32[4]{0:T(128)} %rank_hbm.1, s32[4]{0:T(128)} %slot_hbm.1, s32[5]{0:T(128)} %start_hbm.1), custom_call_target="tpu_custom_call" | custom-call | flops 5033164800 | bytes 16777216 | tf_op jit(solution)/shard_map/first_load/pallas_call | solution.py:277
  12.9 0.5 %collective-permute-start.2 = (bf16[16,4096]{1,0:T(8,128)(2,1)S(1)}, bf16[16,4096]{1,0:T(8,128)(2,1)S(1)}, u32[]{:S(2)}, u32[]{:S(2)}) collective-permute-start(bf16[16,4096]{1,0:T(8,128)(2,1)S(1)} %collective-permute-done.refs_1_.__), channel_id=1, source_target_pairs={{0,4},{4,0},{8,12},{12,8},{1,5},{5,1},{9,13},{13,9},{2,6},{6,2},{1... | collective-permute-start | bytes 393224 | tf_op jit(solution)/shard_map/ppermute | solution.py:249
  13.4 3.6 %last_load.1 = (bf16[4096,512]{1,0:T(8,128)(2,1)S(1)}, bf16[4096,512]{1,0:T(8,128)(2,1)S(1)}) custom-call(bf16[4096,4096]{1,0:T(8,128)(2,1)} %w_hbm.5, f32[1,64,64]{2,1,0:T(8,128)S(1)} %get-tuple-element.25.factor_ref._, bf16[16,4096]{1,0:T(8,128)(2,1)S(1)} %collective-permute-done.refs_1_.__), custom_call_target="tpu_custom_call" | custom-call | flops 5033164800 | bytes 16777216 | tf_op jit(solution)/shard_map/last_load/pallas_call | solution.py:295
  17.1 0.0 collective-permute-done.1.refs_2_
  17.1 0.9 %collective-permute-done.2.refs_3_ = bf16[16,4096]{1,0:T(8,128)(2,1)S(1)} collective-permute-done((bf16[16,4096]{1,0:T(8,128)(2,1)S(1)}, bf16[16,4096]{1,0:T(8,128)(2,1)S(1)}, u32[]{:S(2)}, u32[]{:S(2)}) %collective-permute-start.2) | collective-permute-done | bytes 131104 | tf_op jit(solution)/shard_map/ppermute | solution.py:249
  18.0 0.4 %scaled_rows.1 = (bf16[64,4096]{1,0:T(8,128)(2,1)S(1)}, bf16[64,256]{1,0:T(8,128)(2,1)S(1)}) custom-call(bf16[4096]{0:T(1024)(128)(2,1)S(1)} %copy-done.3, bf16[1,64,4096]{2,1,0:T(8,128)(2,1)S(1)} %bitcast.1, f32[1,64,64]{2,1,0:T(8,128)S(1)} %get-tuple-element.25.factor_ref._, bf16[16,4096]{1,0:T(8,128)(2,1)S(1)} %copy-done.2, ...), custom_call_target="tpu_custom_call" | custom-call | tf_op jit(solution)/shard_map/scaled_rows/pallas_call | solution.py:307
  18.4 0.8 %collective-permute-start.3 = (bf16[64,256]{1,0:T(8,128)(2,1)S(1)}, bf16[64,256]{1,0:T(8,128)(2,1)S(1)}, u32[]{:S(2)}, u32[]{:S(2)}) collective-permute-start(bf16[64,256]{1,0:T(8,128)(2,1)S(1)} %get-tuple-element.30), channel_id=1, source_target_pairs={{0,4},{4,0},{8,12},{12,8},{1,5},{5,1},{9,13},{13,9},{2,6},{6,2},{1... | collective-permute-start | bytes 98312 | tf_op jit(solution)/shard_map/ppermute | solution.py:249
  19.2 3.1 %first_columns.1 = (f32[64,2048]{1,0:T(8,128)S(1)}, bf16[4096,512]{1,0:T(8,128)(2,1)S(1)}) custom-call(bf16[4096,4096]{1,0:T(8,128)(2,1)} %w_hbm.5, bf16[64,4096]{1,0:T(8,128)(2,1)S(1)} %get-tuple-element.26.x_ref, bf16[4096,1024]{1,0:T(8,128)(2,1)S(1)} %get-tuple-element.27.refs_0_, bf16[4096,1024]{1,0:T(8,128)(2,1)S(1)} %get-tuple-element.28.refs_1_), custom_call_target="tpu_custom_call" | custom-call | flops 1073741824 | bytes 16777216 | tf_op jit(solution)/shard_map/first_columns/pallas_call | solution.py:328
  22.3 0.0 collective-permute-done.3
  22.4 1.4 %collective-permute-start.7 = (bf16[64,256]{1,0:T(8,128)(2,1)S(1)}, bf16[64,256]{1,0:T(8,128)(2,1)S(1)}, u32[]{:S(2)}, u32[]{:S(2)}) collective-permute-start(bf16[64,256]{1,0:T(8,128)(2,1)S(1)} %add.6.refs_1_), channel_id=1, source_target_pairs={{0,8},{4,12},{8,0},{12,4},{1,9},{5,13},{9,1},{13,5},{2,10},{6,14},... | collective-permute-start | bytes 98312 | tf_op jit(solution)/shard_map/ppermute | solution.py:249
  23.8 1.6 %middle_columns.1 = (f32[32,3072]{1,0:T(8,128)S(1)}, bf16[32,3072]{1,0:T(8,128)(2,1)S(1)}) custom-call(bf16[64,4096]{1,0:T(8,128)(2,1)S(1)} %get-tuple-element.26.x_ref, f32[64,2048]{1,0:T(8,128)S(1)} %get-tuple-element.29.refs_0_, bf16[64,256]{1,0:T(8,128)(2,1)S(1)} %add.6.refs_1_, bf16[4096,512]{1,0:T(8,128)(2,1)S(1)} %get-tuple-element.31.refs_2_, ...), custom_call_target="tpu_custom_call" | custom-call | flops 6442450944 | bytes 25165824 | tf_op jit(solution)/shard_map/middle_columns/pallas_call | solution.py:344
  25.4 0.1 collective-permute-start.4
  25.5 1.6 %last_columns.1 = (f32[32,1024]{1,0:T(8,128)S(1)}, bf16[32,1024]{1,0:T(8,128)(2,1)S(1)}) custom-call(bf16[64,4096]{1,0:T(8,128)(2,1)S(1)} %get-tuple-element.26.x_ref, bf16[4096,512]{1,0:T(8,128)(2,1)S(1)} %get-tuple-element.37.refs_0_, bf16[4096,512]{1,0:T(8,128)(2,1)S(1)} %get-tuple-element.38.refs_1_), custom_call_target="tpu_custom_call" | custom-call | flops 4294967296 | bytes 8388608 | tf_op jit(solution)/shard_map/last_columns/pallas_call | solution.py:344
  27.0 0.0 copy-start
  27.1 0.6 %collective-permute-start.6 = (bf16[32,1024]{1,0:T(8,128)(2,1)S(1)}, bf16[32,1024]{1,0:T(8,128)(2,1)S(1)}, u32[]{:S(2)}, u32[]{:S(2)}) collective-permute-start(bf16[32,1024]{1,0:T(8,128)(2,1)S(1)} %get-tuple-element.40), channel_id=1, source_target_pairs={{0,1},{1,0},{2,3},{3,2},{4,5},{5,4},{6,7},{7,6},{8,9},{9,8},{10,11... | collective-permute-start | bytes 196616 | tf_op jit(solution)/shard_map/ppermute | solution.py:249
  27.6 0.1 collective-permute-start.8
  27.7 0.0 collective-permute-done.4.refs_1_
  27.8 1.6 %collective-permute-start.5 = (bf16[16,3072]{1,0:T(8,128)(2,1)S(1)}, bf16[16,3072]{1,0:T(8,128)(2,1)S(1)}, u32[]{:S(2)}, u32[]{:S(2)}) collective-permute-start(bf16[16,3072]{1,0:T(8,128)(2,1)S(1)} %get-tuple-element.36), channel_id=1, source_target_pairs={{0,2},{2,0},{1,3},{3,1},{4,6},{6,4},{5,7},{7,5},{8,10},{10,8},{9,1... | collective-permute-start | bytes 294920 | tf_op jit(solution)/shard_map/ppermute | solution.py:249
  29.3 0.2 last_sums.1
  29.5 1.1 %collective-permute-start.9 = (bf16[16,1280]{1,0:T(8,128)(2,1)S(1)}, bf16[16,1280]{1,0:T(8,128)(2,1)S(1)}, u32[]{:S(2)}, u32[]{:S(2)}) collective-permute-start(bf16[16,1280]{1,0:T(8,128)(2,1)S(1)} %get-tuple-element.42), channel_id=1, source_target_pairs={{0,2},{2,0},{1,3},{3,1},{4,6},{6,4},{5,7},{7,5},{8,10},{10,8},{9,1... | collective-permute-start | bytes 122888 | tf_op jit(solution)/shard_map/ppermute | solution.py:249
  30.6 3.3 %collective-permute-done.9.refs_3_ = bf16[16,1280]{1,0:T(8,128)(2,1)S(1)} collective-permute-done((bf16[16,1280]{1,0:T(8,128)(2,1)S(1)}, bf16[16,1280]{1,0:T(8,128)(2,1)S(1)}, u32[]{:S(2)}, u32[]{:S(2)}) %collective-permute-start.9) | collective-permute-done | bytes 40992 | tf_op jit(solution)/shard_map/ppermute | solution.py:249
  33.9 1.1 %query_rows.1 = bf16[16,4096]{1,0:T(8,128)(2,1)} custom-call(f32[64,256]{1,0:T(8,128)S(1)} %get-tuple-element.24.spread_ref, bf16[4,64,4096]{2,1,0:T(8,128)(2,1)S(1)} %copy-done, f32[16,3072]{1,0:T(8,128)S(1)} %get-tuple-element.35.refs_0_, bf16[16,3072]{1,0:T(8,128)(2,1)S(1)} %collective-permute-done.5.refs_1_, f32[16,1280]{1,0:T(8,128)S(1)} %get-tuple-element.41.refs_2_, ...), custom_call_target="tpu_custom_call" | custom-call | tf_op jit(solution)/shard_map/query_rows/pallas_call | solution.py:376
  (15 shorter events, 0.1 us)
Async XLA Ops:
  0.0 12.9 %collective-permute-start = (bf16[16,4096]{1,0:T(8,128)(2,1)}, bf16[16,4096]{1,0:T(8,128)(2,1)S(1)}, u32[]{:S(2)}, u32[]{:S(2)}) collective-permute-start(bf16[16,4096]{1,0:T(8,128)(2,1)} %refs_0_.1), channel_id=1, source_target_pairs={{0,8},{4,12},{8,0},{12,4},{1,9},{5,13},{9,1},{13,5},{2,10},{6,14},... | collective-permute-start | bytes 393224 | tf_op jit(solution)/shard_map/ppermute | solution.py:249
  4.0 13.0 %collective-permute-start.1 = (bf16[16,4096]{1,0:T(8,128)(2,1)}, bf16[16,4096]{1,0:T(8,128)(2,1)S(1)}, u32[]{:S(2)}, u32[]{:S(2)}) collective-permute-start(bf16[16,4096]{1,0:T(8,128)(2,1)} %refs_0_.1), channel_id=1, source_target_pairs={{0,4},{4,0},{8,12},{12,8},{1,5},{5,1},{9,13},{13,9},{2,6},{6,2},{1... | collective-permute-start | bytes 393224 | tf_op jit(solution)/shard_map/ppermute | solution.py:249
  12.9 5.0 %collective-permute-start.2 = (bf16[16,4096]{1,0:T(8,128)(2,1)S(1)}, bf16[16,4096]{1,0:T(8,128)(2,1)S(1)}, u32[]{:S(2)}, u32[]{:S(2)}) collective-permute-start(bf16[16,4096]{1,0:T(8,128)(2,1)S(1)} %collective-permute-done.refs_1_.__), channel_id=1, source_target_pairs={{0,4},{4,0},{8,12},{12,8},{1,5},{5,1},{9,13},{13,9},{2,6},{6,2},{1... | collective-permute-start | bytes 393224 | tf_op jit(solution)/shard_map/ppermute | solution.py:249
  13.4 4.5 %copy-start.1 = (bf16[1,4096,64]{1,2,0:T(8,128)(2,1)S(1)}, bf16[1,4096,64]{1,2,0:T(8,128)(2,1)}, u32[]{:S(2)}) copy-start(bf16[1,4096,64]{1,2,0:T(8,128)(2,1)} %param.12) | copy-start | bytes 1572868
  13.4 4.5 %copy-start.2 = (bf16[16,4096]{1,0:T(8,128)(2,1)S(1)}, bf16[16,4096]{1,0:T(8,128)(2,1)}, u32[]{:S(2)}) copy-start(bf16[16,4096]{1,0:T(8,128)(2,1)} %refs_0_.1) | copy-start | bytes 393220
  13.4 4.5 %copy-start.3 = (bf16[4096]{0:T(1024)(128)(2,1)S(1)}, bf16[4096]{0:T(1024)(128)(2,1)}, u32[]{:S(2)}) copy-start(bf16[4096]{0:T(1024)(128)(2,1)} %gain_ref.1) | copy-start | bytes 24580
  18.4 4.0 %collective-permute-start.3 = (bf16[64,256]{1,0:T(8,128)(2,1)S(1)}, bf16[64,256]{1,0:T(8,128)(2,1)S(1)}, u32[]{:S(2)}, u32[]{:S(2)}) collective-permute-start(bf16[64,256]{1,0:T(8,128)(2,1)S(1)} %get-tuple-element.30), channel_id=1, source_target_pairs={{0,4},{4,0},{8,12},{12,8},{1,5},{5,1},{9,13},{13,9},{2,6},{6,2},{1... | collective-permute-start | bytes 98312 | tf_op jit(solution)/shard_map/ppermute | solution.py:249
  22.4 5.3 %collective-permute-start.7 = (bf16[64,256]{1,0:T(8,128)(2,1)S(1)}, bf16[64,256]{1,0:T(8,128)(2,1)S(1)}, u32[]{:S(2)}, u32[]{:S(2)}) collective-permute-start(bf16[64,256]{1,0:T(8,128)(2,1)S(1)} %add.6.refs_1_), channel_id=1, source_target_pairs={{0,8},{4,12},{8,0},{12,4},{1,9},{5,13},{9,1},{13,5},{2,10},{6,14},... | collective-permute-start | bytes 98312 | tf_op jit(solution)/shard_map/ppermute | solution.py:249
  25.4 2.3 %collective-permute-start.4 = (bf16[32,3072]{1,0:T(8,128)(2,1)S(1)}, bf16[32,3072]{1,0:T(8,128)(2,1)S(1)}, u32[]{:S(2)}, u32[]{:S(2)}) collective-permute-start(bf16[32,3072]{1,0:T(8,128)(2,1)S(1)} %get-tuple-element.34), channel_id=1, source_target_pairs={{0,1},{1,0},{2,3},{3,2},{4,5},{5,4},{6,7},{7,6},{8,9},{9,8},{10,11... | collective-permute-start | bytes 589832 | tf_op jit(solution)/shard_map/ppermute | solution.py:249
  27.0 6.9 %copy-start = (bf16[4,64,4096]{2,1,0:T(8,128)(2,1)S(1)}, bf16[4,64,4096]{2,1,0:T(8,128)(2,1)}, u32[]{:S(2)}) copy-start(bf16[4,64,4096]{2,1,0:T(8,128)(2,1)} %up_ref.1) | copy-start | bytes 6291460
  27.1 2.3 %collective-permute-start.6 = (bf16[32,1024]{1,0:T(8,128)(2,1)S(1)}, bf16[32,1024]{1,0:T(8,128)(2,1)S(1)}, u32[]{:S(2)}, u32[]{:S(2)}) collective-permute-start(bf16[32,1024]{1,0:T(8,128)(2,1)S(1)} %get-tuple-element.40), channel_id=1, source_target_pairs={{0,1},{1,0},{2,3},{3,2},{4,5},{5,4},{6,7},{7,6},{8,9},{9,8},{10,11... | collective-permute-start | bytes 196616 | tf_op jit(solution)/shard_map/ppermute | solution.py:249
  27.6 1.7 %collective-permute-start.8 = (bf16[64,256]{1,0:T(8,128)(2,1)S(1)}, bf16[64,256]{1,0:T(8,128)(2,1)S(1)}, u32[]{:S(2)}, u32[]{:S(2)}) collective-permute-start(bf16[64,256]{1,0:T(8,128)(2,1)S(1)} %add.7.refs_2_), channel_id=1, source_target_pairs={{0,1},{1,0},{2,3},{3,2},{4,5},{5,4},{6,7},{7,6},{8,9},{9,8},{10,11... | collective-permute-start | bytes 98312 | tf_op jit(solution)/shard_map/ppermute | solution.py:249
  27.8 6.1 %collective-permute-start.5 = (bf16[16,3072]{1,0:T(8,128)(2,1)S(1)}, bf16[16,3072]{1,0:T(8,128)(2,1)S(1)}, u32[]{:S(2)}, u32[]{:S(2)}) collective-permute-start(bf16[16,3072]{1,0:T(8,128)(2,1)S(1)} %get-tuple-element.36), channel_id=1, source_target_pairs={{0,2},{2,0},{1,3},{3,1},{4,6},{6,4},{5,7},{7,5},{8,10},{10,8},{9,1... | collective-permute-start | bytes 294920 | tf_op jit(solution)/shard_map/ppermute | solution.py:249
  29.5 4.4 %collective-permute-start.9 = (bf16[16,1280]{1,0:T(8,128)(2,1)S(1)}, bf16[16,1280]{1,0:T(8,128)(2,1)S(1)}, u32[]{:S(2)}, u32[]{:S(2)}) collective-permute-start(bf16[16,1280]{1,0:T(8,128)(2,1)S(1)} %get-tuple-element.42), channel_id=1, source_target_pairs={{0,2},{2,0},{1,3},{3,1},{4,6},{6,4},{5,7},{7,5},{8,10},{10,8},{9,1... | collective-permute-start | bytes 122888 | tf_op jit(solution)/shard_map/ppermute | solution.py:249

commit v17 on v16

--- a/solution.py
+++ b/solution.py
@@ -140,9 +140,10 @@
 def multiply(x_ref, weights, step, out, first):
     for weight in weights:
         width = weight.shape[1]
-        for c in range(0, width, step):
-            out[:, first + c : first + c + step] = jnp.dot(
-                x_ref[...], weight[:, c : c + step], preferred_element_type=jnp.float32
+        wide = min(step, width)
+        for c in range(0, width, wide):
+            out[:, first + c : first + c + wide] = jnp.dot(
+                x_ref[...], weight[:, c : c + wide], preferred_element_type=jnp.float32
             )
         first += width
 
@@ -257,17 +258,17 @@
         sent[k] = send(sent[k - 1], "gx", n_x, 1) if k % 2 else send(hidden, "gx", n_x, k)
     blocks = [sent[k] for k in order]
 
-    step = min(512, columns // 4)
+    step = min(1024, columns // 4)
     pieces = 8
     f32, bf16 = jnp.float32, jnp.bfloat16
     slots, rank_columns = slot_down_factors.shape[0], slot_down_factors.shape[2]
     adapters = adapter_up_factors.shape[0]
     quarter = columns // 4
-    half = quarter // 2 if quarter % (2 * LANES) == 0 else 0
-    if half:
-        loads = [quarter, quarter, half], [half, half]
+    part = quarter // 4
+    if part % LANES == 0:
+        loads, late = ([quarter, quarter], [quarter, part]), quarter - part
     else:
-        loads = [quarter, quarter], [quarter, quarter]
+        loads, late = ([quarter, quarter], [quarter, quarter]), 0
     kept = n_y * rows_here
     roomy = params(4 + (rows * depth >> 16))
 
@@ -326,12 +327,12 @@
         return [jax.ShapeDtypeStruct(shape, f32 if k == 0 else bf16) for k in range(n)]
 
     base, *rest = pl.pallas_call(
-        functools.partial(base_kernel, 2, columns - half, step),
+        functools.partial(base_kernel, 2, columns - late, step),
         out_shape=[jax.ShapeDtypeStruct((rows, 2 * quarter), f32)]
-        + ([pltpu.VMEM((depth, half), query_weight.dtype)] if half else []),
+        + ([pltpu.VMEM((depth, late), query_weight.dtype)] if late else []),
         in_specs=[HBM] + [VMEM] * 3,
-        out_specs=[VMEM] * (2 if half else 1),
-        scratch_shapes=[pltpu.SemaphoreType.DMA((pieces,))] if half else [],
+        out_specs=[VMEM] * (2 if late else 1),
+        scratch_shapes=[pltpu.SemaphoreType.DMA((pieces,))] if late else [],
         cost_estimate=cost(4 * rows * depth * quarter, 4 * depth * quarter),
         compiler_params=roomy,
         name="first_columns",
@@ -353,8 +354,8 @@
         )(x, *bases, *some)
         return spread_out(made, "gz", n_z)
 
-    firsts = product(weights[2 : 4 if half else 3], [base, one_hop], 4, "middle_columns")
-    lasts = product(weights[4 if half else 3 :], [], 8, "last_columns")
+    firsts = product(weights[2:3], [base, one_hop], 4, "middle_columns")
+    lasts = product(weights[3:], [], 8, "last_columns")
     smalls = spread_out([small] * n_z, "gz", n_z)
 
     def chip_sums(parts, sides, name):
@@ -374,7 +375,7 @@
     last_parts = chip_sums(lasts, smalls, "last_sums")
 
     return pl.pallas_call(
-        functools.partial(final_kernel, n_y, n_z, step),
+        functools.partial(final_kernel, n_y, n_z, min(512, columns // 4)),
         out_shape=jax.ShapeDtypeStruct((rows_here, columns), bf16),
         in_specs=[VMEM] * (2 + 2 * n_y),
         out_specs=VMEM,

time: 35.2 us -> 35.2 us (level)
  starting transfers between devices: 11.8 us -> 13 us
  Pallas kernels: 18.9 us -> 18.2 us
  waiting for transfers between devices: 4.21 us -> 3.61 us
    ppermute x10, starting transfers between devices: 11.8 us -> 13 us  [send(): return lax.ppermute(value, axis, [(j, j ^ k) for j in range(n)])]
    pallas_call x1, Pallas kernels: 7.27 us -> 6.02 us  [body(): pl.pallas_call(functools.partial(first_load_kernel, len(loads[0])), out_s...]
    ppermute x10, waiting for transfers between devices: 4.21 us -> 3.61 us  [send(): return lax.ppermute(value, axis, [(j, j ^ k) for j in range(n)])]
    pallas_call x1, Pallas kernels: 3.63 us -> 4.21 us  [body(): pl.pallas_call(functools.partial(last_load_kernel, len(loads[1]), sum(loa...]
  transfers between devices with their start and end apart: 10 -> 10, of which waited for: 2 -> 2; matrix products, arithmetic and copies ran while one was open for 0% -> 0% of each run, Pallas kernels for 50% -> 48%
where the time goes in v17:
time: 35.2 us; the launch traced here: 35 us
  Pallas kernels  18.2 us (52%)
  starting transfers between devices  13 us (37%)
  waiting for transfers between devices  3.61 us (10%)
    ppermute x10, starting transfers between devices, send(): return lax.ppermute(value, axis, [(j, j ^ k) for j in range(n)])  13 us
    pallas_call x1, Pallas kernels, body(): pl.pallas_call(functools.partial(first_load_kernel, len(loads[0])), out_s...  6.02 us
    pallas_call x1, Pallas kernels, body(): pl.pallas_call(functools.partial(last_load_kernel, len(loads[1]), sum(loa...  4.21 us
    ppermute x10, waiting for transfers between devices, send(): return lax.ppermute(value, axis, [(j, j ^ k) for j in range(n)])  3.61 us
    pallas_call x2, Pallas kernels, product(): pl.pallas_call(functools.partial(product_kernel, len(some), n_y, n_z, ste...  3.2 us
    pallas_call x1, Pallas kernels, body(): pl.pallas_call(functools.partial(base_kernel, 2, columns - late, step), o...  3.12 us
    pallas_call x1, Pallas kernels, body(): pl.pallas_call(functools.partial(final_kernel, n_y, n_z, min(512, columns...  1.09 us
  transfers between devices with their start and end apart: 10, of which 2 were waited for; matrix products, arithmetic and copies ran while one was open for 0% of the time, Pallas kernels for 48%

profile of v17, /device:TPU:0, one launch (start us, length us, event | category | flops | bytes accessed | tf_op | source)
XLA Modules:
  0.0 35.0 jit_solution(16218536307185540344)
XLA Ops:
  0.0 4.0 %collective-permute-start = (bf16[16,4096]{1,0:T(8,128)(2,1)}, bf16[16,4096]{1,0:T(8,128)(2,1)S(1)}, u32[]{:S(2)}, u32[]{:S(2)}) collective-permute-start(bf16[16,4096]{1,0:T(8,128)(2,1)} %refs_0_.1), channel_id=1, source_target_pairs={{0,8},{4,12},{8,0},{12,4},{1,9},{5,13},{9,1},{13,5},{2,10},{6,14},... | collective-permute-start | bytes 393224 | tf_op jit(solution)/shard_map/ppermute | solution.py:250
  4.0 1.6 %collective-permute-start.1 = (bf16[16,4096]{1,0:T(8,128)(2,1)}, bf16[16,4096]{1,0:T(8,128)(2,1)S(1)}, u32[]{:S(2)}, u32[]{:S(2)}) collective-permute-start(bf16[16,4096]{1,0:T(8,128)(2,1)} %refs_0_.1), channel_id=1, source_target_pairs={{0,4},{4,0},{8,12},{12,8},{1,5},{5,1},{9,13},{13,9},{2,6},{6,2},{1... | collective-permute-start | bytes 393224 | tf_op jit(solution)/shard_map/ppermute | solution.py:250
  5.6 6.0 %first_load.1 = (f32[1,64,64]{2,1,0:T(8,128)S(1)}, f32[64,256]{1,0:T(8,128)S(1)}, bf16[4096,1024]{1,0:T(8,128)(2,1)S(1)}, bf16[4096,1024]{1,0:T(8,128)(2,1)S(1)}) custom-call(bf16[4096,4096]{1,0:T(8,128)(2,1)} %w_hbm.5, s32[4]{0:T(128)} %rank_hbm.1, s32[4]{0:T(128)} %slot_hbm.1, s32[5]{0:T(128)} %start_hbm.1), custom_call_target="tpu_custom_call" | custom-call | flops 5033164800 | bytes 16777216 | tf_op jit(solution)/shard_map/first_load/pallas_call | solution.py:278
  11.6 0.0 collective-permute-done.refs_1_.__
  11.6 0.5 %collective-permute-start.2 = (bf16[16,4096]{1,0:T(8,128)(2,1)S(1)}, bf16[16,4096]{1,0:T(8,128)(2,1)S(1)}, u32[]{:S(2)}, u32[]{:S(2)}) collective-permute-start(bf16[16,4096]{1,0:T(8,128)(2,1)S(1)} %collective-permute-done.refs_1_.__), channel_id=1, source_target_pairs={{0,4},{4,0},{8,12},{12,8},{1,5},{5,1},{9,13},{13,9},{2,6},{6,2},{1... | collective-permute-start | bytes 393224 | tf_op jit(solution)/shard_map/ppermute | solution.py:250
  12.2 4.2 %last_load.1 = (bf16[4096,1024]{1,0:T(8,128)(2,1)S(1)}, bf16[4096,256]{1,0:T(8,128)(2,1)S(1)}) custom-call(bf16[4096,4096]{1,0:T(8,128)(2,1)} %w_hbm.5, f32[1,64,64]{2,1,0:T(8,128)S(1)} %get-tuple-element.24.factor_ref._, bf16[16,4096]{1,0:T(8,128)(2,1)S(1)} %collective-permute-done.refs_1_.__), custom_call_target="tpu_custom_call" | custom-call | flops 5033164800 | bytes 16777216 | tf_op jit(solution)/shard_map/last_load/pallas_call | solution.py:296
  16.4 0.3 collective-permute-done.2.refs_3_
  16.7 0.4 %scaled_rows.1 = (bf16[64,4096]{1,0:T(8,128)(2,1)S(1)}, bf16[64,256]{1,0:T(8,128)(2,1)S(1)}) custom-call(bf16[4096]{0:T(1024)(128)(2,1)S(1)} %copy-done.3, bf16[1,64,4096]{2,1,0:T(8,128)(2,1)S(1)} %bitcast.1, f32[1,64,64]{2,1,0:T(8,128)S(1)} %get-tuple-element.24.factor_ref._, bf16[16,4096]{1,0:T(8,128)(2,1)S(1)} %copy-done.2, ...), custom_call_target="tpu_custom_call" | custom-call | tf_op jit(solution)/shard_map/scaled_rows/pallas_call | solution.py:308
  17.1 1.4 %collective-permute-start.3 = (bf16[64,256]{1,0:T(8,128)(2,1)S(1)}, bf16[64,256]{1,0:T(8,128)(2,1)S(1)}, u32[]{:S(2)}, u32[]{:S(2)}) collective-permute-start(bf16[64,256]{1,0:T(8,128)(2,1)S(1)} %get-tuple-element.29), channel_id=1, source_target_pairs={{0,4},{4,0},{8,12},{12,8},{1,5},{5,1},{9,13},{13,9},{2,6},{6,2},{1... | collective-permute-start | bytes 98312 | tf_op jit(solution)/shard_map/ppermute | solution.py:250
  18.5 3.1 %first_columns.1 = (f32[64,2048]{1,0:T(8,128)S(1)}, bf16[4096,768]{1,0:T(8,128)(2,1)S(1)}) custom-call(bf16[4096,4096]{1,0:T(8,128)(2,1)} %w_hbm.5, bf16[64,4096]{1,0:T(8,128)(2,1)S(1)} %get-tuple-element.25.x_ref, bf16[4096,1024]{1,0:T(8,128)(2,1)S(1)} %get-tuple-element.26.refs_0_, bf16[4096,1024]{1,0:T(8,128)(2,1)S(1)} %get-tuple-element.27.refs_1_), custom_call_target="tpu_custom_call" | custom-call | flops 1073741824 | bytes 16777216 | tf_op jit(solution)/shard_map/first_columns/pallas_call | solution.py:329
  21.6 0.0 collective-permute-done.3
  21.7 2.1 %collective-permute-start.7 = (bf16[64,256]{1,0:T(8,128)(2,1)S(1)}, bf16[64,256]{1,0:T(8,128)(2,1)S(1)}, u32[]{:S(2)}, u32[]{:S(2)}) collective-permute-start(bf16[64,256]{1,0:T(8,128)(2,1)S(1)} %add.6.refs_1_), channel_id=1, source_target_pairs={{0,8},{4,12},{8,0},{12,4},{1,9},{5,13},{9,1},{13,5},{2,10},{6,14},... | collective-permute-start | bytes 98312 | tf_op jit(solution)/shard_map/ppermute | solution.py:250
  23.8 1.6 %middle_columns.1 = (f32[32,3072]{1,0:T(8,128)S(1)}, bf16[32,3072]{1,0:T(8,128)(2,1)S(1)}) custom-call(bf16[64,4096]{1,0:T(8,128)(2,1)S(1)} %get-tuple-element.25.x_ref, f32[64,2048]{1,0:T(8,128)S(1)} %get-tuple-element.28.refs_0_, bf16[64,256]{1,0:T(8,128)(2,1)S(1)} %add.6.refs_1_, bf16[4096,1024]{1,0:T(8,128)(2,1)S(1)} %get-tuple-element.30.refs_2_), custom_call_target="tpu_custom_call" | custom-call | flops 6442450944 | bytes 25165824 | tf_op jit(solution)/shard_map/middle_columns/pallas_call | solution.py:345
  25.4 0.1 collective-permute-start.4
  25.5 0.0 copy-start
  25.5 1.6 %last_columns.1 = (f32[32,1024]{1,0:T(8,128)S(1)}, bf16[32,1024]{1,0:T(8,128)(2,1)S(1)}) custom-call(bf16[64,4096]{1,0:T(8,128)(2,1)S(1)} %get-tuple-element.25.x_ref, bf16[4096,256]{1,0:T(8,128)(2,1)S(1)} %get-tuple-element.35.refs_0_, bf16[4096,768]{1,0:T(8,128)(2,1)S(1)} %get-tuple-element.36.refs_1_), custom_call_target="tpu_custom_call" | custom-call | flops 4294967296 | bytes 8388608 | tf_op jit(solution)/shard_map/last_columns/pallas_call | solution.py:345
  27.1 0.6 %collective-permute-start.6 = (bf16[32,1024]{1,0:T(8,128)(2,1)S(1)}, bf16[32,1024]{1,0:T(8,128)(2,1)S(1)}, u32[]{:S(2)}, u32[]{:S(2)}) collective-permute-start(bf16[32,1024]{1,0:T(8,128)(2,1)S(1)} %get-tuple-element.38), channel_id=1, source_target_pairs={{0,1},{1,0},{2,3},{3,2},{4,5},{5,4},{6,7},{7,6},{8,9},{9,8},{10,11... | collective-permute-start | bytes 196616 | tf_op jit(solution)/shard_map/ppermute | solution.py:250
  27.7 0.0 collective-permute-done.7
  27.7 0.1 collective-permute-start.8
  27.8 1.6 %collective-permute-start.5 = (bf16[16,3072]{1,0:T(8,128)(2,1)S(1)}, bf16[16,3072]{1,0:T(8,128)(2,1)S(1)}, u32[]{:S(2)}, u32[]{:S(2)}) collective-permute-start(bf16[16,3072]{1,0:T(8,128)(2,1)S(1)} %get-tuple-element.34), channel_id=1, source_target_pairs={{0,2},{2,0},{1,3},{3,1},{4,6},{6,4},{5,7},{7,5},{8,10},{10,8},{9,1... | collective-permute-start | bytes 294920 | tf_op jit(solution)/shard_map/ppermute | solution.py:250
  29.4 0.2 last_sums.1
  29.5 1.1 %collective-permute-start.9 = (bf16[16,1280]{1,0:T(8,128)(2,1)S(1)}, bf16[16,1280]{1,0:T(8,128)(2,1)S(1)}, u32[]{:S(2)}, u32[]{:S(2)}) collective-permute-start(bf16[16,1280]{1,0:T(8,128)(2,1)S(1)} %get-tuple-element.40), channel_id=1, source_target_pairs={{0,2},{2,0},{1,3},{3,1},{4,6},{6,4},{5,7},{7,5},{8,10},{10,8},{9,1... | collective-permute-start | bytes 122888 | tf_op jit(solution)/shard_map/ppermute | solution.py:250
  30.6 3.3 %collective-permute-done.9.refs_3_ = bf16[16,1280]{1,0:T(8,128)(2,1)S(1)} collective-permute-done((bf16[16,1280]{1,0:T(8,128)(2,1)S(1)}, bf16[16,1280]{1,0:T(8,128)(2,1)S(1)}, u32[]{:S(2)}, u32[]{:S(2)}) %collective-permute-start.9) | collective-permute-done | bytes 40992 | tf_op jit(solution)/shard_map/ppermute | solution.py:250
  33.9 1.1 %query_rows.1 = bf16[16,4096]{1,0:T(8,128)(2,1)} custom-call(f32[64,256]{1,0:T(8,128)S(1)} %get-tuple-element.23.spread_ref, bf16[4,64,4096]{2,1,0:T(8,128)(2,1)S(1)} %copy-done, f32[16,3072]{1,0:T(8,128)S(1)} %get-tuple-element.33.refs_0_, bf16[16,3072]{1,0:T(8,128)(2,1)S(1)} %collective-permute-done.5.refs_1_, f32[16,1280]{1,0:T(8,128)S(1)} %get-tuple-element.39.refs_2_, ...), custom_call_target="tpu_custom_call" | custom-call | tf_op jit(solution)/shard_map/query_rows/pallas_call | solution.py:377
  (15 shorter events, 0.1 us)
Async XLA Ops:
  0.0 11.6 %collective-permute-start = (bf16[16,4096]{1,0:T(8,128)(2,1)}, bf16[16,4096]{1,0:T(8,128)(2,1)S(1)}, u32[]{:S(2)}, u32[]{:S(2)}) collective-permute-start(bf16[16,4096]{1,0:T(8,128)(2,1)} %refs_0_.1), channel_id=1, source_target_pairs={{0,8},{4,12},{8,0},{12,4},{1,9},{5,13},{9,1},{13,5},{2,10},{6,14},... | collective-permute-start | bytes 393224 | tf_op jit(solution)/shard_map/ppermute | solution.py:250
  4.0 12.4 %collective-permute-start.1 = (bf16[16,4096]{1,0:T(8,128)(2,1)}, bf16[16,4096]{1,0:T(8,128)(2,1)S(1)}, u32[]{:S(2)}, u32[]{:S(2)}) collective-permute-start(bf16[16,4096]{1,0:T(8,128)(2,1)} %refs_0_.1), channel_id=1, source_target_pairs={{0,4},{4,0},{8,12},{12,8},{1,5},{5,1},{9,13},{13,9},{2,6},{6,2},{1... | collective-permute-start | bytes 393224 | tf_op jit(solution)/shard_map/ppermute | solution.py:250
  11.6 5.0 %collective-permute-start.2 = (bf16[16,4096]{1,0:T(8,128)(2,1)S(1)}, bf16[16,4096]{1,0:T(8,128)(2,1)S(1)}, u32[]{:S(2)}, u32[]{:S(2)}) collective-permute-start(bf16[16,4096]{1,0:T(8,128)(2,1)S(1)} %collective-permute-done.refs_1_.__), channel_id=1, source_target_pairs={{0,4},{4,0},{8,12},{12,8},{1,5},{5,1},{9,13},{13,9},{2,6},{6,2},{1... | collective-permute-start | bytes 393224 | tf_op jit(solution)/shard_map/ppermute | solution.py:250
  12.2 4.5 %copy-start.1 = (bf16[1,4096,64]{1,2,0:T(8,128)(2,1)S(1)}, bf16[1,4096,64]{1,2,0:T(8,128)(2,1)}, u32[]{:S(2)}) copy-start(bf16[1,4096,64]{1,2,0:T(8,128)(2,1)} %param.12) | copy-start | bytes 1572868
  12.2 4.5 %copy-start.2 = (bf16[16,4096]{1,0:T(8,128)(2,1)S(1)}, bf16[16,4096]{1,0:T(8,128)(2,1)}, u32[]{:S(2)}) copy-start(bf16[16,4096]{1,0:T(8,128)(2,1)} %refs_0_.1) | copy-start | bytes 393220
  12.2 4.5 %copy-start.3 = (bf16[4096]{0:T(1024)(128)(2,1)S(1)}, bf16[4096]{0:T(1024)(128)(2,1)}, u32[]{:S(2)}) copy-start(bf16[4096]{0:T(1024)(128)(2,1)} %gain_ref.1) | copy-start | bytes 24580
  17.1 4.5 %collective-permute-start.3 = (bf16[64,256]{1,0:T(8,128)(2,1)S(1)}, bf16[64,256]{1,0:T(8,128)(2,1)S(1)}, u32[]{:S(2)}, u32[]{:S(2)}) collective-permute-start(bf16[64,256]{1,0:T(8,128)(2,1)S(1)} %get-tuple-element.29), channel_id=1, source_target_pairs={{0,4},{4,0},{8,12},{12,8},{1,5},{5,1},{9,13},{13,9},{2,6},{6,2},{1... | collective-permute-start | bytes 98312 | tf_op jit(solution)/shard_map/ppermute | solution.py:250
  21.7 6.0 %collective-permute-start.7 = (bf16[64,256]{1,0:T(8,128)(2,1)S(1)}, bf16[64,256]{1,0:T(8,128)(2,1)S(1)}, u32[]{:S(2)}, u32[]{:S(2)}) collective-permute-start(bf16[64,256]{1,0:T(8,128)(2,1)S(1)} %add.6.refs_1_), channel_id=1, source_target_pairs={{0,8},{4,12},{8,0},{12,4},{1,9},{5,13},{9,1},{13,5},{2,10},{6,14},... | collective-permute-start | bytes 98312 | tf_op jit(solution)/shard_map/ppermute | solution.py:250
  25.4 2.3 %collective-permute-start.4 = (bf16[32,3072]{1,0:T(8,128)(2,1)S(1)}, bf16[32,3072]{1,0:T(8,128)(2,1)S(1)}, u32[]{:S(2)}, u32[]{:S(2)}) collective-permute-start(bf16[32,3072]{1,0:T(8,128)(2,1)S(1)} %get-tuple-element.32), channel_id=1, source_target_pairs={{0,1},{1,0},{2,3},{3,2},{4,5},{5,4},{6,7},{7,6},{8,9},{9,8},{10,11... | collective-permute-start | bytes 589832 | tf_op jit(solution)/shard_map/ppermute | solution.py:250
  25.5 8.4 %copy-start = (bf16[4,64,4096]{2,1,0:T(8,128)(2,1)S(1)}, bf16[4,64,4096]{2,1,0:T(8,128)(2,1)}, u32[]{:S(2)}) copy-start(bf16[4,64,4096]{2,1,0:T(8,128)(2,1)} %up_ref.1) | copy-start | bytes 6291460
  27.1 2.3 %collective-permute-start.6 = (bf16[32,1024]{1,0:T(8,128)(2,1)S(1)}, bf16[32,1024]{1,0:T(8,128)(2,1)S(1)}, u32[]{:S(2)}, u32[]{:S(2)}) collective-permute-start(bf16[32,1024]{1,0:T(8,128)(2,1)S(1)} %get-tuple-element.38), channel_id=1, source_target_pairs={{0,1},{1,0},{2,3},{3,2},{4,5},{5,4},{6,7},{7,6},{8,9},{9,8},{10,11... | collective-permute-start | bytes 196616 | tf_op jit(solution)/shard_map/ppermute | solution.py:250
  27.7 1.7 %collective-permute-start.8 = (bf16[64,256]{1,0:T(8,128)(2,1)S(1)}, bf16[64,256]{1,0:T(8,128)(2,1)S(1)}, u32[]{:S(2)}, u32[]{:S(2)}) collective-permute-start(bf16[64,256]{1,0:T(8,128)(2,1)S(1)} %add.7.refs_2_), channel_id=1, source_target_pairs={{0,1},{1,0},{2,3},{3,2},{4,5},{5,4},{6,7},{7,6},{8,9},{9,8},{10,11... | collective-permute-start | bytes 98312 | tf_op jit(solution)/shard_map/ppermute | solution.py:250
  27.8 6.1 %collective-permute-start.5 = (bf16[16,3072]{1,0:T(8,128)(2,1)S(1)}, bf16[16,3072]{1,0:T(8,128)(2,1)S(1)}, u32[]{:S(2)}, u32[]{:S(2)}) collective-permute-start(bf16[16,3072]{1,0:T(8,128)(2,1)S(1)} %get-tuple-element.34), channel_id=1, source_target_pairs={{0,2},{2,0},{1,3},{3,1},{4,6},{6,4},{5,7},{7,5},{8,10},{10,8},{9,1... | collective-permute-start | bytes 294920 | tf_op jit(solution)/shard_map/ppermute | solution.py:250
  29.5 4.4 %collective-permute-start.9 = (bf16[16,1280]{1,0:T(8,128)(2,1)S(1)}, bf16[16,1280]{1,0:T(8,128)(2,1)S(1)}, u32[]{:S(2)}, u32[]{:S(2)}) collective-permute-start(bf16[16,1280]{1,0:T(8,128)(2,1)S(1)} %get-tuple-element.40), channel_id=1, source_target_pairs={{0,2},{2,0},{1,3},{3,1},{4,6},{6,4},{5,7},{7,5},{8,10},{10,8},{9,1... | collective-permute-start | bytes 122888 | tf_op jit(solution)/shard_map/ppermute | solution.py:250

commit v18 on v17

--- a/solution.py
+++ b/solution.py
@@ -162,6 +162,10 @@
         copy.wait()
 
 
+def last_kernel(n_w, step, x_ref, *refs):
+    multiply(x_ref, refs[:n_w], step, refs[n_w], 0)
+
+
 def product_kernel(n_w, n_y, n_z, step, first, x_ref, *refs):
     if first:
         base_ref, refs = refs[0], refs[2:]
@@ -172,29 +176,29 @@
     write_rows(acc, outs, n_y, n_z)
 
 
-def chip_rows(parts, here):
-    total = parts[0][here, :].astype(jnp.float32)
-    for part in parts[1:]:
-        total = total + part[here, :].astype(jnp.float32)
-    return total
-
-
-def pair_kernel(n_y, n_z, *refs):
-    parts, smalls, outs = refs[:n_z], refs[n_z:-n_y], refs[-n_y:]
-    rows_here = outs[0].shape[0]
-    columns = parts[0].shape[1]
-    y, z = lax.axis_index("gy"), lax.axis_index("gz")
+def first_sums_kernel(n_y, n_z, last_ref, small_ref, *refs):
+    parts, outs, last_outs = refs[:n_z], refs[n_z : n_z + n_y], refs[n_z + n_y :]
+    pair_kernel(n_y, False, *parts, *outs)
+    columns = last_ref.shape[1]
+    write_rows(last_ref, [out.at[:, :columns] for out in last_outs], n_y, n_z)
+    write_rows(small_ref, [out.at[:, columns:] for out in last_outs], n_y, n_z)
+
+
+def pair_kernel(n_y, side, *refs):
+    parts, outs = refs[:-n_y], refs[-n_y:]
+    rows_here, columns = outs[0].shape
+    late = columns - (LANES if side else 0)
+    y = lax.axis_index("gy")
     for k in range(n_y):
-        other = jnp.bitwise_xor(y, k)
-        here = pl.ds(pl.multiple_of(other * rows_here, rows_here), rows_here)
-        outs[k][:, :columns] = chip_rows(parts, here).astype(outs[k].dtype)
-        if smalls:
-            owner = other * n_z + z
-            here = pl.ds(pl.multiple_of(owner * rows_here, rows_here), rows_here)
-            small = chip_rows(smalls, here)
-            square = jnp.broadcast_to(join_wide(small[:, LANES:]), (rows_here, LANES))
-            outs[k][:, columns : columns + LANES] = small[:, :LANES].astype(outs[k].dtype)
-            outs[k][:, columns + LANES :] = split_wide(square).astype(outs[k].dtype)
+        begin = pl.multiple_of(jnp.bitwise_xor(y, k) * rows_here, rows_here)
+        here = pl.ds(begin, rows_here)
+        total = parts[0][here, :].astype(jnp.float32)
+        for part in parts[1:]:
+            total = total + part[here, :].astype(jnp.float32)
+        outs[k][:, :late] = total[:, :late].astype(outs[k].dtype)
+        if side:
+            square = jnp.broadcast_to(join_wide(total[:, late:]), (rows_here, LANES))
+            outs[k][:, late:] = split_wide(square).astype(outs[k].dtype)
 
 
 def final_kernel(n, n_z, step, spread_ref, up_ref, *refs):
@@ -341,7 +345,7 @@
 
     def product(some, bases, times, name):
         first = sum(part.shape[1] for part in bases[:1])
-        wide = first + quarter
+        wide = first + sum(w.shape[1] for w in some)
         made = pl.pallas_call(
             functools.partial(product_kernel, len(some), n_y, n_z, step, first),
             out_shape=shapes(n_z, (kept, wide)),
@@ -354,25 +358,41 @@
         )(x, *bases, *some)
         return spread_out(made, "gz", n_z)
 
-    firsts = product(weights[2:3], [base, one_hop], 4, "middle_columns")
-    lasts = product(weights[3:], [], 8, "last_columns")
-    smalls = spread_out([small] * n_z, "gz", n_z)
-
-    def chip_sums(parts, sides, name):
-        wide = parts[0].shape[1] + (2 * LANES if sides else 0)
-        made = pl.pallas_call(
-            functools.partial(pair_kernel, n_y, n_z),
-            out_shape=shapes(n_y, (rows_here, wide)),
-            in_specs=[VMEM] * (n_z + len(sides)),
-            out_specs=[VMEM] * n_y,
-            cost_estimate=cost(2 * rows * depth * quarter, 2 * depth * quarter),
-            compiler_params=roomy,
-            name=name,
-        )(*parts, *sides)
-        return spread_out(made, "gy", n_y)
-
-    first_parts = chip_sums(firsts, [], "first_sums")
-    last_parts = chip_sums(lasts, smalls, "last_sums")
+    split = 3
+    last_columns = sum(w.shape[1] for w in weights[split:])
+    firsts = product(weights[2:split], [base, one_hop], 4, "middle_columns")
+    last = pl.pallas_call(
+        functools.partial(last_kernel, len(weights) - split, step),
+        out_shape=jax.ShapeDtypeStruct((rows, last_columns), f32),
+        in_specs=[VMEM] * (len(weights) - split + 1),
+        out_specs=VMEM,
+        cost_estimate=cost(16 * rows * depth * quarter, 2 * depth * quarter),
+        compiler_params=roomy,
+        name="last_columns",
+    )(x, *weights[split:])
+    wide = firsts[0].shape[1]
+    made = pl.pallas_call(
+        functools.partial(first_sums_kernel, n_y, n_z),
+        out_shape=shapes(n_y, (rows_here, wide)) + shapes(n_z, (kept, last_columns + 2 * LANES)),
+        in_specs=[VMEM] * (2 + n_z),
+        out_specs=[VMEM] * (n_y + n_z),
+        cost_estimate=cost(0, 0),
+        compiler_params=roomy,
+        name="first_sums",
+    )(last, small, *firsts)
+    first_parts = spread_out(made[:n_y], "gy", n_y)
+    lasts = spread_out(made[n_y:], "gz", n_z)
+
+    made = pl.pallas_call(
+        functools.partial(pair_kernel, n_y, True),
+        out_shape=shapes(n_y, (rows_here, last_columns + 2 * LANES)),
+        in_specs=[VMEM] * n_z,
+        out_specs=[VMEM] * n_y,
+        cost_estimate=cost(0, 0),
+        compiler_params=roomy,
+        name="last_sums",
+    )(*lasts)
+    last_parts = spread_out(made, "gy", n_y)
 
     return pl.pallas_call(
         functools.partial(final_kernel, n_y, n_z, min(512, columns // 4)),

time: 35.2 us -> 34.7 us (0.986)
    pallas_call x2 -> x1, Pallas kernels: 3.2 us -> 1.62 us  [product(): pl.pallas_call(functools.partial(product_kernel, len(some), n_y, n_z, ste...]
    pallas_call x2 -> x3, Pallas kernels: 0.2 us -> 1.77 us  [the longest x1 1.56 us: body(): pl.pallas_call(functools.partial(last_kernel, len(weights) - split, step)...]
    ppermute x10 -> x9, starting transfers between devices: 13 us -> 12.7 us  [send(): return lax.ppermute(value, axis, [(j, j ^ k) for j in range(n)])]
    ppermute x10 -> x9, waiting for transfers between devices: 3.61 us -> 3.38 us  [send(): return lax.ppermute(value, axis, [(j, j ^ k) for j in range(n)])]
  transfers between devices with their start and end apart: 10 -> 9, of which waited for: 2 -> 3; matrix products, arithmetic and copies ran while one was open for 0% -> 0% of each run, Pallas kernels for 48% -> 48%
where the time goes in v18:
time: 34.7 us; the launch traced here: 34.5 us
  Pallas kernels  18.2 us (52%)
  starting transfers between devices  12.7 us (37%)
  waiting for transfers between devices  3.38 us (10%)
    ppermute x9, starting transfers between devices, send(): return lax.ppermute(value, axis, [(j, j ^ k) for j in range(n)])  12.7 us
    pallas_call x1, Pallas kernels, body(): pl.pallas_call(functools.partial(first_load_kernel, len(loads[0])), out_s...  6.02 us
    pallas_call x1, Pallas kernels, body(): pl.pallas_call(functools.partial(last_load_kernel, len(loads[1]), sum(loa...  4.21 us
    ppermute x9, waiting for transfers between devices, send(): return lax.ppermute(value, axis, [(j, j ^ k) for j in range(n)])  3.38 us
    pallas_call x1, Pallas kernels, body(): pl.pallas_call(functools.partial(base_kernel, 2, columns - late, step), o...  3.12 us
    pallas_call x1, Pallas kernels, product(): pl.pallas_call(functools.partial(product_kernel, len(some), n_y, n_z, ste...  1.62 us
    pallas_call x1, Pallas kernels, body(): pl.pallas_call(functools.partial(last_kernel, len(weights) - split, step)...  1.56 us
    pallas_call x1, Pallas kernels, body(): pl.pallas_call(functools.partial(final_kernel, n_y, n_z, min(512, columns...  1.09 us
  transfers between devices with their start and end apart: 9, of which 3 were waited for; matrix products, arithmetic and copies ran while one was open for 0% of the time, Pallas kernels for 48%

profile of v18, /device:TPU:0, one launch (start us, length us, event | category | flops | bytes accessed | tf_op | source)
XLA Modules:
  0.0 34.5 jit_solution(16696044127602927646)
XLA Ops:
  0.0 4.0 %collective-permute-start = (bf16[16,4096]{1,0:T(8,128)(2,1)}, bf16[16,4096]{1,0:T(8,128)(2,1)S(1)}, u32[]{:S(2)}, u32[]{:S(2)}) collective-permute-start(bf16[16,4096]{1,0:T(8,128)(2,1)} %refs_0_.1), channel_id=1, source_target_pairs={{0,8},{4,12},{8,0},{12,4},{1,9},{5,13},{9,1},{13,5},{2,10},{6,14},... | collective-permute-start | bytes 393224 | tf_op jit(solution)/shard_map/ppermute | solution.py:254
  4.0 1.6 %collective-permute-start.1 = (bf16[16,4096]{1,0:T(8,128)(2,1)}, bf16[16,4096]{1,0:T(8,128)(2,1)S(1)}, u32[]{:S(2)}, u32[]{:S(2)}) collective-permute-start(bf16[16,4096]{1,0:T(8,128)(2,1)} %refs_0_.1), channel_id=1, source_target_pairs={{0,4},{4,0},{8,12},{12,8},{1,5},{5,1},{9,13},{13,9},{2,6},{6,2},{1... | collective-permute-start | bytes 393224 | tf_op jit(solution)/shard_map/ppermute | solution.py:254
  5.6 6.0 %first_load.1 = (f32[1,64,64]{2,1,0:T(8,128)S(1)}, f32[64,256]{1,0:T(8,128)S(1)}, bf16[4096,1024]{1,0:T(8,128)(2,1)S(1)}, bf16[4096,1024]{1,0:T(8,128)(2,1)S(1)}) custom-call(bf16[4096,4096]{1,0:T(8,128)(2,1)} %w_hbm.5, s32[4]{0:T(128)} %rank_hbm.1, s32[4]{0:T(128)} %slot_hbm.1, s32[5]{0:T(128)} %start_hbm.1), custom_call_target="tpu_custom_call" | custom-call | flops 5033164800 | bytes 16777216 | tf_op jit(solution)/shard_map/first_load/pallas_call | solution.py:282
  11.6 0.5 %collective-permute-start.2 = (bf16[16,4096]{1,0:T(8,128)(2,1)S(1)}, bf16[16,4096]{1,0:T(8,128)(2,1)S(1)}, u32[]{:S(2)}, u32[]{:S(2)}) collective-permute-start(bf16[16,4096]{1,0:T(8,128)(2,1)S(1)} %collective-permute-done.refs_1_.__), channel_id=1, source_target_pairs={{0,4},{4,0},{8,12},{12,8},{1,5},{5,1},{9,13},{13,9},{2,6},{6,2},{1... | collective-permute-start | bytes 393224 | tf_op jit(solution)/shard_map/ppermute | solution.py:254
  12.2 4.2 %last_load.1 = (bf16[4096,1024]{1,0:T(8,128)(2,1)S(1)}, bf16[4096,256]{1,0:T(8,128)(2,1)S(1)}) custom-call(bf16[4096,4096]{1,0:T(8,128)(2,1)} %w_hbm.5, f32[1,64,64]{2,1,0:T(8,128)S(1)} %get-tuple-element.24.factor_ref._, bf16[16,4096]{1,0:T(8,128)(2,1)S(1)} %collective-permute-done.refs_1_.__), custom_call_target="tpu_custom_call" | custom-call | flops 5033164800 | bytes 16777216 | tf_op jit(solution)/shard_map/last_load/pallas_call | solution.py:300
  16.4 0.0 collective-permute-done.1.refs_2_
  16.4 0.3 collective-permute-done.2.refs_3_
  16.7 0.4 %scaled_rows.1 = (bf16[64,4096]{1,0:T(8,128)(2,1)S(1)}, bf16[64,256]{1,0:T(8,128)(2,1)S(1)}) custom-call(bf16[4096]{0:T(1024)(128)(2,1)S(1)} %copy-done.3, bf16[1,64,4096]{2,1,0:T(8,128)(2,1)S(1)} %bitcast.1, f32[1,64,64]{2,1,0:T(8,128)S(1)} %get-tuple-element.24.factor_ref._, bf16[16,4096]{1,0:T(8,128)(2,1)S(1)} %copy-done.2, ...), custom_call_target="tpu_custom_call" | custom-call | tf_op jit(solution)/shard_map/scaled_rows/pallas_call | solution.py:312
  17.1 1.4 %collective-permute-start.3 = (bf16[64,256]{1,0:T(8,128)(2,1)S(1)}, bf16[64,256]{1,0:T(8,128)(2,1)S(1)}, u32[]{:S(2)}, u32[]{:S(2)}) collective-permute-start(bf16[64,256]{1,0:T(8,128)(2,1)S(1)} %get-tuple-element.30), channel_id=1, source_target_pairs={{0,4},{4,0},{8,12},{12,8},{1,5},{5,1},{9,13},{13,9},{2,6},{6,2},{1... | collective-permute-start | bytes 98312 | tf_op jit(solution)/shard_map/ppermute | solution.py:254
  18.5 3.1 %first_columns.1 = (f32[64,2048]{1,0:T(8,128)S(1)}, bf16[4096,768]{1,0:T(8,128)(2,1)S(1)}) custom-call(bf16[4096,4096]{1,0:T(8,128)(2,1)} %w_hbm.5, bf16[64,4096]{1,0:T(8,128)(2,1)S(1)} %get-tuple-element.25.x_ref, bf16[4096,1024]{1,0:T(8,128)(2,1)S(1)} %get-tuple-element.27.refs_0_, bf16[4096,1024]{1,0:T(8,128)(2,1)S(1)} %get-tuple-element.28.refs_1_), custom_call_target="tpu_custom_call" | custom-call | flops 1073741824 | bytes 16777216 | tf_op jit(solution)/shard_map/first_columns/pallas_call | solution.py:333
  21.6 0.0 collective-permute-done.3
  21.7 2.1 %collective-permute-start.4 = (bf16[64,256]{1,0:T(8,128)(2,1)S(1)}, bf16[64,256]{1,0:T(8,128)(2,1)S(1)}, u32[]{:S(2)}, u32[]{:S(2)}) collective-permute-start(bf16[64,256]{1,0:T(8,128)(2,1)S(1)} %add.6.refs_1_), channel_id=1, source_target_pairs={{0,8},{4,12},{8,0},{12,4},{1,9},{5,13},{9,1},{13,5},{2,10},{6,14},... | collective-permute-start | bytes 98312 | tf_op jit(solution)/shard_map/ppermute | solution.py:254
  23.8 1.6 %middle_columns.1 = (f32[32,3072]{1,0:T(8,128)S(1)}, bf16[32,3072]{1,0:T(8,128)(2,1)S(1)}) custom-call(bf16[64,4096]{1,0:T(8,128)(2,1)S(1)} %get-tuple-element.25.x_ref, f32[64,2048]{1,0:T(8,128)S(1)} %get-tuple-element.31.refs_0_, bf16[64,256]{1,0:T(8,128)(2,1)S(1)} %add.6.refs_1_, bf16[4096,1024]{1,0:T(8,128)(2,1)S(1)} %get-tuple-element.32.refs_2_), custom_call_target="tpu_custom_call" | custom-call | flops 6442450944 | bytes 25165824 | tf_op jit(solution)/shard_map/middle_columns/pallas_call | solution.py:349
  25.4 0.1 collective-permute-start.5
  25.5 0.0 copy-start
  25.5 1.6 %last_columns.1.last_ref = f32[64,1024]{1,0:T(8,128)S(1)} custom-call(bf16[64,4096]{1,0:T(8,128)(2,1)S(1)} %get-tuple-element.25.x_ref, bf16[4096,256]{1,0:T(8,128)(2,1)S(1)} %get-tuple-element.26.refs_0_, bf16[4096,768]{1,0:T(8,128)(2,1)S(1)} %get-tuple-element.29.refs_1_), custom_call_target="tpu_custom_call" | custom-call | flops 4294967296 | bytes 8388608 | tf_op jit(solution)/shard_map/last_columns/pallas_call | solution.py:364
  27.1 0.1 first_sums.1
  27.2 0.6 %collective-permute-start.7 = (bf16[32,1280]{1,0:T(8,128)(2,1)S(1)}, bf16[32,1280]{1,0:T(8,128)(2,1)S(1)}, u32[]{:S(2)}, u32[]{:S(2)}) collective-permute-start(bf16[32,1280]{1,0:T(8,128)(2,1)S(1)} %get-tuple-element.38), channel_id=1, source_target_pairs={{0,1},{1,0},{2,3},{3,2},{4,5},{5,4},{6,7},{7,6},{8,9},{9,8},{10,11... | collective-permute-start | bytes 245768 | tf_op jit(solution)/shard_map/ppermute | solution.py:254
  27.7 1.5 %collective-permute-start.6 = (bf16[16,3072]{1,0:T(8,128)(2,1)S(1)}, bf16[16,3072]{1,0:T(8,128)(2,1)S(1)}, u32[]{:S(2)}, u32[]{:S(2)}) collective-permute-start(bf16[16,3072]{1,0:T(8,128)(2,1)S(1)} %get-tuple-element.36), channel_id=1, source_target_pairs={{0,2},{2,0},{1,3},{3,1},{4,6},{6,4},{5,7},{7,5},{8,10},{10,8},{9,1... | collective-permute-start | bytes 294920 | tf_op jit(solution)/shard_map/ppermute | solution.py:254
  29.2 0.1 last_sums.1
  29.4 1.0 %collective-permute-start.8 = (bf16[16,1280]{1,0:T(8,128)(2,1)S(1)}, bf16[16,1280]{1,0:T(8,128)(2,1)S(1)}, u32[]{:S(2)}, u32[]{:S(2)}) collective-permute-start(bf16[16,1280]{1,0:T(8,128)(2,1)S(1)} %get-tuple-element.40), channel_id=1, source_target_pairs={{0,2},{2,0},{1,3},{3,1},{4,6},{6,4},{5,7},{7,5},{8,10},{10,8},{9,1... | collective-permute-start | bytes 122888 | tf_op jit(solution)/shard_map/ppermute | solution.py:254
  30.3 2.6 %collective-permute-done.6.refs_1_ = bf16[16,3072]{1,0:T(8,128)(2,1)S(1)} collective-permute-done((bf16[16,3072]{1,0:T(8,128)(2,1)S(1)}, bf16[16,3072]{1,0:T(8,128)(2,1)S(1)}, u32[]{:S(2)}, u32[]{:S(2)}) %collective-permute-start.6) | collective-permute-done | bytes 98336 | tf_op jit(solution)/shard_map/ppermute | solution.py:254
  33.0 0.5 %collective-permute-done.8.refs_3_ = bf16[16,1280]{1,0:T(8,128)(2,1)S(1)} collective-permute-done((bf16[16,1280]{1,0:T(8,128)(2,1)S(1)}, bf16[16,1280]{1,0:T(8,128)(2,1)S(1)}, u32[]{:S(2)}, u32[]{:S(2)}) %collective-permute-start.8) | collective-permute-done | bytes 40992 | tf_op jit(solution)/shard_map/ppermute | solution.py:254
  33.4 1.1 %query_rows.1 = bf16[16,4096]{1,0:T(8,128)(2,1)} custom-call(f32[64,256]{1,0:T(8,128)S(1)} %get-tuple-element.23.spread_ref, bf16[4,64,4096]{2,1,0:T(8,128)(2,1)S(1)} %copy-done, f32[16,3072]{1,0:T(8,128)S(1)} %get-tuple-element.35.refs_0_, bf16[16,3072]{1,0:T(8,128)(2,1)S(1)} %collective-permute-done.6.refs_1_, f32[16,1280]{1,0:T(8,128)S(1)} %get-tuple-element.39.refs_2_, ...), custom_call_target="tpu_custom_call" | custom-call | tf_op jit(solution)/shard_map/query_rows/pallas_call | solution.py:397
  (13 shorter events, 0.0 us)
Async XLA Ops:
  0.0 11.6 %collective-permute-start = (bf16[16,4096]{1,0:T(8,128)(2,1)}, bf16[16,4096]{1,0:T(8,128)(2,1)S(1)}, u32[]{:S(2)}, u32[]{:S(2)}) collective-permute-start(bf16[16,4096]{1,0:T(8,128)(2,1)} %refs_0_.1), channel_id=1, source_target_pairs={{0,8},{4,12},{8,0},{12,4},{1,9},{5,13},{9,1},{13,5},{2,10},{6,14},... | collective-permute-start | bytes 393224 | tf_op jit(solution)/shard_map/ppermute | solution.py:254
  4.0 12.4 %collective-permute-start.1 = (bf16[16,4096]{1,0:T(8,128)(2,1)}, bf16[16,4096]{1,0:T(8,128)(2,1)S(1)}, u32[]{:S(2)}, u32[]{:S(2)}) collective-permute-start(bf16[16,4096]{1,0:T(8,128)(2,1)} %refs_0_.1), channel_id=1, source_target_pairs={{0,4},{4,0},{8,12},{12,8},{1,5},{5,1},{9,13},{13,9},{2,6},{6,2},{1... | collective-permute-start | bytes 393224 | tf_op jit(solution)/shard_map/ppermute | solution.py:254
  11.6 5.0 %collective-permute-start.2 = (bf16[16,4096]{1,0:T(8,128)(2,1)S(1)}, bf16[16,4096]{1,0:T(8,128)(2,1)S(1)}, u32[]{:S(2)}, u32[]{:S(2)}) collective-permute-start(bf16[16,4096]{1,0:T(8,128)(2,1)S(1)} %collective-permute-done.refs_1_.__), channel_id=1, source_target_pairs={{0,4},{4,0},{8,12},{12,8},{1,5},{5,1},{9,13},{13,9},{2,6},{6,2},{1... | collective-permute-start | bytes 393224 | tf_op jit(solution)/shard_map/ppermute | solution.py:254
  12.2 4.5 %copy-start.1 = (bf16[1,4096,64]{1,2,0:T(8,128)(2,1)S(1)}, bf16[1,4096,64]{1,2,0:T(8,128)(2,1)}, u32[]{:S(2)}) copy-start(bf16[1,4096,64]{1,2,0:T(8,128)(2,1)} %param.12) | copy-start | bytes 1572868
  12.2 4.5 %copy-start.2 = (bf16[16,4096]{1,0:T(8,128)(2,1)S(1)}, bf16[16,4096]{1,0:T(8,128)(2,1)}, u32[]{:S(2)}) copy-start(bf16[16,4096]{1,0:T(8,128)(2,1)} %refs_0_.1) | copy-start | bytes 393220
  12.2 4.5 %copy-start.3 = (bf16[4096]{0:T(1024)(128)(2,1)S(1)}, bf16[4096]{0:T(1024)(128)(2,1)}, u32[]{:S(2)}) copy-start(bf16[4096]{0:T(1024)(128)(2,1)} %gain_ref.1) | copy-start | bytes 24580
  17.1 4.5 %collective-permute-start.3 = (bf16[64,256]{1,0:T(8,128)(2,1)S(1)}, bf16[64,256]{1,0:T(8,128)(2,1)S(1)}, u32[]{:S(2)}, u32[]{:S(2)}) collective-permute-start(bf16[64,256]{1,0:T(8,128)(2,1)S(1)} %get-tuple-element.30), channel_id=1, source_target_pairs={{0,4},{4,0},{8,12},{12,8},{1,5},{5,1},{9,13},{13,9},{2,6},{6,2},{1... | collective-permute-start | bytes 98312 | tf_op jit(solution)/shard_map/ppermute | solution.py:254
  21.7 5.4 %collective-permute-start.4 = (bf16[64,256]{1,0:T(8,128)(2,1)S(1)}, bf16[64,256]{1,0:T(8,128)(2,1)S(1)}, u32[]{:S(2)}, u32[]{:S(2)}) collective-permute-start(bf16[64,256]{1,0:T(8,128)(2,1)S(1)} %add.6.refs_1_), channel_id=1, source_target_pairs={{0,8},{4,12},{8,0},{12,4},{1,9},{5,13},{9,1},{13,5},{2,10},{6,14},... | collective-permute-start | bytes 98312 | tf_op jit(solution)/shard_map/ppermute | solution.py:254
  25.4 1.7 %collective-permute-start.5 = (bf16[32,3072]{1,0:T(8,128)(2,1)S(1)}, bf16[32,3072]{1,0:T(8,128)(2,1)S(1)}, u32[]{:S(2)}, u32[]{:S(2)}) collective-permute-start(bf16[32,3072]{1,0:T(8,128)(2,1)S(1)} %get-tuple-element.34), channel_id=1, source_target_pairs={{0,1},{1,0},{2,3},{3,2},{4,5},{5,4},{6,7},{7,6},{8,9},{9,8},{10,11... | collective-permute-start | bytes 589832 | tf_op jit(solution)/shard_map/ppermute | solution.py:254
  25.5 7.9 %copy-start = (bf16[4,64,4096]{2,1,0:T(8,128)(2,1)S(1)}, bf16[4,64,4096]{2,1,0:T(8,128)(2,1)}, u32[]{:S(2)}) copy-start(bf16[4,64,4096]{2,1,0:T(8,128)(2,1)} %up_ref.1) | copy-start | bytes 6291460
  27.2 2.0 %collective-permute-start.7 = (bf16[32,1280]{1,0:T(8,128)(2,1)S(1)}, bf16[32,1280]{1,0:T(8,128)(2,1)S(1)}, u32[]{:S(2)}, u32[]{:S(2)}) collective-permute-start(bf16[32,1280]{1,0:T(8,128)(2,1)S(1)} %get-tuple-element.38), channel_id=1, source_target_pairs={{0,1},{1,0},{2,3},{3,2},{4,5},{5,4},{6,7},{7,6},{8,9},{9,8},{10,11... | collective-permute-start | bytes 245768 | tf_op jit(solution)/shard_map/ppermute | solution.py:254
  27.7 5.2 %collective-permute-start.6 = (bf16[16,3072]{1,0:T(8,128)(2,1)S(1)}, bf16[16,3072]{1,0:T(8,128)(2,1)S(1)}, u32[]{:S(2)}, u32[]{:S(2)}) collective-permute-start(bf16[16,3072]{1,0:T(8,128)(2,1)S(1)} %get-tuple-element.36), channel_id=1, source_target_pairs={{0,2},{2,0},{1,3},{3,1},{4,6},{6,4},{5,7},{7,5},{8,10},{10,8},{9,1... | collective-permute-start | bytes 294920 | tf_op jit(solution)/shard_map/ppermute | solution.py:254
  29.4 4.0 %collective-permute-start.8 = (bf16[16,1280]{1,0:T(8,128)(2,1)S(1)}, bf16[16,1280]{1,0:T(8,128)(2,1)S(1)}, u32[]{:S(2)}, u32[]{:S(2)}) collective-permute-start(bf16[16,1280]{1,0:T(8,128)(2,1)S(1)} %get-tuple-element.40), channel_id=1, source_target_pairs={{0,2},{2,0},{1,3},{3,1},{4,6},{6,4},{5,7},{7,5},{8,10},{10,8},{9,1... | collective-permute-start | bytes 122888 | tf_op jit(solution)/shard_map/ppermute | solution.py:254

commit v19 on v18

--- a/solution.py
+++ b/solution.py
@@ -176,12 +176,21 @@
     write_rows(acc, outs, n_y, n_z)
 
 
-def first_sums_kernel(n_y, n_z, last_ref, small_ref, *refs):
-    parts, outs, last_outs = refs[:n_z], refs[n_z : n_z + n_y], refs[n_z + n_y :]
-    pair_kernel(n_y, False, *parts, *outs)
+def pack_kernel(n_y, n_z, last_ref, small_ref, *outs):
     columns = last_ref.shape[1]
-    write_rows(last_ref, [out.at[:, :columns] for out in last_outs], n_y, n_z)
-    write_rows(small_ref, [out.at[:, columns:] for out in last_outs], n_y, n_z)
+    write_rows(last_ref, [out.at[:, :columns] for out in outs], n_y, n_z)
+    write_rows(small_ref, [out.at[:, columns:] for out in outs], n_y, n_z)
+
+
+def first_sums_kernel(n_y, _, *refs):
+    pair_kernel(n_y, False, *refs)
+
+
+def add_kernel(*refs):
+    total = refs[0][...]
+    for part in refs[1:-1]:
+        total = total + part[...].astype(jnp.float32)
+    refs[-1][...] = total
 
 
 def pair_kernel(n_y, side, *refs):
@@ -201,10 +210,10 @@
             outs[k][:, late:] = split_wide(square).astype(outs[k].dtype)
 
 
-def final_kernel(n, n_z, step, spread_ref, up_ref, *refs):
-    firsts, lasts, out_ref = refs[:n], refs[n : 2 * n], refs[2 * n]
+def final_kernel(n_z, step, spread_ref, up_ref, first_ref, *refs):
+    lasts, out_ref = refs[:-1], refs[-1]
     rows_here, columns = out_ref.shape
-    done = firsts[0].shape[1]
+    done = first_ref.shape[1]
     late = columns - done
     adapters, rank_columns, _ = up_ref.shape
 
@@ -223,7 +232,7 @@
     spread = jnp.where(live > 0, spread, 0.0).astype(jnp.bfloat16)
     for c in range(0, columns, step):
         if c < done:
-            base = added(firsts, c, c + step)
+            base = first_ref[:, c : c + step]
         else:
             base = added(lasts, c - done, c - done + step)
         up = up_ref[:, :, c : c + step].reshape(adapters * rank_columns, step)
@@ -372,16 +381,26 @@
     )(x, *weights[split:])
     wide = firsts[0].shape[1]
     made = pl.pallas_call(
-        functools.partial(first_sums_kernel, n_y, n_z),
-        out_shape=shapes(n_y, (rows_here, wide)) + shapes(n_z, (kept, last_columns + 2 * LANES)),
-        in_specs=[VMEM] * (2 + n_z),
-        out_specs=[VMEM] * (n_y + n_z),
+        functools.partial(first_sums_kernel, n_y),
+        out_shape=shapes(n_y, (rows_here, wide)),
+        in_specs=[ANY] + [VMEM] * n_z,
+        out_specs=[VMEM] * n_y,
         cost_estimate=cost(0, 0),
         compiler_params=roomy,
         name="first_sums",
-    )(last, small, *firsts)
-    first_parts = spread_out(made[:n_y], "gy", n_y)
-    lasts = spread_out(made[n_y:], "gz", n_z)
+    )(last, *firsts)
+    first_parts = spread_out(made, "gy", n_y)
+
+    made = pl.pallas_call(
+        functools.partial(pack_kernel, n_y, n_z),
+        out_shape=shapes(n_z, (kept, last_columns + 2 * LANES)),
+        in_specs=[VMEM] * 2,
+        out_specs=[VMEM] * n_z,
+        cost_estimate=cost(0, 0),
+        compiler_params=roomy,
+        name="pack_last",
+    )(last, small)
+    lasts = spread_out(made, "gz", n_z)
 
     made = pl.pallas_call(
         functools.partial(pair_kernel, n_y, True),
@@ -394,14 +413,24 @@
     )(*lasts)
     last_parts = spread_out(made, "gy", n_y)
 
+    first_total = pl.pallas_call(
+        add_kernel,
+        out_shape=jax.ShapeDtypeStruct((rows_here, wide), f32),
+        in_specs=[VMEM] * n_y,
+        out_specs=VMEM,
+        cost_estimate=cost(16 * rows * depth * quarter, 0),
+        compiler_params=roomy,
+        name="first_total",
+    )(*first_parts)
+
     return pl.pallas_call(
-        functools.partial(final_kernel, n_y, n_z, min(512, columns // 4)),
+        functools.partial(final_kernel, n_z, min(512, columns // 4)),
         out_shape=jax.ShapeDtypeStruct((rows_here, columns), bf16),
-        in_specs=[VMEM] * (2 + 2 * n_y),
+        in_specs=[VMEM] * (3 + n_y),
         out_specs=VMEM,
         compiler_params=roomy,
         name="query_rows",
-    )(spread, adapter_up_factors, *first_parts, *last_parts)
+    )(spread, adapter_up_factors, first_total, *last_parts)
 
 
 def solution(mesh):

time: 34.7 us -> 35.5 us (1.023)
  waiting for transfers between devices: 3.38 us -> 4.8 us
  starting transfers between devices: 12.7 us -> 12.1 us
    ppermute x9, waiting for transfers between devices: 3.38 us -> 4.8 us  [send(): return lax.ppermute(value, axis, [(j, j ^ k) for j in range(n)])]
    ppermute x9, starting transfers between devices: 12.7 us -> 12.1 us  [send(): return lax.ppermute(value, axis, [(j, j ^ k) for j in range(n)])]
    pallas_call x2 -> x4, Pallas kernels: 1.15 us -> 1.19 us  [the longest x1 1.09 us: body(): pl.pallas_call(functools.partial(final_kernel, n_z, min(512, columns // 4...]
  transfers between devices with their start and end apart: 9 -> 9, of which waited for: 3 -> 4; matrix products, arithmetic and copies ran while one was open for 0% -> 0% of each run, Pallas kernels for 48% -> 47%
where the time goes in v19:
time: 35.5 us; the launch traced here: 35.4 us
  Pallas kernels  18.3 us (52%)
  starting transfers between devices  12.1 us (34%)
  waiting for transfers between devices  4.8 us (14%)
    ppermute x9, starting transfers between devices, send(): return lax.ppermute(value, axis, [(j, j ^ k) for j in range(n)])  12.1 us
    pallas_call x1, Pallas kernels, body(): pl.pallas_call(functools.partial(first_load_kernel, len(loads[0])), out_s...  6.02 us
    ppermute x9, waiting for transfers between devices, send(): return lax.ppermute(value, axis, [(j, j ^ k) for j in range(n)])  4.8 us
    pallas_call x1, Pallas kernels, body(): pl.pallas_call(functools.partial(last_load_kernel, len(loads[1]), sum(loa...  4.21 us
    pallas_call x1, Pallas kernels, body(): pl.pallas_call(functools.partial(base_kernel, 2, columns - late, step), o...  3.12 us
    pallas_call x1, Pallas kernels, product(): pl.pallas_call(functools.partial(product_kernel, len(some), n_y, n_z, ste...  1.62 us
    pallas_call x1, Pallas kernels, body(): pl.pallas_call(functools.partial(last_kernel, len(weights) - split, step)...  1.56 us
    pallas_call x1, Pallas kernels, body(): pl.pallas_call(functools.partial(final_kernel, n_z, min(512, columns // 4...  1.09 us
  transfers between devices with their start and end apart: 9, of which 4 were waited for; matrix products, arithmetic and copies ran while one was open for 0% of the time, Pallas kernels for 47%

profile of v19, /device:TPU:0, one launch (start us, length us, event | category | flops | bytes accessed | tf_op | source)
XLA Modules:
  0.0 35.4 jit_solution(10015936183703845674)
XLA Ops:
  0.0 4.0 %collective-permute-start = (bf16[16,4096]{1,0:T(8,128)(2,1)}, bf16[16,4096]{1,0:T(8,128)(2,1)S(1)}, u32[]{:S(2)}, u32[]{:S(2)}) collective-permute-start(bf16[16,4096]{1,0:T(8,128)(2,1)} %refs_0_.1), channel_id=1, source_target_pairs={{0,8},{4,12},{8,0},{12,4},{1,9},{5,13},{9,1},{13,5},{2,10},{6,14},... | collective-permute-start | bytes 393224 | tf_op jit(solution)/shard_map/ppermute | solution.py:263
  4.0 1.6 %collective-permute-start.1 = (bf16[16,4096]{1,0:T(8,128)(2,1)}, bf16[16,4096]{1,0:T(8,128)(2,1)S(1)}, u32[]{:S(2)}, u32[]{:S(2)}) collective-permute-start(bf16[16,4096]{1,0:T(8,128)(2,1)} %refs_0_.1), channel_id=1, source_target_pairs={{0,4},{4,0},{8,12},{12,8},{1,5},{5,1},{9,13},{13,9},{2,6},{6,2},{1... | collective-permute-start | bytes 393224 | tf_op jit(solution)/shard_map/ppermute | solution.py:263
  5.6 6.0 %first_load.1 = (f32[1,64,64]{2,1,0:T(8,128)S(1)}, f32[64,256]{1,0:T(8,128)S(1)}, bf16[4096,1024]{1,0:T(8,128)(2,1)S(1)}, bf16[4096,1024]{1,0:T(8,128)(2,1)S(1)}) custom-call(bf16[4096,4096]{1,0:T(8,128)(2,1)} %w_hbm.5, s32[4]{0:T(128)} %rank_hbm.1, s32[4]{0:T(128)} %slot_hbm.1, s32[5]{0:T(128)} %start_hbm.1), custom_call_target="tpu_custom_call" | custom-call | flops 5033164800 | bytes 16777216 | tf_op jit(solution)/shard_map/first_load/pallas_call | solution.py:291
  11.6 0.0 collective-permute-done.refs_1_.__
  11.6 0.5 %collective-permute-start.2 = (bf16[16,4096]{1,0:T(8,128)(2,1)S(1)}, bf16[16,4096]{1,0:T(8,128)(2,1)S(1)}, u32[]{:S(2)}, u32[]{:S(2)}) collective-permute-start(bf16[16,4096]{1,0:T(8,128)(2,1)S(1)} %collective-permute-done.refs_1_.__), channel_id=1, source_target_pairs={{0,4},{4,0},{8,12},{12,8},{1,5},{5,1},{9,13},{13,9},{2,6},{6,2},{1... | collective-permute-start | bytes 393224 | tf_op jit(solution)/shard_map/ppermute | solution.py:263
  12.2 4.2 %last_load.1 = (bf16[4096,1024]{1,0:T(8,128)(2,1)S(1)}, bf16[4096,256]{1,0:T(8,128)(2,1)S(1)}) custom-call(bf16[4096,4096]{1,0:T(8,128)(2,1)} %w_hbm.5, f32[1,64,64]{2,1,0:T(8,128)S(1)} %get-tuple-element.24.factor_ref._, bf16[16,4096]{1,0:T(8,128)(2,1)S(1)} %collective-permute-done.refs_1_.__), custom_call_target="tpu_custom_call" | custom-call | flops 5033164800 | bytes 16777216 | tf_op jit(solution)/shard_map/last_load/pallas_call | solution.py:309
  16.4 0.3 collective-permute-done.2.refs_3_
  16.7 0.4 %scaled_rows.1 = (bf16[64,4096]{1,0:T(8,128)(2,1)S(1)}, bf16[64,256]{1,0:T(8,128)(2,1)S(1)}) custom-call(bf16[4096]{0:T(1024)(128)(2,1)S(1)} %copy-done.3, bf16[1,64,4096]{2,1,0:T(8,128)(2,1)S(1)} %bitcast.1, f32[1,64,64]{2,1,0:T(8,128)S(1)} %get-tuple-element.24.factor_ref._, bf16[16,4096]{1,0:T(8,128)(2,1)S(1)} %copy-done.2, ...), custom_call_target="tpu_custom_call" | custom-call | tf_op jit(solution)/shard_map/scaled_rows/pallas_call | solution.py:321
  17.1 1.4 %collective-permute-start.3 = (bf16[64,256]{1,0:T(8,128)(2,1)S(1)}, bf16[64,256]{1,0:T(8,128)(2,1)S(1)}, u32[]{:S(2)}, u32[]{:S(2)}) collective-permute-start(bf16[64,256]{1,0:T(8,128)(2,1)S(1)} %get-tuple-element.31), channel_id=1, source_target_pairs={{0,4},{4,0},{8,12},{12,8},{1,5},{5,1},{9,13},{13,9},{2,6},{6,2},{1... | collective-permute-start | bytes 98312 | tf_op jit(solution)/shard_map/ppermute | solution.py:263
  18.5 3.1 %first_columns.1 = (f32[64,2048]{1,0:T(8,128)S(1)}, bf16[4096,768]{1,0:T(8,128)(2,1)S(1)}) custom-call(bf16[4096,4096]{1,0:T(8,128)(2,1)} %w_hbm.5, bf16[64,4096]{1,0:T(8,128)(2,1)S(1)} %get-tuple-element.25.x_ref, bf16[4096,1024]{1,0:T(8,128)(2,1)S(1)} %get-tuple-element.27.refs_0_, bf16[4096,1024]{1,0:T(8,128)(2,1)S(1)} %get-tuple-element.28.refs_1_), custom_call_target="tpu_custom_call" | custom-call | flops 1073741824 | bytes 16777216 | tf_op jit(solution)/shard_map/first_columns/pallas_call | solution.py:342
  21.7 2.1 %collective-permute-start.6 = (bf16[64,256]{1,0:T(8,128)(2,1)S(1)}, bf16[64,256]{1,0:T(8,128)(2,1)S(1)}, u32[]{:S(2)}, u32[]{:S(2)}) collective-permute-start(bf16[64,256]{1,0:T(8,128)(2,1)S(1)} %add.6.refs_1_), channel_id=1, source_target_pairs={{0,8},{4,12},{8,0},{12,4},{1,9},{5,13},{9,1},{13,5},{2,10},{6,14},... | collective-permute-start | bytes 98312 | tf_op jit(solution)/shard_map/ppermute | solution.py:263
  23.8 1.6 %middle_columns.1 = (f32[32,3072]{1,0:T(8,128)S(1)}, bf16[32,3072]{1,0:T(8,128)(2,1)S(1)}) custom-call(bf16[64,4096]{1,0:T(8,128)(2,1)S(1)} %get-tuple-element.25.x_ref, f32[64,2048]{1,0:T(8,128)S(1)} %get-tuple-element.30.refs_0_, bf16[64,256]{1,0:T(8,128)(2,1)S(1)} %add.6.refs_1_, bf16[4096,1024]{1,0:T(8,128)(2,1)S(1)} %get-tuple-element.32.refs_2_), custom_call_target="tpu_custom_call" | custom-call | flops 6442450944 | bytes 25165824 | tf_op jit(solution)/shard_map/middle_columns/pallas_call | solution.py:358
  25.4 0.1 collective-permute-start.4
  25.5 1.6 %last_columns.1._.last_ref = f32[64,1024]{1,0:T(8,128)S(1)} custom-call(bf16[64,4096]{1,0:T(8,128)(2,1)S(1)} %get-tuple-element.25.x_ref, bf16[4096,256]{1,0:T(8,128)(2,1)S(1)} %get-tuple-element.26.refs_0_, bf16[4096,768]{1,0:T(8,128)(2,1)S(1)} %get-tuple-element.29.refs_1_), custom_call_target="tpu_custom_call" | custom-call | flops 4294967296 | bytes 8388608 | tf_op jit(solution)/shard_map/last_columns/pallas_call | solution.py:373
  27.1 0.0 collective-permute-done.4.refs_1_
  27.1 0.0 copy-start
  27.2 1.6 %collective-permute-start.5 = (bf16[16,3072]{1,0:T(8,128)(2,1)S(1)}, bf16[16,3072]{1,0:T(8,128)(2,1)S(1)}, u32[]{:S(2)}, u32[]{:S(2)}) collective-permute-start(bf16[16,3072]{1,0:T(8,128)(2,1)S(1)} %get-tuple-element.36), channel_id=1, source_target_pairs={{0,2},{2,0},{1,3},{3,1},{4,6},{6,4},{5,7},{7,5},{8,10},{10,8},{9,1... | collective-permute-start | bytes 294920 | tf_op jit(solution)/shard_map/ppermute | solution.py:263
  28.8 0.3 collective-permute-start.7
  29.0 1.1 %collective-permute-done.7.refs_1_ = bf16[32,1280]{1,0:T(8,128)(2,1)S(1)} collective-permute-done((bf16[32,1280]{1,0:T(8,128)(2,1)S(1)}, bf16[32,1280]{1,0:T(8,128)(2,1)S(1)}, u32[]{:S(2)}, u32[]{:S(2)}) %collective-permute-start.7) | collective-permute-done | bytes 81952 | tf_op jit(solution)/shard_map/ppermute | solution.py:263
  30.1 0.1 last_sums.1
  30.3 0.6 %collective-permute-start.8 = (bf16[16,1280]{1,0:T(8,128)(2,1)S(1)}, bf16[16,1280]{1,0:T(8,128)(2,1)S(1)}, u32[]{:S(2)}, u32[]{:S(2)}) collective-permute-start(bf16[16,1280]{1,0:T(8,128)(2,1)S(1)} %get-tuple-element.40), channel_id=1, source_target_pairs={{0,2},{2,0},{1,3},{3,1},{4,6},{6,4},{5,7},{7,5},{8,10},{10,8},{9,1... | collective-permute-start | bytes 122888 | tf_op jit(solution)/shard_map/ppermute | solution.py:263
  30.8 1.6 %collective-permute-done.5.refs_1_ = bf16[16,3072]{1,0:T(8,128)(2,1)S(1)} collective-permute-done((bf16[16,3072]{1,0:T(8,128)(2,1)S(1)}, bf16[16,3072]{1,0:T(8,128)(2,1)S(1)}, u32[]{:S(2)}, u32[]{:S(2)}) %collective-permute-start.5) | collective-permute-done | bytes 98336 | tf_op jit(solution)/shard_map/ppermute | solution.py:263
  32.4 1.9 %collective-permute-done.8.refs_1_ = bf16[16,1280]{1,0:T(8,128)(2,1)S(1)} collective-permute-done((bf16[16,1280]{1,0:T(8,128)(2,1)S(1)}, bf16[16,1280]{1,0:T(8,128)(2,1)S(1)}, u32[]{:S(2)}, u32[]{:S(2)}) %collective-permute-start.8) | collective-permute-done | bytes 40992 | tf_op jit(solution)/shard_map/ppermute | solution.py:263
  34.3 1.1 %query_rows.1 = bf16[16,4096]{1,0:T(8,128)(2,1)} custom-call(f32[64,256]{1,0:T(8,128)S(1)} %get-tuple-element.23.spread_ref, bf16[4,64,4096]{2,1,0:T(8,128)(2,1)S(1)} %copy-done, f32[16,3072]{1,0:T(8,128)S(1)} %first_total.1.first_ref, f32[16,1280]{1,0:T(8,128)S(1)} %get-tuple-element.39.refs_0_, bf16[16,1280]{1,0:T(8,128)(2,1)S(1)} %collective-permute-done.8.refs_1_), custom_call_target="tpu_custom_call" | custom-call | tf_op jit(solution)/shard_map/query_rows/pallas_call | solution.py:426
  (15 shorter events, 0.1 us)
Async XLA Ops:
  0.0 11.6 %collective-permute-start = (bf16[16,4096]{1,0:T(8,128)(2,1)}, bf16[16,4096]{1,0:T(8,128)(2,1)S(1)}, u32[]{:S(2)}, u32[]{:S(2)}) collective-permute-start(bf16[16,4096]{1,0:T(8,128)(2,1)} %refs_0_.1), channel_id=1, source_target_pairs={{0,8},{4,12},{8,0},{12,4},{1,9},{5,13},{9,1},{13,5},{2,10},{6,14},... | collective-permute-start | bytes 393224 | tf_op jit(solution)/shard_map/ppermute | solution.py:263
  4.0 12.4 %collective-permute-start.1 = (bf16[16,4096]{1,0:T(8,128)(2,1)}, bf16[16,4096]{1,0:T(8,128)(2,1)S(1)}, u32[]{:S(2)}, u32[]{:S(2)}) collective-permute-start(bf16[16,4096]{1,0:T(8,128)(2,1)} %refs_0_.1), channel_id=1, source_target_pairs={{0,4},{4,0},{8,12},{12,8},{1,5},{5,1},{9,13},{13,9},{2,6},{6,2},{1... | collective-permute-start | bytes 393224 | tf_op jit(solution)/shard_map/ppermute | solution.py:263
  11.6 5.0 %collective-permute-start.2 = (bf16[16,4096]{1,0:T(8,128)(2,1)S(1)}, bf16[16,4096]{1,0:T(8,128)(2,1)S(1)}, u32[]{:S(2)}, u32[]{:S(2)}) collective-permute-start(bf16[16,4096]{1,0:T(8,128)(2,1)S(1)} %collective-permute-done.refs_1_.__), channel_id=1, source_target_pairs={{0,4},{4,0},{8,12},{12,8},{1,5},{5,1},{9,13},{13,9},{2,6},{6,2},{1... | collective-permute-start | bytes 393224 | tf_op jit(solution)/shard_map/ppermute | solution.py:263
  12.2 4.5 %copy-start.1 = (bf16[1,4096,64]{1,2,0:T(8,128)(2,1)S(1)}, bf16[1,4096,64]{1,2,0:T(8,128)(2,1)}, u32[]{:S(2)}) copy-start(bf16[1,4096,64]{1,2,0:T(8,128)(2,1)} %param.12) | copy-start | bytes 1572868
  12.2 4.5 %copy-start.2 = (bf16[16,4096]{1,0:T(8,128)(2,1)S(1)}, bf16[16,4096]{1,0:T(8,128)(2,1)}, u32[]{:S(2)}) copy-start(bf16[16,4096]{1,0:T(8,128)(2,1)} %refs_0_.1) | copy-start | bytes 393220
  12.2 4.5 %copy-start.3 = (bf16[4096]{0:T(1024)(128)(2,1)S(1)}, bf16[4096]{0:T(1024)(128)(2,1)}, u32[]{:S(2)}) copy-start(bf16[4096]{0:T(1024)(128)(2,1)} %gain_ref.1) | copy-start | bytes 24580
  17.1 4.5 %collective-permute-start.3 = (bf16[64,256]{1,0:T(8,128)(2,1)S(1)}, bf16[64,256]{1,0:T(8,128)(2,1)S(1)}, u32[]{:S(2)}, u32[]{:S(2)}) collective-permute-start(bf16[64,256]{1,0:T(8,128)(2,1)S(1)} %get-tuple-element.31), channel_id=1, source_target_pairs={{0,4},{4,0},{8,12},{12,8},{1,5},{5,1},{9,13},{13,9},{2,6},{6,2},{1... | collective-permute-start | bytes 98312 | tf_op jit(solution)/shard_map/ppermute | solution.py:263
  21.7 7.0 %collective-permute-start.6 = (bf16[64,256]{1,0:T(8,128)(2,1)S(1)}, bf16[64,256]{1,0:T(8,128)(2,1)S(1)}, u32[]{:S(2)}, u32[]{:S(2)}) collective-permute-start(bf16[64,256]{1,0:T(8,128)(2,1)S(1)} %add.6.refs_1_), channel_id=1, source_target_pairs={{0,8},{4,12},{8,0},{12,4},{1,9},{5,13},{9,1},{13,5},{2,10},{6,14},... | collective-permute-start | bytes 98312 | tf_op jit(solution)/shard_map/ppermute | solution.py:263
  25.4 1.6 %collective-permute-start.4 = (bf16[32,3072]{1,0:T(8,128)(2,1)S(1)}, bf16[32,3072]{1,0:T(8,128)(2,1)S(1)}, u32[]{:S(2)}, u32[]{:S(2)}) collective-permute-start(bf16[32,3072]{1,0:T(8,128)(2,1)S(1)} %get-tuple-element.34), channel_id=1, source_target_pairs={{0,1},{1,0},{2,3},{3,2},{4,5},{5,4},{6,7},{7,6},{8,9},{9,8},{10,11... | collective-permute-start | bytes 589832 | tf_op jit(solution)/shard_map/ppermute | solution.py:263
  27.1 7.2 %copy-start = (bf16[4,64,4096]{2,1,0:T(8,128)(2,1)S(1)}, bf16[4,64,4096]{2,1,0:T(8,128)(2,1)}, u32[]{:S(2)}) copy-start(bf16[4,64,4096]{2,1,0:T(8,128)(2,1)} %up_ref.1) | copy-start | bytes 6291460
  27.2 5.3 %collective-permute-start.5 = (bf16[16,3072]{1,0:T(8,128)(2,1)S(1)}, bf16[16,3072]{1,0:T(8,128)(2,1)S(1)}, u32[]{:S(2)}, u32[]{:S(2)}) collective-permute-start(bf16[16,3072]{1,0:T(8,128)(2,1)S(1)} %get-tuple-element.36), channel_id=1, source_target_pairs={{0,2},{2,0},{1,3},{3,1},{4,6},{6,4},{5,7},{7,5},{8,10},{10,8},{9,1... | collective-permute-start | bytes 294920 | tf_op jit(solution)/shard_map/ppermute | solution.py:263
  28.8 1.3 %collective-permute-start.7 = (bf16[32,1280]{1,0:T(8,128)(2,1)S(1)}, bf16[32,1280]{1,0:T(8,128)(2,1)S(1)}, u32[]{:S(2)}, u32[]{:S(2)}) collective-permute-start(bf16[32,1280]{1,0:T(8,128)(2,1)S(1)} %get-tuple-element.38), channel_id=1, source_target_pairs={{0,1},{1,0},{2,3},{3,2},{4,5},{5,4},{6,7},{7,6},{8,9},{9,8},{10,11... | collective-permute-start | bytes 245768 | tf_op jit(solution)/shard_map/ppermute | solution.py:263
  30.3 4.0 %collective-permute-start.8 = (bf16[16,1280]{1,0:T(8,128)(2,1)S(1)}, bf16[16,1280]{1,0:T(8,128)(2,1)S(1)}, u32[]{:S(2)}, u32[]{:S(2)}) collective-permute-start(bf16[16,1280]{1,0:T(8,128)(2,1)S(1)} %get-tuple-element.40), channel_id=1, source_target_pairs={{0,2},{2,0},{1,3},{3,1},{4,6},{6,4},{5,7},{7,5},{8,10},{10,8},{9,1... | collective-permute-start | bytes 122888 | tf_op jit(solution)/shard_map/ppermute | solution.py:263

commit v20 on v18

--- a/solution.py
+++ b/solution.py
@@ -39,11 +39,10 @@
     ]
 
 
-def load(w_hbm, first, weights, sems, meanwhile):
+def load(w_hbm, firsts, weights, sems, meanwhile):
     copies = []
     for j, w_vmem in enumerate(weights):
-        copies += weight_copies(w_hbm, first, w_vmem, sems.at[j])
-        first += w_vmem.shape[1]
+        copies += weight_copies(w_hbm, firsts[j], w_vmem, sems.at[j])
     for copy in copies:
         copy.start()
     meanwhile()
@@ -51,7 +50,7 @@
         copy.wait()
 
 
-def first_load_kernel(n, w_hbm, rank_hbm, slot_hbm, start_hbm, factor_ref, spread_ref, *refs):
+def first_load_kernel(n, firsts, w_hbm, rank_hbm, slot_hbm, start_hbm, factor_ref, spread_ref, *refs):
     weights, sems, scalar_sems = refs[:n], refs[n], refs[n + 1]
     rank_ref, slot_ref, start_ref = refs[n + 2 :]
 
@@ -80,11 +79,11 @@
             live = (row >= start_ref[a]) & (row < start_ref[a + 1])
             spread_ref[:, a * rank_columns : (a + 1) * rank_columns] = jnp.where(live, 1.0, 0.0)
 
-    load(w_hbm, 0, weights, sems, masks)
-
-
-def last_load_kernel(n, first, w_hbm, _, __, *refs):
-    load(w_hbm, first, refs[:n], refs[n], lambda: None)
+    load(w_hbm, firsts, weights, sems, masks)
+
+
+def last_load_kernel(n, firsts, w_hbm, _, __, *refs):
+    load(w_hbm, firsts, refs[:n], refs[n], lambda: None)
 
 
 def split_wide(value):
@@ -270,9 +269,11 @@
     quarter = columns // 4
     part = quarter // 4
     if part % LANES == 0:
-        loads, late = ([quarter, quarter], [quarter, part]), quarter - part
+        loads, late = ([quarter, quarter, part], [quarter]), quarter - part
+        firsts = [0, quarter, 3 * quarter], [2 * quarter]
     else:
         loads, late = ([quarter, quarter], [quarter, quarter]), 0
+        firsts = [0, quarter], [2 * quarter, 3 * quarter]
     kept = n_y * rows_here
     roomy = params(4 + (rows * depth >> 16))
 
@@ -280,7 +281,7 @@
     weight_hbm = pltpu.with_memory_space_constraint(query_weight, pltpu.HBM)
     load_cost = cost(300 * query_weight.size, query_weight.size)
     factor, spread, *weights = pl.pallas_call(
-        functools.partial(first_load_kernel, len(loads[0])),
+        functools.partial(first_load_kernel, len(loads[0]), firsts[0]),
         out_shape=[
             jax.ShapeDtypeStruct((slots, rows, rank_columns), f32),
             jax.ShapeDtypeStruct((rows, adapters * rank_columns), f32),
@@ -298,7 +299,7 @@
         name="first_load",
     )(weight_hbm, *[pltpu.with_memory_space_constraint(v, pltpu.HBM) for v in scalars])
     weights += pl.pallas_call(
-        functools.partial(last_load_kernel, len(loads[1]), sum(loads[0])),
+        functools.partial(last_load_kernel, len(loads[1]), firsts[1]),
         out_shape=[pltpu.VMEM((depth, wide), query_weight.dtype) for wide in loads[1]],
         in_specs=[HBM, ANY, ANY],
         out_specs=[VMEM] * len(loads[1]),
@@ -308,6 +309,8 @@
         name="last_load",
     )(weight_hbm, factor, blocks[1])
     weights = [pltpu.with_memory_space_constraint(w, pltpu.VMEM) for w in weights]
+    if late:
+        weights[2:] = weights[:1:-1]
 
     x, small = pl.pallas_call(
         functools.partial(rows_kernel, order, depth * groups),
@@ -360,7 +363,7 @@
 
     split = 3
     last_columns = sum(w.shape[1] for w in weights[split:])
-    firsts = product(weights[2:split], [base, one_hop], 4, "middle_columns")
+    base_parts = product(weights[2:split], [base, one_hop], 4, "middle_columns")
     last = pl.pallas_call(
         functools.partial(last_kernel, len(weights) - split, step),
         out_shape=jax.ShapeDtypeStruct((rows, last_columns), f32),
@@ -370,7 +373,7 @@
         compiler_params=roomy,
         name="last_columns",
     )(x, *weights[split:])
-    wide = firsts[0].shape[1]
+    wide = base_parts[0].shape[1]
     made = pl.pallas_call(
         functools.partial(first_sums_kernel, n_y, n_z),
         out_shape=shapes(n_y, (rows_here, wide)) + shapes(n_z, (kept, last_columns + 2 * LANES)),
@@ -379,7 +382,7 @@
         cost_estimate=cost(0, 0),
         compiler_params=roomy,
         name="first_sums",
-    )(last, small, *firsts)
+    )(last, small, *base_parts)
     first_parts = spread_out(made[:n_y], "gy", n_y)
     lasts = spread_out(made[n_y:], "gz", n_z)
 

time: 34.7 us -> 34.7 us (level)
  waiting for transfers between devices: 3.38 us -> 4.14 us
  starting transfers between devices: 12.7 us -> 12 us
    ppermute x9, waiting for transfers between devices: 3.38 us -> 4.14 us  [send(): return lax.ppermute(value, axis, [(j, j ^ k) for j in range(n)])]
    ppermute x9, starting transfers between devices: 12.7 us -> 12 us  [send(): return lax.ppermute(value, axis, [(j, j ^ k) for j in range(n)])]
  transfers between devices with their start and end apart: 9 -> 9, of which waited for: 3 -> 4; matrix products, arithmetic and copies ran while one was open for 0% -> 0% of each run, Pallas kernels for 48% -> 48%
where the time goes in v20:
time: 34.7 us; the launch traced here: 34.5 us
  Pallas kernels  18.2 us (52%)
  starting transfers between devices  12 us (35%)
  waiting for transfers between devices  4.14 us (12%)
    ppermute x9, starting transfers between devices, send(): return lax.ppermute(value, axis, [(j, j ^ k) for j in range(n)])  12 us
    pallas_call x1, Pallas kernels, body(): pl.pallas_call(functools.partial(first_load_kernel, len(loads[0]), firsts...  6.66 us
    ppermute x9, waiting for transfers between devices, send(): return lax.ppermute(value, axis, [(j, j ^ k) for j in range(n)])  4.14 us
    pallas_call x1, Pallas kernels, body(): pl.pallas_call(functools.partial(last_load_kernel, len(loads[1]), firsts[...  3.56 us
    pallas_call x1, Pallas kernels, body(): pl.pallas_call(functools.partial(base_kernel, 2, columns - late, step), o...  3.12 us
    pallas_call x1, Pallas kernels, product(): pl.pallas_call(functools.partial(product_kernel, len(some), n_y, n_z, ste...  1.62 us
    pallas_call x1, Pallas kernels, body(): pl.pallas_call(functools.partial(last_kernel, len(weights) - split, step)...  1.56 us
    pallas_call x1, Pallas kernels, body(): pl.pallas_call(functools.partial(final_kernel, n_y, n_z, min(512, columns...  1.09 us
  transfers between devices with their start and end apart: 9, of which 4 were waited for; matrix products, arithmetic and copies ran while one was open for 0% of the time, Pallas kernels for 48%

profile of v20, /device:TPU:0, one launch (start us, length us, event | category | flops | bytes accessed | tf_op | source)
XLA Modules:
  0.0 34.5 jit_solution(6375423597294966946)
XLA Ops:
  0.0 4.0 %collective-permute-start = (bf16[16,4096]{1,0:T(8,128)(2,1)}, bf16[16,4096]{1,0:T(8,128)(2,1)S(1)}, u32[]{:S(2)}, u32[]{:S(2)}) collective-permute-start(bf16[16,4096]{1,0:T(8,128)(2,1)} %refs_0_.1), channel_id=1, source_target_pairs={{0,8},{4,12},{8,0},{12,4},{1,9},{5,13},{9,1},{13,5},{2,10},{6,14},... | collective-permute-start | bytes 393224 | tf_op jit(solution)/shard_map/ppermute | solution.py:253
  4.0 1.6 %collective-permute-start.1 = (bf16[16,4096]{1,0:T(8,128)(2,1)}, bf16[16,4096]{1,0:T(8,128)(2,1)S(1)}, u32[]{:S(2)}, u32[]{:S(2)}) collective-permute-start(bf16[16,4096]{1,0:T(8,128)(2,1)} %refs_0_.1), channel_id=1, source_target_pairs={{0,4},{4,0},{8,12},{12,8},{1,5},{5,1},{9,13},{13,9},{2,6},{6,2},{1... | collective-permute-start | bytes 393224 | tf_op jit(solution)/shard_map/ppermute | solution.py:253
  5.6 6.7 %first_load.1 = (f32[1,64,64]{2,1,0:T(8,128)S(1)}, f32[64,256]{1,0:T(8,128)S(1)}, bf16[4096,1024]{1,0:T(8,128)(2,1)S(1)}, bf16[4096,1024]{1,0:T(8,128)(2,1)S(1)}, bf16[4096,256]{1,0:T(8,128)(2,1)S(1)}) custom-call(bf16[4096,4096]{1,0:T(8,128)(2,1)} %w_hbm.5, s32[4]{0:T(128)} %rank_hbm.1, s32[4]{0:T(128)} %slot_hbm.1, s32[5]{0:T(128)} %start_hbm.1), custom_call_target="tpu_custom_call" | custom-call | flops 5033164800 | bytes 16777216 | tf_op jit(solution)/shard_map/first_load/pallas_call | solution.py:283
  12.3 0.5 %collective-permute-start.2 = (bf16[16,4096]{1,0:T(8,128)(2,1)S(1)}, bf16[16,4096]{1,0:T(8,128)(2,1)S(1)}, u32[]{:S(2)}, u32[]{:S(2)}) collective-permute-start(bf16[16,4096]{1,0:T(8,128)(2,1)S(1)} %collective-permute-done.refs_1_.__), channel_id=1, source_target_pairs={{0,4},{4,0},{8,12},{12,8},{1,5},{5,1},{9,13},{13,9},{2,6},{6,2},{1... | collective-permute-start | bytes 393224 | tf_op jit(solution)/shard_map/ppermute | solution.py:253
  12.8 3.6 %last_load.1.refs_2_ = bf16[4096,1024]{1,0:T(8,128)(2,1)S(1)} custom-call(bf16[4096,4096]{1,0:T(8,128)(2,1)} %w_hbm.5, f32[1,64,64]{2,1,0:T(8,128)S(1)} %get-tuple-element.23.factor_ref._, bf16[16,4096]{1,0:T(8,128)(2,1)S(1)} %collective-permute-done.refs_1_.__), custom_call_target="tpu_custom_call" | custom-call | flops 5033164800 | bytes 16777216 | tf_op jit(solution)/shard_map/last_load/pallas_call | solution.py:301
  16.4 0.0 collective-permute-done.1.refs_2_
  16.4 0.9 %collective-permute-done.2.refs_3_ = bf16[16,4096]{1,0:T(8,128)(2,1)S(1)} collective-permute-done((bf16[16,4096]{1,0:T(8,128)(2,1)S(1)}, bf16[16,4096]{1,0:T(8,128)(2,1)S(1)}, u32[]{:S(2)}, u32[]{:S(2)}) %collective-permute-start.2) | collective-permute-done | bytes 131104 | tf_op jit(solution)/shard_map/ppermute | solution.py:253
  17.3 0.4 %scaled_rows.1 = (bf16[64,4096]{1,0:T(8,128)(2,1)S(1)}, bf16[64,256]{1,0:T(8,128)(2,1)S(1)}) custom-call(bf16[4096]{0:T(1024)(128)(2,1)S(1)} %copy-done.3, bf16[1,64,4096]{2,1,0:T(8,128)(2,1)S(1)} %bitcast.1, f32[1,64,64]{2,1,0:T(8,128)S(1)} %get-tuple-element.23.factor_ref._, bf16[16,4096]{1,0:T(8,128)(2,1)S(1)} %copy-done.2, ...), custom_call_target="tpu_custom_call" | custom-call | tf_op jit(solution)/shard_map/scaled_rows/pallas_call | solution.py:315
  17.8 0.7 %collective-permute-start.3 = (bf16[64,256]{1,0:T(8,128)(2,1)S(1)}, bf16[64,256]{1,0:T(8,128)(2,1)S(1)}, u32[]{:S(2)}, u32[]{:S(2)}) collective-permute-start(bf16[64,256]{1,0:T(8,128)(2,1)S(1)} %get-tuple-element.29), channel_id=1, source_target_pairs={{0,4},{4,0},{8,12},{12,8},{1,5},{5,1},{9,13},{13,9},{2,6},{6,2},{1... | collective-permute-start | bytes 98312 | tf_op jit(solution)/shard_map/ppermute | solution.py:253
  18.5 3.1 %first_columns.1 = (f32[64,2048]{1,0:T(8,128)S(1)}, bf16[4096,768]{1,0:T(8,128)(2,1)S(1)}) custom-call(bf16[4096,4096]{1,0:T(8,128)(2,1)} %w_hbm.5, bf16[64,4096]{1,0:T(8,128)(2,1)S(1)} %get-tuple-element.24.x_ref, bf16[4096,1024]{1,0:T(8,128)(2,1)S(1)} %get-tuple-element.26.refs_0_, bf16[4096,1024]{1,0:T(8,128)(2,1)S(1)} %get-tuple-element.27.refs_1_), custom_call_target="tpu_custom_call" | custom-call | flops 1073741824 | bytes 16777216 | tf_op jit(solution)/shard_map/first_columns/pallas_call | solution.py:336
  21.6 0.1 collective-permute-done.3
  21.8 2.0 %collective-permute-start.4 = (bf16[64,256]{1,0:T(8,128)(2,1)S(1)}, bf16[64,256]{1,0:T(8,128)(2,1)S(1)}, u32[]{:S(2)}, u32[]{:S(2)}) collective-permute-start(bf16[64,256]{1,0:T(8,128)(2,1)S(1)} %add.6.refs_1_), channel_id=1, source_target_pairs={{0,8},{4,12},{8,0},{12,4},{1,9},{5,13},{9,1},{13,5},{2,10},{6,14},... | collective-permute-start | bytes 98312 | tf_op jit(solution)/shard_map/ppermute | solution.py:253
  23.8 1.6 %middle_columns.1 = (f32[32,3072]{1,0:T(8,128)S(1)}, bf16[32,3072]{1,0:T(8,128)(2,1)S(1)}) custom-call(bf16[64,4096]{1,0:T(8,128)(2,1)S(1)} %get-tuple-element.24.x_ref, f32[64,2048]{1,0:T(8,128)S(1)} %get-tuple-element.30.refs_0_, bf16[64,256]{1,0:T(8,128)(2,1)S(1)} %add.6.refs_1_, bf16[4096,1024]{1,0:T(8,128)(2,1)S(1)} %last_load.1.refs_2_), custom_call_target="tpu_custom_call" | custom-call | flops 6442450944 | bytes 25165824 | tf_op jit(solution)/shard_map/middle_columns/pallas_call | solution.py:352
  25.4 0.1 collective-permute-start.5
  25.5 0.0 copy-start
  25.5 1.6 %last_columns.1.last_ref = f32[64,1024]{1,0:T(8,128)S(1)} custom-call(bf16[64,4096]{1,0:T(8,128)(2,1)S(1)} %get-tuple-element.24.x_ref, bf16[4096,256]{1,0:T(8,128)(2,1)S(1)} %get-tuple-element.25.refs_0_, bf16[4096,768]{1,0:T(8,128)(2,1)S(1)} %get-tuple-element.28.refs_1_), custom_call_target="tpu_custom_call" | custom-call | flops 4294967296 | bytes 8388608 | tf_op jit(solution)/shard_map/last_columns/pallas_call | solution.py:367
  27.1 0.1 first_sums.1
  27.2 0.6 %collective-permute-start.7 = (bf16[32,1280]{1,0:T(8,128)(2,1)S(1)}, bf16[32,1280]{1,0:T(8,128)(2,1)S(1)}, u32[]{:S(2)}, u32[]{:S(2)}) collective-permute-start(bf16[32,1280]{1,0:T(8,128)(2,1)S(1)} %get-tuple-element.36), channel_id=1, source_target_pairs={{0,1},{1,0},{2,3},{3,2},{4,5},{5,4},{6,7},{7,6},{8,9},{9,8},{10,11... | collective-permute-start | bytes 245768 | tf_op jit(solution)/shard_map/ppermute | solution.py:253
  27.7 1.5 %collective-permute-start.6 = (bf16[16,3072]{1,0:T(8,128)(2,1)S(1)}, bf16[16,3072]{1,0:T(8,128)(2,1)S(1)}, u32[]{:S(2)}, u32[]{:S(2)}) collective-permute-start(bf16[16,3072]{1,0:T(8,128)(2,1)S(1)} %get-tuple-element.34), channel_id=1, source_target_pairs={{0,2},{2,0},{1,3},{3,1},{4,6},{6,4},{5,7},{7,5},{8,10},{10,8},{9,1... | collective-permute-start | bytes 294920 | tf_op jit(solution)/shard_map/ppermute | solution.py:253
  29.2 0.1 last_sums.1
  29.4 1.0 %collective-permute-start.8 = (bf16[16,1280]{1,0:T(8,128)(2,1)S(1)}, bf16[16,1280]{1,0:T(8,128)(2,1)S(1)}, u32[]{:S(2)}, u32[]{:S(2)}) collective-permute-start(bf16[16,1280]{1,0:T(8,128)(2,1)S(1)} %get-tuple-element.38), channel_id=1, source_target_pairs={{0,2},{2,0},{1,3},{3,1},{4,6},{6,4},{5,7},{7,5},{8,10},{10,8},{9,1... | collective-permute-start | bytes 122888 | tf_op jit(solution)/shard_map/ppermute | solution.py:253
  30.4 2.6 %collective-permute-done.6.refs_1_ = bf16[16,3072]{1,0:T(8,128)(2,1)S(1)} collective-permute-done((bf16[16,3072]{1,0:T(8,128)(2,1)S(1)}, bf16[16,3072]{1,0:T(8,128)(2,1)S(1)}, u32[]{:S(2)}, u32[]{:S(2)}) %collective-permute-start.6) | collective-permute-done | bytes 98336 | tf_op jit(solution)/shard_map/ppermute | solution.py:253
  33.0 0.5 %collective-permute-done.8.refs_3_ = bf16[16,1280]{1,0:T(8,128)(2,1)S(1)} collective-permute-done((bf16[16,1280]{1,0:T(8,128)(2,1)S(1)}, bf16[16,1280]{1,0:T(8,128)(2,1)S(1)}, u32[]{:S(2)}, u32[]{:S(2)}) %collective-permute-start.8) | collective-permute-done | bytes 40992 | tf_op jit(solution)/shard_map/ppermute | solution.py:253
  33.4 1.1 %query_rows.1 = bf16[16,4096]{1,0:T(8,128)(2,1)} custom-call(f32[64,256]{1,0:T(8,128)S(1)} %get-tuple-element.22.spread_ref, bf16[4,64,4096]{2,1,0:T(8,128)(2,1)S(1)} %copy-done, f32[16,3072]{1,0:T(8,128)S(1)} %get-tuple-element.33.refs_0_, bf16[16,3072]{1,0:T(8,128)(2,1)S(1)} %collective-permute-done.6.refs_1_, f32[16,1280]{1,0:T(8,128)S(1)} %get-tuple-element.37.refs_2_, ...), custom_call_target="tpu_custom_call" | custom-call | tf_op jit(solution)/shard_map/query_rows/pallas_call | solution.py:400
  (13 shorter events, 0.0 us)
Async XLA Ops:
  0.0 12.3 %collective-permute-start = (bf16[16,4096]{1,0:T(8,128)(2,1)}, bf16[16,4096]{1,0:T(8,128)(2,1)S(1)}, u32[]{:S(2)}, u32[]{:S(2)}) collective-permute-start(bf16[16,4096]{1,0:T(8,128)(2,1)} %refs_0_.1), channel_id=1, source_target_pairs={{0,8},{4,12},{8,0},{12,4},{1,9},{5,13},{9,1},{13,5},{2,10},{6,14},... | collective-permute-start | bytes 393224 | tf_op jit(solution)/shard_map/ppermute | solution.py:253
  4.0 12.3 %collective-permute-start.1 = (bf16[16,4096]{1,0:T(8,128)(2,1)}, bf16[16,4096]{1,0:T(8,128)(2,1)S(1)}, u32[]{:S(2)}, u32[]{:S(2)}) collective-permute-start(bf16[16,4096]{1,0:T(8,128)(2,1)} %refs_0_.1), channel_id=1, source_target_pairs={{0,4},{4,0},{8,12},{12,8},{1,5},{5,1},{9,13},{13,9},{2,6},{6,2},{1... | collective-permute-start | bytes 393224 | tf_op jit(solution)/shard_map/ppermute | solution.py:253
  12.3 5.0 %collective-permute-start.2 = (bf16[16,4096]{1,0:T(8,128)(2,1)S(1)}, bf16[16,4096]{1,0:T(8,128)(2,1)S(1)}, u32[]{:S(2)}, u32[]{:S(2)}) collective-permute-start(bf16[16,4096]{1,0:T(8,128)(2,1)S(1)} %collective-permute-done.refs_1_.__), channel_id=1, source_target_pairs={{0,4},{4,0},{8,12},{12,8},{1,5},{5,1},{9,13},{13,9},{2,6},{6,2},{1... | collective-permute-start | bytes 393224 | tf_op jit(solution)/shard_map/ppermute | solution.py:253
  12.8 4.5 %copy-start.1 = (bf16[1,4096,64]{1,2,0:T(8,128)(2,1)S(1)}, bf16[1,4096,64]{1,2,0:T(8,128)(2,1)}, u32[]{:S(2)}) copy-start(bf16[1,4096,64]{1,2,0:T(8,128)(2,1)} %param.12) | copy-start | bytes 1572868
  12.8 4.5 %copy-start.2 = (bf16[16,4096]{1,0:T(8,128)(2,1)S(1)}, bf16[16,4096]{1,0:T(8,128)(2,1)}, u32[]{:S(2)}) copy-start(bf16[16,4096]{1,0:T(8,128)(2,1)} %refs_0_.1) | copy-start | bytes 393220
  12.8 4.5 %copy-start.3 = (bf16[4096]{0:T(1024)(128)(2,1)S(1)}, bf16[4096]{0:T(1024)(128)(2,1)}, u32[]{:S(2)}) copy-start(bf16[4096]{0:T(1024)(128)(2,1)} %gain_ref.1) | copy-start | bytes 24580
  17.8 4.0 %collective-permute-start.3 = (bf16[64,256]{1,0:T(8,128)(2,1)S(1)}, bf16[64,256]{1,0:T(8,128)(2,1)S(1)}, u32[]{:S(2)}, u32[]{:S(2)}) collective-permute-start(bf16[64,256]{1,0:T(8,128)(2,1)S(1)} %get-tuple-element.29), channel_id=1, source_target_pairs={{0,4},{4,0},{8,12},{12,8},{1,5},{5,1},{9,13},{13,9},{2,6},{6,2},{1... | collective-permute-start | bytes 98312 | tf_op jit(solution)/shard_map/ppermute | solution.py:253
  21.8 5.3 %collective-permute-start.4 = (bf16[64,256]{1,0:T(8,128)(2,1)S(1)}, bf16[64,256]{1,0:T(8,128)(2,1)S(1)}, u32[]{:S(2)}, u32[]{:S(2)}) collective-permute-start(bf16[64,256]{1,0:T(8,128)(2,1)S(1)} %add.6.refs_1_), channel_id=1, source_target_pairs={{0,8},{4,12},{8,0},{12,4},{1,9},{5,13},{9,1},{13,5},{2,10},{6,14},... | collective-permute-start | bytes 98312 | tf_op jit(solution)/shard_map/ppermute | solution.py:253
  25.4 1.7 %collective-permute-start.5 = (bf16[32,3072]{1,0:T(8,128)(2,1)S(1)}, bf16[32,3072]{1,0:T(8,128)(2,1)S(1)}, u32[]{:S(2)}, u32[]{:S(2)}) collective-permute-start(bf16[32,3072]{1,0:T(8,128)(2,1)S(1)} %get-tuple-element.32), channel_id=1, source_target_pairs={{0,1},{1,0},{2,3},{3,2},{4,5},{5,4},{6,7},{7,6},{8,9},{9,8},{10,11... | collective-permute-start | bytes 589832 | tf_op jit(solution)/shard_map/ppermute | solution.py:253
  25.5 7.9 %copy-start = (bf16[4,64,4096]{2,1,0:T(8,128)(2,1)S(1)}, bf16[4,64,4096]{2,1,0:T(8,128)(2,1)}, u32[]{:S(2)}) copy-start(bf16[4,64,4096]{2,1,0:T(8,128)(2,1)} %up_ref.1) | copy-start | bytes 6291460
  27.2 2.0 %collective-permute-start.7 = (bf16[32,1280]{1,0:T(8,128)(2,1)S(1)}, bf16[32,1280]{1,0:T(8,128)(2,1)S(1)}, u32[]{:S(2)}, u32[]{:S(2)}) collective-permute-start(bf16[32,1280]{1,0:T(8,128)(2,1)S(1)} %get-tuple-element.36), channel_id=1, source_target_pairs={{0,1},{1,0},{2,3},{3,2},{4,5},{5,4},{6,7},{7,6},{8,9},{9,8},{10,11... | collective-permute-start | bytes 245768 | tf_op jit(solution)/shard_map/ppermute | solution.py:253
  27.7 5.2 %collective-permute-start.6 = (bf16[16,3072]{1,0:T(8,128)(2,1)S(1)}, bf16[16,3072]{1,0:T(8,128)(2,1)S(1)}, u32[]{:S(2)}, u32[]{:S(2)}) collective-permute-start(bf16[16,3072]{1,0:T(8,128)(2,1)S(1)} %get-tuple-element.34), channel_id=1, source_target_pairs={{0,2},{2,0},{1,3},{3,1},{4,6},{6,4},{5,7},{7,5},{8,10},{10,8},{9,1... | collective-permute-start | bytes 294920 | tf_op jit(solution)/shard_map/ppermute | solution.py:253
  29.4 4.0 %collective-permute-start.8 = (bf16[16,1280]{1,0:T(8,128)(2,1)S(1)}, bf16[16,1280]{1,0:T(8,128)(2,1)S(1)}, u32[]{:S(2)}, u32[]{:S(2)}) collective-permute-start(bf16[16,1280]{1,0:T(8,128)(2,1)S(1)} %get-tuple-element.38), channel_id=1, source_target_pairs={{0,2},{2,0},{1,3},{3,1},{4,6},{6,4},{5,7},{7,5},{8,10},{10,8},{9,1... | collective-permute-start | bytes 122888 | tf_op jit(solution)/shard_map/ppermute | solution.py:253

commit v21 on v20

--- a/solution.py
+++ b/solution.py
@@ -90,11 +90,11 @@
     high = value.astype(jnp.bfloat16).astype(jnp.float32)
     low = jnp.where(high < jnp.inf, value - high, 0.0)
     lane = lax.broadcasted_iota(jnp.int32, value.shape, 1)
-    return jnp.where(lane < LANES // 2, high, low)
+    return jnp.where(lane < value.shape[1] // 2, high, low)
 
 
 def join_wide(value):
-    return value[:, :1] + value[:, LANES - 1 :]
+    return value[:, :1] + value[:, value.shape[1] - 1 :]
 
 
 def rows_kernel(order, width, gain_ref, down_ref, factor_ref, *refs):
@@ -104,15 +104,10 @@
     home = lax.axis_index("gx")
     block_rows = blocks[0].shape[0]
     gain = gain_ref[...].astype(jnp.float32).reshape(1, gain_ref.shape[0])
-    small_ref[...] = jnp.zeros(small_ref.shape, small_ref.dtype)
     for k, block in zip(order, blocks):
         begin = pl.multiple_of(jnp.bitwise_xor(home, k) * block_rows, block_rows)
         values = block[...].astype(jnp.float32)
         x_ref[pl.ds(begin, block_rows), :] = (values * gain).astype(jnp.bfloat16)
-        if k == 0:
-            squares = jnp.sum(values * values, axis=1, keepdims=True) / width
-            squares = split_wide(jnp.broadcast_to(squares, (block_rows, LANES)))
-            small_ref[pl.ds(begin, block_rows), LANES:] = squares.astype(jnp.bfloat16)
     slots, rows, rank_columns = factor_ref.shape
     total = jnp.zeros((rows, rank_columns), jnp.float32)
     for s in range(slots):
@@ -121,7 +116,14 @@
         )
         factor = factor_ref[s]
         total = total + jnp.where(factor > 0, projected * factor, 0.0)
-    small_ref[:, :rank_columns] = total.astype(small_ref.dtype)
+    spare = LANES - rank_columns
+    small = jnp.concatenate([total, jnp.zeros((rows, spare), jnp.float32)], axis=1)
+    small_ref[...] = small.astype(small_ref.dtype)
+    values = blocks[0][...].astype(jnp.float32)
+    squares = jnp.sum(values * values, axis=1, keepdims=True) / width
+    squares = split_wide(jnp.broadcast_to(squares, (block_rows, spare)))
+    begin = pl.multiple_of(home * block_rows, block_rows)
+    small_ref[pl.ds(begin, block_rows), rank_columns:] = squares.astype(small_ref.dtype)
 
 
 def write_rows(acc, outs, n_y, n_z):
@@ -177,16 +179,16 @@
 
 def first_sums_kernel(n_y, n_z, last_ref, small_ref, *refs):
     parts, outs, last_outs = refs[:n_z], refs[n_z : n_z + n_y], refs[n_z + n_y :]
-    pair_kernel(n_y, False, *parts, *outs)
+    pair_kernel(n_y, 0, *parts, *outs)
     columns = last_ref.shape[1]
     write_rows(last_ref, [out.at[:, :columns] for out in last_outs], n_y, n_z)
     write_rows(small_ref, [out.at[:, columns:] for out in last_outs], n_y, n_z)
 
 
-def pair_kernel(n_y, side, *refs):
+def pair_kernel(n_y, rank_columns, *refs):
     parts, outs = refs[:-n_y], refs[-n_y:]
     rows_here, columns = outs[0].shape
-    late = columns - (LANES if side else 0)
+    late = columns - (LANES if rank_columns else 0)
     y = lax.axis_index("gy")
     for k in range(n_y):
         begin = pl.multiple_of(jnp.bitwise_xor(y, k) * rows_here, rows_here)
@@ -195,9 +197,11 @@
         for part in parts[1:]:
             total = total + part[here, :].astype(jnp.float32)
         outs[k][:, :late] = total[:, :late].astype(outs[k].dtype)
-        if side:
-            square = jnp.broadcast_to(join_wide(total[:, late:]), (rows_here, LANES))
-            outs[k][:, late:] = split_wide(square).astype(outs[k].dtype)
+        if rank_columns:
+            square = join_wide(total[:, late + rank_columns :])
+            square = jnp.broadcast_to(square, (rows_here, LANES - rank_columns))
+            side = [total[:, late : late + rank_columns], split_wide(square)]
+            outs[k][:, late:] = jnp.concatenate(side, axis=1).astype(outs[k].dtype)
 
 
 def final_kernel(n, n_z, step, spread_ref, up_ref, *refs):
@@ -213,8 +217,8 @@
             total = total + part[:, begin:end].astype(jnp.float32)
         return total
 
-    side = added(lasts, late, late + 2 * LANES)
-    mean_sq = join_wide(side[:, LANES:])
+    side = added(lasts, late, late + LANES)
+    mean_sq = join_wide(side[:, rank_columns:])
     scale = lax.rsqrt(mean_sq + EPSILON)
     owner = lax.axis_index("gy") * n_z + lax.axis_index("gz")
     live = spread_ref[pl.ds(pl.multiple_of(owner * rows_here, rows_here), rows_here), :]
@@ -316,7 +320,7 @@
         functools.partial(rows_kernel, order, depth * groups),
         out_shape=(
             jax.ShapeDtypeStruct((rows, depth), bf16),
-            jax.ShapeDtypeStruct((rows, 2 * LANES), bf16),
+            jax.ShapeDtypeStruct((rows, LANES), bf16),
         ),
         in_specs=[VMEM] * (3 + n_x),
         out_specs=(VMEM,) * 2,
@@ -376,7 +380,7 @@
     wide = base_parts[0].shape[1]
     made = pl.pallas_call(
         functools.partial(first_sums_kernel, n_y, n_z),
-        out_shape=shapes(n_y, (rows_here, wide)) + shapes(n_z, (kept, last_columns + 2 * LANES)),
+        out_shape=shapes(n_y, (rows_here, wide)) + shapes(n_z, (kept, last_columns + LANES)),
         in_specs=[VMEM] * (2 + n_z),
         out_specs=[VMEM] * (n_y + n_z),
         cost_estimate=cost(0, 0),
@@ -387,8 +391,8 @@
     lasts = spread_out(made[n_y:], "gz", n_z)
 
     made = pl.pallas_call(
-        functools.partial(pair_kernel, n_y, True),
-        out_shape=shapes(n_y, (rows_here, last_columns + 2 * LANES)),
+        functools.partial(pair_kernel, n_y, rank_columns),
+        out_shape=shapes(n_y, (rows_here, last_columns + LANES)),
         in_specs=[VMEM] * n_z,
         out_specs=[VMEM] * n_y,
         cost_estimate=cost(0, 0),

time: 34.7 us -> 34.7 us (level)
  transfers between devices with their start and end apart: 9 -> 9, of which waited for: 4 -> 3; matrix products, arithmetic and copies ran while one was open for 0% -> 0% of each run, Pallas kernels for 48% -> 49%
where the time goes in v21:
time: 34.7 us; the launch traced here: 34.5 us
  Pallas kernels  18.3 us (53%)
  starting transfers between devices  12 us (35%)
  waiting for transfers between devices  4 us (12%)
    ppermute x9, starting transfers between devices, send(): return lax.ppermute(value, axis, [(j, j ^ k) for j in range(n)])  12 us
    pallas_call x1, Pallas kernels, body(): pl.pallas_call(functools.partial(first_load_kernel, len(loads[0]), firsts...  6.66 us
    ppermute x9, waiting for transfers between devices, send(): return lax.ppermute(value, axis, [(j, j ^ k) for j in range(n)])  4 us
    pallas_call x1, Pallas kernels, body(): pl.pallas_call(functools.partial(last_load_kernel, len(loads[1]), firsts[...  3.56 us
    pallas_call x1, Pallas kernels, body(): pl.pallas_call(functools.partial(base_kernel, 2, columns - late, step), o...  3.12 us
    pallas_call x1, Pallas kernels, product(): pl.pallas_call(functools.partial(product_kernel, len(some), n_y, n_z, ste...  1.62 us
    pallas_call x1, Pallas kernels, body(): pl.pallas_call(functools.partial(last_kernel, len(weights) - split, step)...  1.56 us
    pallas_call x1, Pallas kernels, body(): pl.pallas_call(functools.partial(final_kernel, n_y, n_z, min(512, columns...  1.09 us
  transfers between devices with their start and end apart: 9, of which 3 were waited for; matrix products, arithmetic and copies ran while one was open for 0% of the time, Pallas kernels for 49%

profile of v21, /device:TPU:0, one launch (start us, length us, event | category | flops | bytes accessed | tf_op | source)
XLA Modules:
  0.0 34.5 jit_solution(8247872446593511396)
XLA Ops:
  0.0 4.0 %collective-permute-start = (bf16[16,4096]{1,0:T(8,128)(2,1)}, bf16[16,4096]{1,0:T(8,128)(2,1)S(1)}, u32[]{:S(2)}, u32[]{:S(2)}) collective-permute-start(bf16[16,4096]{1,0:T(8,128)(2,1)} %refs_0_.1), channel_id=1, source_target_pairs={{0,8},{4,12},{8,0},{12,4},{1,9},{5,13},{9,1},{13,5},{2,10},{6,14},... | collective-permute-start | bytes 393224 | tf_op jit(solution)/shard_map/ppermute | solution.py:257
  4.0 1.6 %collective-permute-start.1 = (bf16[16,4096]{1,0:T(8,128)(2,1)}, bf16[16,4096]{1,0:T(8,128)(2,1)S(1)}, u32[]{:S(2)}, u32[]{:S(2)}) collective-permute-start(bf16[16,4096]{1,0:T(8,128)(2,1)} %refs_0_.1), channel_id=1, source_target_pairs={{0,4},{4,0},{8,12},{12,8},{1,5},{5,1},{9,13},{13,9},{2,6},{6,2},{1... | collective-permute-start | bytes 393224 | tf_op jit(solution)/shard_map/ppermute | solution.py:257
  5.6 6.7 %first_load.1 = (f32[1,64,64]{2,1,0:T(8,128)S(1)}, f32[64,256]{1,0:T(8,128)S(1)}, bf16[4096,1024]{1,0:T(8,128)(2,1)S(1)}, bf16[4096,1024]{1,0:T(8,128)(2,1)S(1)}, bf16[4096,256]{1,0:T(8,128)(2,1)S(1)}) custom-call(bf16[4096,4096]{1,0:T(8,128)(2,1)} %w_hbm.5, s32[4]{0:T(128)} %rank_hbm.1, s32[4]{0:T(128)} %slot_hbm.1, s32[5]{0:T(128)} %start_hbm.1), custom_call_target="tpu_custom_call" | custom-call | flops 5033164800 | bytes 16777216 | tf_op jit(solution)/shard_map/first_load/pallas_call | solution.py:287
  12.3 0.0 collective-permute-done.refs_1_.__
  12.3 0.5 %collective-permute-start.2 = (bf16[16,4096]{1,0:T(8,128)(2,1)S(1)}, bf16[16,4096]{1,0:T(8,128)(2,1)S(1)}, u32[]{:S(2)}, u32[]{:S(2)}) collective-permute-start(bf16[16,4096]{1,0:T(8,128)(2,1)S(1)} %collective-permute-done.refs_1_.__), channel_id=1, source_target_pairs={{0,4},{4,0},{8,12},{12,8},{1,5},{5,1},{9,13},{13,9},{2,6},{6,2},{1... | collective-permute-start | bytes 393224 | tf_op jit(solution)/shard_map/ppermute | solution.py:257
  12.8 3.6 %last_load.1.refs_2_ = bf16[4096,1024]{1,0:T(8,128)(2,1)S(1)} custom-call(bf16[4096,4096]{1,0:T(8,128)(2,1)} %w_hbm.5, f32[1,64,64]{2,1,0:T(8,128)S(1)} %get-tuple-element.23.factor_ref._, bf16[16,4096]{1,0:T(8,128)(2,1)S(1)} %collective-permute-done.refs_1_.__), custom_call_target="tpu_custom_call" | custom-call | flops 5033164800 | bytes 16777216 | tf_op jit(solution)/shard_map/last_load/pallas_call | solution.py:305
  16.4 0.9 %collective-permute-done.2.refs_3_ = bf16[16,4096]{1,0:T(8,128)(2,1)S(1)} collective-permute-done((bf16[16,4096]{1,0:T(8,128)(2,1)S(1)}, bf16[16,4096]{1,0:T(8,128)(2,1)S(1)}, u32[]{:S(2)}, u32[]{:S(2)}) %collective-permute-start.2) | collective-permute-done | bytes 131104 | tf_op jit(solution)/shard_map/ppermute | solution.py:257
  17.3 0.4 %scaled_rows.1 = (bf16[64,4096]{1,0:T(8,128)(2,1)S(1)}, bf16[64,128]{1,0:T(8,128)(2,1)S(1)}) custom-call(bf16[4096]{0:T(1024)(128)(2,1)S(1)} %copy-done.3, bf16[1,64,4096]{2,1,0:T(8,128)(2,1)S(1)} %bitcast.1, f32[1,64,64]{2,1,0:T(8,128)S(1)} %get-tuple-element.23.factor_ref._, bf16[16,4096]{1,0:T(8,128)(2,1)S(1)} %copy-done.2, ...), custom_call_target="tpu_custom_call" | custom-call | tf_op jit(solution)/shard_map/scaled_rows/pallas_call | solution.py:319
  17.8 0.7 %collective-permute-start.3 = (bf16[64,128]{1,0:T(8,128)(2,1)S(1)}, bf16[64,128]{1,0:T(8,128)(2,1)S(1)}, u32[]{:S(2)}, u32[]{:S(2)}) collective-permute-start(bf16[64,128]{1,0:T(8,128)(2,1)S(1)} %get-tuple-element.29), channel_id=1, source_target_pairs={{0,4},{4,0},{8,12},{12,8},{1,5},{5,1},{9,13},{13,9},{2,6},{6,2},{1... | collective-permute-start | bytes 49160 | tf_op jit(solution)/shard_map/ppermute | solution.py:257
  18.5 3.1 %first_columns.1 = (f32[64,2048]{1,0:T(8,128)S(1)}, bf16[4096,768]{1,0:T(8,128)(2,1)S(1)}) custom-call(bf16[4096,4096]{1,0:T(8,128)(2,1)} %w_hbm.5, bf16[64,4096]{1,0:T(8,128)(2,1)S(1)} %get-tuple-element.24.x_ref, bf16[4096,1024]{1,0:T(8,128)(2,1)S(1)} %get-tuple-element.26.refs_0_, bf16[4096,1024]{1,0:T(8,128)(2,1)S(1)} %get-tuple-element.27.refs_1_), custom_call_target="tpu_custom_call" | custom-call | flops 1073741824 | bytes 16777216 | tf_op jit(solution)/shard_map/first_columns/pallas_call | solution.py:340
  21.7 2.1 %collective-permute-start.4 = (bf16[64,128]{1,0:T(8,128)(2,1)S(1)}, bf16[64,128]{1,0:T(8,128)(2,1)S(1)}, u32[]{:S(2)}, u32[]{:S(2)}) collective-permute-start(bf16[64,128]{1,0:T(8,128)(2,1)S(1)} %add.6.refs_1_), channel_id=1, source_target_pairs={{0,8},{4,12},{8,0},{12,4},{1,9},{5,13},{9,1},{13,5},{2,10},{6,14},... | collective-permute-start | bytes 49160 | tf_op jit(solution)/shard_map/ppermute | solution.py:257
  23.8 1.6 %middle_columns.1 = (f32[32,3072]{1,0:T(8,128)S(1)}, bf16[32,3072]{1,0:T(8,128)(2,1)S(1)}) custom-call(bf16[64,4096]{1,0:T(8,128)(2,1)S(1)} %get-tuple-element.24.x_ref, f32[64,2048]{1,0:T(8,128)S(1)} %get-tuple-element.30.refs_0_, bf16[64,128]{1,0:T(8,128)(2,1)S(1)} %add.6.refs_1_, bf16[4096,1024]{1,0:T(8,128)(2,1)S(1)} %last_load.1.refs_2_), custom_call_target="tpu_custom_call" | custom-call | flops 6442450944 | bytes 25165824 | tf_op jit(solution)/shard_map/middle_columns/pallas_call | solution.py:356
  25.4 0.1 collective-permute-start.5
  25.5 0.0 copy-start
  25.5 1.6 %last_columns.1.last_ref = f32[64,1024]{1,0:T(8,128)S(1)} custom-call(bf16[64,4096]{1,0:T(8,128)(2,1)S(1)} %get-tuple-element.24.x_ref, bf16[4096,256]{1,0:T(8,128)(2,1)S(1)} %get-tuple-element.25.refs_0_, bf16[4096,768]{1,0:T(8,128)(2,1)S(1)} %get-tuple-element.28.refs_1_), custom_call_target="tpu_custom_call" | custom-call | flops 4294967296 | bytes 8388608 | tf_op jit(solution)/shard_map/last_columns/pallas_call | solution.py:371
  27.1 0.0 collective-permute-done.4
  27.1 0.1 first_sums.1
  27.2 0.6 %collective-permute-start.7 = (bf16[32,1152]{1,0:T(8,128)(2,1)S(1)}, bf16[32,1152]{1,0:T(8,128)(2,1)S(1)}, u32[]{:S(2)}, u32[]{:S(2)}) collective-permute-start(bf16[32,1152]{1,0:T(8,128)(2,1)S(1)} %get-tuple-element.36), channel_id=1, source_target_pairs={{0,1},{1,0},{2,3},{3,2},{4,5},{5,4},{6,7},{7,6},{8,9},{9,8},{10,11... | collective-permute-start | bytes 221192 | tf_op jit(solution)/shard_map/ppermute | solution.py:257
  27.7 1.5 %collective-permute-start.6 = (bf16[16,3072]{1,0:T(8,128)(2,1)S(1)}, bf16[16,3072]{1,0:T(8,128)(2,1)S(1)}, u32[]{:S(2)}, u32[]{:S(2)}) collective-permute-start(bf16[16,3072]{1,0:T(8,128)(2,1)S(1)} %get-tuple-element.34), channel_id=1, source_target_pairs={{0,2},{2,0},{1,3},{3,1},{4,6},{6,4},{5,7},{7,5},{8,10},{10,8},{9,1... | collective-permute-start | bytes 294920 | tf_op jit(solution)/shard_map/ppermute | solution.py:257
  29.2 0.2 last_sums.1
  29.5 0.9 %collective-permute-start.8 = (bf16[16,1152]{1,0:T(8,128)(2,1)S(1)}, bf16[16,1152]{1,0:T(8,128)(2,1)S(1)}, u32[]{:S(2)}, u32[]{:S(2)}) collective-permute-start(bf16[16,1152]{1,0:T(8,128)(2,1)S(1)} %get-tuple-element.38), channel_id=1, source_target_pairs={{0,2},{2,0},{1,3},{3,1},{4,6},{6,4},{5,7},{7,5},{8,10},{10,8},{9,1... | collective-permute-start | bytes 110600 | tf_op jit(solution)/shard_map/ppermute | solution.py:257
  30.4 2.5 %collective-permute-done.6.refs_1_ = bf16[16,3072]{1,0:T(8,128)(2,1)S(1)} collective-permute-done((bf16[16,3072]{1,0:T(8,128)(2,1)S(1)}, bf16[16,3072]{1,0:T(8,128)(2,1)S(1)}, u32[]{:S(2)}, u32[]{:S(2)}) %collective-permute-start.6) | collective-permute-done | bytes 98336 | tf_op jit(solution)/shard_map/ppermute | solution.py:257
  32.9 0.5 %collective-permute-done.8.refs_3_ = bf16[16,1152]{1,0:T(8,128)(2,1)S(1)} collective-permute-done((bf16[16,1152]{1,0:T(8,128)(2,1)S(1)}, bf16[16,1152]{1,0:T(8,128)(2,1)S(1)}, u32[]{:S(2)}, u32[]{:S(2)}) %collective-permute-start.8) | collective-permute-done | bytes 36896 | tf_op jit(solution)/shard_map/ppermute | solution.py:257
  33.4 1.1 %query_rows.1 = bf16[16,4096]{1,0:T(8,128)(2,1)} custom-call(f32[64,256]{1,0:T(8,128)S(1)} %get-tuple-element.22.spread_ref, bf16[4,64,4096]{2,1,0:T(8,128)(2,1)S(1)} %copy-done, f32[16,3072]{1,0:T(8,128)S(1)} %get-tuple-element.33.refs_0_, bf16[16,3072]{1,0:T(8,128)(2,1)S(1)} %collective-permute-done.6.refs_1_, f32[16,1152]{1,0:T(8,128)S(1)} %get-tuple-element.37.refs_2_, ...), custom_call_target="tpu_custom_call" | custom-call | tf_op jit(solution)/shard_map/query_rows/pallas_call | solution.py:404
  (13 shorter events, 0.0 us)
Async XLA Ops:
  0.0 12.3 %collective-permute-start = (bf16[16,4096]{1,0:T(8,128)(2,1)}, bf16[16,4096]{1,0:T(8,128)(2,1)S(1)}, u32[]{:S(2)}, u32[]{:S(2)}) collective-permute-start(bf16[16,4096]{1,0:T(8,128)(2,1)} %refs_0_.1), channel_id=1, source_target_pairs={{0,8},{4,12},{8,0},{12,4},{1,9},{5,13},{9,1},{13,5},{2,10},{6,14},... | collective-permute-start | bytes 393224 | tf_op jit(solution)/shard_map/ppermute | solution.py:257
  4.0 12.3 %collective-permute-start.1 = (bf16[16,4096]{1,0:T(8,128)(2,1)}, bf16[16,4096]{1,0:T(8,128)(2,1)S(1)}, u32[]{:S(2)}, u32[]{:S(2)}) collective-permute-start(bf16[16,4096]{1,0:T(8,128)(2,1)} %refs_0_.1), channel_id=1, source_target_pairs={{0,4},{4,0},{8,12},{12,8},{1,5},{5,1},{9,13},{13,9},{2,6},{6,2},{1... | collective-permute-start | bytes 393224 | tf_op jit(solution)/shard_map/ppermute | solution.py:257
  12.3 5.0 %collective-permute-start.2 = (bf16[16,4096]{1,0:T(8,128)(2,1)S(1)}, bf16[16,4096]{1,0:T(8,128)(2,1)S(1)}, u32[]{:S(2)}, u32[]{:S(2)}) collective-permute-start(bf16[16,4096]{1,0:T(8,128)(2,1)S(1)} %collective-permute-done.refs_1_.__), channel_id=1, source_target_pairs={{0,4},{4,0},{8,12},{12,8},{1,5},{5,1},{9,13},{13,9},{2,6},{6,2},{1... | collective-permute-start | bytes 393224 | tf_op jit(solution)/shard_map/ppermute | solution.py:257
  12.8 4.5 %copy-start.1 = (bf16[1,4096,64]{1,2,0:T(8,128)(2,1)S(1)}, bf16[1,4096,64]{1,2,0:T(8,128)(2,1)}, u32[]{:S(2)}) copy-start(bf16[1,4096,64]{1,2,0:T(8,128)(2,1)} %param.12) | copy-start | bytes 1572868
  12.8 4.5 %copy-start.2 = (bf16[16,4096]{1,0:T(8,128)(2,1)S(1)}, bf16[16,4096]{1,0:T(8,128)(2,1)}, u32[]{:S(2)}) copy-start(bf16[16,4096]{1,0:T(8,128)(2,1)} %refs_0_.1) | copy-start | bytes 393220
  12.8 4.5 %copy-start.3 = (bf16[4096]{0:T(1024)(128)(2,1)S(1)}, bf16[4096]{0:T(1024)(128)(2,1)}, u32[]{:S(2)}) copy-start(bf16[4096]{0:T(1024)(128)(2,1)} %gain_ref.1) | copy-start | bytes 24580
  17.8 3.9 %collective-permute-start.3 = (bf16[64,128]{1,0:T(8,128)(2,1)S(1)}, bf16[64,128]{1,0:T(8,128)(2,1)S(1)}, u32[]{:S(2)}, u32[]{:S(2)}) collective-permute-start(bf16[64,128]{1,0:T(8,128)(2,1)S(1)} %get-tuple-element.29), channel_id=1, source_target_pairs={{0,4},{4,0},{8,12},{12,8},{1,5},{5,1},{9,13},{13,9},{2,6},{6,2},{1... | collective-permute-start | bytes 49160 | tf_op jit(solution)/shard_map/ppermute | solution.py:257
  21.7 5.4 %collective-permute-start.4 = (bf16[64,128]{1,0:T(8,128)(2,1)S(1)}, bf16[64,128]{1,0:T(8,128)(2,1)S(1)}, u32[]{:S(2)}, u32[]{:S(2)}) collective-permute-start(bf16[64,128]{1,0:T(8,128)(2,1)S(1)} %add.6.refs_1_), channel_id=1, source_target_pairs={{0,8},{4,12},{8,0},{12,4},{1,9},{5,13},{9,1},{13,5},{2,10},{6,14},... | collective-permute-start | bytes 49160 | tf_op jit(solution)/shard_map/ppermute | solution.py:257
  25.4 1.7 %collective-permute-start.5 = (bf16[32,3072]{1,0:T(8,128)(2,1)S(1)}, bf16[32,3072]{1,0:T(8,128)(2,1)S(1)}, u32[]{:S(2)}, u32[]{:S(2)}) collective-permute-start(bf16[32,3072]{1,0:T(8,128)(2,1)S(1)} %get-tuple-element.32), channel_id=1, source_target_pairs={{0,1},{1,0},{2,3},{3,2},{4,5},{5,4},{6,7},{7,6},{8,9},{9,8},{10,11... | collective-permute-start | bytes 589832 | tf_op jit(solution)/shard_map/ppermute | solution.py:257
  25.5 7.9 %copy-start = (bf16[4,64,4096]{2,1,0:T(8,128)(2,1)S(1)}, bf16[4,64,4096]{2,1,0:T(8,128)(2,1)}, u32[]{:S(2)}) copy-start(bf16[4,64,4096]{2,1,0:T(8,128)(2,1)} %up_ref.1) | copy-start | bytes 6291460
  27.2 2.0 %collective-permute-start.7 = (bf16[32,1152]{1,0:T(8,128)(2,1)S(1)}, bf16[32,1152]{1,0:T(8,128)(2,1)S(1)}, u32[]{:S(2)}, u32[]{:S(2)}) collective-permute-start(bf16[32,1152]{1,0:T(8,128)(2,1)S(1)} %get-tuple-element.36), channel_id=1, source_target_pairs={{0,1},{1,0},{2,3},{3,2},{4,5},{5,4},{6,7},{7,6},{8,9},{9,8},{10,11... | collective-permute-start | bytes 221192 | tf_op jit(solution)/shard_map/ppermute | solution.py:257
  27.7 5.2 %collective-permute-start.6 = (bf16[16,3072]{1,0:T(8,128)(2,1)S(1)}, bf16[16,3072]{1,0:T(8,128)(2,1)S(1)}, u32[]{:S(2)}, u32[]{:S(2)}) collective-permute-start(bf16[16,3072]{1,0:T(8,128)(2,1)S(1)} %get-tuple-element.34), channel_id=1, source_target_pairs={{0,2},{2,0},{1,3},{3,1},{4,6},{6,4},{5,7},{7,5},{8,10},{10,8},{9,1... | collective-permute-start | bytes 294920 | tf_op jit(solution)/shard_map/ppermute | solution.py:257
  29.5 4.0 %collective-permute-start.8 = (bf16[16,1152]{1,0:T(8,128)(2,1)S(1)}, bf16[16,1152]{1,0:T(8,128)(2,1)S(1)}, u32[]{:S(2)}, u32[]{:S(2)}) collective-permute-start(bf16[16,1152]{1,0:T(8,128)(2,1)S(1)} %get-tuple-element.38), channel_id=1, source_target_pairs={{0,2},{2,0},{1,3},{3,1},{4,6},{6,4},{5,7},{7,5},{8,10},{10,8},{9,1... | collective-permute-start | bytes 110600 | tf_op jit(solution)/shard_map/ppermute | solution.py:257

commit v22 on v21

--- a/solution.py
+++ b/solution.py
@@ -328,11 +328,11 @@
         name="scaled_rows",
     )(attention_norm_gain, jnp.swapaxes(slot_down_factors, 1, 2), factor, *blocks)
 
-    one_hop = small = small + send(small, "gx", n_x, 1)
-    hop = 2
-    while hop < n_x:
+    hop = n_x // 2
+    crossed = small = small + send(small, "gx", n_x, hop)
+    while hop > 1:
+        hop //= 2
         small = small + send(small, "gx", n_x, hop)
-        hop *= 2
 
     def shapes(n, shape):
         return [jax.ShapeDtypeStruct(shape, f32 if k == 0 else bf16) for k in range(n)]
@@ -367,7 +367,7 @@
 
     split = 3
     last_columns = sum(w.shape[1] for w in weights[split:])
-    base_parts = product(weights[2:split], [base, one_hop], 4, "middle_columns")
+    base_parts = product(weights[2:split], [base, crossed], 4, "middle_columns")
     last = pl.pallas_call(
         functools.partial(last_kernel, len(weights) - split, step),
         out_shape=jax.ShapeDtypeStruct((rows, last_columns), f32),

time: 34.7 us -> 34.7 us (level)
  waiting for transfers between devices: 4 us -> 4.51 us
  starting transfers between devices: 12 us -> 11.5 us
    ppermute x9, waiting for transfers between devices: 4 us -> 4.51 us  [send(): return lax.ppermute(value, axis, [(j, j ^ k) for j in range(n)])]
    ppermute x9, starting transfers between devices: 12 us -> 11.5 us  [send(): return lax.ppermute(value, axis, [(j, j ^ k) for j in range(n)])]
  transfers between devices with their start and end apart: 9 -> 9, of which waited for: 3 -> 4; matrix products, arithmetic and copies ran while one was open for 0% -> 0% of each run, Pallas kernels for 49% -> 49%
where the time goes in v22:
time: 34.7 us; the launch traced here: 34.5 us
  Pallas kernels  18.3 us (53%)
  starting transfers between devices  11.5 us (33%)
  waiting for transfers between devices  4.51 us (13%)
    ppermute x9, starting transfers between devices, send(): return lax.ppermute(value, axis, [(j, j ^ k) for j in range(n)])  11.5 us
    pallas_call x1, Pallas kernels, body(): pl.pallas_call(functools.partial(first_load_kernel, len(loads[0]), firsts...  6.66 us
    ppermute x9, waiting for transfers between devices, send(): return lax.ppermute(value, axis, [(j, j ^ k) for j in range(n)])  4.51 us
    pallas_call x1, Pallas kernels, body(): pl.pallas_call(functools.partial(last_load_kernel, len(loads[1]), firsts[...  3.56 us
    pallas_call x1, Pallas kernels, body(): pl.pallas_call(functools.partial(base_kernel, 2, columns - late, step), o...  3.12 us
    pallas_call x1, Pallas kernels, product(): pl.pallas_call(functools.partial(product_kernel, len(some), n_y, n_z, ste...  1.62 us
    pallas_call x1, Pallas kernels, body(): pl.pallas_call(functools.partial(last_kernel, len(weights) - split, step)...  1.56 us
    pallas_call x1, Pallas kernels, body(): pl.pallas_call(functools.partial(final_kernel, n_y, n_z, min(512, columns...  1.09 us
  transfers between devices with their start and end apart: 9, of which 4 were waited for; matrix products, arithmetic and copies ran while one was open for 0% of the time, Pallas kernels for 49%

profile of v22, /device:TPU:0, one launch (start us, length us, event | category | flops | bytes accessed | tf_op | source)
XLA Modules:
  0.0 34.5 jit_solution(17175618725174842567)
XLA Ops:
  0.0 4.0 %collective-permute-start = (bf16[16,4096]{1,0:T(8,128)(2,1)}, bf16[16,4096]{1,0:T(8,128)(2,1)S(1)}, u32[]{:S(2)}, u32[]{:S(2)}) collective-permute-start(bf16[16,4096]{1,0:T(8,128)(2,1)} %refs_0_.1), channel_id=1, source_target_pairs={{0,8},{4,12},{8,0},{12,4},{1,9},{5,13},{9,1},{13,5},{2,10},{6,14},... | collective-permute-start | bytes 393224 | tf_op jit(solution)/shard_map/ppermute | solution.py:257
  4.0 1.6 %collective-permute-start.1 = (bf16[16,4096]{1,0:T(8,128)(2,1)}, bf16[16,4096]{1,0:T(8,128)(2,1)S(1)}, u32[]{:S(2)}, u32[]{:S(2)}) collective-permute-start(bf16[16,4096]{1,0:T(8,128)(2,1)} %refs_0_.1), channel_id=1, source_target_pairs={{0,4},{4,0},{8,12},{12,8},{1,5},{5,1},{9,13},{13,9},{2,6},{6,2},{1... | collective-permute-start | bytes 393224 | tf_op jit(solution)/shard_map/ppermute | solution.py:257
  5.6 6.7 %first_load.1 = (f32[1,64,64]{2,1,0:T(8,128)S(1)}, f32[64,256]{1,0:T(8,128)S(1)}, bf16[4096,1024]{1,0:T(8,128)(2,1)S(1)}, bf16[4096,1024]{1,0:T(8,128)(2,1)S(1)}, bf16[4096,256]{1,0:T(8,128)(2,1)S(1)}) custom-call(bf16[4096,4096]{1,0:T(8,128)(2,1)} %w_hbm.5, s32[4]{0:T(128)} %rank_hbm.1, s32[4]{0:T(128)} %slot_hbm.1, s32[5]{0:T(128)} %start_hbm.1), custom_call_target="tpu_custom_call" | custom-call | flops 5033164800 | bytes 16777216 | tf_op jit(solution)/shard_map/first_load/pallas_call | solution.py:287
  12.3 0.5 %collective-permute-start.2 = (bf16[16,4096]{1,0:T(8,128)(2,1)S(1)}, bf16[16,4096]{1,0:T(8,128)(2,1)S(1)}, u32[]{:S(2)}, u32[]{:S(2)}) collective-permute-start(bf16[16,4096]{1,0:T(8,128)(2,1)S(1)} %collective-permute-done.refs_1_.__), channel_id=1, source_target_pairs={{0,4},{4,0},{8,12},{12,8},{1,5},{5,1},{9,13},{13,9},{2,6},{6,2},{1... | collective-permute-start | bytes 393224 | tf_op jit(solution)/shard_map/ppermute | solution.py:257
  12.8 3.6 %last_load.1.refs_2_ = bf16[4096,1024]{1,0:T(8,128)(2,1)S(1)} custom-call(bf16[4096,4096]{1,0:T(8,128)(2,1)} %w_hbm.5, f32[1,64,64]{2,1,0:T(8,128)S(1)} %get-tuple-element.23.factor_ref._, bf16[16,4096]{1,0:T(8,128)(2,1)S(1)} %collective-permute-done.refs_1_.__), custom_call_target="tpu_custom_call" | custom-call | flops 5033164800 | bytes 16777216 | tf_op jit(solution)/shard_map/last_load/pallas_call | solution.py:305
  16.4 0.0 collective-permute-done.1.refs_2_
  16.4 0.9 %collective-permute-done.2.refs_3_ = bf16[16,4096]{1,0:T(8,128)(2,1)S(1)} collective-permute-done((bf16[16,4096]{1,0:T(8,128)(2,1)S(1)}, bf16[16,4096]{1,0:T(8,128)(2,1)S(1)}, u32[]{:S(2)}, u32[]{:S(2)}) %collective-permute-start.2) | collective-permute-done | bytes 131104 | tf_op jit(solution)/shard_map/ppermute | solution.py:257
  17.3 0.4 %scaled_rows.1 = (bf16[64,4096]{1,0:T(8,128)(2,1)S(1)}, bf16[64,128]{1,0:T(8,128)(2,1)S(1)}) custom-call(bf16[4096]{0:T(1024)(128)(2,1)S(1)} %copy-done.3, bf16[1,64,4096]{2,1,0:T(8,128)(2,1)S(1)} %bitcast.1, f32[1,64,64]{2,1,0:T(8,128)S(1)} %get-tuple-element.23.factor_ref._, bf16[16,4096]{1,0:T(8,128)(2,1)S(1)} %copy-done.2, ...), custom_call_target="tpu_custom_call" | custom-call | tf_op jit(solution)/shard_map/scaled_rows/pallas_call | solution.py:319
  17.8 1.1 %collective-permute-start.3 = (bf16[64,128]{1,0:T(8,128)(2,1)S(1)}, bf16[64,128]{1,0:T(8,128)(2,1)S(1)}, u32[]{:S(2)}, u32[]{:S(2)}) collective-permute-start(bf16[64,128]{1,0:T(8,128)(2,1)S(1)} %get-tuple-element.29), channel_id=1, source_target_pairs={{0,8},{4,12},{8,0},{12,4},{1,9},{5,13},{9,1},{13,5},{2,10},{6,14},... | collective-permute-start | bytes 49160 | tf_op jit(solution)/shard_map/ppermute | solution.py:257
  18.8 3.1 %first_columns.1 = (f32[64,2048]{1,0:T(8,128)S(1)}, bf16[4096,768]{1,0:T(8,128)(2,1)S(1)}) custom-call(bf16[4096,4096]{1,0:T(8,128)(2,1)} %w_hbm.5, bf16[64,4096]{1,0:T(8,128)(2,1)S(1)} %get-tuple-element.24.x_ref, bf16[4096,1024]{1,0:T(8,128)(2,1)S(1)} %get-tuple-element.26.refs_0_, bf16[4096,1024]{1,0:T(8,128)(2,1)S(1)} %get-tuple-element.27.refs_1_), custom_call_target="tpu_custom_call" | custom-call | flops 1073741824 | bytes 16777216 | tf_op jit(solution)/shard_map/first_columns/pallas_call | solution.py:340
  22.0 0.5 %collective-permute-done.3 = bf16[64,128]{1,0:T(8,128)(2,1)S(1)} collective-permute-done((bf16[64,128]{1,0:T(8,128)(2,1)S(1)}, bf16[64,128]{1,0:T(8,128)(2,1)S(1)}, u32[]{:S(2)}, u32[]{:S(2)}) %collective-permute-start.3) | collective-permute-done | bytes 16416 | tf_op jit(solution)/shard_map/ppermute | solution.py:257
  22.5 1.3 %collective-permute-start.4 = (bf16[64,128]{1,0:T(8,128)(2,1)S(1)}, bf16[64,128]{1,0:T(8,128)(2,1)S(1)}, u32[]{:S(2)}, u32[]{:S(2)}) collective-permute-start(bf16[64,128]{1,0:T(8,128)(2,1)S(1)} %add.6.refs_1_), channel_id=1, source_target_pairs={{0,4},{4,0},{8,12},{12,8},{1,5},{5,1},{9,13},{13,9},{2,6},{6,2},{1... | collective-permute-start | bytes 49160 | tf_op jit(solution)/shard_map/ppermute | solution.py:257
  23.8 1.6 %middle_columns.1 = (f32[32,3072]{1,0:T(8,128)S(1)}, bf16[32,3072]{1,0:T(8,128)(2,1)S(1)}) custom-call(bf16[64,4096]{1,0:T(8,128)(2,1)S(1)} %get-tuple-element.24.x_ref, f32[64,2048]{1,0:T(8,128)S(1)} %get-tuple-element.30.refs_0_, bf16[64,128]{1,0:T(8,128)(2,1)S(1)} %add.6.refs_1_, bf16[4096,1024]{1,0:T(8,128)(2,1)S(1)} %last_load.1.refs_2_), custom_call_target="tpu_custom_call" | custom-call | flops 6442450944 | bytes 25165824 | tf_op jit(solution)/shard_map/middle_columns/pallas_call | solution.py:356
  25.4 0.1 collective-permute-start.5
  25.5 0.0 copy-start
  25.5 1.6 %last_columns.1.last_ref = f32[64,1024]{1,0:T(8,128)S(1)} custom-call(bf16[64,4096]{1,0:T(8,128)(2,1)S(1)} %get-tuple-element.24.x_ref, bf16[4096,256]{1,0:T(8,128)(2,1)S(1)} %get-tuple-element.25.refs_0_, bf16[4096,768]{1,0:T(8,128)(2,1)S(1)} %get-tuple-element.28.refs_1_), custom_call_target="tpu_custom_call" | custom-call | flops 4294967296 | bytes 8388608 | tf_op jit(solution)/shard_map/last_columns/pallas_call | solution.py:371
  27.1 0.1 first_sums.1
  27.2 0.6 %collective-permute-start.7 = (bf16[32,1152]{1,0:T(8,128)(2,1)S(1)}, bf16[32,1152]{1,0:T(8,128)(2,1)S(1)}, u32[]{:S(2)}, u32[]{:S(2)}) collective-permute-start(bf16[32,1152]{1,0:T(8,128)(2,1)S(1)} %get-tuple-element.36), channel_id=1, source_target_pairs={{0,1},{1,0},{2,3},{3,2},{4,5},{5,4},{6,7},{7,6},{8,9},{9,8},{10,11... | collective-permute-start | bytes 221192 | tf_op jit(solution)/shard_map/ppermute | solution.py:257
  27.7 1.5 %collective-permute-start.6 = (bf16[16,3072]{1,0:T(8,128)(2,1)S(1)}, bf16[16,3072]{1,0:T(8,128)(2,1)S(1)}, u32[]{:S(2)}, u32[]{:S(2)}) collective-permute-start(bf16[16,3072]{1,0:T(8,128)(2,1)S(1)} %get-tuple-element.34), channel_id=1, source_target_pairs={{0,2},{2,0},{1,3},{3,1},{4,6},{6,4},{5,7},{7,5},{8,10},{10,8},{9,1... | collective-permute-start | bytes 294920 | tf_op jit(solution)/shard_map/ppermute | solution.py:257
  29.2 0.2 last_sums.1
  29.5 0.9 %collective-permute-start.8 = (bf16[16,1152]{1,0:T(8,128)(2,1)S(1)}, bf16[16,1152]{1,0:T(8,128)(2,1)S(1)}, u32[]{:S(2)}, u32[]{:S(2)}) collective-permute-start(bf16[16,1152]{1,0:T(8,128)(2,1)S(1)} %get-tuple-element.38), channel_id=1, source_target_pairs={{0,2},{2,0},{1,3},{3,1},{4,6},{6,4},{5,7},{7,5},{8,10},{10,8},{9,1... | collective-permute-start | bytes 110600 | tf_op jit(solution)/shard_map/ppermute | solution.py:257
  30.4 2.5 %collective-permute-done.6.refs_1_ = bf16[16,3072]{1,0:T(8,128)(2,1)S(1)} collective-permute-done((bf16[16,3072]{1,0:T(8,128)(2,1)S(1)}, bf16[16,3072]{1,0:T(8,128)(2,1)S(1)}, u32[]{:S(2)}, u32[]{:S(2)}) %collective-permute-start.6) | collective-permute-done | bytes 98336 | tf_op jit(solution)/shard_map/ppermute | solution.py:257
  32.9 0.5 %collective-permute-done.8.refs_3_ = bf16[16,1152]{1,0:T(8,128)(2,1)S(1)} collective-permute-done((bf16[16,1152]{1,0:T(8,128)(2,1)S(1)}, bf16[16,1152]{1,0:T(8,128)(2,1)S(1)}, u32[]{:S(2)}, u32[]{:S(2)}) %collective-permute-start.8) | collective-permute-done | bytes 36896 | tf_op jit(solution)/shard_map/ppermute | solution.py:257
  33.4 1.1 %query_rows.1 = bf16[16,4096]{1,0:T(8,128)(2,1)} custom-call(f32[64,256]{1,0:T(8,128)S(1)} %get-tuple-element.22.spread_ref, bf16[4,64,4096]{2,1,0:T(8,128)(2,1)S(1)} %copy-done, f32[16,3072]{1,0:T(8,128)S(1)} %get-tuple-element.33.refs_0_, bf16[16,3072]{1,0:T(8,128)(2,1)S(1)} %collective-permute-done.6.refs_1_, f32[16,1152]{1,0:T(8,128)S(1)} %get-tuple-element.37.refs_2_, ...), custom_call_target="tpu_custom_call" | custom-call | tf_op jit(solution)/shard_map/query_rows/pallas_call | solution.py:404
  (13 shorter events, 0.0 us)
Async XLA Ops:
  0.0 12.3 %collective-permute-start = (bf16[16,4096]{1,0:T(8,128)(2,1)}, bf16[16,4096]{1,0:T(8,128)(2,1)S(1)}, u32[]{:S(2)}, u32[]{:S(2)}) collective-permute-start(bf16[16,4096]{1,0:T(8,128)(2,1)} %refs_0_.1), channel_id=1, source_target_pairs={{0,8},{4,12},{8,0},{12,4},{1,9},{5,13},{9,1},{13,5},{2,10},{6,14},... | collective-permute-start | bytes 393224 | tf_op jit(solution)/shard_map/ppermute | solution.py:257
  4.0 12.3 %collective-permute-start.1 = (bf16[16,4096]{1,0:T(8,128)(2,1)}, bf16[16,4096]{1,0:T(8,128)(2,1)S(1)}, u32[]{:S(2)}, u32[]{:S(2)}) collective-permute-start(bf16[16,4096]{1,0:T(8,128)(2,1)} %refs_0_.1), channel_id=1, source_target_pairs={{0,4},{4,0},{8,12},{12,8},{1,5},{5,1},{9,13},{13,9},{2,6},{6,2},{1... | collective-permute-start | bytes 393224 | tf_op jit(solution)/shard_map/ppermute | solution.py:257
  12.3 5.0 %collective-permute-start.2 = (bf16[16,4096]{1,0:T(8,128)(2,1)S(1)}, bf16[16,4096]{1,0:T(8,128)(2,1)S(1)}, u32[]{:S(2)}, u32[]{:S(2)}) collective-permute-start(bf16[16,4096]{1,0:T(8,128)(2,1)S(1)} %collective-permute-done.refs_1_.__), channel_id=1, source_target_pairs={{0,4},{4,0},{8,12},{12,8},{1,5},{5,1},{9,13},{13,9},{2,6},{6,2},{1... | collective-permute-start | bytes 393224 | tf_op jit(solution)/shard_map/ppermute | solution.py:257
  12.8 4.5 %copy-start.1 = (bf16[1,4096,64]{1,2,0:T(8,128)(2,1)S(1)}, bf16[1,4096,64]{1,2,0:T(8,128)(2,1)}, u32[]{:S(2)}) copy-start(bf16[1,4096,64]{1,2,0:T(8,128)(2,1)} %param.12) | copy-start | bytes 1572868
  12.8 4.5 %copy-start.2 = (bf16[16,4096]{1,0:T(8,128)(2,1)S(1)}, bf16[16,4096]{1,0:T(8,128)(2,1)}, u32[]{:S(2)}) copy-start(bf16[16,4096]{1,0:T(8,128)(2,1)} %refs_0_.1) | copy-start | bytes 393220
  12.8 4.5 %copy-start.3 = (bf16[4096]{0:T(1024)(128)(2,1)S(1)}, bf16[4096]{0:T(1024)(128)(2,1)}, u32[]{:S(2)}) copy-start(bf16[4096]{0:T(1024)(128)(2,1)} %gain_ref.1) | copy-start | bytes 24580
  17.8 4.7 %collective-permute-start.3 = (bf16[64,128]{1,0:T(8,128)(2,1)S(1)}, bf16[64,128]{1,0:T(8,128)(2,1)S(1)}, u32[]{:S(2)}, u32[]{:S(2)}) collective-permute-start(bf16[64,128]{1,0:T(8,128)(2,1)S(1)} %get-tuple-element.29), channel_id=1, source_target_pairs={{0,8},{4,12},{8,0},{12,4},{1,9},{5,13},{9,1},{13,5},{2,10},{6,14},... | collective-permute-start | bytes 49160 | tf_op jit(solution)/shard_map/ppermute | solution.py:257
  22.5 4.6 %collective-permute-start.4 = (bf16[64,128]{1,0:T(8,128)(2,1)S(1)}, bf16[64,128]{1,0:T(8,128)(2,1)S(1)}, u32[]{:S(2)}, u32[]{:S(2)}) collective-permute-start(bf16[64,128]{1,0:T(8,128)(2,1)S(1)} %add.6.refs_1_), channel_id=1, source_target_pairs={{0,4},{4,0},{8,12},{12,8},{1,5},{5,1},{9,13},{13,9},{2,6},{6,2},{1... | collective-permute-start | bytes 49160 | tf_op jit(solution)/shard_map/ppermute | solution.py:257
  25.4 1.7 %collective-permute-start.5 = (bf16[32,3072]{1,0:T(8,128)(2,1)S(1)}, bf16[32,3072]{1,0:T(8,128)(2,1)S(1)}, u32[]{:S(2)}, u32[]{:S(2)}) collective-permute-start(bf16[32,3072]{1,0:T(8,128)(2,1)S(1)} %get-tuple-element.32), channel_id=1, source_target_pairs={{0,1},{1,0},{2,3},{3,2},{4,5},{5,4},{6,7},{7,6},{8,9},{9,8},{10,11... | collective-permute-start | bytes 589832 | tf_op jit(solution)/shard_map/ppermute | solution.py:257
  25.5 7.9 %copy-start = (bf16[4,64,4096]{2,1,0:T(8,128)(2,1)S(1)}, bf16[4,64,4096]{2,1,0:T(8,128)(2,1)}, u32[]{:S(2)}) copy-start(bf16[4,64,4096]{2,1,0:T(8,128)(2,1)} %up_ref.1) | copy-start | bytes 6291460
  27.2 2.0 %collective-permute-start.7 = (bf16[32,1152]{1,0:T(8,128)(2,1)S(1)}, bf16[32,1152]{1,0:T(8,128)(2,1)S(1)}, u32[]{:S(2)}, u32[]{:S(2)}) collective-permute-start(bf16[32,1152]{1,0:T(8,128)(2,1)S(1)} %get-tuple-element.36), channel_id=1, source_target_pairs={{0,1},{1,0},{2,3},{3,2},{4,5},{5,4},{6,7},{7,6},{8,9},{9,8},{10,11... | collective-permute-start | bytes 221192 | tf_op jit(solution)/shard_map/ppermute | solution.py:257
  27.7 5.2 %collective-permute-start.6 = (bf16[16,3072]{1,0:T(8,128)(2,1)S(1)}, bf16[16,3072]{1,0:T(8,128)(2,1)S(1)}, u32[]{:S(2)}, u32[]{:S(2)}) collective-permute-start(bf16[16,3072]{1,0:T(8,128)(2,1)S(1)} %get-tuple-element.34), channel_id=1, source_target_pairs={{0,2},{2,0},{1,3},{3,1},{4,6},{6,4},{5,7},{7,5},{8,10},{10,8},{9,1... | collective-permute-start | bytes 294920 | tf_op jit(solution)/shard_map/ppermute | solution.py:257
  29.5 4.0 %collective-permute-start.8 = (bf16[16,1152]{1,0:T(8,128)(2,1)S(1)}, bf16[16,1152]{1,0:T(8,128)(2,1)S(1)}, u32[]{:S(2)}, u32[]{:S(2)}) collective-permute-start(bf16[16,1152]{1,0:T(8,128)(2,1)S(1)} %get-tuple-element.38), channel_id=1, source_target_pairs={{0,2},{2,0},{1,3},{3,1},{4,6},{6,4},{5,7},{7,5},{8,10},{10,8},{9,1... | collective-permute-start | bytes 110600 | tf_op jit(solution)/shard_map/ppermute | solution.py:257

commit v23 on v22

--- a/solution.py
+++ b/solution.py
@@ -274,7 +274,7 @@
     part = quarter // 4
     if part % LANES == 0:
         loads, late = ([quarter, quarter, part], [quarter]), quarter - part
-        firsts = [0, quarter, 3 * quarter], [2 * quarter]
+        firsts = [0, quarter, 2 * quarter], [2 * quarter + part]
     else:
         loads, late = ([quarter, quarter], [quarter, quarter]), 0
         firsts = [0, quarter], [2 * quarter, 3 * quarter]
@@ -313,8 +313,8 @@
         name="last_load",
     )(weight_hbm, factor, blocks[1])
     weights = [pltpu.with_memory_space_constraint(w, pltpu.VMEM) for w in weights]
-    if late:
-        weights[2:] = weights[:1:-1]
+    soon = 3 if late else 2
+    base_columns = sum(w.shape[1] for w in weights[:soon])
 
     x, small = pl.pallas_call(
         functools.partial(rows_kernel, order, depth * groups),
@@ -338,16 +338,16 @@
         return [jax.ShapeDtypeStruct(shape, f32 if k == 0 else bf16) for k in range(n)]
 
     base, *rest = pl.pallas_call(
-        functools.partial(base_kernel, 2, columns - late, step),
-        out_shape=[jax.ShapeDtypeStruct((rows, 2 * quarter), f32)]
+        functools.partial(base_kernel, soon, columns - late, step),
+        out_shape=[jax.ShapeDtypeStruct((rows, base_columns), f32)]
         + ([pltpu.VMEM((depth, late), query_weight.dtype)] if late else []),
-        in_specs=[HBM] + [VMEM] * 3,
+        in_specs=[HBM] + [VMEM] * (1 + soon),
         out_specs=[VMEM] * (2 if late else 1),
         scratch_shapes=[pltpu.SemaphoreType.DMA((pieces,))] if late else [],
         cost_estimate=cost(4 * rows * depth * quarter, 4 * depth * quarter),
         compiler_params=roomy,
         name="first_columns",
-    )(weight_hbm, x, *weights[:2])
+    )(weight_hbm, x, *weights[:soon])
     weights += [pltpu.with_memory_space_constraint(w, pltpu.VMEM) for w in rest]
 
     def product(some, bases, times, name):
@@ -365,9 +365,9 @@
         )(x, *bases, *some)
         return spread_out(made, "gz", n_z)
 
-    split = 3
+    split = soon + 1
     last_columns = sum(w.shape[1] for w in weights[split:])
-    base_parts = product(weights[2:split], [base, crossed], 4, "middle_columns")
+    base_parts = product(weights[soon:split], [base, crossed], 4, "middle_columns")
     last = pl.pallas_call(
         functools.partial(last_kernel, len(weights) - split, step),
         out_shape=jax.ShapeDtypeStruct((rows, last_columns), f32),
@@ -402,7 +402,7 @@
     last_parts = spread_out(made, "gy", n_y)
 
     return pl.pallas_call(
-        functools.partial(final_kernel, n_y, n_z, min(512, columns // 4)),
+        functools.partial(final_kernel, n_y, n_z, min(256, columns // 4)),
         out_shape=jax.ShapeDtypeStruct((rows_here, columns), bf16),
         in_specs=[VMEM] * (2 + 2 * n_y),
         out_specs=VMEM,

time: 34.7 us -> 35.6 us (1.026)
  waiting for transfers between devices: 4.51 us -> 5.8 us
  starting transfers between devices: 11.5 us -> 11.1 us
    ppermute x9, waiting for transfers between devices: 4.51 us -> 5.8 us  [send(): return lax.ppermute(value, axis, [(j, j ^ k) for j in range(n)])]
    ppermute x9, starting transfers between devices: 11.5 us -> 11.1 us  [send(): return lax.ppermute(value, axis, [(j, j ^ k) for j in range(n)])]
    pallas_call x2, Pallas kernels: 4.21 us -> 4.62 us  [the longest x1 3.53 us: body(): pl.pallas_call(functools.partial(base_kernel, soon, columns - late, step)...]
    pallas_call x1, Pallas kernels: 1.56 us -> 1.19 us  [body(): pl.pallas_call(functools.partial(last_kernel, len(weights) - split, step)...]
  transfers between devices with their start and end apart: 9 -> 9, of which waited for: 4 -> 5; matrix products, arithmetic and copies ran while one was open for 0% -> 0% of each run, Pallas kernels for 49% -> 47%
where the time goes in v23:
time: 35.6 us; the launch traced here: 35.4 us
  Pallas kernels  18.4 us (52%)
  starting transfers between devices  11.1 us (31%)
  waiting for transfers between devices  5.8 us (16%)
    ppermute x9, starting transfers between devices, send(): return lax.ppermute(value, axis, [(j, j ^ k) for j in range(n)])  11.1 us
    pallas_call x1, Pallas kernels, body(): pl.pallas_call(functools.partial(first_load_kernel, len(loads[0]), firsts...  6.66 us
    ppermute x9, waiting for transfers between devices, send(): return lax.ppermute(value, axis, [(j, j ^ k) for j in range(n)])  5.8 us
    pallas_call x1, Pallas kernels, body(): pl.pallas_call(functools.partial(last_load_kernel, len(loads[1]), firsts[...  3.56 us
    pallas_call x1, Pallas kernels, body(): pl.pallas_call(functools.partial(base_kernel, soon, columns - late, step)...  3.53 us
    pallas_call x1, Pallas kernels, product(): pl.pallas_call(functools.partial(product_kernel, len(some), n_y, n_z, ste...  1.64 us
    pallas_call x1, Pallas kernels, body(): pl.pallas_call(functools.partial(last_kernel, len(weights) - split, step)...  1.19 us
    pallas_call x1, Pallas kernels, body(): pl.pallas_call(functools.partial(final_kernel, n_y, n_z, min(256, columns...  1.09 us
  transfers between devices with their start and end apart: 9, of which 5 were waited for; matrix products, arithmetic and copies ran while one was open for 0% of the time, Pallas kernels for 47%

profile of v23, /device:TPU:0, one launch (start us, length us, event | category | flops | bytes accessed | tf_op | source)
XLA Modules:
  0.0 35.4 jit_solution(1890291129998412788)
XLA Ops:
  0.0 4.0 %collective-permute-start = (bf16[16,4096]{1,0:T(8,128)(2,1)}, bf16[16,4096]{1,0:T(8,128)(2,1)S(1)}, u32[]{:S(2)}, u32[]{:S(2)}) collective-permute-start(bf16[16,4096]{1,0:T(8,128)(2,1)} %refs_0_.1), channel_id=1, source_target_pairs={{0,8},{4,12},{8,0},{12,4},{1,9},{5,13},{9,1},{13,5},{2,10},{6,14},... | collective-permute-start | bytes 393224 | tf_op jit(solution)/shard_map/ppermute | solution.py:257
  4.0 1.6 %collective-permute-start.1 = (bf16[16,4096]{1,0:T(8,128)(2,1)}, bf16[16,4096]{1,0:T(8,128)(2,1)S(1)}, u32[]{:S(2)}, u32[]{:S(2)}) collective-permute-start(bf16[16,4096]{1,0:T(8,128)(2,1)} %refs_0_.1), channel_id=1, source_target_pairs={{0,4},{4,0},{8,12},{12,8},{1,5},{5,1},{9,13},{13,9},{2,6},{6,2},{1... | collective-permute-start | bytes 393224 | tf_op jit(solution)/shard_map/ppermute | solution.py:257
  5.6 6.7 %first_load.1 = (f32[1,64,64]{2,1,0:T(8,128)S(1)}, f32[64,256]{1,0:T(8,128)S(1)}, bf16[4096,1024]{1,0:T(8,128)(2,1)S(1)}, bf16[4096,1024]{1,0:T(8,128)(2,1)S(1)}, bf16[4096,256]{1,0:T(8,128)(2,1)S(1)}) custom-call(bf16[4096,4096]{1,0:T(8,128)(2,1)} %w_hbm.5, s32[4]{0:T(128)} %rank_hbm.1, s32[4]{0:T(128)} %slot_hbm.1, s32[5]{0:T(128)} %start_hbm.1), custom_call_target="tpu_custom_call" | custom-call | flops 5033164800 | bytes 16777216 | tf_op jit(solution)/shard_map/first_load/pallas_call | solution.py:287
  12.3 0.5 %collective-permute-start.2 = (bf16[16,4096]{1,0:T(8,128)(2,1)S(1)}, bf16[16,4096]{1,0:T(8,128)(2,1)S(1)}, u32[]{:S(2)}, u32[]{:S(2)}) collective-permute-start(bf16[16,4096]{1,0:T(8,128)(2,1)S(1)} %collective-permute-done.refs_1_.__), channel_id=1, source_target_pairs={{0,4},{4,0},{8,12},{12,8},{1,5},{5,1},{9,13},{13,9},{2,6},{6,2},{1... | collective-permute-start | bytes 393224 | tf_op jit(solution)/shard_map/ppermute | solution.py:257
  12.8 3.6 %last_load.1.refs_2_ = bf16[4096,1024]{1,0:T(8,128)(2,1)S(1)} custom-call(bf16[4096,4096]{1,0:T(8,128)(2,1)} %w_hbm.5, f32[1,64,64]{2,1,0:T(8,128)S(1)} %get-tuple-element.23.factor_ref._, bf16[16,4096]{1,0:T(8,128)(2,1)S(1)} %collective-permute-done.refs_1_.__), custom_call_target="tpu_custom_call" | custom-call | flops 5033164800 | bytes 16777216 | tf_op jit(solution)/shard_map/last_load/pallas_call | solution.py:305
  16.4 0.9 %collective-permute-done.2.refs_3_ = bf16[16,4096]{1,0:T(8,128)(2,1)S(1)} collective-permute-done((bf16[16,4096]{1,0:T(8,128)(2,1)S(1)}, bf16[16,4096]{1,0:T(8,128)(2,1)S(1)}, u32[]{:S(2)}, u32[]{:S(2)}) %collective-permute-start.2) | collective-permute-done | bytes 131104 | tf_op jit(solution)/shard_map/ppermute | solution.py:257
  17.3 0.4 %scaled_rows.1 = (bf16[64,4096]{1,0:T(8,128)(2,1)S(1)}, bf16[64,128]{1,0:T(8,128)(2,1)S(1)}) custom-call(bf16[4096]{0:T(1024)(128)(2,1)S(1)} %copy-done.3, bf16[1,64,4096]{2,1,0:T(8,128)(2,1)S(1)} %bitcast.1, f32[1,64,64]{2,1,0:T(8,128)S(1)} %get-tuple-element.23.factor_ref._, bf16[16,4096]{1,0:T(8,128)(2,1)S(1)} %copy-done.2, ...), custom_call_target="tpu_custom_call" | custom-call | tf_op jit(solution)/shard_map/scaled_rows/pallas_call | solution.py:319
  17.8 1.1 %collective-permute-start.3 = (bf16[64,128]{1,0:T(8,128)(2,1)S(1)}, bf16[64,128]{1,0:T(8,128)(2,1)S(1)}, u32[]{:S(2)}, u32[]{:S(2)}) collective-permute-start(bf16[64,128]{1,0:T(8,128)(2,1)S(1)} %get-tuple-element.29), channel_id=1, source_target_pairs={{0,8},{4,12},{8,0},{12,4},{1,9},{5,13},{9,1},{13,5},{2,10},{6,14},... | collective-permute-start | bytes 49160 | tf_op jit(solution)/shard_map/ppermute | solution.py:257
  18.8 3.5 %first_columns.1 = (f32[64,2304]{1,0:T(8,128)S(1)}, bf16[4096,768]{1,0:T(8,128)(2,1)S(1)}) custom-call(bf16[4096,4096]{1,0:T(8,128)(2,1)} %w_hbm.5, bf16[64,4096]{1,0:T(8,128)(2,1)S(1)} %get-tuple-element.24.x_ref, bf16[4096,1024]{1,0:T(8,128)(2,1)S(1)} %get-tuple-element.25.refs_0_, bf16[4096,1024]{1,0:T(8,128)(2,1)S(1)} %get-tuple-element.26.refs_1_, ...), custom_call_target="tpu_custom_call" | custom-call | flops 1073741824 | bytes 16777216 | tf_op jit(solution)/shard_map/first_columns/pallas_call | solution.py:340
  22.4 0.1 collective-permute-done.3
  22.5 1.7 %collective-permute-start.4 = (bf16[64,128]{1,0:T(8,128)(2,1)S(1)}, bf16[64,128]{1,0:T(8,128)(2,1)S(1)}, u32[]{:S(2)}, u32[]{:S(2)}) collective-permute-start(bf16[64,128]{1,0:T(8,128)(2,1)S(1)} %add.6.refs_1_), channel_id=1, source_target_pairs={{0,4},{4,0},{8,12},{12,8},{1,5},{5,1},{9,13},{13,9},{2,6},{6,2},{1... | collective-permute-start | bytes 49160 | tf_op jit(solution)/shard_map/ppermute | solution.py:257
  24.2 1.6 %middle_columns.1 = (f32[32,3328]{1,0:T(8,128)S(1)}, bf16[32,3328]{1,0:T(8,128)(2,1)S(1)}) custom-call(bf16[64,4096]{1,0:T(8,128)(2,1)S(1)} %get-tuple-element.24.x_ref, f32[64,2304]{1,0:T(8,128)S(1)} %get-tuple-element.30.refs_0_, bf16[64,128]{1,0:T(8,128)(2,1)S(1)} %add.6.refs_1_, bf16[4096,1024]{1,0:T(8,128)(2,1)S(1)} %last_load.1.refs_2_), custom_call_target="tpu_custom_call" | custom-call | flops 6979321856 | bytes 27262976 | tf_op jit(solution)/shard_map/middle_columns/pallas_call | solution.py:356
  25.9 0.1 collective-permute-start.5
  25.9 0.0 copy-start
  26.0 1.2 %last_columns.1.last_ref = f32[64,768]{1,0:T(8,128)S(1)} custom-call(bf16[64,4096]{1,0:T(8,128)(2,1)S(1)} %get-tuple-element.24.x_ref, bf16[4096,768]{1,0:T(8,128)(2,1)S(1)} %get-tuple-element.28.refs_0_), custom_call_target="tpu_custom_call" | custom-call | flops 4294967296 | bytes 8388608 | tf_op jit(solution)/shard_map/last_columns/pallas_call | solution.py:371
  27.2 0.2 collective-permute-done.5.refs_1_
  27.4 0.1 first_sums.1
  27.5 1.5 %collective-permute-start.6 = (bf16[16,3328]{1,0:T(8,128)(2,1)S(1)}, bf16[16,3328]{1,0:T(8,128)(2,1)S(1)}, u32[]{:S(2)}, u32[]{:S(2)}) collective-permute-start(bf16[16,3328]{1,0:T(8,128)(2,1)S(1)} %get-tuple-element.34), channel_id=1, source_target_pairs={{0,2},{2,0},{1,3},{3,1},{4,6},{6,4},{5,7},{7,5},{8,10},{10,8},{9,1... | collective-permute-start | bytes 319496 | tf_op jit(solution)/shard_map/ppermute | solution.py:257
  29.0 0.0 collective-permute-start.7
  29.0 1.2 %collective-permute-done.7.refs_1_ = bf16[32,896]{1,0:T(8,128)(2,1)S(1)} collective-permute-done((bf16[32,896]{1,0:T(8,128)(2,1)S(1)}, bf16[32,896]{1,0:T(8,128)(2,1)S(1)}, u32[]{:S(2)}, u32[]{:S(2)}) %collective-permute-start.7) | collective-permute-done | bytes 57376 | tf_op jit(solution)/shard_map/ppermute | solution.py:257
  30.2 0.2 last_sums.1
  30.5 0.6 %collective-permute-start.8 = (bf16[16,896]{1,0:T(8,128)(2,1)S(1)}, bf16[16,896]{1,0:T(8,128)(2,1)S(1)}, u32[]{:S(2)}, u32[]{:S(2)}) collective-permute-start(bf16[16,896]{1,0:T(8,128)(2,1)S(1)} %get-tuple-element.38), channel_id=1, source_target_pairs={{0,2},{2,0},{1,3},{3,1},{4,6},{6,4},{5,7},{7,5},{8,10},{10,8},{9,1... | collective-permute-start | bytes 86024 | tf_op jit(solution)/shard_map/ppermute | solution.py:257
  31.0 3.3 %collective-permute-done.8.refs_3_ = bf16[16,896]{1,0:T(8,128)(2,1)S(1)} collective-permute-done((bf16[16,896]{1,0:T(8,128)(2,1)S(1)}, bf16[16,896]{1,0:T(8,128)(2,1)S(1)}, u32[]{:S(2)}, u32[]{:S(2)}) %collective-permute-start.8) | collective-permute-done | bytes 28704 | tf_op jit(solution)/shard_map/ppermute | solution.py:257
  34.4 1.1 %query_rows.1 = bf16[16,4096]{1,0:T(8,128)(2,1)} custom-call(f32[64,256]{1,0:T(8,128)S(1)} %get-tuple-element.22.spread_ref, bf16[4,64,4096]{2,1,0:T(8,128)(2,1)S(1)} %copy-done, f32[16,3328]{1,0:T(8,128)S(1)} %get-tuple-element.33.refs_0_, bf16[16,3328]{1,0:T(8,128)(2,1)S(1)} %collective-permute-done.6.refs_1_, f32[16,896]{1,0:T(8,128)S(1)} %get-tuple-element.37.refs_2_, ...), custom_call_target="tpu_custom_call" | custom-call | tf_op jit(solution)/shard_map/query_rows/pallas_call | solution.py:404
  (13 shorter events, 0.0 us)
Async XLA Ops:
  0.0 12.3 %collective-permute-start = (bf16[16,4096]{1,0:T(8,128)(2,1)}, bf16[16,4096]{1,0:T(8,128)(2,1)S(1)}, u32[]{:S(2)}, u32[]{:S(2)}) collective-permute-start(bf16[16,4096]{1,0:T(8,128)(2,1)} %refs_0_.1), channel_id=1, source_target_pairs={{0,8},{4,12},{8,0},{12,4},{1,9},{5,13},{9,1},{13,5},{2,10},{6,14},... | collective-permute-start | bytes 393224 | tf_op jit(solution)/shard_map/ppermute | solution.py:257
  4.0 12.3 %collective-permute-start.1 = (bf16[16,4096]{1,0:T(8,128)(2,1)}, bf16[16,4096]{1,0:T(8,128)(2,1)S(1)}, u32[]{:S(2)}, u32[]{:S(2)}) collective-permute-start(bf16[16,4096]{1,0:T(8,128)(2,1)} %refs_0_.1), channel_id=1, source_target_pairs={{0,4},{4,0},{8,12},{12,8},{1,5},{5,1},{9,13},{13,9},{2,6},{6,2},{1... | collective-permute-start | bytes 393224 | tf_op jit(solution)/shard_map/ppermute | solution.py:257
  12.3 5.0 %collective-permute-start.2 = (bf16[16,4096]{1,0:T(8,128)(2,1)S(1)}, bf16[16,4096]{1,0:T(8,128)(2,1)S(1)}, u32[]{:S(2)}, u32[]{:S(2)}) collective-permute-start(bf16[16,4096]{1,0:T(8,128)(2,1)S(1)} %collective-permute-done.refs_1_.__), channel_id=1, source_target_pairs={{0,4},{4,0},{8,12},{12,8},{1,5},{5,1},{9,13},{13,9},{2,6},{6,2},{1... | collective-permute-start | bytes 393224 | tf_op jit(solution)/shard_map/ppermute | solution.py:257
  12.8 4.5 %copy-start.1 = (bf16[1,4096,64]{1,2,0:T(8,128)(2,1)S(1)}, bf16[1,4096,64]{1,2,0:T(8,128)(2,1)}, u32[]{:S(2)}) copy-start(bf16[1,4096,64]{1,2,0:T(8,128)(2,1)} %param.12) | copy-start | bytes 1572868
  12.8 4.5 %copy-start.2 = (bf16[16,4096]{1,0:T(8,128)(2,1)S(1)}, bf16[16,4096]{1,0:T(8,128)(2,1)}, u32[]{:S(2)}) copy-start(bf16[16,4096]{1,0:T(8,128)(2,1)} %refs_0_.1) | copy-start | bytes 393220
  12.8 4.5 %copy-start.3 = (bf16[4096]{0:T(1024)(128)(2,1)S(1)}, bf16[4096]{0:T(1024)(128)(2,1)}, u32[]{:S(2)}) copy-start(bf16[4096]{0:T(1024)(128)(2,1)} %gain_ref.1) | copy-start | bytes 24580
  17.8 4.7 %collective-permute-start.3 = (bf16[64,128]{1,0:T(8,128)(2,1)S(1)}, bf16[64,128]{1,0:T(8,128)(2,1)S(1)}, u32[]{:S(2)}, u32[]{:S(2)}) collective-permute-start(bf16[64,128]{1,0:T(8,128)(2,1)S(1)} %get-tuple-element.29), channel_id=1, source_target_pairs={{0,8},{4,12},{8,0},{12,4},{1,9},{5,13},{9,1},{13,5},{2,10},{6,14},... | collective-permute-start | bytes 49160 | tf_op jit(solution)/shard_map/ppermute | solution.py:257
  22.5 4.7 %collective-permute-start.4 = (bf16[64,128]{1,0:T(8,128)(2,1)S(1)}, bf16[64,128]{1,0:T(8,128)(2,1)S(1)}, u32[]{:S(2)}, u32[]{:S(2)}) collective-permute-start(bf16[64,128]{1,0:T(8,128)(2,1)S(1)} %add.6.refs_1_), channel_id=1, source_target_pairs={{0,4},{4,0},{8,12},{12,8},{1,5},{5,1},{9,13},{13,9},{2,6},{6,2},{1... | collective-permute-start | bytes 49160 | tf_op jit(solution)/shard_map/ppermute | solution.py:257
  25.9 1.5 %collective-permute-start.5 = (bf16[32,3328]{1,0:T(8,128)(2,1)S(1)}, bf16[32,3328]{1,0:T(8,128)(2,1)S(1)}, u32[]{:S(2)}, u32[]{:S(2)}) collective-permute-start(bf16[32,3328]{1,0:T(8,128)(2,1)S(1)} %get-tuple-element.32), channel_id=1, source_target_pairs={{0,1},{1,0},{2,3},{3,2},{4,5},{5,4},{6,7},{7,6},{8,9},{9,8},{10,11... | collective-permute-start | bytes 638984 | tf_op jit(solution)/shard_map/ppermute | solution.py:257
  25.9 8.4 %copy-start = (bf16[4,64,4096]{2,1,0:T(8,128)(2,1)S(1)}, bf16[4,64,4096]{2,1,0:T(8,128)(2,1)}, u32[]{:S(2)}) copy-start(bf16[4,64,4096]{2,1,0:T(8,128)(2,1)} %up_ref.1) | copy-start | bytes 6291460
  27.5 6.9 %collective-permute-start.6 = (bf16[16,3328]{1,0:T(8,128)(2,1)S(1)}, bf16[16,3328]{1,0:T(8,128)(2,1)S(1)}, u32[]{:S(2)}, u32[]{:S(2)}) collective-permute-start(bf16[16,3328]{1,0:T(8,128)(2,1)S(1)} %get-tuple-element.34), channel_id=1, source_target_pairs={{0,2},{2,0},{1,3},{3,1},{4,6},{6,4},{5,7},{7,5},{8,10},{10,8},{9,1... | collective-permute-start | bytes 319496 | tf_op jit(solution)/shard_map/ppermute | solution.py:257
  29.0 1.2 %collective-permute-start.7 = (bf16[32,896]{1,0:T(8,128)(2,1)S(1)}, bf16[32,896]{1,0:T(8,128)(2,1)S(1)}, u32[]{:S(2)}, u32[]{:S(2)}) collective-permute-start(bf16[32,896]{1,0:T(8,128)(2,1)S(1)} %get-tuple-element.36), channel_id=1, source_target_pairs={{0,1},{1,0},{2,3},{3,2},{4,5},{5,4},{6,7},{7,6},{8,9},{9,8},{10,11... | collective-permute-start | bytes 172040 | tf_op jit(solution)/shard_map/ppermute | solution.py:257
  30.5 3.9 %collective-permute-start.8 = (bf16[16,896]{1,0:T(8,128)(2,1)S(1)}, bf16[16,896]{1,0:T(8,128)(2,1)S(1)}, u32[]{:S(2)}, u32[]{:S(2)}) collective-permute-start(bf16[16,896]{1,0:T(8,128)(2,1)S(1)} %get-tuple-element.38), channel_id=1, source_target_pairs={{0,2},{2,0},{1,3},{3,1},{4,6},{6,4},{5,7},{7,5},{8,10},{10,8},{9,1... | collective-permute-start | bytes 86024 | tf_op jit(solution)/shard_map/ppermute | solution.py:257

commit v24 on v23

--- a/solution.py
+++ b/solution.py
@@ -395,7 +395,7 @@
         out_shape=shapes(n_y, (rows_here, last_columns + LANES)),
         in_specs=[VMEM] * n_z,
         out_specs=[VMEM] * n_y,
-        cost_estimate=cost(0, 0),
+        cost_estimate=cost(4 * rows * depth * quarter, 0),
         compiler_params=roomy,
         name="last_sums",
     )(*lasts)

time: 35.6 us -> 34.8 us (0.978)
  waiting for transfers between devices: 5.8 us -> 4.3 us
  starting transfers between devices: 11.1 us -> 11.8 us
    ppermute x9, waiting for transfers between devices: 5.8 us -> 4.3 us  [send(): return lax.ppermute(value, axis, [(j, j ^ k) for j in range(n)])]
    ppermute x9, starting transfers between devices: 11.1 us -> 11.8 us  [send(): return lax.ppermute(value, axis, [(j, j ^ k) for j in range(n)])]
  transfers between devices with their start and end apart: 9 -> 9, of which waited for: 5 -> 4; matrix products, arithmetic and copies ran while one was open for 0% -> 0% of each run, Pallas kernels for 47% -> 49%
where the time goes in v24:
time: 34.8 us; the launch traced here: 34.6 us
  Pallas kernels  18.4 us (53%)
  starting transfers between devices  11.8 us (34%)
  waiting for transfers between devices  4.3 us (12%)
    ppermute x9, starting transfers between devices, send(): return lax.ppermute(value, axis, [(j, j ^ k) for j in range(n)])  11.8 us
    pallas_call x1, Pallas kernels, body(): pl.pallas_call(functools.partial(first_load_kernel, len(loads[0]), firsts...  6.66 us
    ppermute x9, waiting for transfers between devices, send(): return lax.ppermute(value, axis, [(j, j ^ k) for j in range(n)])  4.3 us
    pallas_call x1, Pallas kernels, body(): pl.pallas_call(functools.partial(last_load_kernel, len(loads[1]), firsts[...  3.56 us
    pallas_call x1, Pallas kernels, body(): pl.pallas_call(functools.partial(base_kernel, soon, columns - late, step)...  3.53 us
    pallas_call x1, Pallas kernels, product(): pl.pallas_call(functools.partial(product_kernel, len(some), n_y, n_z, ste...  1.64 us
    pallas_call x1, Pallas kernels, body(): pl.pallas_call(functools.partial(last_kernel, len(weights) - split, step)...  1.19 us
    pallas_call x1, Pallas kernels, body(): pl.pallas_call(functools.partial(final_kernel, n_y, n_z, min(256, columns...  1.09 us
  transfers between devices with their start and end apart: 9, of which 4 were waited for; matrix products, arithmetic and copies ran while one was open for 0% of the time, Pallas kernels for 49%

profile of v24, /device:TPU:0, one launch (start us, length us, event | category | flops | bytes accessed | tf_op | source)
XLA Modules:
  0.0 34.6 jit_solution(1222194223600939350)
XLA Ops:
  0.0 4.0 %collective-permute-start = (bf16[16,4096]{1,0:T(8,128)(2,1)}, bf16[16,4096]{1,0:T(8,128)(2,1)S(1)}, u32[]{:S(2)}, u32[]{:S(2)}) collective-permute-start(bf16[16,4096]{1,0:T(8,128)(2,1)} %refs_0_.1), channel_id=1, source_target_pairs={{0,8},{4,12},{8,0},{12,4},{1,9},{5,13},{9,1},{13,5},{2,10},{6,14},... | collective-permute-start | bytes 393224 | tf_op jit(solution)/shard_map/ppermute | solution.py:257
  4.0 1.6 %collective-permute-start.1 = (bf16[16,4096]{1,0:T(8,128)(2,1)}, bf16[16,4096]{1,0:T(8,128)(2,1)S(1)}, u32[]{:S(2)}, u32[]{:S(2)}) collective-permute-start(bf16[16,4096]{1,0:T(8,128)(2,1)} %refs_0_.1), channel_id=1, source_target_pairs={{0,4},{4,0},{8,12},{12,8},{1,5},{5,1},{9,13},{13,9},{2,6},{6,2},{1... | collective-permute-start | bytes 393224 | tf_op jit(solution)/shard_map/ppermute | solution.py:257
  5.6 6.7 %first_load.1 = (f32[1,64,64]{2,1,0:T(8,128)S(1)}, f32[64,256]{1,0:T(8,128)S(1)}, bf16[4096,1024]{1,0:T(8,128)(2,1)S(1)}, bf16[4096,1024]{1,0:T(8,128)(2,1)S(1)}, bf16[4096,256]{1,0:T(8,128)(2,1)S(1)}) custom-call(bf16[4096,4096]{1,0:T(8,128)(2,1)} %w_hbm.5, s32[4]{0:T(128)} %rank_hbm.1, s32[4]{0:T(128)} %slot_hbm.1, s32[5]{0:T(128)} %start_hbm.1), custom_call_target="tpu_custom_call" | custom-call | flops 5033164800 | bytes 16777216 | tf_op jit(solution)/shard_map/first_load/pallas_call | solution.py:287
  12.3 0.0 collective-permute-done.refs_1_.__
  12.3 0.5 %collective-permute-start.2 = (bf16[16,4096]{1,0:T(8,128)(2,1)S(1)}, bf16[16,4096]{1,0:T(8,128)(2,1)S(1)}, u32[]{:S(2)}, u32[]{:S(2)}) collective-permute-start(bf16[16,4096]{1,0:T(8,128)(2,1)S(1)} %collective-permute-done.refs_1_.__), channel_id=1, source_target_pairs={{0,4},{4,0},{8,12},{12,8},{1,5},{5,1},{9,13},{13,9},{2,6},{6,2},{1... | collective-permute-start | bytes 393224 | tf_op jit(solution)/shard_map/ppermute | solution.py:257
  12.8 3.6 %last_load.1.refs_2_ = bf16[4096,1024]{1,0:T(8,128)(2,1)S(1)} custom-call(bf16[4096,4096]{1,0:T(8,128)(2,1)} %w_hbm.5, f32[1,64,64]{2,1,0:T(8,128)S(1)} %get-tuple-element.23.factor_ref._, bf16[16,4096]{1,0:T(8,128)(2,1)S(1)} %collective-permute-done.refs_1_.__), custom_call_target="tpu_custom_call" | custom-call | flops 5033164800 | bytes 16777216 | tf_op jit(solution)/shard_map/last_load/pallas_call | solution.py:305
  16.4 0.9 %collective-permute-done.2.refs_3_ = bf16[16,4096]{1,0:T(8,128)(2,1)S(1)} collective-permute-done((bf16[16,4096]{1,0:T(8,128)(2,1)S(1)}, bf16[16,4096]{1,0:T(8,128)(2,1)S(1)}, u32[]{:S(2)}, u32[]{:S(2)}) %collective-permute-start.2) | collective-permute-done | bytes 131104 | tf_op jit(solution)/shard_map/ppermute | solution.py:257
  17.3 0.4 %scaled_rows.1 = (bf16[64,4096]{1,0:T(8,128)(2,1)S(1)}, bf16[64,128]{1,0:T(8,128)(2,1)S(1)}) custom-call(bf16[4096]{0:T(1024)(128)(2,1)S(1)} %copy-done.3, bf16[1,64,4096]{2,1,0:T(8,128)(2,1)S(1)} %bitcast.1, f32[1,64,64]{2,1,0:T(8,128)S(1)} %get-tuple-element.23.factor_ref._, bf16[16,4096]{1,0:T(8,128)(2,1)S(1)} %copy-done.2, ...), custom_call_target="tpu_custom_call" | custom-call | tf_op jit(solution)/shard_map/scaled_rows/pallas_call | solution.py:319
  17.8 1.1 %collective-permute-start.3 = (bf16[64,128]{1,0:T(8,128)(2,1)S(1)}, bf16[64,128]{1,0:T(8,128)(2,1)S(1)}, u32[]{:S(2)}, u32[]{:S(2)}) collective-permute-start(bf16[64,128]{1,0:T(8,128)(2,1)S(1)} %get-tuple-element.29), channel_id=1, source_target_pairs={{0,8},{4,12},{8,0},{12,4},{1,9},{5,13},{9,1},{13,5},{2,10},{6,14},... | collective-permute-start | bytes 49160 | tf_op jit(solution)/shard_map/ppermute | solution.py:257
  18.8 3.5 %first_columns.1 = (f32[64,2304]{1,0:T(8,128)S(1)}, bf16[4096,768]{1,0:T(8,128)(2,1)S(1)}) custom-call(bf16[4096,4096]{1,0:T(8,128)(2,1)} %w_hbm.5, bf16[64,4096]{1,0:T(8,128)(2,1)S(1)} %get-tuple-element.24.x_ref, bf16[4096,1024]{1,0:T(8,128)(2,1)S(1)} %get-tuple-element.25.refs_0_, bf16[4096,1024]{1,0:T(8,128)(2,1)S(1)} %get-tuple-element.26.refs_1_, ...), custom_call_target="tpu_custom_call" | custom-call | flops 1073741824 | bytes 16777216 | tf_op jit(solution)/shard_map/first_columns/pallas_call | solution.py:340
  22.4 0.1 collective-permute-done.3
  22.5 1.7 %collective-permute-start.4 = (bf16[64,128]{1,0:T(8,128)(2,1)S(1)}, bf16[64,128]{1,0:T(8,128)(2,1)S(1)}, u32[]{:S(2)}, u32[]{:S(2)}) collective-permute-start(bf16[64,128]{1,0:T(8,128)(2,1)S(1)} %add.6.refs_1_), channel_id=1, source_target_pairs={{0,4},{4,0},{8,12},{12,8},{1,5},{5,1},{9,13},{13,9},{2,6},{6,2},{1... | collective-permute-start | bytes 49160 | tf_op jit(solution)/shard_map/ppermute | solution.py:257
  24.2 1.6 %middle_columns.1 = (f32[32,3328]{1,0:T(8,128)S(1)}, bf16[32,3328]{1,0:T(8,128)(2,1)S(1)}) custom-call(bf16[64,4096]{1,0:T(8,128)(2,1)S(1)} %get-tuple-element.24.x_ref, f32[64,2304]{1,0:T(8,128)S(1)} %get-tuple-element.30.refs_0_, bf16[64,128]{1,0:T(8,128)(2,1)S(1)} %add.6.refs_1_, bf16[4096,1024]{1,0:T(8,128)(2,1)S(1)} %last_load.1.refs_2_), custom_call_target="tpu_custom_call" | custom-call | flops 6979321856 | bytes 27262976 | tf_op jit(solution)/shard_map/middle_columns/pallas_call | solution.py:356
  25.9 0.1 collective-permute-start.5
  25.9 0.0 copy-start
  26.0 1.2 %last_columns.1.last_ref = f32[64,768]{1,0:T(8,128)S(1)} custom-call(bf16[64,4096]{1,0:T(8,128)(2,1)S(1)} %get-tuple-element.24.x_ref, bf16[4096,768]{1,0:T(8,128)(2,1)S(1)} %get-tuple-element.28.refs_0_), custom_call_target="tpu_custom_call" | custom-call | flops 4294967296 | bytes 8388608 | tf_op jit(solution)/shard_map/last_columns/pallas_call | solution.py:371
  27.2 0.2 collective-permute-done.5.refs_1_
  27.4 0.1 first_sums.1
  27.5 0.4 %collective-permute-start.7 = (bf16[32,896]{1,0:T(8,128)(2,1)S(1)}, bf16[32,896]{1,0:T(8,128)(2,1)S(1)}, u32[]{:S(2)}, u32[]{:S(2)}) collective-permute-start(bf16[32,896]{1,0:T(8,128)(2,1)S(1)} %get-tuple-element.36), channel_id=1, source_target_pairs={{0,1},{1,0},{2,3},{3,2},{4,5},{5,4},{6,7},{7,6},{8,9},{9,8},{10,11... | collective-permute-start | bytes 172040 | tf_op jit(solution)/shard_map/ppermute | solution.py:257
  27.8 1.5 %collective-permute-start.6 = (bf16[16,3328]{1,0:T(8,128)(2,1)S(1)}, bf16[16,3328]{1,0:T(8,128)(2,1)S(1)}, u32[]{:S(2)}, u32[]{:S(2)}) collective-permute-start(bf16[16,3328]{1,0:T(8,128)(2,1)S(1)} %get-tuple-element.34), channel_id=1, source_target_pairs={{0,2},{2,0},{1,3},{3,1},{4,6},{6,4},{5,7},{7,5},{8,10},{10,8},{9,1... | collective-permute-start | bytes 319496 | tf_op jit(solution)/shard_map/ppermute | solution.py:257
  29.3 0.2 last_sums.1
  29.5 1.0 %collective-permute-start.8 = (bf16[16,896]{1,0:T(8,128)(2,1)S(1)}, bf16[16,896]{1,0:T(8,128)(2,1)S(1)}, u32[]{:S(2)}, u32[]{:S(2)}) collective-permute-start(bf16[16,896]{1,0:T(8,128)(2,1)S(1)} %get-tuple-element.38), channel_id=1, source_target_pairs={{0,2},{2,0},{1,3},{3,1},{4,6},{6,4},{5,7},{7,5},{8,10},{10,8},{9,1... | collective-permute-start | bytes 86024 | tf_op jit(solution)/shard_map/ppermute | solution.py:257
  30.5 3.0 %collective-permute-done.8.refs_3_ = bf16[16,896]{1,0:T(8,128)(2,1)S(1)} collective-permute-done((bf16[16,896]{1,0:T(8,128)(2,1)S(1)}, bf16[16,896]{1,0:T(8,128)(2,1)S(1)}, u32[]{:S(2)}, u32[]{:S(2)}) %collective-permute-start.8) | collective-permute-done | bytes 28704 | tf_op jit(solution)/shard_map/ppermute | solution.py:257
  33.5 1.1 %query_rows.1 = bf16[16,4096]{1,0:T(8,128)(2,1)} custom-call(f32[64,256]{1,0:T(8,128)S(1)} %get-tuple-element.22.spread_ref, bf16[4,64,4096]{2,1,0:T(8,128)(2,1)S(1)} %copy-done, f32[16,3328]{1,0:T(8,128)S(1)} %get-tuple-element.33.refs_0_, bf16[16,3328]{1,0:T(8,128)(2,1)S(1)} %collective-permute-done.6.refs_1_, f32[16,896]{1,0:T(8,128)S(1)} %get-tuple-element.37.refs_2_, ...), custom_call_target="tpu_custom_call" | custom-call | tf_op jit(solution)/shard_map/query_rows/pallas_call | solution.py:404
  (13 shorter events, 0.0 us)
Async XLA Ops:
  0.0 12.3 %collective-permute-start = (bf16[16,4096]{1,0:T(8,128)(2,1)}, bf16[16,4096]{1,0:T(8,128)(2,1)S(1)}, u32[]{:S(2)}, u32[]{:S(2)}) collective-permute-start(bf16[16,4096]{1,0:T(8,128)(2,1)} %refs_0_.1), channel_id=1, source_target_pairs={{0,8},{4,12},{8,0},{12,4},{1,9},{5,13},{9,1},{13,5},{2,10},{6,14},... | collective-permute-start | bytes 393224 | tf_op jit(solution)/shard_map/ppermute | solution.py:257
  4.0 12.3 %collective-permute-start.1 = (bf16[16,4096]{1,0:T(8,128)(2,1)}, bf16[16,4096]{1,0:T(8,128)(2,1)S(1)}, u32[]{:S(2)}, u32[]{:S(2)}) collective-permute-start(bf16[16,4096]{1,0:T(8,128)(2,1)} %refs_0_.1), channel_id=1, source_target_pairs={{0,4},{4,0},{8,12},{12,8},{1,5},{5,1},{9,13},{13,9},{2,6},{6,2},{1... | collective-permute-start | bytes 393224 | tf_op jit(solution)/shard_map/ppermute | solution.py:257
  12.3 5.0 %collective-permute-start.2 = (bf16[16,4096]{1,0:T(8,128)(2,1)S(1)}, bf16[16,4096]{1,0:T(8,128)(2,1)S(1)}, u32[]{:S(2)}, u32[]{:S(2)}) collective-permute-start(bf16[16,4096]{1,0:T(8,128)(2,1)S(1)} %collective-permute-done.refs_1_.__), channel_id=1, source_target_pairs={{0,4},{4,0},{8,12},{12,8},{1,5},{5,1},{9,13},{13,9},{2,6},{6,2},{1... | collective-permute-start | bytes 393224 | tf_op jit(solution)/shard_map/ppermute | solution.py:257
  12.8 4.5 %copy-start.1 = (bf16[1,4096,64]{1,2,0:T(8,128)(2,1)S(1)}, bf16[1,4096,64]{1,2,0:T(8,128)(2,1)}, u32[]{:S(2)}) copy-start(bf16[1,4096,64]{1,2,0:T(8,128)(2,1)} %param.12) | copy-start | bytes 1572868
  12.8 4.5 %copy-start.2 = (bf16[16,4096]{1,0:T(8,128)(2,1)S(1)}, bf16[16,4096]{1,0:T(8,128)(2,1)}, u32[]{:S(2)}) copy-start(bf16[16,4096]{1,0:T(8,128)(2,1)} %refs_0_.1) | copy-start | bytes 393220
  12.8 4.5 %copy-start.3 = (bf16[4096]{0:T(1024)(128)(2,1)S(1)}, bf16[4096]{0:T(1024)(128)(2,1)}, u32[]{:S(2)}) copy-start(bf16[4096]{0:T(1024)(128)(2,1)} %gain_ref.1) | copy-start | bytes 24580
  17.8 4.7 %collective-permute-start.3 = (bf16[64,128]{1,0:T(8,128)(2,1)S(1)}, bf16[64,128]{1,0:T(8,128)(2,1)S(1)}, u32[]{:S(2)}, u32[]{:S(2)}) collective-permute-start(bf16[64,128]{1,0:T(8,128)(2,1)S(1)} %get-tuple-element.29), channel_id=1, source_target_pairs={{0,8},{4,12},{8,0},{12,4},{1,9},{5,13},{9,1},{13,5},{2,10},{6,14},... | collective-permute-start | bytes 49160 | tf_op jit(solution)/shard_map/ppermute | solution.py:257
  22.5 4.7 %collective-permute-start.4 = (bf16[64,128]{1,0:T(8,128)(2,1)S(1)}, bf16[64,128]{1,0:T(8,128)(2,1)S(1)}, u32[]{:S(2)}, u32[]{:S(2)}) collective-permute-start(bf16[64,128]{1,0:T(8,128)(2,1)S(1)} %add.6.refs_1_), channel_id=1, source_target_pairs={{0,4},{4,0},{8,12},{12,8},{1,5},{5,1},{9,13},{13,9},{2,6},{6,2},{1... | collective-permute-start | bytes 49160 | tf_op jit(solution)/shard_map/ppermute | solution.py:257
  25.9 1.5 %collective-permute-start.5 = (bf16[32,3328]{1,0:T(8,128)(2,1)S(1)}, bf16[32,3328]{1,0:T(8,128)(2,1)S(1)}, u32[]{:S(2)}, u32[]{:S(2)}) collective-permute-start(bf16[32,3328]{1,0:T(8,128)(2,1)S(1)} %get-tuple-element.32), channel_id=1, source_target_pairs={{0,1},{1,0},{2,3},{3,2},{4,5},{5,4},{6,7},{7,6},{8,9},{9,8},{10,11... | collective-permute-start | bytes 638984 | tf_op jit(solution)/shard_map/ppermute | solution.py:257
  25.9 7.6 %copy-start = (bf16[4,64,4096]{2,1,0:T(8,128)(2,1)S(1)}, bf16[4,64,4096]{2,1,0:T(8,128)(2,1)}, u32[]{:S(2)}) copy-start(bf16[4,64,4096]{2,1,0:T(8,128)(2,1)} %up_ref.1) | copy-start | bytes 6291460
  27.5 1.8 %collective-permute-start.7 = (bf16[32,896]{1,0:T(8,128)(2,1)S(1)}, bf16[32,896]{1,0:T(8,128)(2,1)S(1)}, u32[]{:S(2)}, u32[]{:S(2)}) collective-permute-start(bf16[32,896]{1,0:T(8,128)(2,1)S(1)} %get-tuple-element.36), channel_id=1, source_target_pairs={{0,1},{1,0},{2,3},{3,2},{4,5},{5,4},{6,7},{7,6},{8,9},{9,8},{10,11... | collective-permute-start | bytes 172040 | tf_op jit(solution)/shard_map/ppermute | solution.py:257
  27.8 5.7 %collective-permute-start.6 = (bf16[16,3328]{1,0:T(8,128)(2,1)S(1)}, bf16[16,3328]{1,0:T(8,128)(2,1)S(1)}, u32[]{:S(2)}, u32[]{:S(2)}) collective-permute-start(bf16[16,3328]{1,0:T(8,128)(2,1)S(1)} %get-tuple-element.34), channel_id=1, source_target_pairs={{0,2},{2,0},{1,3},{3,1},{4,6},{6,4},{5,7},{7,5},{8,10},{10,8},{9,1... | collective-permute-start | bytes 319496 | tf_op jit(solution)/shard_map/ppermute | solution.py:257
  29.5 4.0 %collective-permute-start.8 = (bf16[16,896]{1,0:T(8,128)(2,1)S(1)}, bf16[16,896]{1,0:T(8,128)(2,1)S(1)}, u32[]{:S(2)}, u32[]{:S(2)}) collective-permute-start(bf16[16,896]{1,0:T(8,128)(2,1)S(1)} %get-tuple-element.38), channel_id=1, source_target_pairs={{0,2},{2,0},{1,3},{3,1},{4,6},{6,4},{5,7},{7,5},{8,10},{10,8},{9,1... | collective-permute-start | bytes 86024 | tf_op jit(solution)/shard_map/ppermute | solution.py:257
